TPU v7x, 256 devices: a whole 4x4x8 slice. The times are simulated.
256 devices in a mesh: frow: 8 (over x, core), fcol: 32 (over z, y).
Axes of the slice: x: 4, y: 4, z: 8, core: 2. Of those that a mesh axis runs over, the one named last changes fastest.
Arguments:
- facet_image: bfloat16 [4096, 16384], P('frow', 'fcol'), may hold values from -6 to 6
- row_offsets: int32 [2], replicated, may hold values from 0 to 65280
- col_offsets: int32 [2], replicated, may hold values from 0 to 65280
- vis_subgrid: int32 [131072], P(('frow', 'fcol')), may hold values from 0 to 3
- vis_u: int32 [131072], P(('frow', 'fcol')), may hold values from 0 to 255
- vis_v: int32 [131072], P(('frow', 'fcol')), may hold values from 0 to 255
- observed: float32 [2, 131072], P(None, ('frow', 'fcol')), may hold values from -6 to 6
Outputs:
- facet_residual: float32 [4096, 16384], P('frow', 'fcol')
- residual_vis: float32 [2, 131072], P(None, ('frow', 'fcol'))
Inputs may be any that keep to these rules, and one draw needn't show every extreme that they name: `vis_subgrid`: subgrid numbers count row by row over the 2 x 2 subgrids.
All inputs are finite; a program needn't handle non-finite values.
Results may differ from a plain program's by a relative error of at most 0.023.
Values may be sent and summed in bfloat16 or wider, within the bound.
No kernel may reach another device: no remote copies, remote signals or barrier semaphores. Data moves between devices by JAX's collectives and lax.ppermute only.
A program may use at most 64 MiB of HBM per device.

v0:
```python
import math

import jax
import jax.numpy as jnp
from jax import lax
from jax.sharding import PartitionSpec as P

SKY = 65536
SG = 256
NR = 2
NC = 2


def wrapped(frequency, position):
    high_part = frequency // 256
    low_part = frequency % 256
    return (high_part * (position * 256 % SKY) + low_part * position) % SKY


def sky_tables(start, positions):
    frequency = start + jnp.arange(SG, dtype=jnp.int32)[:, None]
    angles = wrapped(frequency, positions[None, :]).astype(jnp.float32) * (2.0 * math.pi / SKY)
    return (jnp.cos(angles).astype(jnp.bfloat16), jnp.sin(angles).astype(jnp.bfloat16))


def grid_tables():
    counter = jnp.arange(SG, dtype=jnp.int32)
    angles = (counter[:, None] * counter[None, :] % SG).astype(jnp.float32) * (2.0 * math.pi / SG)
    return (jnp.cos(angles).astype(jnp.bfloat16), jnp.sin(angles).astype(jnp.bfloat16))


def contract_first(left, right):
    return lax.dot_general(
        left, right, (((0,), (0,)), ((), ())), preferred_element_type=jnp.float32
    )


def contract_last(left, right):
    return lax.dot_general(
        left, right, (((1,), (1,)), ((), ())), preferred_element_type=jnp.float32
    )


def shards(facet_image, row_offsets, col_offsets, vis_subgrid, vis_u, vis_v, observed):
    f32 = jnp.float32
    bf16 = jnp.bfloat16
    rows_count = lax.axis_size("frow")
    cols_count = lax.axis_size("fcol")
    facet_side = facet_image.shape[0]
    subgrids = NR * NC
    scale_in = 1.0 / (facet_side * math.sqrt(rows_count * cols_count))
    scale_out = 1.0 / (SG * math.sqrt(subgrids))
    row_pos = lax.axis_index("frow") * (SKY // rows_count) + jnp.arange(
        facet_side, dtype=jnp.int32
    ) * (SKY // (rows_count * facet_side))
    col_pos = lax.axis_index("fcol") * (SKY // cols_count) + jnp.arange(
        facet_side, dtype=jnp.int32
    ) * (SKY // (cols_count * facet_side))
    row_tabs = [
        jnp.concatenate(sky_tables(row_offsets[row_pick], row_pos), 0) for row_pick in range(NR)
    ]
    col_tabs = [
        jnp.concatenate(sky_tables(col_offsets[col_pick], col_pos), 0) for col_pick in range(NC)
    ]
    col_halves = [
        contract_last(facet_image, col_tabs[col_pick]).astype(bf16) for col_pick in range(NC)
    ]
    blocks_out = []
    for row_pick in range(NR):
        for col_pick in range(NC):
            product = jnp.dot(row_tabs[row_pick], col_halves[col_pick], preferred_element_type=f32)
            part_real = product[:SG, :SG] - product[SG:, SG:]
            part_imag = -(product[:SG, SG:] + product[SG:, :SG])
            blocks_out.append(jnp.concatenate([part_real, part_imag], 1) * scale_in)
    stacked = jnp.concatenate(blocks_out, 0)
    summed = lax.psum(stacked, ("frow", "fcol"))
    grid_bf = summed.astype(bf16)
    kcos, ksin = grid_tables()
    forward_block = jnp.concatenate(
        [jnp.concatenate([kcos, ksin], 1), jnp.concatenate([-ksin, kcos], 1)], 0
    )
    w_both = (
        jnp.dot(grid_bf, forward_block, preferred_element_type=f32)
        .astype(bf16)
        .reshape(subgrids, SG, 2 * SG)
    )
    with_cos = jnp.einsum("au,sav->suv", kcos, w_both, preferred_element_type=f32)
    with_sin = jnp.einsum("au,sav->suv", ksin, w_both, preferred_element_type=f32)
    hat_real = (with_cos[:, :, :SG] - with_sin[:, :, SG:]) / SG
    hat_imag = (with_sin[:, :, :SG] + with_cos[:, :, SG:]) / SG
    cell_ids = (vis_subgrid * SG + vis_u) * SG + vis_v
    model_vis = jnp.stack(
        [jnp.take(hat_real.reshape(-1), cell_ids), jnp.take(hat_imag.reshape(-1), cell_ids)]
    )
    residual = observed - model_vis
    cells_all = subgrids * SG * SG
    inverse_block = jnp.concatenate(
        [jnp.concatenate([kcos, -ksin], 1), jnp.concatenate([ksin, kcos], 1)], 0
    )
    local_real = jax.ops.segment_sum(residual[0], cell_ids, num_segments=cells_all)
    local_imag = jax.ops.segment_sum(residual[1], cell_ids, num_segments=cells_all)
    ghat_real, ghat_imag = lax.psum((local_real, local_imag), ("frow", "fcol"))
    ghat_both = jnp.concatenate(
        [
            ghat_real.reshape(subgrids * SG, SG).astype(bf16),
            ghat_imag.reshape(subgrids * SG, SG).astype(bf16),
        ],
        1,
    )
    v_flat = jnp.dot(ghat_both, inverse_block, preferred_element_type=f32).astype(bf16)
    v_both = v_flat.reshape(subgrids, SG, 2 * SG)
    back_cos = jnp.einsum("au,suv->sav", kcos, v_both, preferred_element_type=f32)
    back_sin = jnp.einsum("au,suv->sav", ksin, v_both, preferred_element_type=f32)
    back_real = ((back_cos[:, :, :SG] + back_sin[:, :, SG:]) / SG).astype(bf16)
    back_imag = ((back_cos[:, :, SG:] - back_sin[:, :, :SG]) / SG).astype(bf16)
    image = jnp.zeros((facet_side, facet_side), f32)
    for col_pick in range(NC):
        u_both = jnp.zeros((facet_side, 2 * SG), f32)
        for row_pick in range(NR):
            sub_index = row_pick * NC + col_pick
            g_real = back_real[sub_index]
            g_imag = back_imag[sub_index]
            right_side = jnp.concatenate(
                [jnp.concatenate([g_real, g_imag], 1), jnp.concatenate([-g_imag, g_real], 1)], 0
            )
            u_both = u_both + contract_first(row_tabs[row_pick], right_side)
        col_cos = col_tabs[col_pick][:SG]
        col_sin = col_tabs[col_pick][SG:]
        image = image + jnp.dot(
            u_both.astype(bf16), jnp.concatenate([col_cos, -col_sin], 0), preferred_element_type=f32
        )
    return (image * scale_out, residual)


def solution(mesh):
    in_specs = (
        P("frow", "fcol"),
        P(),
        P(),
        P(("frow", "fcol")),
        P(("frow", "fcol")),
        P(("frow", "fcol")),
        P(None, ("frow", "fcol")),
    )
    out_specs = (P("frow", "fcol"), P(None, ("frow", "fcol")))
    return jax.shard_map(shards, mesh=mesh, in_specs=in_specs, out_specs=out_specs, check_vma=False)
```

profile of v0, /device:TPU:1, one launch (start us, length us, event | category | flops | bytes accessed | tf_op | source)
XLA Modules:
  0.0 241.6 jit_solution(13558053591533307488)
XLA Ops:
  0.7 1.3 fusion.145
  2.0 0.7 and_select_fusion.4
  2.7 0.7 and_select_fusion.2
  3.3 4.6 %sine_convert_fusion.2 = (bf16[256,512]{1,0:T(8,128)(2,1)S(1)}, bf16[256,512]{1,0:T(8,128)(2,1)S(1)}, bf16[256,512]{1,0:T(8,128)(2,1)S(1)}, bf16[256,512]{1,0:T(8,128)(2,1)S(1)}) fusion(s32[512]{0:T(512)S(1)} %get-tuple-element.54, s32[256]{0:T(256)S(1)} %get-tuple-element.55, s32[512]{0:T(512)S(1)} %get-tuple-element.53, s32[256]{0:T(256)S(1)} %get-tuple-element.56, ...), kind=kLoop, calls=%fused_computation.116 | loop fusion | flops 4718592 | bytes 1056768 | tf_op jit(solution)/shard_map/convert_element_type | solution.py:23
  8.0 0.7 copy-done.5
  8.7 0.5 convolution_convert_fusion.3
  9.2 0.6 fusion.144
  9.8 0.7 and_select_fusion.6
  10.4 0.7 and_select_fusion
  11.1 4.6 %cosine_convert_fusion.3 = (bf16[256,512]{1,0:T(8,128)(2,1)S(1)}, bf16[256,512]{1,0:T(8,128)(2,1)S(1)}, bf16[256,512]{1,0:T(8,128)(2,1)S(1)}, bf16[256,512]{1,0:T(8,128)(2,1)S(1)}) fusion(s32[512]{0:T(512)S(1)} %get-tuple-element.60, s32[256]{0:T(256)S(1)} %get-tuple-element.61, s32[512]{0:T(512)S(1)} %get-tuple-element.59, s32[256]{0:T(256)S(1)} %get-tuple-element.62, ...), kind=kLoop, calls=%fused_computation.123 | loop fusion | flops 4718592 | bytes 1056768 | tf_op jit(solution)/shard_map/convert_element_type | solution.py:23
  15.8 0.5 fusion.142
  16.3 0.1 slice_subtract_fusion.5
  16.4 0.5 convolution_convert_fusion.2
  16.9 0.5 fusion.141
  17.5 0.5 fusion.140
  18.1 0.5 fusion.139
  18.6 0.2 pad_maximum_fusion
  18.9 90.1 %all-reduce.3 = bf16[1024,512]{0,1:T(8,128)(2,1)} all-reduce(f32[1024,512]{0,1:T(8,128)S(1)} %pad_maximum_fusion), channel_id=1, replica_groups=mesh['frow'=8,'fcol'=32] {'frow','fcol'}, use_global_device_ids=true, to_apply=%region_0.1 | all-reduce | flops 524288 | bytes 3145728 | tf_op jit(solution)/shard_map/psum | solution.py:76
  109.1 1.1 sine_convert_fusion.4
  110.2 1.0 fusion.100
  111.2 2.0 convolution_convert_fusion.1
  113.2 1.4 convolution_bitcast_fusion.2
  114.6 1.4 convolution_bitcast_fusion.3
  116.0 1.3 fusion.9
  117.3 0.3 copy.16
  117.7 0.5 copy.24
  118.2 0.1 copy-done.22
  118.3 0.6 compare_select_fusion
  118.9 4.3 %gather_fusion.1 = f32[512]{0:T(512)} fusion(f32[262144]{0:T(1024)S(1)} %bitcast.67, s32[1024]{0:T(1024)S(1)} %pad_clamp_fusion), kind=kCustom, calls=%fused_computation.1.clone | custom fusion | bytes 6144 | tf_op jit(solution)/shard_map/jit(_take)/gather | solution.py:93
  123.2 1.6 copy.15
  124.8 0.5 copy.23
  125.4 3.1 %gather_fusion = f32[512]{0:T(512)S(1)} fusion(f32[262144]{0:T(1024)S(1)} %bitcast.68, s32[1024]{0:T(1024)S(1)} %pad_clamp_fusion), kind=kCustom, calls=%fused_computation.clone | custom fusion | bytes 6144 | tf_op jit(solution)/shard_map/jit(_take)/gather | solution.py:93
  128.6 0.6 fusion.143
  129.2 3.5 %scatter_custom_fusion = f32[262144]{0:T(1024)S(1)} fusion(s32[512]{0:T(512)S(1)} %copy-done.18, f32[512]{0:T(512)S(1)} %bitcast.78, f32[]{:T(128)} %constant.157.clone.1), kind=kCustom, calls=%fused_computation.120 | custom fusion | flops 512 | bytes 1048580 | tf_op jit(solution)/shard_map/scatter-add | solution.py:100
  132.7 3.7 %scatter_custom_fusion.1 = f32[262144]{0:T(1024)S(1)} fusion(s32[512]{0:T(512)} %get-tuple-element.6, f32[512]{0:T(512)} %bitcast.77, f32[]{:T(128)} %constant.157.clone.1), kind=kCustom, calls=%fused_computation.118 | custom fusion | flops 512 | bytes 1049088 | tf_op jit(solution)/shard_map/scatter-add | solution.py:101
  136.4 84.2 %all-reduce.4 = (bf16[262144]{0:T(1024)(128)(2,1)}, bf16[262144]{0:T(1024)(128)(2,1)}) all-reduce(f32[262144]{0:T(1024)S(1)} %scatter_custom_fusion.1, f32[262144]{0:T(1024)S(1)} %scatter_custom_fusion), channel_id=1, replica_groups=mesh['frow'=8,'fcol'=32] {'frow','fcol'}, use_global_device_ids=true, to_apply=%region_4.6 | all-reduce | flops 524288 | bytes 3145728 | tf_op jit(solution)/shard_map/psum | solution.py:102
  220.6 1.3 convert_element_type.148
  221.8 1.2 convert_element_type.150
  223.1 0.7 convolution_convert_fusion
  223.8 1.4 convolution_bitcast_fusion
  225.2 1.4 convolution_bitcast_fusion.1
  226.6 0.4 fusion.5
  227.1 0.8 copy-done.2
  227.9 1.5 fusion.59
  229.4 1.5 fusion.36
  230.9 4.4 %fusion.138 = (bf16[256,512]{1,0:T(8,128)(2,1)S(1)}, bf16[256,512]{1,0:T(8,128)(2,1)S(1)}) fusion(s32[512]{0:T(512)S(1)} %get-tuple-element.54, s32[256]{0:T(256)S(1)} %copy-done.15, s32[512]{0:T(512)S(1)} %get-tuple-element.53, s32[256]{0:T(256)S(1)} %copy-done.17, s32[256]{0:T(256)S(1)} %get-tuple-element.55, s32[256]{0:T(256)S(1)} %copy-done.13), kind=kLoop, calls=%fused_computation.238 | loop fusion | flops 5242880 | bytes 532480 | tf_op jit(solution)/shard_map/neg | solution.py:130
  235.3 3.0 %fusion.3 = f32[512,512]{1,0:T(8,128)} fusion(f32[512,512]{1,0:T(8,128)} %fusion.36, bf16[256,512]{1,0:T(8,128)(2,1)S(1)} %copy-done.6, bf16[256,256]{0,1:T(8,128)(2,1)S(1)} %get-tuple-element.29, bf16[256,256]{0,1:T(8,128)(2,1)S(1)} %get-tuple-element.25, bf16[256,256]{0,1:T(8,128)(2,1)S(1)} %get-tuple-element.21, ...), kind=kOutput, calls=%fused_computation.19 | convolution fusion | flops 541589504 | bytes 3538944 | tf_op jit(solution)/shard_map/dot_general | solution.py:129
  238.3 3.3 %fusion = f32[512,512]{1,0:T(8,128)} fusion(f32[512,512]{1,0:T(8,128)} %fusion.3, f32[512,512]{1,0:T(8,128)} %fusion.59, bf16[256,512]{1,0:T(8,128)(2,1)S(1)} %copy-done.4, bf16[256,256]{0,1:T(8,128)(2,1)S(1)} %get-tuple-element.27, bf16[256,256]{0,1:T(8,128)(2,1)S(1)} %get-tuple-element.23, bf16[256,256]{0,1:T(8,128)(2,1)S(1)} %get-tuple-element.19, ...), kind=kOutput, calls=%fused_computation.12 | convolution fusion | flops 542113792 | bytes 4587520 | tf_op jit(solution)/shard_map/dot_general | solution.py:129
  (62 shorter events, 0.6 us)
Async XLA Ops:
  0.6 8.1 %copy-start = (bf16[512,512]{1,0:T(8,128)(2,1)S(1)}, bf16[512,512]{1,0:T(8,128)(2,1)}, u32[]{:S(2)}) copy-start(bf16[512,512]{1,0:T(8,128)(2,1)} %param.9) | copy-start | bytes 1572868
  0.6 8.5 %copy-start.24 = (s32[2]{0:T(128)S(1)}, s32[2]{0:T(128)}, u32[]{:S(2)}) copy-start(s32[2]{0:T(128)} %param.10) | copy-start | bytes 28
  2.7 13.6 %copy-start.12 = (s32[256]{0:T(256)}, s32[256]{0:T(256)S(1)}, u32[]{:S(2)}) copy-start(s32[256]{0:T(256)S(1)} %get-tuple-element.56) | copy-start | bytes 3076
  3.3 12.9 %copy-start.14 = (s32[256]{0:T(256)}, s32[256]{0:T(256)S(1)}, u32[]{:S(2)}) copy-start(s32[256]{0:T(256)S(1)} %get-tuple-element.57) | copy-start | bytes 3076
  3.3 12.9 %copy-start.16 = (s32[256]{0:T(256)}, s32[256]{0:T(256)S(1)}, u32[]{:S(2)}) copy-start(s32[256]{0:T(256)S(1)} %get-tuple-element.58) | copy-start | bytes 3076
  8.0 0.7 copy-start.5
  8.0 8.4 %copy-start.3 = (bf16[256,512]{1,0:T(8,128)(2,1)}, bf16[256,512]{1,0:T(8,128)(2,1)S(1)}, u32[]{:S(2)}) copy-start(bf16[256,512]{1,0:T(8,128)(2,1)S(1)} %get-tuple-element.45) | copy-start | bytes 786436
  15.7 1.1 copy-start.1
  110.1 3.0 %copy-start.7 = (bf16[256,256]{1,0:T(8,128)(2,1)}, bf16[256,256]{1,0:T(8,128)(2,1)S(1)}, u32[]{:S(2)}) copy-start(bf16[256,256]{1,0:T(8,128)(2,1)S(1)} %get-tuple-element.66) | copy-start | bytes 393220
  111.2 2.0 copy-start.9
  117.3 0.9 copy-start.21
  117.6 0.7 copy-start.22
  117.7 0.7 copy-start.23
  125.3 3.2 %copy-start.18 = (s32[512]{0:T(512)S(1)}, s32[512]{0:T(512)}, u32[]{:S(2)}) copy-start(s32[512]{0:T(512)} %get-tuple-element.6) | copy-start | bytes 6148
  125.3 3.2 %copy-start.19 = (f32[512]{0:T(512)S(1)}, f32[512]{0:T(512)}, u32[]{:S(2)}) copy-start(f32[512]{0:T(512)} %gather_fusion.1) | copy-start | bytes 6148
  125.3 3.2 %copy-start.20 = (f32[2,512]{1,0:T(2,128)S(1)}, f32[2,512]{1,0:T(2,128)}, u32[]{:S(2)}) copy-start(f32[2,512]{1,0:T(2,128)} %param.15) | copy-start | bytes 12292
  128.6 92.0 %copy-start.11 = (f32[2,512]{1,0:T(2,128)}, f32[2,512]{1,0:T(2,128)S(1)}, u32[]{:S(2)}) copy-start(f32[2,512]{1,0:T(2,128)S(1)} %maximum_subtract_fusion) | copy-start | bytes 12292
  220.6 2.5 %copy-start.8 = (bf16[256,256]{1,0:T(8,128)(2,1)S(1)}, bf16[256,256]{1,0:T(8,128)(2,1)}, u32[]{:S(2)}) copy-start(bf16[256,256]{1,0:T(8,128)(2,1)} %copy-done.7) | copy-start | bytes 393220
  220.6 2.5 %copy-start.10 = (bf16[256,256]{1,0:T(8,128)(2,1)S(1)}, bf16[256,256]{1,0:T(8,128)(2,1)}, u32[]{:S(2)}) copy-start(bf16[256,256]{1,0:T(8,128)(2,1)} %copy-done.9) | copy-start | bytes 393220
  227.0 1.0 copy-start.2
  229.4 1.5 copy-start.13
  229.4 1.5 copy-start.15
  229.4 1.5 copy-start.17
  229.4 5.8 %copy-start.6 = (bf16[256,512]{1,0:T(8,128)(2,1)S(1)}, bf16[256,512]{1,0:T(8,128)(2,1)}, u32[]{:S(2)}) copy-start(bf16[256,512]{1,0:T(8,128)(2,1)} %copy-done.5) | copy-start | bytes 786436
  235.3 3.0 %copy-start.4 = (bf16[256,512]{1,0:T(8,128)(2,1)S(1)}, bf16[256,512]{1,0:T(8,128)(2,1)}, u32[]{:S(2)}) copy-start(bf16[256,512]{1,0:T(8,128)(2,1)} %copy-done.3) | copy-start | bytes 786436
where the time goes:
time: 242 us
  blocking collectives  174 us (72%)
  other arithmetic  28.6 us (12%)
  matrix products  20.3 us (8%)
  local copies, waits for them, and re-layouts  17.1 us (7%)
    psum x1, blocking collectives, shards(): summed = lax.psum(stacked, ('frow', 'fcol'))  90.1 us
    psum x1, blocking collectives, shards(): ghat_real, ghat_imag = lax.psum((local_real, local_imag), ('frow', 'fcol'))  84.2 us
    dot_general x2, matrix products, shards(): jnp.dot(u_both.astype(bf16), jnp.concatenate([col_cos, -col_sin], 0), pre...  6.28 us

commit v1 on v0

v1 whole, which is shorter than its diff:
```python
import math

import jax
import jax.numpy as jnp
import numpy as np
from jax import lax
from jax.sharding import PartitionSpec as P

SKY = 65536
SG = 256
NR = 2
NC = 2
HALF = SG // 2
BOTH = ("frow", "fcol")


def wrapped(frequency, position):
    high_part = frequency // 256
    low_part = frequency % 256
    return (high_part * (position * 256 % SKY) + low_part * position) % SKY


def phase_tables(frequency, position):
    angles = wrapped(frequency, position).astype(jnp.float32) * (2.0 * math.pi / SKY)
    return jnp.cos(angles), jnp.sin(angles)


def outer_tables(frequency, step, position):
    coarse_c, coarse_s = phase_tables(frequency[::16, None], position[None, :])
    fine_c, fine_s = phase_tables(step * jnp.arange(16, dtype=jnp.int32)[:, None], position[None, :])
    cos = coarse_c[:, None] * fine_c[None] - coarse_s[:, None] * fine_s[None]
    sin = coarse_s[:, None] * fine_c[None] + coarse_c[:, None] * fine_s[None]
    shape = (frequency.shape[0], position.shape[0])
    return cos.reshape(shape).astype(jnp.bfloat16), sin.reshape(shape).astype(jnp.bfloat16)


def grid_tables():
    counter = np.arange(SG)
    angles = (counter[:, None] * counter[None, :] % SG).astype(np.float64) * (2.0 * math.pi / SG)
    return (jnp.asarray(np.cos(angles), jnp.bfloat16), jnp.asarray(np.sin(angles), jnp.bfloat16))


def exchange(blocks, axes, groups):
    return lax.all_to_all(blocks, axes, 0, 0, tiled=True, axis_index_groups=groups)


def dot(left, right):
    return jnp.dot(left, right, preferred_element_type=jnp.float32)


def contract_first(left, right):
    return lax.dot_general(left, right, (((0,), (0,)), ((), ())), preferred_element_type=jnp.float32)


def contract_last(left, right):
    return lax.dot_general(left, right, (((1,), (1,)), ((), ())), preferred_element_type=jnp.float32)


def shards(facet, row_offsets, col_offsets, vis_subgrid, vis_u, vis_v, observed):
    f32, bf16 = jnp.float32, jnp.bfloat16
    rows_count, cols_count = lax.axis_size("frow"), lax.axis_size("fcol")
    side = facet.shape[0]
    n_vis = vis_u.shape[0]
    chips = rows_count // 2
    x_groups = [[2 * chip + core for chip in range(chips)] for core in range(2)]
    core_groups = [[2 * chip, 2 * chip + 1] for chip in range(chips)]
    grid_groups = [
        [(2 * chip + core) * cols_count + col for core in range(2) for col in range(cols_count)] for chip in range(chips)
    ]
    row_index, col_index = lax.axis_index("frow"), lax.axis_index("fcol")
    core = row_index % 2
    chip = row_index // 2
    scale_in = 1.0 / (side * math.sqrt(rows_count * cols_count))
    scale_out = 1.0 / (SG * math.sqrt(NR * NC))
    swap = [(index, index ^ 1) for index in range(rows_count)]

    facet_pair = jnp.concatenate([facet, lax.ppermute(facet, "frow", swap)], 0)
    vis_own = jnp.concatenate(
        [jnp.stack([vis_subgrid, vis_u, vis_v]).astype(bf16), observed.astype(bf16), jnp.zeros((3, n_vis), bf16)], 0
    )
    vis_pair = jnp.concatenate([vis_own, lax.ppermute(vis_own, "frow", swap)], 1)
    vis_all = exchange(jnp.broadcast_to(vis_pair, (chips,) + vis_pair.shape), "frow", x_groups)
    vis_n = vis_all.transpose(1, 0, 2).reshape(8, -1)

    counter = jnp.arange(SG, dtype=jnp.int32)
    line = jnp.arange(side, dtype=jnp.int32)
    row_step = SKY // (rows_count * side)
    col_step = SKY // (cols_count * side)
    row_pos = row_index * (SKY // rows_count) + line * row_step
    row_pos_pair = jnp.concatenate([row_pos, (row_index ^ 1) * (SKY // rows_count) + line * row_step])
    col_pos = col_index * (SKY // cols_count) + line * col_step

    row_tabs = [outer_tables(row_offsets[r] + counter, 1, row_pos_pair) for r in range(NR)]
    col_tabs = [outer_tables(col_offsets[c] + counter, 1, col_pos) for c in range(NC)]

    parts = []
    halves = []
    for c in range(NC):
        tab = jnp.concatenate([lax.dynamic_slice_in_dim(t, core * HALF, HALF, 0) for t in col_tabs[c]], 0)
        halves.append(contract_last(facet_pair, tab).astype(bf16))
    right = jnp.concatenate(halves, 1)
    for r in range(NR):
        with_cos = dot(row_tabs[r][0], right)
        with_sin = dot(row_tabs[r][1], right)
        for c in range(NC):
            at = 2 * c * HALF
            cp, cq = with_cos[:, at:at + HALF], with_cos[:, at + HALF:at + 2 * HALF]
            sp, sq = with_sin[:, at:at + HALF], with_sin[:, at + HALF:at + 2 * HALF]
            parts.append(jnp.stack([(cp - sq) * scale_in, -(cq + sp) * scale_in]).astype(bf16))
    mine = exchange(jnp.stack(parts), "frow", x_groups).astype(f32).sum(0).astype(bf16)

    in_sub = vis_n[0:1] == chip.astype(bf16)
    vis_u_hot = ((vis_n[1:2] == counter[:, None].astype(bf16)) & in_sub).astype(bf16)
    v_half = (core * HALF + jnp.arange(HALF, dtype=jnp.int32))[:, None].astype(bf16)
    v_hot = vis_n[2:3] == v_half
    zero = jnp.zeros((), bf16)
    weights = jnp.concatenate(
        [
            jnp.where(v_hot, vis_n[3:4], zero),
            jnp.where(v_hot, vis_n[4:5], zero),
            v_hot.astype(bf16),
        ],
        0,
    )
    sums = contract_last(vis_u_hot, weights).astype(bf16)
    planes = jnp.concatenate([mine, sums.reshape(SG, 3, HALF).transpose(1, 0, 2)], 0)
    rows_each = SG // cols_count
    pieces = planes.reshape(5, cols_count, rows_each, HALF).transpose(1, 0, 2, 3)
    piece = exchange(pieces, "fcol", None).astype(f32).sum(0).astype(bf16)
    gathered = exchange(jnp.broadcast_to(piece, (2 * cols_count,) + piece.shape), BOTH, grid_groups)
    full = (
        gathered.reshape(2, cols_count, 5, rows_each, HALF)
        .transpose(2, 1, 3, 0, 4)
        .reshape(5, SG, SG)
    )

    kcos, ksin = grid_tables()
    forward_block = jnp.concatenate(
        [jnp.concatenate([kcos, ksin], 1), jnp.concatenate([-ksin, kcos], 1)], 0
    )
    inverse_block = jnp.concatenate(
        [jnp.concatenate([kcos, -ksin], 1), jnp.concatenate([ksin, kcos], 1)], 0
    )
    w_both = dot(jnp.concatenate([full[0], full[1]], 1), forward_block).astype(bf16)
    with_cos = dot(kcos, w_both)
    with_sin = dot(ksin, w_both)
    hat_real = (with_cos[:, :SG] - with_sin[:, SG:]) / SG
    hat_imag = (with_sin[:, :SG] + with_cos[:, SG:]) / SG
    count = full[4].astype(f32)
    ghat = jnp.concatenate(
        [full[2].astype(f32) - count * hat_real, full[3].astype(f32) - count * hat_imag], 1
    ).astype(bf16)
    v_both = dot(ghat, inverse_block).astype(bf16)
    back_cos = dot(kcos, v_both)
    back_sin = dot(ksin, v_both)
    back = jnp.stack(
        [
            ((back_cos[:, :SG] + back_sin[:, SG:]) / SG).astype(bf16),
            ((back_cos[:, SG:] - back_sin[:, :SG]) / SG).astype(bf16),
        ]
    )
    my_half = lax.dynamic_slice_in_dim(back, core * HALF, HALF, 1)
    by_chip = exchange(jnp.broadcast_to(my_half, (chips,) + my_half.shape), "frow", x_groups)
    by_core = exchange(jnp.broadcast_to(by_chip, (2,) + by_chip.shape), "frow", core_groups)
    back_all = by_core.transpose(1, 2, 0, 3, 4).reshape(NR * NC, 2, SG, SG)

    ask = vis_all[:, :3, :n_vis].transpose(1, 0, 2).reshape(3, -1)
    u_hot = ((ask[1:2] == counter[:, None].astype(bf16)) & (ask[0:1] == chip.astype(bf16))).astype(bf16)
    v_hot_ask = (ask[2:3] == counter[:, None].astype(bf16)).astype(f32)
    hat_both = jnp.concatenate([hat_real, hat_imag], 1)
    hat_high = hat_both.astype(bf16)
    hat_low = (hat_both - hat_high.astype(f32)).astype(bf16)
    lines = contract_first(hat_high, u_hot) + contract_first(hat_low, u_hot)
    values = jnp.stack([(lines[:SG] * v_hot_ask).sum(0), (lines[SG:] * v_hot_ask).sum(0)])
    answers = exchange(values.reshape(2, chips, n_vis).transpose(1, 0, 2), "frow", x_groups)
    residual = observed - answers.sum(0)

    image = jnp.zeros((side, side), f32)
    for c in range(NC):
        u_both = jnp.zeros((side, 2 * SG), f32)
        for r in range(NR):
            g_real, g_imag = back_all[r * NC + c, 0], back_all[r * NC + c, 1]
            right_side = jnp.concatenate(
                [jnp.concatenate([g_real, g_imag], 1), jnp.concatenate([-g_imag, g_real], 1)], 0
            )
            tab = jnp.concatenate([t[:, :side] for t in row_tabs[r]], 0)
            u_both = u_both + contract_first(tab, right_side)
        image = image + dot(u_both.astype(bf16), jnp.concatenate([col_tabs[c][0], -col_tabs[c][1]], 0))
    return (image * scale_out, residual)


def solution(mesh):
    in_specs = (
        P("frow", "fcol"),
        P(),
        P(),
        P(("frow", "fcol")),
        P(("frow", "fcol")),
        P(("frow", "fcol")),
        P(None, ("frow", "fcol")),
    )
    out_specs = (P("frow", "fcol"), P(None, ("frow", "fcol")))
    return jax.shard_map(shards, mesh=mesh, in_specs=in_specs, out_specs=out_specs, check_vma=False)
```

time: 242 us -> 140 us (0.58)
  blocking collectives: 174 us -> 26.9 us
  waiting for transfers between devices: 0 us -> 37.1 us
  starting transfers between devices: 0 us -> 25.9 us
  other arithmetic: 28.6 us -> 13.9 us
  local copies, waits for them, and re-layouts: 17.1 us -> 13.7 us
    psum x2 -> x0, blocking collectives: 174 us -> none  [the longest x1 90.1 us: shards(): summed = lax.psum(stacked, ('frow', 'fcol'))]
    all_to_all x0 -> x5, waiting for transfers between devices: none -> 37.1 us  [exchange(): lax.all_to_all(blocks, axes, 0, 0, tiled=True, axis_index_groups=groups)]
    all_to_all x0 -> x2, blocking collectives: none -> 26.9 us  [exchange(): lax.all_to_all(blocks, axes, 0, 0, tiled=True, axis_index_groups=groups)]
    all_to_all x0 -> x5, starting transfers between devices: none -> 22.5 us  [exchange(): lax.all_to_all(blocks, axes, 0, 0, tiled=True, axis_index_groups=groups)]
    convert_element_type x4 -> x7, other arithmetic: 10.8 us -> 3.11 us  [the longest x1 1.28 us: shards(): v_hot.astype(bf16)]
    gather x2 -> x0, local copies, waits for them, and re-layouts: 7.41 us -> none  [the longest x1 4.27 us: shards(): jnp.take(hat_imag.reshape(-1), cell_ids)]
    scatter-add x2 -> x0, other arithmetic: 7.18 us -> none  [the longest x1 3.66 us: shards(): jax.ops.segment_sum(residual[1], cell_ids, num_segments=cells_all)]
    dot_general x12 -> x14, matrix products: 16.4 us -> 11.1 us  [dot(): return jnp.dot(left, right, preferred_element_type=jnp.float32)]
  transfers between devices with their start and end apart: 0 -> 7, of which waited for: 0 -> 5; matrix products, arithmetic and copies ran while one was open for 0% -> 16% of each run, Pallas kernels for 0% -> 0%
where the time goes in v1:
time: 140 us; the launch traced here: 139 us
  waiting for transfers between devices  37.1 us (26%)
  blocking collectives  26.9 us (19%)
  starting transfers between devices  25.9 us (18%)
  matrix products  20.7 us (15%)
  other arithmetic  13.9 us (10%)
  local copies, waits for them, and re-layouts  13.7 us (10%)
    all_to_all x5, waiting for transfers between devices, exchange(): lax.all_to_all(blocks, axes, 0, 0, tiled=True, axis_index_groups=groups)  37.1 us
    all_to_all x2, blocking collectives, exchange(): lax.all_to_all(blocks, axes, 0, 0, tiled=True, axis_index_groups=groups)  26.9 us
    all_to_all x5, starting transfers between devices, exchange(): lax.all_to_all(blocks, axes, 0, 0, tiled=True, axis_index_groups=groups)  22.5 us
    dot_general x14, matrix products, dot(): return jnp.dot(left, right, preferred_element_type=jnp.float32)  11.1 us
    dot_general x3, matrix products, contract_last(): lax.dot_general(left, right, (((1,), (1,)), ((), ())), preferred_element_...  4.78 us
    dot_general x4, matrix products, contract_first(): lax.dot_general(left, right, (((0,), (0,)), ((), ())), preferred_element_...  4.77 us
    ppermute x1, starting transfers between devices, shards(): lax.ppermute(vis_own, 'frow', swap)  3.32 us
    unnamed x37, local copies, waits for them, and re-layouts  3.26 us
  transfers between devices with their start and end apart: 7, of which 5 were waited for; matrix products, arithmetic and copies ran while one was open for 16% of the time, Pallas kernels for 0%

profile of v1, /device:TPU:1, one launch (start us, length us, event | category | flops | bytes accessed | tf_op | source)
XLA Modules:
  0.0 139.5 jit_solution(14009663869529694302)
XLA Ops:
  0.6 0.7 convert.63
  1.3 0.7 convert.64
  2.0 0.7 convert.65
  2.7 0.7 convert_element_type.261
  3.4 3.3 %collective-permute-start.1 = (bf16[8,512]{1,0:T(8,128)(2,1)S(1)}, bf16[8,512]{1,0:T(8,128)(2,1)S(1)}, u32[]{:S(2)}, u32[]{:S(2)}) collective-permute-start(bf16[8,512]{1,0:T(8,128)(2,1)S(1)} %concatenate.149), channel_id=1, source_target_pairs={{0,32},{32,0},{64,96},{96,64},{128,160},{160,128},{192,224},{224,1... | collective-permute-start | bytes 24584 | tf_op jit(solution)/shard_map/ppermute | solution.py:81
  6.9 1.9 %constant_dynamic-update-slice_fusion.1 = bf16[1024,512]{1,0:T(8,128)(2,1)} fusion(bf16[512,512]{1,0:T(8,128)(2,1)} %param.9), kind=kLoop, calls=%fused_computation.238 | loop fusion | bytes 1048576
  8.7 1.3 fusion.190
  10.1 0.6 iota_add_fusion.3
  10.8 0.7 iota_add_fusion
  11.6 1.3 fusion.191
  12.9 0.6 iota_add_fusion.2
  13.7 0.7 iota_add_fusion.1
  15.4 0.8 constant_dynamic-slice_fusion
  16.2 0.7 constant_dynamic-slice_fusion.2
  16.9 0.9 fusion.151
  17.7 0.7 subtract_convert_fusion.1
  18.5 0.6 broadcast_in_dim.29
  19.1 3.3 %all-to-all-start.1 = ((bf16[4,8,1024]{2,1,0:T(8,128)(2,1)}), bf16[4,8,1024]{2,1,0:T(8,128)(2,1)S(1)}, u32[]{:S(2)}, u32[]{:S(2)}) async-start(bf16[4,8,1024]{2,1,0:T(8,128)(2,1)} %broadcast_in_dim.29), calls=%async_computation.1 | async-start | bytes 131072 | tf_op jit(solution)/shard_map/all_to_all | solution.py:44
  22.4 4.4 %all-to-all-done.1 = bf16[4,8,1024]{2,1,0:T(8,128)(2,1)S(1)} async-done(((bf16[4,8,1024]{2,1,0:T(8,128)(2,1)}), bf16[4,8,1024]{2,1,0:T(8,128)(2,1)S(1)}, u32[]{:S(2)}, u32[]{:S(2)}) %all-to-all-start.1) | async-done | bytes 65568 | tf_op jit(solution)/shard_map/all_to_all | solution.py:44
  27.1 1.5 %compare_select_fusion.1 = (bf16[128,4096]{1,0:T(8,128)(2,1)}, bf16[128,4096]{1,0:T(8,128)(2,1)}) fusion(bf16[4096]{0:T(1024)(128)(2,1)S(1)} %get-tuple-element.92, bf16[4096]{0:T(1024)(128)(2,1)S(1)} %bitcast.165, bf16[128]{0:T(256)(128)(2,1)S(1)} %add_convert_fusion.4, bf16[4096]{0:T(1024)(128)(2,1)S(1)} %get-tuple-element.91), kind=kLoop, calls=%fused_computation.6 | loop fusion | flops 1572864 | bytes 2121984 | tf_op jit(solution)/shard_map/jit(_where)/select_n | solution.py:119
  28.7 1.3 compare_convert_fusion
  33.2 0.9 maximum_maximum_fusion
  34.1 3.5 %all-to-all-start = ((bf16[4,2,256,128]{3,2,1,0:T(8,128)(2,1)}), bf16[4,2,256,128]{3,2,1,0:T(8,128)(2,1)S(1)}, u32[]{:S(2)}, u32[]{:S(2)}) async-start(bf16[4,2,256,128]{3,2,1,0:T(8,128)(2,1)} %maximum_maximum_fusion), calls=%async_computation | async-start | bytes 1048576 | tf_op jit(solution)/shard_map/all_to_all | solution.py:44
  37.6 3.8 %fusion.18 = bf16[256,384]{1,0:T(8,128)(2,1)} fusion(bf16[128,4096]{1,0:T(8,128)(2,1)} %compare_convert_fusion, bf16[128,4096]{1,0:T(8,128)(2,1)} %get-tuple-element.58, bf16[128,4096]{1,0:T(8,128)(2,1)} %get-tuple-element.57, pred[4096]{0:T(1024)(128)(4,1)S(1)} %bitcast.183, bf16[4096]{0:T(1024)(128)(2,1)S(1)} %bitcast.181, ...), kind=kOutput, calls=%fused_computation.32 | convolution fusion | flops 819036160 | bytes 3355136 | tf_op jit(solution)/shard_map/dot_general | solution.py:56
  41.4 1.1 copy.22
  42.5 2.7 %all-to-all-done = bf16[4,2,256,128]{3,2,1,0:T(8,128)(2,1)S(1)} async-done(((bf16[4,2,256,128]{3,2,1,0:T(8,128)(2,1)}), bf16[4,2,256,128]{3,2,1,0:T(8,128)(2,1)S(1)}, u32[]{:S(2)}, u32[]{:S(2)}) %all-to-all-start) | async-done | bytes 524320 | tf_op jit(solution)/shard_map/all_to_all | solution.py:44
  45.7 20.6 %all_to_all.35 = bf16[32,5,8,128]{3,2,1,0:T(8,128)(2,1)S(1)} all-to-all(bf16[32,5,8,128]{3,2,1,0:T(8,128)(2,1)S(1)} %copy.25), channel_id=1, replica_groups=mesh['frow'=8,'fcol'=32] {'fcol'}, dimensions={0} | all-to-all | bytes 655360 | tf_op jit(solution)/shard_map/all_to_all | solution.py:44
  66.4 0.9 broadcast_in_dim.35
  67.3 9.0 %all-to-all-start.3 = ((bf16[64,5,8,128]{3,2,1,0:T(8,128)(2,1)}), bf16[64,5,8,128]{3,2,1,0:T(8,128)(2,1)S(1)}, u32[]{:S(2)}, u32[]{:S(2)}) async-start(bf16[64,5,8,128]{3,2,1,0:T(8,128)(2,1)} %broadcast_in_dim.35), calls=%async_computation.3 | async-start | bytes 1310720 | tf_op jit(solution)/shard_map/all_to_all | solution.py:44
  76.3 0.7 slice.262
  77.0 0.7 slice.261
  78.0 18.3 %all-to-all-done.3 = bf16[64,5,8,128]{3,2,1,0:T(8,128)(2,1)S(1)} async-done(((bf16[64,5,8,128]{3,2,1,0:T(8,128)(2,1)}), bf16[64,5,8,128]{3,2,1,0:T(8,128)(2,1)S(1)}, u32[]{:S(2)}, u32[]{:S(2)}) %all-to-all-start.3) | async-done | bytes 655392 | tf_op jit(solution)/shard_map/all_to_all | solution.py:44
  96.6 1.2 fusion.16
  99.7 0.9 fusion.10
  100.7 1.0 convolution_add_fusion
  102.1 0.6 maximum_bitcast_fusion
  102.7 3.3 %all-to-all-start.6 = ((f32[4,2,512]{2,1,0:T(2,128)}), f32[4,2,512]{2,1,0:T(2,128)S(1)}, u32[]{:S(2)}, u32[]{:S(2)}) async-start(f32[4,2,512]{2,1,0:T(2,128)} %maximum_bitcast_fusion), calls=%async_computation.6 | async-start | bytes 32768 | tf_op jit(solution)/shard_map/all_to_all | solution.py:44
  106.1 4.1 %all-to-all-done.6 = f32[4,2,512]{2,1,0:T(2,128)S(1)} async-done(((f32[4,2,512]{2,1,0:T(2,128)}), f32[4,2,512]{2,1,0:T(2,128)S(1)}, u32[]{:S(2)}, u32[]{:S(2)}) %all-to-all-start.6) | async-done | bytes 16416 | tf_op jit(solution)/shard_map/all_to_all | solution.py:44
  110.2 0.8 broadcast_in_dim.36
  111.0 3.5 %all-to-all-start.4 = ((bf16[4,2,128,256]{3,2,1,0:T(8,128)(2,1)}), bf16[4,2,128,256]{3,2,1,0:T(8,128)(2,1)S(1)}, u32[]{:S(2)}, u32[]{:S(2)}) async-start(bf16[4,2,128,256]{3,2,1,0:T(8,128)(2,1)} %broadcast_in_dim.36), calls=%async_computation.4 | async-start | bytes 1048576 | tf_op jit(solution)/shard_map/all_to_all | solution.py:44
  114.6 0.6 sub.94
  115.2 7.6 %all-to-all-done.4 = bf16[4,2,128,256]{3,2,1,0:T(8,128)(2,1)S(1)} async-done(((bf16[4,2,128,256]{3,2,1,0:T(8,128)(2,1)}), bf16[4,2,128,256]{3,2,1,0:T(8,128)(2,1)S(1)}, u32[]{:S(2)}, u32[]{:S(2)}) %all-to-all-start.4) | async-done | bytes 524320 | tf_op jit(solution)/shard_map/all_to_all | solution.py:44
  122.8 6.3 %all_to_all.36 = bf16[2,4,2,128,256]{4,3,2,1,0:T(8,128)(2,1)S(1)} all-to-all(bf16[2,4,2,128,256]{4,3,2,1,0:T(8,128)(2,1)S(1)} %broadcast_in_dim.37), channel_id=1, replica_groups={{0,32},{64,96},{128,160},{192,224},{1,33},{65,97},{129,161},{193,225},{..., dimensions={0} | all-to-all | bytes 2097152 | tf_op jit(solution)/shard_map/all_to_all | solution.py:44
  129.4 0.8 copy-done.9
  130.3 1.4 %fusion.52 = f32[512,512]{1,0:T(8,128)} fusion(bf16[256,256]{1,0:T(8,128)(2,1)S(1)} %get-tuple-element.13, bf16[256,256]{1,0:T(8,128)(2,1)S(1)} %get-tuple-element.19, bf16[256,256]{1,0:T(8,128)(2,1)S(1)} %get-tuple-element.12, bf16[256,512]{1,0:T(8,128)(2,1)S(1)} %copy-done.9, bf16[256,512]{1,0:T(8,128)(2,1)S(1)} %copy-done.10), kind=kOutput, calls=%fused_computation.63 | convolution fusion | flops 271581184 | bytes 1966080 | tf_op jit(solution)/shard_map/dot_general | solution.py:52
  131.7 1.4 %fusion.27 = f32[512,512]{1,0:T(8,128)} fusion(bf16[256,256]{1,0:T(8,128)(2,1)S(1)} %get-tuple-element.17, bf16[256,256]{1,0:T(8,128)(2,1)S(1)} %get-tuple-element.21, bf16[256,256]{1,0:T(8,128)(2,1)S(1)} %get-tuple-element.16, bf16[256,512]{1,0:T(8,128)(2,1)S(1)} %copy-done.9, bf16[256,512]{1,0:T(8,128)(2,1)S(1)} %copy-done.10), kind=kOutput, calls=%fused_computation.44 | convolution fusion | flops 271581184 | bytes 1966080 | tf_op jit(solution)/shard_map/dot_general | solution.py:52
  133.2 3.0 %fusion.15 = f32[512,512]{1,0:T(8,128)} fusion(f32[512,512]{1,0:T(8,128)} %fusion.27, bf16[256,256]{1,0:T(8,128)(2,1)S(1)} %get-tuple-element.15, bf16[256,256]{1,0:T(8,128)(2,1)S(1)} %get-tuple-element.20, bf16[256,256]{1,0:T(8,128)(2,1)S(1)} %get-tuple-element.14, bf16[256,512]{1,0:T(8,128)(2,1)S(1)} %bitcast_negate_fusion.1, ...), kind=kOutput, calls=%fused_computation.27 | convolution fusion | flops 541589504 | bytes 3538944 | tf_op jit(solution)/shard_map/dot_general | solution.py:48
  136.2 3.3 %fusion.12 = f32[512,512]{1,0:T(8,128)} fusion(f32[512,512]{1,0:T(8,128)} %fusion.15, f32[512,512]{1,0:T(8,128)} %fusion.52, bf16[256,256]{1,0:T(8,128)(2,1)S(1)} %get-tuple-element.11, bf16[256,256]{1,0:T(8,128)(2,1)S(1)} %get-tuple-element.18, bf16[256,256]{1,0:T(8,128)(2,1)S(1)} %get-tuple-element.10, bf16[256,512]{1,0:T(8,128)(2,1)S(1)} %bitcast_negate_fusion, ...), kind=kOutput, calls=%fused_computation.20 | convolution fusion | flops 542113792 | bytes 4587520 | tf_op jit(solution)/shard_map/dot_general | solution.py:48
  (102 shorter events, 8.8 us)
Async XLA Ops:
  3.4 15.0 %collective-permute-start.1 = (bf16[8,512]{1,0:T(8,128)(2,1)S(1)}, bf16[8,512]{1,0:T(8,128)(2,1)S(1)}, u32[]{:S(2)}, u32[]{:S(2)}) collective-permute-start(bf16[8,512]{1,0:T(8,128)(2,1)S(1)} %concatenate.149), channel_id=1, source_target_pairs={{0,32},{32,0},{64,96},{96,64},{128,160},{160,128},{192,224},{224,1... | collective-permute-start | bytes 24584 | tf_op jit(solution)/shard_map/ppermute | solution.py:81
  6.8 23.2 %collective-permute-start = (bf16[512,512]{1,0:T(8,128)(2,1)}, bf16[512,512]{1,0:T(8,128)(2,1)S(1)}, u32[]{:S(2)}, u32[]{:S(2)}) collective-permute-start(bf16[512,512]{1,0:T(8,128)(2,1)} %param.9), channel_id=1, source_target_pairs={{0,32},{32,0},{64,96},{96,64},{128,160},{160,128},{192,224},{224,1... | collective-permute-start | bytes 1572872 | tf_op jit(solution)/shard_map/ppermute | solution.py:77
  15.3 2.4 %copy-start = (bf16[16,16,512]{2,1,0:T(8,128)(2,1)}, bf16[16,16,512]{2,1,0:T(8,128)(2,1)S(1)}, u32[]{:S(2)}) copy-start(bf16[16,16,512]{2,1,0:T(8,128)(2,1)S(1)} %get-tuple-element.50) | copy-start | bytes 786436
  15.3 2.4 %copy-start.2 = (bf16[16,16,512]{2,1,0:T(8,128)(2,1)}, bf16[16,16,512]{2,1,0:T(8,128)(2,1)S(1)}, u32[]{:S(2)}) copy-start(bf16[16,16,512]{2,1,0:T(8,128)(2,1)S(1)} %get-tuple-element.45) | copy-start | bytes 786436
  19.1 7.7 %all-to-all-start.1 = ((bf16[4,8,1024]{2,1,0:T(8,128)(2,1)}), bf16[4,8,1024]{2,1,0:T(8,128)(2,1)S(1)}, u32[]{:S(2)}, u32[]{:S(2)}) async-start(bf16[4,8,1024]{2,1,0:T(8,128)(2,1)} %broadcast_in_dim.29), calls=%async_computation.1 | async-start | bytes 131072 | tf_op jit(solution)/shard_map/all_to_all | solution.py:44
  26.9 3.1 %copy-start.8 = (bf16[1024,512]{1,0:T(8,128)(2,1)S(1)}, bf16[1024,512]{1,0:T(8,128)(2,1)}, u32[]{:S(2)}) copy-start(bf16[1024,512]{1,0:T(8,128)(2,1)} %constant_dynamic-update-slice_fusion.1) | copy-start | bytes 3145732
  27.1 2.9 %copy-start.13 = (bf16[128,512]{1,0:T(8,128)(2,1)S(1)}, bf16[128,512]{1,0:T(8,128)(2,1)}, u32[]{:S(2)}) copy-start(bf16[128,512]{1,0:T(8,128)(2,1)} %constant_dynamic-slice_fusion) | copy-start | bytes 393220
  28.7 1.8 %copy-start.12 = (bf16[128,512]{1,0:T(8,128)(2,1)S(1)}, bf16[128,512]{1,0:T(8,128)(2,1)}, u32[]{:S(2)}) copy-start(bf16[128,512]{1,0:T(8,128)(2,1)} %constant_dynamic-slice_fusion.2) | copy-start | bytes 393220
  34.1 11.1 %all-to-all-start = ((bf16[4,2,256,128]{3,2,1,0:T(8,128)(2,1)}), bf16[4,2,256,128]{3,2,1,0:T(8,128)(2,1)S(1)}, u32[]{:S(2)}, u32[]{:S(2)}) async-start(bf16[4,2,256,128]{3,2,1,0:T(8,128)(2,1)} %maximum_maximum_fusion), calls=%async_computation | async-start | bytes 1048576 | tf_op jit(solution)/shard_map/all_to_all | solution.py:44
  67.3 29.0 %all-to-all-start.3 = ((bf16[64,5,8,128]{3,2,1,0:T(8,128)(2,1)}), bf16[64,5,8,128]{3,2,1,0:T(8,128)(2,1)S(1)}, u32[]{:S(2)}, u32[]{:S(2)}) async-start(bf16[64,5,8,128]{3,2,1,0:T(8,128)(2,1)} %broadcast_in_dim.35), calls=%async_computation.3 | async-start | bytes 1310720 | tf_op jit(solution)/shard_map/all_to_all | solution.py:44
  77.0 19.4 %copy-start.7 = (bf16[256,512]{1,0:T(8,128)(2,1)S(1)}, bf16[256,512]{1,0:T(8,128)(2,1)}, u32[]{:S(2)}) copy-start(bf16[256,512]{1,0:T(8,128)(2,1)} %constant.255) | copy-start | bytes 786436
  77.8 20.1 %copy-start.5 = (bf16[256,256]{1,0:T(8,128)(2,1)S(1)}, bf16[256,256]{1,0:T(8,128)(2,1)}, u32[]{:S(2)}) copy-start(bf16[256,256]{1,0:T(8,128)(2,1)} %constant.247.clone) | copy-start | bytes 393220
  96.3 1.8 %copy-start.4 = (bf16[256,256]{1,0:T(8,128)(2,1)S(1)}, bf16[256,256]{1,0:T(8,128)(2,1)}, u32[]{:S(2)}) copy-start(bf16[256,256]{1,0:T(8,128)(2,1)} %constant.246.clone) | copy-start | bytes 393220
  96.6 1.8 %copy-start.11 = (bf16[256,512]{1,0:T(8,128)(2,1)S(1)}, bf16[256,512]{1,0:T(8,128)(2,1)}, u32[]{:S(2)}) copy-start(bf16[256,512]{1,0:T(8,128)(2,1)} %constant.257) | copy-start | bytes 786436
  98.1 1.0 copy-start.6
  102.7 7.4 %all-to-all-start.6 = ((f32[4,2,512]{2,1,0:T(2,128)}), f32[4,2,512]{2,1,0:T(2,128)S(1)}, u32[]{:S(2)}, u32[]{:S(2)}) async-start(f32[4,2,512]{2,1,0:T(2,128)} %maximum_bitcast_fusion), calls=%async_computation.6 | async-start | bytes 32768 | tf_op jit(solution)/shard_map/all_to_all | solution.py:44
  106.0 8.6 %copy-start.14 = (f32[2,512]{1,0:T(2,128)S(1)}, f32[2,512]{1,0:T(2,128)}, u32[]{:S(2)}) copy-start(f32[2,512]{1,0:T(2,128)} %param.15) | copy-start | bytes 12292
  111.0 11.8 %all-to-all-start.4 = ((bf16[4,2,128,256]{3,2,1,0:T(8,128)(2,1)}), bf16[4,2,128,256]{3,2,1,0:T(8,128)(2,1)S(1)}, u32[]{:S(2)}, u32[]{:S(2)}) async-start(bf16[4,2,128,256]{3,2,1,0:T(8,128)(2,1)} %broadcast_in_dim.36), calls=%async_computation.4 | async-start | bytes 1048576 | tf_op jit(solution)/shard_map/all_to_all | solution.py:44
  129.3 1.0 copy-start.9
  129.3 1.0 copy-start.10
  131.7 1.4 %copy-start.3 = (bf16[16,16,512]{2,1,0:T(8,128)(2,1)S(1)}, bf16[16,16,512]{2,1,0:T(8,128)(2,1)}, u32[]{:S(2)}) copy-start(bf16[16,16,512]{2,1,0:T(8,128)(2,1)} %copy-done.2) | copy-start | bytes 786436
  133.2 3.0 %copy-start.1 = (bf16[16,16,512]{2,1,0:T(8,128)(2,1)S(1)}, bf16[16,16,512]{2,1,0:T(8,128)(2,1)}, u32[]{:S(2)}) copy-start(bf16[16,16,512]{2,1,0:T(8,128)(2,1)} %copy-done) | copy-start | bytes 786436

commit v2 on v1

v2 whole, which is shorter than its diff:
```python
import functools
import math

import jax
import jax.numpy as jnp
import ml_dtypes
import numpy as np
from jax import lax
from jax.experimental import pallas as pl
from jax.experimental.pallas import tpu as pltpu
from jax.sharding import PartitionSpec as P

SKY = 65536
SG = 256
NR = 2
NC = 2
HALF = SG // 2
BOTH = ("frow", "fcol")


def wave(count):
    count = count & (SKY - 1)
    turned = count + SKY // 8
    near = (turned & (SKY // 4 - 1)) - SKY // 8
    quarter = lax.shift_right_logical(turned, 14) & 3
    t = near.astype(jnp.float32) * (2.0 * math.pi / SKY)
    q = t * t
    sin = t * (1.0 + q * (-1.0 / 6 + q * (1.0 / 120 + q * (-1.0 / 5040 + q * (1.0 / 362880)))))
    cos = 1.0 + q * (-0.5 + q * (1.0 / 24 + q * (-1.0 / 720 + q * (1.0 / 40320))))
    odd = (quarter & 1) == 1
    one, two = jnp.where(odd, sin, cos), jnp.where(odd, cos, sin)
    return (
        jnp.where((quarter == 1) | (quarter == 2), -one, one),
        jnp.where(quarter >= 2, -two, two),
    )


def lanes(n):
    return lax.broadcasted_iota(jnp.int32, (1, n), 1)


def sublanes(n):
    return lax.broadcasted_iota(jnp.int32, (n, 1), 0)


def spread(coarse, fine, store):
    for k in range(coarse[0].shape[0]):
        c, s = coarse[0][k:k + 1], coarse[1][k:k + 1]
        store(k * 16, c * fine[0] - s * fine[1], s * fine[0] + c * fine[1])


def forward_tables_kernel(rows_count, cols_count, info, facet, row_tab, col_tab, pq):
    bf16 = jnp.bfloat16
    side = facet.shape[0]
    row_index, col_index = info[4], info[5]
    core = row_index % 2
    unit = sublanes(16)

    col_step = SKY // (cols_count * side)
    col_base = col_index * (SKY // cols_count)
    for c in range(NC):
        freq = info[2 + c] + core * HALF + lanes(HALF)
        coarse = wave((col_base + 16 * col_step * sublanes(side // 16)) * freq)
        fine = wave((col_step * unit) * freq)

        def store(at, cos, sin, c=c):
            col_tab[at:at + 16, 2 * c * HALF:(2 * c + 1) * HALF] = cos.astype(bf16)
            col_tab[at:at + 16, (2 * c + 1) * HALF:(2 * c + 2) * HALF] = sin.astype(bf16)

        spread(coarse, fine, store)
    pq[...] = jnp.dot(facet[...], col_tab[...], preferred_element_type=jnp.float32).astype(bf16)

    row_step = SKY // (rows_count * side)
    for f in range(2):
        base = (row_index ^ f) * (SKY // rows_count)
        pos = base + row_step * lanes(side)
        fine = wave(unit * pos)
        for r in range(NR):
            coarse = wave((info[r] + 16 * unit) * pos)

            def store(at, cos, sin, r=r, f=f):
                row_tab[2 * r, at:at + 16, f * side:(f + 1) * side] = cos.astype(bf16)
                row_tab[2 * r + 1, at:at + 16, f * side:(f + 1) * side] = sin.astype(bf16)

            spread(coarse, fine, store)


def contributions_kernel(scale, facet, row_tab, col_tab, pq, out, right):
    side = facet.shape[0]
    f32, bf16 = jnp.float32, jnp.bfloat16
    right[:side] = pq[...]
    right[side:] = jnp.dot(facet[...], col_tab[...], preferred_element_type=f32).astype(bf16)
    for r in range(NR):
        with_cos = jnp.dot(row_tab[2 * r], right[...], preferred_element_type=f32)
        with_sin = jnp.dot(row_tab[2 * r + 1], right[...], preferred_element_type=f32)
        for c in range(NC):
            at = 2 * c * HALF
            cp, cq = with_cos[:, at:at + HALF], with_cos[:, at + HALF:at + 2 * HALF]
            sp, sq = with_sin[:, at:at + HALF], with_sin[:, at + HALF:at + 2 * HALF]
            out[r * NC + c, 0] = ((cp - sq) * scale).astype(bf16)
            out[r * NC + c, 1] = (-(cq + sp) * scale).astype(bf16)


def back_tables_kernel(rows_count, cols_count, side, info, row_tab, col_tab):
    bf16 = jnp.bfloat16
    row_index, col_index = info[4], info[5]
    unit = sublanes(16)
    row_step = SKY // (rows_count * side)
    row_base = row_index * (SKY // rows_count)
    for r in range(NR):
        freq = info[r] + lanes(SG)
        coarse = wave((row_base + 16 * row_step * sublanes(side // 16)) * freq)
        fine = wave((row_step * unit) * freq)

        def store(at, cos, sin, r=r):
            row_tab[2 * r, at:at + 16] = cos.astype(bf16)
            row_tab[2 * r + 1, at:at + 16] = sin.astype(bf16)

        spread(coarse, fine, store)
    col_step = SKY // (cols_count * side)
    pos = col_index * (SKY // cols_count) + col_step * lanes(side)
    fine = wave(unit * pos)
    for c in range(NC):
        coarse = wave((info[2 + c] + 16 * unit) * pos)

        def store(at, cos, sin, c=c):
            col_tab[2 * c, at:at + 16] = cos.astype(bf16)
            col_tab[2 * c + 1, at:at + 16] = (-sin).astype(bf16)

        spread(coarse, fine, store)


def image_kernel(scale, back, row_tab, col_tab, out, grid, both):
    f32, bf16 = jnp.float32, jnp.bfloat16
    for c in range(NC):
        real = imag = None
        for r in range(NR):
            for k in range(2):
                for half in range(2):
                    grid[:, k * SG + half * HALF:k * SG + (half + 1) * HALF] = back[half, r * NC + c, k]
            cos = jnp.dot(row_tab[2 * r], grid[...], preferred_element_type=f32)
            sin = jnp.dot(row_tab[2 * r + 1], grid[...], preferred_element_type=f32)
            re, im = cos[:, :SG] - sin[:, SG:], cos[:, SG:] + sin[:, :SG]
            real = re if real is None else real + re
            imag = im if imag is None else imag + im
        both[:, :SG] = real.astype(bf16)
        both[:, SG:] = imag.astype(bf16)
        part = jnp.dot(both[:, :SG], col_tab[2 * c], preferred_element_type=f32)
        part = part + jnp.dot(both[:, SG:], col_tab[2 * c + 1], preferred_element_type=f32)
        if c == 0:
            out[...] = part
        else:
            out[...] = (out[...] + part) * scale


def grids_kernel(full, kcos, ksin, forward, inverse, hat, back, cat):
    f32, bf16 = jnp.float32, jnp.bfloat16
    cat[:, :SG] = full[0]
    cat[:, SG:] = full[1]
    cat[...] = jnp.dot(cat[...], forward[...], preferred_element_type=f32).astype(bf16)
    with_cos = jnp.dot(kcos[...], cat[...], preferred_element_type=f32)
    with_sin = jnp.dot(ksin[...], cat[...], preferred_element_type=f32)
    hat_real = (with_cos[:, :SG] - with_sin[:, SG:]) * (1.0 / SG)
    hat_imag = (with_sin[:, :SG] + with_cos[:, SG:]) * (1.0 / SG)
    for k, part in enumerate((hat_real, hat_imag)):
        high = part.astype(bf16)
        hat[0, k] = high
        hat[1, k] = (part - high.astype(f32)).astype(bf16)
    count = full[4].astype(f32)
    cat[:, :SG] = (full[2].astype(f32) - count * hat_real).astype(bf16)
    cat[:, SG:] = (full[3].astype(f32) - count * hat_imag).astype(bf16)
    cat[...] = jnp.dot(cat[...], inverse[...], preferred_element_type=f32).astype(bf16)
    with_cos = jnp.dot(kcos[...], cat[...], preferred_element_type=f32)
    with_sin = jnp.dot(ksin[...], cat[...], preferred_element_type=f32)
    real = ((with_cos[:, :SG] + with_sin[:, SG:]) * (1.0 / SG)).astype(bf16)
    imag = ((with_cos[:, SG:] - with_sin[:, :SG]) * (1.0 / SG)).astype(bf16)
    for half in range(2):
        back[half, 0] = real[:, half * HALF:(half + 1) * HALF]
        back[half, 1] = imag[:, half * HALF:(half + 1) * HALF]


def answers_kernel(info, ask, hat, out):
    f32, bf16 = jnp.float32, jnp.bfloat16
    row_index = info[4]
    core = row_index % 2
    chip = (row_index // 2).astype(f32)
    n = ask.shape[2]
    counter = sublanes(SG).astype(f32)
    dims = (((0,), (0,)), ((), ()))
    for k in range(ask.shape[0] // 2):
        mine = ask[2 * k + core].astype(f32)
        hot = jnp.where((mine[1:2] == counter) & (mine[0:1] == chip), 1.0, 0.0).astype(bf16)
        pick = mine[2:3] == counter
        for part in range(2):
            line = lax.dot_general(hat[0, part], hot, dims, preferred_element_type=f32)
            line = line + lax.dot_general(hat[1, part], hot, dims, preferred_element_type=f32)
            out[k, part:part + 1] = jnp.sum(jnp.where(pick, line, 0.0), axis=0, keepdims=True)


def pack_kernel(subgrid, u, v, observed, out):
    f32 = jnp.float32
    zero = jnp.zeros((3, u.shape[1]), f32)
    rows = [subgrid[...].astype(f32), u[...].astype(f32), v[...].astype(f32), observed[...], zero]
    out[...] = jnp.concatenate(rows, 0).astype(jnp.bfloat16)


def gridding_kernel(info, vis, out):
    f32, bf16 = jnp.float32, jnp.bfloat16
    row_index = info[4]
    chip = (row_index // 2).astype(f32)
    v_at = (sublanes(HALF) + (row_index % 2) * HALF).astype(f32)
    counter = sublanes(SG).astype(f32)
    total = jnp.zeros((SG, 3 * HALF), f32)
    for k in range(vis.shape[0]):
        one = vis[k].astype(f32)
        hot = jnp.where((one[1:2] == counter) & (one[0:1] == chip), 1.0, 0.0).astype(bf16)
        pick = one[2:3] == v_at
        right = jnp.concatenate(
            [jnp.where(pick, one[3:4], 0.0), jnp.where(pick, one[4:5], 0.0), jnp.where(pick, 1.0, 0.0)], 0
        ).astype(bf16)
        total = total + lax.dot_general(hot, right, (((1,), (1,)), ((), ())), preferred_element_type=f32)
    for p in range(3):
        out[p] = total[:, p * HALF:(p + 1) * HALF].astype(bf16)


def call(kernel, out_shape, name, scratch=(), scalars=0, cost=0):
    smem, vmem = pl.BlockSpec(memory_space=pltpu.SMEM), pl.BlockSpec(memory_space=pltpu.VMEM)

    def run(*args):
        return pl.pallas_call(
            kernel,
            out_shape=out_shape,
            in_specs=[smem] * scalars + [vmem] * (len(args) - scalars),
            out_specs=jax.tree.map(lambda _: vmem, out_shape),
            scratch_shapes=list(scratch),
            compiler_params=pltpu.CompilerParams(vmem_limit_bytes=24 * 2**20),
            cost_estimate=pl.CostEstimate(flops=cost, bytes_accessed=2**20, transcendentals=0),
            name=name,
        )(*args)

    return run


def grid_tables():
    counter = np.arange(SG)
    angles = (counter[:, None] * counter[None, :] % SG).astype(np.float64) * (2.0 * math.pi / SG)
    return np.cos(angles).astype(ml_dtypes.bfloat16), np.sin(angles).astype(ml_dtypes.bfloat16)


def exchange(blocks, axes, groups):
    return lax.all_to_all(blocks, axes, 0, 0, tiled=True, axis_index_groups=groups)


def shape(*dims, dtype=jnp.bfloat16):
    return jax.ShapeDtypeStruct(dims, dtype)


def shards(facet, row_offsets, col_offsets, vis_subgrid, vis_u, vis_v, observed):
    f32, bf16 = jnp.float32, jnp.bfloat16
    rows_count, cols_count = lax.axis_size("frow"), lax.axis_size("fcol")
    side = facet.shape[0]
    n_vis = vis_u.shape[0]
    chips = rows_count // 2
    x_groups = [[2 * chip + core for chip in range(chips)] for core in range(2)]
    core_groups = [[2 * chip, 2 * chip + 1] for chip in range(chips)]
    grid_groups = [
        [(2 * chip + core) * cols_count + col for core in range(2) for col in range(cols_count)] for chip in range(chips)
    ]
    row_index, col_index = lax.axis_index("frow"), lax.axis_index("fcol")
    core = row_index % 2
    scale_in = 1.0 / (side * math.sqrt(rows_count * cols_count))
    scale_out = 1.0 / (SG * math.sqrt(NR * NC))
    info = jnp.concatenate([row_offsets, col_offsets, jnp.stack([row_index, col_index])]).astype(jnp.int32)

    facet_other = lax.ppermute(facet, "frow", [(index, index ^ 1) for index in range(rows_count)])
    vis_own = call(pack_kernel, shape(8, n_vis), "pack")(
        vis_subgrid.reshape(1, n_vis), vis_u.reshape(1, n_vis), vis_v.reshape(1, n_vis), observed
    )
    vis_all = exchange(jnp.broadcast_to(vis_own, (rows_count, 8, n_vis)), "frow", None)

    row_tab, col_tab, pq = call(
        functools.partial(forward_tables_kernel, rows_count, cols_count),
        (shape(4, SG, 2 * side), shape(side, 4 * HALF), shape(side, 4 * HALF)),
        "forward_tables", scalars=1, cost=10**9,
    )(info, facet)
    parts = call(
        functools.partial(contributions_kernel, scale_in), shape(NR * NC, 2, SG, HALF), "contributions",
        scratch=[pltpu.VMEM((2 * side, 4 * HALF), bf16)], cost=2 * 10**9,
    )(facet_other, row_tab, col_tab, pq)
    mine = exchange(parts, "frow", x_groups).astype(f32).sum(0).astype(bf16)

    sums = call(gridding_kernel, shape(3, SG, HALF), "gridding", scalars=1, cost=10**9)(info, vis_all)
    planes = jnp.concatenate([mine, sums], 0)
    rows_each = SG // cols_count
    pieces = planes.reshape(5, cols_count, rows_each, HALF).transpose(1, 0, 2, 3)
    piece = exchange(pieces, "fcol", None).astype(f32).sum(0).astype(bf16)
    gathered = exchange(jnp.broadcast_to(piece, (2 * cols_count,) + piece.shape), BOTH, grid_groups)
    full = (
        gathered.reshape(2, cols_count, 5, rows_each, HALF)
        .transpose(2, 1, 3, 0, 4)
        .reshape(5, SG, SG)
    )

    kcos, ksin = grid_tables()
    forward_block = np.concatenate([np.concatenate([kcos, ksin], 1), np.concatenate([-ksin, kcos], 1)], 0)
    inverse_block = np.concatenate([np.concatenate([kcos, -ksin], 1), np.concatenate([ksin, kcos], 1)], 0)
    hat, back = call(
        grids_kernel, (shape(2, 2, SG, SG), shape(2, 2, SG, HALF)), "grids",
        scratch=[pltpu.VMEM((SG, 2 * SG), bf16)], cost=10**9,
    )(full, kcos, ksin, forward_block, inverse_block)
    my_half = lax.dynamic_index_in_dim(back, core, 0, False)
    by_chip = exchange(jnp.broadcast_to(my_half, (chips,) + my_half.shape), "frow", x_groups)
    by_core = exchange(jnp.broadcast_to(by_chip, (2,) + by_chip.shape), "frow", core_groups)

    values = call(answers_kernel, shape(chips, 2, n_vis, dtype=f32), "answers", scalars=1, cost=10**9)(info, vis_all, hat)
    answers = exchange(values, "frow", x_groups)
    residual = observed - answers.sum(0)

    back_row, back_col = call(
        functools.partial(back_tables_kernel, rows_count, cols_count, side),
        (shape(4, side, SG), shape(4, SG, side)), "back_tables", scalars=1, cost=10**9,
    )(info)
    image = call(
        functools.partial(image_kernel, scale_out), shape(side, side, dtype=f32), "image",
        scratch=[pltpu.VMEM((SG, 2 * SG), bf16), pltpu.VMEM((side, 2 * SG), bf16)], cost=2 * 10**9,
    )(by_core, back_row, back_col)
    return (image, residual)


def solution(mesh):
    in_specs = (
        P("frow", "fcol"),
        P(),
        P(),
        P(("frow", "fcol")),
        P(("frow", "fcol")),
        P(("frow", "fcol")),
        P(None, ("frow", "fcol")),
    )
    out_specs = (P("frow", "fcol"), P(None, ("frow", "fcol")))
    return jax.shard_map(shards, mesh=mesh, in_specs=in_specs, out_specs=out_specs, check_vma=False)
```

time: 140 us -> 115 us (0.82)
  matrix products: 20.7 us -> 0 us
  Pallas kernels: 0 us -> 14 us
  other arithmetic: 13.9 us -> 1.56 us
  local copies, waits for them, and re-layouts: 13.7 us -> 6.54 us
    dot_general x21 -> x0, matrix products: 20.7 us -> none  [the longest x14 11.1 us: dot(): return jnp.dot(left, right, preferred_element_type=jnp.float32)]
    pallas_call x0 -> x8, Pallas kernels: none -> 14 us  [run(): pl.pallas_call(kernel, out_shape=out_shape, in_specs=[smem] * scalars + [...]
    slice x12 -> x0, local copies, waits for them, and re-layouts: 4.73 us -> none  [the longest x4 1.49 us: shards(): tab = jnp.concatenate([t[:, :side] for t in row_tabs[r]], 0)]
    another operation x8 -> x0, other arithmetic: 3.14 us -> none
    convert_element_type x7 -> x0, other arithmetic: 3.11 us -> none  [the longest x1 1.28 us: shards(): v_hot.astype(bf16)]
    add x5 -> x0, other arithmetic: 2.61 us -> none  [the longest x2 1.3 us: shards(): row_offsets[r] + counter]
    select_n x6 -> x0, other arithmetic: 1.6 us -> none  [the longest x1 1.54 us: shards(): jnp.where(v_hot, vis_n[3:4], zero)]
    dynamic_slice x4 -> x0, local copies, waits for them, and re-layouts: 1.48 us -> none  [shards(): lax.dynamic_slice_in_dim(t, core * HALF, HALF, 0)]
  transfers between devices with their start and end apart: 7 -> 6, of which waited for: 5 -> 4; matrix products, arithmetic and copies ran while one was open for 16% -> 2% of each run, Pallas kernels for 0% -> 7%
where the time goes in v2:
time: 115 us; the launch traced here: 114 us
  waiting for transfers between devices  37.5 us (33%)
  blocking collectives  28 us (24%)
  starting transfers between devices  25.8 us (22%)
  Pallas kernels  14 us (12%)
  local copies, waits for them, and re-layouts  6.54 us (6%)
  other arithmetic  1.56 us (1%)
    all_to_all x5, waiting for transfers between devices, exchange(): lax.all_to_all(blocks, axes, 0, 0, tiled=True, axis_index_groups=groups)  37.5 us
    all_to_all x2, blocking collectives, exchange(): lax.all_to_all(blocks, axes, 0, 0, tiled=True, axis_index_groups=groups)  28 us
    all_to_all x5, starting transfers between devices, exchange(): lax.all_to_all(blocks, axes, 0, 0, tiled=True, axis_index_groups=groups)  22.5 us
    pallas_call x8, Pallas kernels, run(): pl.pallas_call(kernel, out_shape=out_shape, in_specs=[smem] * scalars + [...  14 us
    unnamed x20, local copies, waits for them, and re-layouts  3.81 us
    ppermute x1, starting transfers between devices, shards(): lax.ppermute(facet, 'frow', [(index, index ^ 1) for index in range(rows_c...  3.33 us
  transfers between devices with their start and end apart: 6, of which 4 were waited for; matrix products, arithmetic and copies ran while one was open for 2% of the time, Pallas kernels for 7%

profile of v2, /device:TPU:1, one launch (start us, length us, event | category | flops | bytes accessed | tf_op | source)
XLA Modules:
  0.0 114.3 jit_solution(12361012372871644497)
XLA Ops:
  0.6 3.3 %collective-permute-start = (bf16[512,512]{1,0:T(8,128)(2,1)}, bf16[512,512]{1,0:T(8,128)(2,1)S(1)}, u32[]{:S(2)}, u32[]{:S(2)}) collective-permute-start(bf16[512,512]{1,0:T(8,128)(2,1)} %facet.1), channel_id=1, source_target_pairs={{0,32},{32,0},{64,96},{96,64},{128,160},{160,128},{192,224},{224,1... | collective-permute-start | bytes 1572872 | tf_op jit(solution)/shard_map/ppermute | solution.py:275
  4.0 0.0 copy-start
  4.0 0.7 copy-done
  4.6 0.7 copy-done.2
  5.3 0.0 copy-start.3
  5.3 0.7 copy-done.3
  6.0 0.7 copy-done.4
  6.7 0.6 broadcast_in_dim.12
  7.3 3.3 %all-to-all-start.1 = ((bf16[8,8,512]{2,1,0:T(8,128)(2,1)}), bf16[8,8,512]{2,1,0:T(8,128)(2,1)S(1)}, u32[]{:S(2)}, u32[]{:S(2)}) async-start(bf16[8,8,512]{2,1,0:T(8,128)(2,1)} %broadcast_in_dim.12), calls=%async_computation.1 | async-start | bytes 131072 | tf_op jit(solution)/shard_map/all_to_all | solution.py:251
  10.6 0.8 pad_add_fusion.info
  11.4 1.0 copy-done.5
  12.4 1.9 %forward_tables.1 = (bf16[4,256,1024]{2,1,0:T(8,128)(2,1)S(1)}, bf16[512,512]{1,0:T(8,128)(2,1)S(1)}, bf16[512,512]{1,0:T(8,128)(2,1)S(1)}) custom-call(s32[6]{0:T(128)S(1)} %pad_add_fusion.info, bf16[512,512]{1,0:T(8,128)(2,1)S(1)} %copy-done.5), custom_call_target="tpu_custom_call" | custom-call | flops 1000000000 | bytes 1048576 | tf_op jit(solution)/shard_map/forward_tables/pallas_call | solution.py:230
  14.3 0.0 collective-permute-done.facet
  14.3 2.3 %contributions.1 = bf16[4,2,256,128]{3,2,1,0:T(8,128)(2,1)} custom-call(bf16[512,512]{1,0:T(8,128)(2,1)S(1)} %collective-permute-done.facet, bf16[4,256,1024]{2,1,0:T(8,128)(2,1)S(1)} %get-tuple-element.9.row_tab, bf16[512,512]{1,0:T(8,128)(2,1)S(1)} %get-tuple-element.10.col_tab, bf16[512,512]{1,0:T(8,128)(2,1)S(1)} %get-tuple-element.11.pq), custom_call_target="tpu_custom_call" | custom-call | flops 2000000000 | bytes 1048576 | tf_op jit(solution)/shard_map/contributions/pallas_call | solution.py:230
  16.7 0.0 all-to-all-done.1.vis.ask
  16.7 4.1 %all-to-all-start = ((bf16[4,2,256,128]{3,2,1,0:T(8,128)(2,1)}), bf16[4,2,256,128]{3,2,1,0:T(8,128)(2,1)S(1)}, u32[]{:S(2)}, u32[]{:S(2)}) async-start(bf16[4,2,256,128]{3,2,1,0:T(8,128)(2,1)} %contributions.1), calls=%async_computation | async-start | bytes 1048576 | tf_op jit(solution)/shard_map/all_to_all | solution.py:251
  20.8 1.8 %gridding.1 = bf16[3,256,128]{2,1,0:T(8,128)(2,1)S(1)} custom-call(s32[6]{0:T(128)S(1)} %pad_add_fusion.info, bf16[8,8,512]{2,1,0:T(8,128)(2,1)S(1)} %all-to-all-done.1.vis.ask), custom_call_target="tpu_custom_call" | custom-call | flops 1000000000 | bytes 1048576 | tf_op jit(solution)/shard_map/gridding/pallas_call | solution.py:230
  22.6 7.1 %all-to-all-done = bf16[4,2,256,128]{3,2,1,0:T(8,128)(2,1)S(1)} async-done(((bf16[4,2,256,128]{3,2,1,0:T(8,128)(2,1)}), bf16[4,2,256,128]{3,2,1,0:T(8,128)(2,1)S(1)}, u32[]{:S(2)}, u32[]{:S(2)}) %all-to-all-start) | async-done | bytes 524320 | tf_op jit(solution)/shard_map/all_to_all | solution.py:251
  29.7 0.1 reduce_sum.33
  29.8 0.1 copy_bitcast_fusion.1
  29.9 0.0 copy-start.6
  29.9 0.0 copy-start.7
  29.9 0.0 copy-start.8
  29.9 0.0 copy-start.9
  29.9 21.7 %all_to_all.35 = bf16[32,5,8,128]{3,2,1,0:T(8,128)(2,1)S(1)} all-to-all(bf16[32,5,8,128]{3,2,1,0:T(8,128)(2,1)S(1)} %copy_bitcast_fusion.1), channel_id=1, replica_groups=mesh['frow'=8,'fcol'=32] {'fcol'}, dimensions={0} | all-to-all | bytes 655360 | tf_op jit(solution)/shard_map/all_to_all | solution.py:251
  51.7 0.1 reduce_sum.34
  51.7 0.9 broadcast_in_dim.13
  52.6 8.3 %all-to-all-start.3 = ((bf16[64,5,8,128]{3,2,1,0:T(8,128)(2,1)}), bf16[64,5,8,128]{3,2,1,0:T(8,128)(2,1)S(1)}, u32[]{:S(2)}, u32[]{:S(2)}) async-start(bf16[64,5,8,128]{3,2,1,0:T(8,128)(2,1)} %broadcast_in_dim.13), calls=%async_computation.3 | async-start | bytes 1310720 | tf_op jit(solution)/shard_map/all_to_all | solution.py:251
  61.0 20.0 %all-to-all-done.3 = bf16[64,5,8,128]{3,2,1,0:T(8,128)(2,1)S(1)} async-done(((bf16[64,5,8,128]{3,2,1,0:T(8,128)(2,1)}), bf16[64,5,8,128]{3,2,1,0:T(8,128)(2,1)S(1)}, u32[]{:S(2)}, u32[]{:S(2)}) %all-to-all-start.3) | async-done | bytes 655392 | tf_op jit(solution)/shard_map/all_to_all | solution.py:251
  81.0 0.1 copy.18
  81.1 0.0 copy-done.6
  81.1 0.0 copy-done.7
  81.1 0.0 copy-done.8
  81.1 0.0 copy-done.9
  81.1 1.1 grids.1
  82.3 2.5 %answers.1 = f32[4,2,512]{2,1,0:T(2,128)} custom-call(s32[6]{0:T(128)S(1)} %pad_add_fusion.info, bf16[8,8,512]{2,1,0:T(8,128)(2,1)S(1)} %all-to-all-done.1.vis.ask, bf16[2,2,256,256]{3,2,1,0:T(8,128)(2,1)S(1)} %get-tuple-element.15.hat), custom_call_target="tpu_custom_call" | custom-call | flops 1000000000 | bytes 1048576 | tf_op jit(solution)/shard_map/answers/pallas_call | solution.py:230
  84.8 3.3 %all-to-all-start.6 = ((f32[4,2,512]{2,1,0:T(2,128)}), f32[4,2,512]{2,1,0:T(2,128)S(1)}, u32[]{:S(2)}, u32[]{:S(2)}) async-start(f32[4,2,512]{2,1,0:T(2,128)} %answers.1), calls=%async_computation.6 | async-start | bytes 32768 | tf_op jit(solution)/shard_map/all_to_all | solution.py:251
  88.1 4.2 %all-to-all-done.6 = f32[4,2,512]{2,1,0:T(2,128)S(1)} async-done(((f32[4,2,512]{2,1,0:T(2,128)}), f32[4,2,512]{2,1,0:T(2,128)S(1)}, u32[]{:S(2)}, u32[]{:S(2)}) %all-to-all-start.6) | async-done | bytes 16416 | tf_op jit(solution)/shard_map/all_to_all | solution.py:251
  92.2 0.9 broadcast_in_dim.14
  93.1 3.5 %all-to-all-start.4 = ((bf16[4,2,256,128]{3,2,1,0:T(8,128)(2,1)}), bf16[4,2,256,128]{3,2,1,0:T(8,128)(2,1)S(1)}, u32[]{:S(2)}, u32[]{:S(2)}) async-start(bf16[4,2,256,128]{3,2,1,0:T(8,128)(2,1)} %broadcast_in_dim.14), calls=%async_computation.4 | async-start | bytes 1048576 | tf_op jit(solution)/shard_map/all_to_all | solution.py:251
  96.6 0.0 copy-start.1
  96.6 1.4 %back_tables.1 = (bf16[4,512,256]{2,1,0:T(8,128)(2,1)S(1)}, bf16[4,256,512]{2,1,0:T(8,128)(2,1)S(1)}) custom-call(s32[6]{0:T(128)S(1)} %pad_add_fusion.info), custom_call_target="tpu_custom_call" | custom-call | flops 1000000000 | bytes 1048576 | tf_op jit(solution)/shard_map/back_tables/pallas_call | solution.py:230
  98.0 0.0 copy-done.1
  98.0 0.6 sub.3
  98.6 6.3 %all-to-all-done.4 = bf16[4,2,256,128]{3,2,1,0:T(8,128)(2,1)S(1)} async-done(((bf16[4,2,256,128]{3,2,1,0:T(8,128)(2,1)}), bf16[4,2,256,128]{3,2,1,0:T(8,128)(2,1)S(1)}, u32[]{:S(2)}, u32[]{:S(2)}) %all-to-all-start.4) | async-done | bytes 524320 | tf_op jit(solution)/shard_map/all_to_all | solution.py:251
  104.9 0.2 broadcast_in_dim.15
  105.1 6.3 %all_to_all.36.back = bf16[2,4,2,256,128]{4,3,2,1,0:T(8,128)(2,1)S(1)} all-to-all(bf16[2,4,2,256,128]{4,3,2,1,0:T(8,128)(2,1)S(1)} %broadcast_in_dim.15), channel_id=1, replica_groups={{0,32},{64,96},{128,160},{192,224},{1,33},{65,97},{129,161},{193,225},{..., dimensions={0} | all-to-all | bytes 2097152 | tf_op jit(solution)/shard_map/all_to_all | solution.py:251
  111.4 2.9 %image.1 = f32[512,512]{1,0:T(8,128)} custom-call(bf16[2,4,2,256,128]{4,3,2,1,0:T(8,128)(2,1)S(1)} %all_to_all.36.back, bf16[4,512,256]{2,1,0:T(8,128)(2,1)S(1)} %get-tuple-element.13.row_tab, bf16[4,256,512]{2,1,0:T(8,128)(2,1)S(1)} %get-tuple-element.14.col_tab), custom_call_target="tpu_custom_call" | custom-call | flops 2000000000 | bytes 1048576 | tf_op jit(solution)/shard_map/image/pallas_call | solution.py:230
  (6 shorter events, 0.1 us)
Async XLA Ops:
  0.6 13.7 %collective-permute-start = (bf16[512,512]{1,0:T(8,128)(2,1)}, bf16[512,512]{1,0:T(8,128)(2,1)S(1)}, u32[]{:S(2)}, u32[]{:S(2)}) collective-permute-start(bf16[512,512]{1,0:T(8,128)(2,1)} %facet.1), channel_id=1, source_target_pairs={{0,32},{32,0},{64,96},{96,64},{128,160},{160,128},{192,224},{224,1... | collective-permute-start | bytes 1572872 | tf_op jit(solution)/shard_map/ppermute | solution.py:275
  4.0 0.7 copy-start
  4.6 0.7 copy-start.2
  5.3 0.7 copy-start.3
  6.0 0.7 copy-start.4
  7.3 9.4 %all-to-all-start.1 = ((bf16[8,8,512]{2,1,0:T(8,128)(2,1)}), bf16[8,8,512]{2,1,0:T(8,128)(2,1)S(1)}, u32[]{:S(2)}, u32[]{:S(2)}) async-start(bf16[8,8,512]{2,1,0:T(8,128)(2,1)} %broadcast_in_dim.12), calls=%async_computation.1 | async-start | bytes 131072 | tf_op jit(solution)/shard_map/all_to_all | solution.py:251
  11.4 1.0 copy-start.5
  16.7 13.1 %all-to-all-start = ((bf16[4,2,256,128]{3,2,1,0:T(8,128)(2,1)}), bf16[4,2,256,128]{3,2,1,0:T(8,128)(2,1)S(1)}, u32[]{:S(2)}, u32[]{:S(2)}) async-start(bf16[4,2,256,128]{3,2,1,0:T(8,128)(2,1)} %contributions.1), calls=%async_computation | async-start | bytes 1048576 | tf_op jit(solution)/shard_map/all_to_all | solution.py:251
  29.9 51.2 %copy-start.6 = (bf16[512,512]{1,0:T(8,128)(2,1)S(1)}, bf16[512,512]{1,0:T(8,128)(2,1)}, u32[]{:S(2)}) copy-start(bf16[512,512]{1,0:T(8,128)(2,1)} %constant.41.clone.forward) | copy-start | bytes 1572868
  29.9 51.2 %copy-start.7 = (bf16[512,512]{1,0:T(8,128)(2,1)S(1)}, bf16[512,512]{1,0:T(8,128)(2,1)}, u32[]{:S(2)}) copy-start(bf16[512,512]{1,0:T(8,128)(2,1)} %constant.42.clone.inverse) | copy-start | bytes 1572868
  29.9 51.2 %copy-start.8 = (bf16[256,256]{1,0:T(8,128)(2,1)S(1)}, bf16[256,256]{1,0:T(8,128)(2,1)}, u32[]{:S(2)}) copy-start(bf16[256,256]{1,0:T(8,128)(2,1)} %constant.39.clone.kcos) | copy-start | bytes 393220
  29.9 51.2 %copy-start.9 = (bf16[256,256]{1,0:T(8,128)(2,1)S(1)}, bf16[256,256]{1,0:T(8,128)(2,1)}, u32[]{:S(2)}) copy-start(bf16[256,256]{1,0:T(8,128)(2,1)} %constant.40.clone.ksin) | copy-start | bytes 393220
  52.6 28.3 %all-to-all-start.3 = ((bf16[64,5,8,128]{3,2,1,0:T(8,128)(2,1)}), bf16[64,5,8,128]{3,2,1,0:T(8,128)(2,1)S(1)}, u32[]{:S(2)}, u32[]{:S(2)}) async-start(bf16[64,5,8,128]{3,2,1,0:T(8,128)(2,1)} %broadcast_in_dim.13), calls=%async_computation.3 | async-start | bytes 1310720 | tf_op jit(solution)/shard_map/all_to_all | solution.py:251
  84.8 7.4 %all-to-all-start.6 = ((f32[4,2,512]{2,1,0:T(2,128)}), f32[4,2,512]{2,1,0:T(2,128)S(1)}, u32[]{:S(2)}, u32[]{:S(2)}) async-start(f32[4,2,512]{2,1,0:T(2,128)} %answers.1), calls=%async_computation.6 | async-start | bytes 32768 | tf_op jit(solution)/shard_map/all_to_all | solution.py:251
  93.1 11.8 %all-to-all-start.4 = ((bf16[4,2,256,128]{3,2,1,0:T(8,128)(2,1)}), bf16[4,2,256,128]{3,2,1,0:T(8,128)(2,1)S(1)}, u32[]{:S(2)}, u32[]{:S(2)}) async-start(bf16[4,2,256,128]{3,2,1,0:T(8,128)(2,1)} %broadcast_in_dim.14), calls=%async_computation.4 | async-start | bytes 1048576 | tf_op jit(solution)/shard_map/all_to_all | solution.py:251
  96.6 1.4 %copy-start.1 = (f32[2,512]{1,0:T(2,128)S(1)}, f32[2,512]{1,0:T(2,128)}, u32[]{:S(2)}) copy-start(f32[2,512]{1,0:T(2,128)} %observed.1) | copy-start | bytes 12292

commit v3 on v2

v3 whole, which is shorter than its diff:
```python
import functools
import math

import jax
import jax.numpy as jnp
import ml_dtypes
import numpy as np
from jax import lax
from jax.experimental import pallas as pl
from jax.experimental.pallas import tpu as pltpu
from jax.sharding import PartitionSpec as P

SKY = 65536
SG = 256
NR = 2
NC = 2
HALF = SG // 2
LANES = 128


def wave(count):
    count = count & (SKY - 1)
    turned = count + SKY // 8
    near = (turned & (SKY // 4 - 1)) - SKY // 8
    quarter = lax.shift_right_logical(turned, 14) & 3
    t = near.astype(jnp.float32) * (2.0 * math.pi / SKY)
    q = t * t
    sin = t * (1.0 + q * (-1.0 / 6 + q * (1.0 / 120 + q * (-1.0 / 5040 + q * (1.0 / 362880)))))
    cos = 1.0 + q * (-0.5 + q * (1.0 / 24 + q * (-1.0 / 720 + q * (1.0 / 40320))))
    odd = (quarter & 1) == 1
    one, two = jnp.where(odd, sin, cos), jnp.where(odd, cos, sin)
    return (
        jnp.where((quarter == 1) | (quarter == 2), -one, one),
        jnp.where(quarter >= 2, -two, two),
    )


def lanes(n):
    return lax.broadcasted_iota(jnp.int32, (1, n), 1)


def sublanes(n):
    return lax.broadcasted_iota(jnp.int32, (n, 1), 0)


def spread(coarse, fine, store):
    for k in range(coarse[0].shape[0]):
        c, s = coarse[0][k:k + 1], coarse[1][k:k + 1]
        store(k * 16, c * fine[0] - s * fine[1], s * fine[0] + c * fine[1])


def back_tables_kernel(rows_count, cols_count, side, info, row_tab, col_tab):
    bf16 = jnp.bfloat16
    row_index, col_index = info[4], info[5]
    unit = sublanes(16)
    row_step = SKY // (rows_count * side)
    row_base = row_index * (SKY // rows_count)
    for r in range(NR):
        freq = info[r] + lanes(SG)
        coarse = wave((row_base + 16 * row_step * sublanes(side // 16)) * freq)
        fine = wave((row_step * unit) * freq)

        def store(at, cos, sin, r=r):
            row_tab[2 * r, at:at + 16] = cos.astype(bf16)
            row_tab[2 * r + 1, at:at + 16] = sin.astype(bf16)

        spread(coarse, fine, store)
    col_step = SKY // (cols_count * side)
    pos = col_index * (SKY // cols_count) + col_step * lanes(side)
    fine = wave(unit * pos)
    for c in range(NC):
        coarse = wave((info[2 + c] + 16 * unit) * pos)

        def store(at, cos, sin, c=c):
            col_tab[2 * c, at:at + 16] = cos.astype(bf16)
            col_tab[2 * c + 1, at:at + 16] = (-sin).astype(bf16)

        spread(coarse, fine, store)


def columns_kernel(cols_count, info, facet, subgrid, u, v, observed, out, col_tab):
    f32, bf16 = jnp.float32, jnp.bfloat16
    side = facet.shape[0]
    col_index = info[5]
    unit = sublanes(16)
    col_step = SKY // (cols_count * side)
    col_base = col_index * (SKY // cols_count)
    rows = [subgrid[...].astype(f32), u[...].astype(f32), v[...].astype(f32), observed[...]]
    vis = jnp.concatenate(rows + [jnp.zeros((11, side), f32)], 0).astype(bf16)
    for c in range(NC):
        freq = info[2 + c] + lanes(SG)
        coarse = wave((col_base + 16 * col_step * sublanes(side // 16)) * freq)
        fine = wave((col_step * unit) * freq)

        def store(at, cos, sin, c=c):
            for h in range(2):
                half = slice(h * HALF, (h + 1) * HALF)
                left = (2 * h + c) * SG
                col_tab[at:at + 16, left:left + HALF] = cos[:, half].astype(bf16)
                col_tab[at:at + 16, left + HALF:left + SG] = sin[:, half].astype(bf16)

        spread(coarse, fine, store)
    for h in range(2):
        part = jnp.dot(facet[...], col_tab[:, 2 * h * SG:2 * (h + 1) * SG], preferred_element_type=f32)
        out[h, :side] = part.astype(bf16)
        out[h, side:] = vis


def row_tables_kernel(rows_count, side, info, row_tab):
    bf16 = jnp.bfloat16
    chip = info[4] // 2
    unit = sublanes(16)
    row_step = SKY // (rows_count * side)
    for f in range(2):
        pos = (2 * chip + f) * (SKY // rows_count) + row_step * lanes(side)
        fine = wave(unit * pos)
        for r in range(NR):
            coarse = wave((info[r] + 16 * unit) * pos)

            def store(at, cos, sin, r=r, f=f):
                row_tab[2 * r, at:at + 16, f * side:(f + 1) * side] = cos.astype(bf16)
                row_tab[2 * r + 1, at:at + 16, f * side:(f + 1) * side] = sin.astype(bf16)

            spread(coarse, fine, store)


def contributions_kernel(scale, halves, row_tab, out, right):
    f32, bf16 = jnp.float32, jnp.bfloat16
    side = row_tab.shape[2] // 2
    vis = []
    for f in range(2):
        right[f * side:(f + 1) * side] = halves[f, :side]
        some = halves[f, side:]
        vis += [some[:, k * LANES:(k + 1) * LANES] for k in range(side // LANES)]
    for s in range(NR * NC):
        for k, some in enumerate(vis):
            at = 2 * SG + 16 * k
            out[s, at:at + 16] = some
    for r in range(NR):
        with_cos = jnp.dot(row_tab[2 * r], right[...], preferred_element_type=f32)
        with_sin = jnp.dot(row_tab[2 * r + 1], right[...], preferred_element_type=f32)
        for c in range(NC):
            at = 2 * c * HALF
            cp, cq = with_cos[:, at:at + HALF], with_cos[:, at + HALF:at + 2 * HALF]
            sp, sq = with_sin[:, at:at + HALF], with_sin[:, at + HALF:at + 2 * HALF]
            out[r * NC + c, :SG] = ((cp - sq) * scale).astype(bf16)
            out[r * NC + c, SG:2 * SG] = (-(cq + sp) * scale).astype(bf16)


def vis_rows(block):
    count = block.shape[0] // 16
    return jnp.concatenate([block[16 * k:16 * k + 8] for k in range(count)], 1)


def gridding_kernel(info, parts, pieces, planes):
    f32, bf16 = jnp.float32, jnp.bfloat16
    row_index = info[4]
    chip = (row_index // 2).astype(f32)
    v_at = (sublanes(HALF) + (row_index % 2) * HALF).astype(f32)
    counter = sublanes(SG).astype(f32)
    count = parts.shape[0]
    total = jnp.zeros((SG, 3 * HALF), f32)
    for k in range(count):
        one = vis_rows(parts[k, 2 * SG:].astype(f32))
        hot = jnp.where((one[1:2] == counter) & (one[0:1] == chip), 1.0, 0.0).astype(bf16)
        pick = one[2:3] == v_at
        right = jnp.concatenate(
            [jnp.where(pick, one[3:4], 0.0), jnp.where(pick, one[4:5], 0.0), jnp.where(pick, 1.0, 0.0)], 0
        ).astype(bf16)
        total = total + lax.dot_general(hot, right, (((1,), (1,)), ((), ())), preferred_element_type=f32)
    for p in range(2):
        some = parts[0, p * SG:(p + 1) * SG].astype(f32)
        for k in range(1, count):
            some = some + parts[k, p * SG:(p + 1) * SG].astype(f32)
        planes[p] = some
    for p in range(3):
        planes[2 + p] = total[:, p * HALF:(p + 1) * HALF]
    each = SG // pieces.shape[0]
    for j in range(pieces.shape[0]):
        rows = [planes[p, j * each:(j + 1) * each] for p in range(5)]
        pieces[j] = jnp.concatenate(rows, 0).astype(bf16)


def pieces_sum_kernel(pieces, out):
    f32, bf16 = jnp.float32, jnp.bfloat16
    total = pieces[0].astype(f32)
    for j in range(1, pieces.shape[0]):
        total = total + pieces[j].astype(f32)
    total = total.astype(bf16)
    for j in range(out.shape[0]):
        out[j] = total


def grids_kernel(info, pieces, vis, kcos, ksin, forward, inverse, out, planes, cat, hat):
    f32, bf16 = jnp.float32, jnp.bfloat16
    row_index = info[4]
    core = row_index % 2
    chip = (row_index // 2).astype(f32)
    count = pieces.shape[1]
    each = SG // count
    for h in range(2):
        for j in range(count):
            some = pieces[h, j].astype(f32)
            for p in range(5):
                planes[p, j * each:(j + 1) * each, h * HALF:(h + 1) * HALF] = some[p * each:(p + 1) * each]
    cat[:, :SG] = planes[0].astype(bf16)
    cat[:, SG:] = planes[1].astype(bf16)
    cat[...] = jnp.dot(cat[...], forward[...], preferred_element_type=f32).astype(bf16)
    with_cos = jnp.dot(kcos[...], cat[...], preferred_element_type=f32)
    with_sin = jnp.dot(ksin[...], cat[...], preferred_element_type=f32)
    hat_real = (with_cos[:, :SG] - with_sin[:, SG:]) * (1.0 / SG)
    hat_imag = (with_sin[:, :SG] + with_cos[:, SG:]) * (1.0 / SG)
    hat[:, :SG] = hat_real.astype(bf16)
    hat[:, SG:] = hat_imag.astype(bf16)
    cat[:, :SG] = (planes[2] - planes[4] * hat_real).astype(bf16)
    cat[:, SG:] = (planes[3] - planes[4] * hat_imag).astype(bf16)
    cat[...] = jnp.dot(cat[...], inverse[...], preferred_element_type=f32).astype(bf16)
    with_cos = jnp.dot(kcos[...], cat[...], preferred_element_type=f32)
    with_sin = jnp.dot(ksin[...], cat[...], preferred_element_type=f32)
    real = (with_cos[:, :SG] + with_sin[:, SG:]) * (1.0 / SG)
    imag = (with_cos[:, SG:] - with_sin[:, :SG]) * (1.0 / SG)
    real = jnp.where(core == 0, real[:, :HALF], real[:, HALF:]).astype(bf16)
    imag = jnp.where(core == 0, imag[:, :HALF], imag[:, HALF:]).astype(bf16)
    counter = sublanes(SG).astype(f32)
    each = vis.shape[1] // 2
    for k in range(vis.shape[0]):
        out[k, :SG] = real
        out[k, SG:2 * SG] = imag
        ask = vis_rows(jnp.where(core == 0, vis[k, :each].astype(f32), vis[k, each:].astype(f32)))
        hot = jnp.where((ask[1:2] == counter) & (ask[0:1] == chip), 1.0, 0.0).astype(bf16)
        pick = ask[2:3] == counter
        line = lax.dot_general(hat[...], hot, (((0,), (0,)), ((), ())), preferred_element_type=f32)
        rows = []
        for part in range(2):
            value = jnp.sum(jnp.where(pick, line[part * SG:(part + 1) * SG], 0.0), axis=0, keepdims=True)
            rows += [value[:, i * LANES:(i + 1) * LANES] for i in range(value.shape[1] // LANES)]
        rows.append(jnp.zeros((16 - len(rows), LANES), f32))
        out[k, 2 * SG:] = jnp.concatenate(rows, 0).astype(bf16)


def image_kernel(scale, info, back, row_tab, col_tab, observed, out, residual, grid, both):
    f32, bf16 = jnp.float32, jnp.bfloat16
    core = info[4] % 2
    model = jnp.zeros((16, LANES), f32)
    for s in range(NR * NC):
        model = model + jnp.where(core == 0, back[0, s, 2 * SG:].astype(f32), back[1, s, 2 * SG:].astype(f32))
    count = observed.shape[1] // LANES
    for part in range(2):
        for i in range(count):
            at = slice(i * LANES, (i + 1) * LANES)
            residual[part:part + 1, at] = observed[part:part + 1, at] - model[part * count + i:part * count + i + 1]
    for c in range(NC):
        real = imag = None
        for r in range(NR):
            for k in range(2):
                for half in range(2):
                    at = k * SG + half * HALF
                    grid[:, at:at + HALF] = back[half, r * NC + c, k * SG:(k + 1) * SG]
            cos = jnp.dot(row_tab[2 * r], grid[...], preferred_element_type=f32)
            sin = jnp.dot(row_tab[2 * r + 1], grid[...], preferred_element_type=f32)
            re, im = cos[:, :SG] - sin[:, SG:], cos[:, SG:] + sin[:, :SG]
            real = re if real is None else real + re
            imag = im if imag is None else imag + im
        both[:, :SG] = real.astype(bf16)
        both[:, SG:] = imag.astype(bf16)
        part = jnp.dot(both[:, :SG], col_tab[2 * c], preferred_element_type=f32)
        part = part + jnp.dot(both[:, SG:], col_tab[2 * c + 1], preferred_element_type=f32)
        if c == 0:
            out[...] = part
        else:
            out[...] = (out[...] + part) * scale


def call(kernel, out_shape, name, scratch=(), scalars=0, cost=0):
    smem, vmem = pl.BlockSpec(memory_space=pltpu.SMEM), pl.BlockSpec(memory_space=pltpu.VMEM)

    def run(*args):
        return pl.pallas_call(
            kernel,
            out_shape=out_shape,
            in_specs=[smem] * scalars + [vmem] * (len(args) - scalars),
            out_specs=jax.tree.map(lambda _: vmem, out_shape),
            scratch_shapes=list(scratch),
            compiler_params=pltpu.CompilerParams(vmem_limit_bytes=24 * 2**20),
            cost_estimate=pl.CostEstimate(flops=cost, bytes_accessed=2**20, transcendentals=0),
            name=name,
        )(*args)

    return run


def grid_tables():
    counter = np.arange(SG)
    angles = (counter[:, None] * counter[None, :] % SG).astype(np.float64) * (2.0 * math.pi / SG)
    return np.cos(angles).astype(ml_dtypes.bfloat16), np.sin(angles).astype(ml_dtypes.bfloat16)


def exchange(blocks, axes, groups):
    return lax.all_to_all(blocks, axes, 0, 0, tiled=True, axis_index_groups=groups)


def shape(*dims, dtype=jnp.bfloat16):
    return jax.ShapeDtypeStruct(dims, dtype)


def shards(facet, row_offsets, col_offsets, vis_subgrid, vis_u, vis_v, observed):
    f32, bf16 = jnp.float32, jnp.bfloat16
    rows_count, cols_count = lax.axis_size("frow"), lax.axis_size("fcol")
    side = facet.shape[0]
    n_vis = vis_u.shape[0]
    chips = rows_count // 2
    each = SG // cols_count
    x_groups = [[2 * chip + core for chip in range(chips)] for core in range(2)]
    core_groups = [[2 * chip, 2 * chip + 1] for chip in range(chips)]
    row_index, col_index = lax.axis_index("frow"), lax.axis_index("fcol")
    scale_in = 1.0 / (side * math.sqrt(rows_count * cols_count))
    scale_out = 1.0 / (SG * math.sqrt(NR * NC))
    info = jnp.concatenate([row_offsets, col_offsets, jnp.stack([row_index, col_index])]).astype(jnp.int32)

    halves = call(
        functools.partial(columns_kernel, cols_count), shape(2, side + 16, 4 * HALF), "columns",
        scratch=[pltpu.VMEM((side, 8 * HALF), bf16)], scalars=1, cost=10**9,
    )(info, facet, vis_subgrid.reshape(1, n_vis), vis_u.reshape(1, n_vis), vis_v.reshape(1, n_vis), observed)
    halves = exchange(halves, "frow", core_groups)
    row_tab = call(
        functools.partial(row_tables_kernel, rows_count, side), shape(4, SG, 2 * side), "row_tables", scalars=1, cost=10**9
    )(info)
    vis_rows_count = 16 * 2 * n_vis // LANES
    parts = call(
        functools.partial(contributions_kernel, scale_in), shape(NR * NC, 2 * SG + vis_rows_count, HALF), "contributions",
        scratch=[pltpu.VMEM((2 * side, 4 * HALF), bf16)], cost=2 * 10**9,
    )(halves, row_tab)
    parts = exchange(parts, "frow", x_groups)

    pieces = call(
        gridding_kernel, shape(cols_count, 5 * each, HALF), "gridding",
        scratch=[pltpu.VMEM((5, SG, HALF), f32)], scalars=1, cost=10**9,
    )(info, parts)
    pieces = exchange(pieces, "fcol", None)
    pieces = call(pieces_sum_kernel, shape(cols_count, 5 * each, HALF), "pieces_sum", cost=10**6)(pieces)
    pieces = exchange(pieces, "fcol", None)
    pieces = exchange(jnp.broadcast_to(pieces, (2,) + pieces.shape), "frow", core_groups)

    kcos, ksin = grid_tables()
    forward_block = np.concatenate([np.concatenate([kcos, ksin], 1), np.concatenate([-ksin, kcos], 1)], 0)
    inverse_block = np.concatenate([np.concatenate([kcos, -ksin], 1), np.concatenate([ksin, kcos], 1)], 0)
    back = call(
        grids_kernel, shape(chips, 2 * SG + 16, HALF), "grids",
        scratch=[pltpu.VMEM((5, SG, SG), f32), pltpu.VMEM((SG, 2 * SG), bf16), pltpu.VMEM((SG, 2 * SG), bf16)],
        scalars=1, cost=10**9,
    )(info, pieces, parts[:, 2 * SG:], kcos, ksin, forward_block, inverse_block)
    back = exchange(back, "frow", x_groups)
    back = exchange(jnp.broadcast_to(back, (2,) + back.shape), "frow", core_groups)

    back_row, back_col = call(
        functools.partial(back_tables_kernel, rows_count, cols_count, side),
        (shape(4, side, SG), shape(4, SG, side)), "back_tables", scalars=1, cost=10**9,
    )(info)
    return call(
        functools.partial(image_kernel, scale_out),
        (shape(side, side, dtype=f32), shape(2, n_vis, dtype=f32)), "image",
        scratch=[pltpu.VMEM((SG, 2 * SG), bf16), pltpu.VMEM((side, 2 * SG), bf16)], scalars=1, cost=2 * 10**9,
    )(info, back, back_row, back_col, observed)


def solution(mesh):
    in_specs = (
        P("frow", "fcol"),
        P(),
        P(),
        P(("frow", "fcol")),
        P(("frow", "fcol")),
        P(("frow", "fcol")),
        P(None, ("frow", "fcol")),
    )
    out_specs = (P("frow", "fcol"), P(None, ("frow", "fcol")))
    return jax.shard_map(shards, mesh=mesh, in_specs=in_specs, out_specs=out_specs, check_vma=False)
```

time: 115 us -> 105 us (0.913)
  blocking collectives: 28 us -> 47.7 us
  waiting for transfers between devices: 37.5 us -> 19.2 us
  starting transfers between devices: 25.8 us -> 16.3 us
  local copies, waits for them, and re-layouts: 6.54 us -> 4.04 us
  Pallas kernels: 14 us -> 15.5 us
    all_to_all x2 -> x4, blocking collectives: 28 us -> 47.7 us  [exchange(): lax.all_to_all(blocks, axes, 0, 0, tiled=True, axis_index_groups=groups)]
    all_to_all x5 -> x3, waiting for transfers between devices: 37.5 us -> 19.2 us  [exchange(): lax.all_to_all(blocks, axes, 0, 0, tiled=True, axis_index_groups=groups)]
    all_to_all x5 -> x3, starting transfers between devices: 22.5 us -> 16.3 us  [exchange(): lax.all_to_all(blocks, axes, 0, 0, tiled=True, axis_index_groups=groups)]
    ppermute x1 -> x0, starting transfers between devices: 3.33 us -> none  [shards(): lax.ppermute(facet, 'frow', [(index, index ^ 1) for index in range(rows_c...]
    broadcast_in_dim x4 -> x2, local copies, waits for them, and re-layouts: 2.6 us -> 0.23 us  [the longest x1 0.14 us: shards(): jnp.broadcast_to(back, (2,) + back.shape)]
    pallas_call x8, Pallas kernels: 14 us -> 15.5 us  [run(): pl.pallas_call(kernel, out_shape=out_shape, in_specs=[smem] * scalars + [...]
  transfers between devices with their start and end apart: 6 -> 3, of which waited for: 4 -> 3; matrix products, arithmetic and copies ran while one was open for 2% -> 0% of each run, Pallas kernels for 7% -> 3%
where the time goes in v3:
time: 105 us; the launch traced here: 104 us
  blocking collectives  47.7 us (45%)
  waiting for transfers between devices  19.2 us (18%)
  starting transfers between devices  16.3 us (16%)
  Pallas kernels  15.5 us (15%)
  local copies, waits for them, and re-layouts  4.04 us (4%)
    all_to_all x4, blocking collectives, exchange(): lax.all_to_all(blocks, axes, 0, 0, tiled=True, axis_index_groups=groups)  47.7 us
    all_to_all x3, waiting for transfers between devices, exchange(): lax.all_to_all(blocks, axes, 0, 0, tiled=True, axis_index_groups=groups)  19.2 us
    all_to_all x3, starting transfers between devices, exchange(): lax.all_to_all(blocks, axes, 0, 0, tiled=True, axis_index_groups=groups)  16.3 us
    pallas_call x8, Pallas kernels, run(): pl.pallas_call(kernel, out_shape=out_shape, in_specs=[smem] * scalars + [...  15.5 us
    unnamed x20, local copies, waits for them, and re-layouts  3.81 us
  transfers between devices with their start and end apart: 3, of which 3 were waited for; matrix products, arithmetic and copies ran while one was open for 0% of the time, Pallas kernels for 3%

profile of v3, /device:TPU:1, one launch (start us, length us, event | category | flops | bytes accessed | tf_op | source)
XLA Modules:
  0.0 104.2 jit_solution(1097133746016786188)
XLA Ops:
  0.6 0.8 pad_add_fusion.info
  1.4 0.0 copy-start
  1.4 1.0 copy-done
  2.4 0.0 copy-start.1
  2.4 0.7 copy-done.1
  3.1 0.0 copy-start.3
  3.1 0.7 copy-done.3
  3.8 0.0 copy-start.4
  3.8 0.7 copy-done.4
  4.5 0.0 copy-start.5
  4.5 0.7 copy-done.5
  5.2 2.4 %columns.1 = bf16[2,528,512]{2,1,0:T(8,128)(2,1)} custom-call(s32[6]{0:T(128)S(1)} %pad_add_fusion.info, bf16[512,512]{1,0:T(8,128)(2,1)S(1)} %copy-done, s32[1,512]{1,0:T(1,128)S(1)} %bitcast.5, s32[1,512]{1,0:T(1,128)S(1)} %bitcast.6, s32[1,512]{1,0:T(1,128)S(1)} %bitcast.7, f32[2,512]{1,0:T(2,128)S(1)} %copy-done.1), custom_call_target="tpu_custom_call" | custom-call | flops 1000000000 | bytes 1048576 | tf_op jit(solution)/shard_map/columns/pallas_call | solution.py:278
  7.5 6.8 %all-to-all-start = ((bf16[2,528,512]{2,1,0:T(8,128)(2,1)}), bf16[2,528,512]{2,1,0:T(8,128)(2,1)S(1)}, u32[]{:S(2)}, u32[]{:S(2)}) async-start(bf16[2,528,512]{2,1,0:T(8,128)(2,1)} %columns.1), calls=%async_computation | async-start | bytes 2162688 | tf_op jit(solution)/shard_map/all_to_all | solution.py:299
  14.3 1.3 %row_tables.1.row_tab = bf16[4,256,1024]{2,1,0:T(8,128)(2,1)S(1)} custom-call(s32[6]{0:T(128)S(1)} %pad_add_fusion.info), custom_call_target="tpu_custom_call" | custom-call | flops 1000000000 | bytes 1048576 | tf_op jit(solution)/shard_map/row_tables/pallas_call | solution.py:278
  15.7 0.4 all-to-all-done.halves
  16.1 1.3 %contributions.1 = bf16[4,640,128]{2,1,0:T(8,128)(2,1)S(1)} custom-call(bf16[2,528,512]{2,1,0:T(8,128)(2,1)S(1)} %all-to-all-done.halves, bf16[4,256,1024]{2,1,0:T(8,128)(2,1)S(1)} %row_tables.1.row_tab), custom_call_target="tpu_custom_call" | custom-call | flops 2000000000 | bytes 1048576 | tf_op jit(solution)/shard_map/contributions/pallas_call | solution.py:278
  17.4 13.0 %all_to_all.35.parts = bf16[4,640,128]{2,1,0:T(8,128)(2,1)S(1)} all-to-all(bf16[4,640,128]{2,1,0:T(8,128)(2,1)S(1)} %contributions.1), channel_id=1, replica_groups={{0,64,128,192},{32,96,160,224},{1,65,129,193},{33,97,161,225},{2,66,130..., dimensions={0} | all-to-all | bytes 1310720 | tf_op jit(solution)/shard_map/all_to_all | solution.py:299
  30.4 1.8 %gridding.1 = bf16[32,40,128]{2,1,0:T(8,128)(2,1)S(1)} custom-call(s32[6]{0:T(128)S(1)} %pad_add_fusion.info, bf16[4,640,128]{2,1,0:T(8,128)(2,1)S(1)} %all_to_all.35.parts), custom_call_target="tpu_custom_call" | custom-call | flops 1000000000 | bytes 1048576 | tf_op jit(solution)/shard_map/gridding/pallas_call | solution.py:278
  32.3 20.8 %all_to_all.36.pieces = bf16[32,40,128]{2,1,0:T(8,128)(2,1)S(1)} all-to-all(bf16[32,40,128]{2,1,0:T(8,128)(2,1)S(1)} %gridding.1), channel_id=1, replica_groups=mesh['frow'=8,'fcol'=32] {'fcol'}, dimensions={0} | all-to-all | bytes 655360 | tf_op jit(solution)/shard_map/all_to_all | solution.py:299
  53.1 0.8 pieces_sum.1
  53.9 6.0 %all-to-all-start.3 = ((bf16[32,40,128]{2,1,0:T(8,128)(2,1)}), bf16[32,40,128]{2,1,0:T(8,128)(2,1)S(1)}, u32[]{:S(2)}, u32[]{:S(2)}) async-start(bf16[32,40,128]{2,1,0:T(8,128)(2,1)} %pieces_sum.1), calls=%async_computation.3 | async-start | bytes 655360 | tf_op jit(solution)/shard_map/all_to_all | solution.py:299
  59.9 0.0 copy-start.6
  59.9 0.0 copy-start.7
  59.9 0.0 copy-start.8
  60.0 0.0 copy-start.9
  60.0 10.8 %all-to-all-done.3 = bf16[32,40,128]{2,1,0:T(8,128)(2,1)S(1)} async-done(((bf16[32,40,128]{2,1,0:T(8,128)(2,1)}), bf16[32,40,128]{2,1,0:T(8,128)(2,1)S(1)}, u32[]{:S(2)}, u32[]{:S(2)}) %all-to-all-start.3) | async-done | bytes 327712 | tf_op jit(solution)/shard_map/all_to_all | solution.py:299
  70.8 0.1 broadcast_in_dim.6
  70.9 8.4 %all_to_all.37.pieces = bf16[2,32,40,128]{3,2,1,0:T(8,128)(2,1)S(1)} all-to-all(bf16[2,32,40,128]{3,2,1,0:T(8,128)(2,1)S(1)} %broadcast_in_dim.6), channel_id=1, replica_groups={{0,32},{64,96},{128,160},{192,224},{1,33},{65,97},{129,161},{193,225},{..., dimensions={0} | all-to-all | bytes 1310720 | tf_op jit(solution)/shard_map/all_to_all | solution.py:299
  79.3 0.0 copy-done.6
  79.3 0.0 copy-done.7
  79.3 0.0 copy-done.8
  79.3 0.0 copy-done.9
  79.3 3.0 %grids.1 = bf16[4,528,128]{2,1,0:T(8,128)(2,1)} custom-call(s32[6]{0:T(128)S(1)} %pad_add_fusion.info, bf16[2,32,40,128]{3,2,1,0:T(8,128)(2,1)S(1)} %all_to_all.37.pieces, bf16[4,128,128]{2,1,0:T(8,128)(2,1)S(1)} %slice.4.vis, bf16[256,256]{1,0:T(8,128)(2,1)S(1)} %copy-done.9, bf16[256,256]{1,0:T(8,128)(2,1)S(1)} %copy-done.8, ...), custom_call_target="tpu_custom_call" | custom-call | flops 1000000000 | bytes 1048576 | tf_op jit(solution)/shard_map/grids/pallas_call | solution.py:278
  82.3 3.5 %all-to-all-start.5 = ((bf16[4,528,128]{2,1,0:T(8,128)(2,1)}), bf16[4,528,128]{2,1,0:T(8,128)(2,1)S(1)}, u32[]{:S(2)}, u32[]{:S(2)}) async-start(bf16[4,528,128]{2,1,0:T(8,128)(2,1)} %grids.1), calls=%async_computation.5 | async-start | bytes 1081344 | tf_op jit(solution)/shard_map/all_to_all | solution.py:299
  85.8 1.4 %back_tables.1 = (bf16[4,512,256]{2,1,0:T(8,128)(2,1)S(1)}, bf16[4,256,512]{2,1,0:T(8,128)(2,1)S(1)}) custom-call(s32[6]{0:T(128)S(1)} %pad_add_fusion.info), custom_call_target="tpu_custom_call" | custom-call | flops 1000000000 | bytes 1048576 | tf_op jit(solution)/shard_map/back_tables/pallas_call | solution.py:278
  87.2 8.0 %all-to-all-done.5 = bf16[4,528,128]{2,1,0:T(8,128)(2,1)S(1)} async-done(((bf16[4,528,128]{2,1,0:T(8,128)(2,1)}), bf16[4,528,128]{2,1,0:T(8,128)(2,1)S(1)}, u32[]{:S(2)}, u32[]{:S(2)}) %all-to-all-start.5) | async-done | bytes 540704 | tf_op jit(solution)/shard_map/all_to_all | solution.py:299
  95.2 0.1 broadcast_in_dim.7
  95.3 0.0 copy-start.2
  95.3 5.4 %all_to_all.38.back = bf16[2,4,528,128]{3,2,1,0:T(8,128)(2,1)S(1)} all-to-all(bf16[2,4,528,128]{3,2,1,0:T(8,128)(2,1)S(1)} %broadcast_in_dim.7), channel_id=1, replica_groups={{0,32},{64,96},{128,160},{192,224},{1,33},{65,97},{129,161},{193,225},{..., dimensions={0} | all-to-all | bytes 2162688 | tf_op jit(solution)/shard_map/all_to_all | solution.py:299
  100.7 0.0 copy-done.2
  100.7 3.5 %image.1 = (f32[512,512]{1,0:T(8,128)}, f32[2,512]{1,0:T(2,128)}) custom-call(s32[6]{0:T(128)S(1)} %pad_add_fusion.info, bf16[2,4,528,128]{3,2,1,0:T(8,128)(2,1)S(1)} %all_to_all.38.back, bf16[4,512,256]{2,1,0:T(8,128)(2,1)S(1)} %get-tuple-element.4.row_tab, bf16[4,256,512]{2,1,0:T(8,128)(2,1)S(1)} %get-tuple-element.5.col_tab, f32[2,512]{1,0:T(2,128)S(1)} %copy-done.2), custom_call_target="tpu_custom_call" | custom-call | flops 2000000000 | bytes 1048576 | tf_op jit(solution)/shard_map/image/pallas_call | solution.py:278
  (1 shorter events, 0.0 us)
Async XLA Ops:
  1.4 1.0 %copy-start = (bf16[512,512]{1,0:T(8,128)(2,1)S(1)}, bf16[512,512]{1,0:T(8,128)(2,1)}, u32[]{:S(2)}) copy-start(bf16[512,512]{1,0:T(8,128)(2,1)} %facet.1) | copy-start | bytes 1572868
  2.4 0.7 copy-start.1
  3.1 0.7 copy-start.3
  3.8 0.7 copy-start.4
  4.5 0.7 copy-start.5
  7.5 8.6 %all-to-all-start = ((bf16[2,528,512]{2,1,0:T(8,128)(2,1)}), bf16[2,528,512]{2,1,0:T(8,128)(2,1)S(1)}, u32[]{:S(2)}, u32[]{:S(2)}) async-start(bf16[2,528,512]{2,1,0:T(8,128)(2,1)} %columns.1), calls=%async_computation | async-start | bytes 2162688 | tf_op jit(solution)/shard_map/all_to_all | solution.py:299
  53.9 16.9 %all-to-all-start.3 = ((bf16[32,40,128]{2,1,0:T(8,128)(2,1)}), bf16[32,40,128]{2,1,0:T(8,128)(2,1)S(1)}, u32[]{:S(2)}, u32[]{:S(2)}) async-start(bf16[32,40,128]{2,1,0:T(8,128)(2,1)} %pieces_sum.1), calls=%async_computation.3 | async-start | bytes 655360 | tf_op jit(solution)/shard_map/all_to_all | solution.py:299
  59.9 19.4 %copy-start.6 = (bf16[512,512]{1,0:T(8,128)(2,1)S(1)}, bf16[512,512]{1,0:T(8,128)(2,1)}, u32[]{:S(2)}) copy-start(bf16[512,512]{1,0:T(8,128)(2,1)} %constant.20.clone.inverse) | copy-start | bytes 1572868
  59.9 19.4 %copy-start.7 = (bf16[512,512]{1,0:T(8,128)(2,1)S(1)}, bf16[512,512]{1,0:T(8,128)(2,1)}, u32[]{:S(2)}) copy-start(bf16[512,512]{1,0:T(8,128)(2,1)} %constant.19.clone.forward) | copy-start | bytes 1572868
  59.9 19.3 %copy-start.8 = (bf16[256,256]{1,0:T(8,128)(2,1)S(1)}, bf16[256,256]{1,0:T(8,128)(2,1)}, u32[]{:S(2)}) copy-start(bf16[256,256]{1,0:T(8,128)(2,1)} %constant.18.clone.ksin) | copy-start | bytes 393220
  60.0 19.3 %copy-start.9 = (bf16[256,256]{1,0:T(8,128)(2,1)S(1)}, bf16[256,256]{1,0:T(8,128)(2,1)}, u32[]{:S(2)}) copy-start(bf16[256,256]{1,0:T(8,128)(2,1)} %constant.17.clone.kcos) | copy-start | bytes 393220
  82.3 12.8 %all-to-all-start.5 = ((bf16[4,528,128]{2,1,0:T(8,128)(2,1)}), bf16[4,528,128]{2,1,0:T(8,128)(2,1)S(1)}, u32[]{:S(2)}, u32[]{:S(2)}) async-start(bf16[4,528,128]{2,1,0:T(8,128)(2,1)} %grids.1), calls=%async_computation.5 | async-start | bytes 1081344 | tf_op jit(solution)/shard_map/all_to_all | solution.py:299
  95.3 5.4 %copy-start.2 = (f32[2,512]{1,0:T(2,128)S(1)}, f32[2,512]{1,0:T(2,128)}, u32[]{:S(2)}) copy-start(f32[2,512]{1,0:T(2,128)} %observed.3) | copy-start | bytes 12292

commit v4 on v3

v4 whole, which is shorter than its diff:
```python
import functools
import math

import jax
import jax.numpy as jnp
import ml_dtypes
import numpy as np
from jax import lax
from jax.experimental import pallas as pl
from jax.experimental.pallas import tpu as pltpu
from jax.sharding import PartitionSpec as P

SKY = 65536
SG = 256
NR = 2
NC = 2
HALF = SG // 2
LANES = 128


def wave(count):
    count = count & (SKY - 1)
    turned = count + SKY // 8
    near = (turned & (SKY // 4 - 1)) - SKY // 8
    quarter = lax.shift_right_logical(turned, 14) & 3
    t = near.astype(jnp.float32) * (2.0 * math.pi / SKY)
    q = t * t
    sin = t * (1.0 + q * (-1.0 / 6 + q * (1.0 / 120 + q * (-1.0 / 5040 + q * (1.0 / 362880)))))
    cos = 1.0 + q * (-0.5 + q * (1.0 / 24 + q * (-1.0 / 720 + q * (1.0 / 40320))))
    odd = (quarter & 1) == 1
    one, two = jnp.where(odd, sin, cos), jnp.where(odd, cos, sin)
    return (
        jnp.where((quarter == 1) | (quarter == 2), -one, one),
        jnp.where(quarter >= 2, -two, two),
    )


def lanes(n):
    return lax.broadcasted_iota(jnp.int32, (1, n), 1)


def sublanes(n):
    return lax.broadcasted_iota(jnp.int32, (n, 1), 0)


def spread(coarse, fine, store):
    for k in range(coarse[0].shape[0]):
        c, s = coarse[0][k:k + 1], coarse[1][k:k + 1]
        store(k * 16, c * fine[0] - s * fine[1], s * fine[0] + c * fine[1])


def place():
    return lax.axis_index("frow"), lax.axis_index("fcol")


def columns_kernel(cols_count, offsets, facet, subgrid, u, v, observed, out, col_tab, image, indices, seen, sems):
    f32, bf16 = jnp.float32, jnp.bfloat16
    side = facet.shape[0]
    copies = [
        pltpu.make_async_copy(facet, image, sems.at[0]),
        pltpu.make_async_copy(subgrid, indices.at[0], sems.at[1]),
        pltpu.make_async_copy(u, indices.at[1], sems.at[2]),
        pltpu.make_async_copy(v, indices.at[2], sems.at[3]),
        pltpu.make_async_copy(observed, seen, sems.at[4]),
    ]
    for copy in copies:
        copy.start()
    _, col_index = place()
    unit = sublanes(16)
    col_step = SKY // (cols_count * side)
    col_base = col_index * (SKY // cols_count)
    for c in range(NC):
        freq = offsets[c] + lanes(SG)
        coarse = wave((col_base + 16 * col_step * sublanes(side // 16)) * freq)
        fine = wave((col_step * unit) * freq)

        def store(at, cos, sin, c=c):
            for h in range(2):
                half = slice(h * HALF, (h + 1) * HALF)
                left = (2 * h + c) * SG
                col_tab[at:at + 16, left:left + HALF] = cos[:, half].astype(bf16)
                col_tab[at:at + 16, left + HALF:left + SG] = sin[:, half].astype(bf16)

        spread(coarse, fine, store)
    for copy in copies:
        copy.wait()
    vis = jnp.concatenate([indices[n].astype(f32) for n in range(3)] + [seen[...], jnp.zeros((3, side), f32)], 0)
    vis = jnp.concatenate([vis[:, :side // 2], vis[:, side // 2:]], 0).astype(bf16)
    for h in range(2):
        part = jnp.dot(image[...], col_tab[:, 2 * h * SG:2 * (h + 1) * SG], preferred_element_type=f32)
        out[h, :side] = part.astype(bf16)
        out[h, side:, :side // 2] = vis
        out[h, side:, side // 2:] = vis


def row_tables_kernel(rows_count, side, offsets, row_tab):
    bf16 = jnp.bfloat16
    row_index, _ = place()
    chip = row_index // 2
    unit = sublanes(16)
    row_step = SKY // (rows_count * side)
    for f in range(2):
        pos = (2 * chip + f) * (SKY // rows_count) + row_step * lanes(side)
        fine = wave(unit * pos)
        for r in range(NR):
            coarse = wave((offsets[r] + 16 * unit) * pos)

            def store(at, cos, sin, r=r, f=f):
                row_tab[2 * r, at:at + 16, f * side:(f + 1) * side] = cos.astype(bf16)
                row_tab[2 * r + 1, at:at + 16, f * side:(f + 1) * side] = sin.astype(bf16)

            spread(coarse, fine, store)


def contributions_kernel(scale, halves, row_tab, out, right):
    f32, bf16 = jnp.float32, jnp.bfloat16
    side = row_tab.shape[2] // 2
    vis = []
    for f in range(2):
        right[f * side:(f + 1) * side] = halves[f, :side]
        some = halves[f, side:]
        vis += [some[:, k * LANES:(k + 1) * LANES] for k in range(side // 2 // LANES)]
    for s in range(NR * NC):
        for k, some in enumerate(vis):
            at = 2 * SG + 16 * k
            out[s, at:at + 16] = some
    for r in range(NR):
        with_cos = jnp.dot(row_tab[2 * r], right[...], preferred_element_type=f32)
        with_sin = jnp.dot(row_tab[2 * r + 1], right[...], preferred_element_type=f32)
        for c in range(NC):
            at = 2 * c * HALF
            cp, cq = with_cos[:, at:at + HALF], with_cos[:, at + HALF:at + 2 * HALF]
            sp, sq = with_sin[:, at:at + HALF], with_sin[:, at + HALF:at + 2 * HALF]
            out[r * NC + c, :SG] = ((cp - sq) * scale).astype(bf16)
            out[r * NC + c, SG:2 * SG] = (-(cq + sp) * scale).astype(bf16)


def vis_rows(block):
    count = block.shape[0] // 16
    return jnp.concatenate(
        [block[16 * k + 8 * part:16 * k + 8 * part + 8] for part in range(2) for k in range(count)], 1
    )


def gridding_kernel(parts, pieces, planes):
    f32, bf16 = jnp.float32, jnp.bfloat16
    row_index, _ = place()
    chip = (row_index // 2).astype(f32)
    v_at = (sublanes(HALF) + (row_index % 2) * HALF).astype(f32)
    counter = sublanes(SG).astype(f32)
    count = parts.shape[0]
    total = jnp.zeros((SG, 3 * HALF), f32)
    for k in range(count):
        one = vis_rows(parts[k, 2 * SG:].astype(f32))
        u_here = jnp.where(one[0:1] == chip, one[1:2], -1.0)
        hot = jnp.where(u_here == counter, 1.0, 0.0).astype(bf16)
        pick = one[2:3] == v_at
        right = jnp.concatenate(
            [jnp.where(pick, one[3:4], 0.0), jnp.where(pick, one[4:5], 0.0), jnp.where(pick, 1.0, 0.0)], 0
        ).astype(bf16)
        total = total + lax.dot_general(hot, right, (((1,), (1,)), ((), ())), preferred_element_type=f32)
    for p in range(2):
        some = parts[0, p * SG:(p + 1) * SG].astype(f32)
        for k in range(1, count):
            some = some + parts[k, p * SG:(p + 1) * SG].astype(f32)
        planes[p] = some
    for p in range(3):
        planes[2 + p] = total[:, p * HALF:(p + 1) * HALF]
    each = SG // pieces.shape[0]
    for j in range(pieces.shape[0]):
        rows = [planes[p, j * each:(j + 1) * each] for p in range(5)]
        pieces[j] = jnp.concatenate(rows, 0).astype(bf16)


def pieces_sum_kernel(pieces, out):
    f32, bf16 = jnp.float32, jnp.bfloat16
    total = pieces[0].astype(f32)
    for j in range(1, pieces.shape[0]):
        total = total + pieces[j].astype(f32)
    total = total.astype(bf16)
    for j in range(out.shape[0]):
        out[j] = total


def grids_kernel(pieces, parts, grid_left, forward, inverse_left, inverse, out, planes, cat, tall, hat):
    f32, bf16 = jnp.float32, jnp.bfloat16
    row_index, _ = place()
    core = row_index % 2
    chip = (row_index // 2).astype(f32)
    count = pieces.shape[1]
    each = SG // count
    for h in range(2):
        for j in range(count):
            some = pieces[h, j].astype(f32)
            for p in range(5):
                planes[p, j * each:(j + 1) * each, h * HALF:(h + 1) * HALF] = some[p * each:(p + 1) * each]
    cat[:, :SG] = planes[0].astype(bf16)
    cat[:, SG:] = planes[1].astype(bf16)
    wide = jnp.dot(cat[...], forward[...], preferred_element_type=f32).astype(bf16)
    tall[:SG] = wide[:, :SG]
    tall[SG:] = wide[:, SG:]
    model = jnp.dot(grid_left[...], tall[...], preferred_element_type=f32) * (1.0 / SG)
    hat_real, hat_imag = model[:SG], model[SG:]
    cat[:, :SG] = (planes[2] - planes[4] * hat_real).astype(bf16)
    cat[:, SG:] = (planes[3] - planes[4] * hat_imag).astype(bf16)
    hat[:, :SG] = hat_real.astype(bf16)
    hat[:, SG:] = hat_imag.astype(bf16)
    wide = jnp.dot(cat[...], inverse[...], preferred_element_type=f32)
    for k in range(2):
        some = wide[:, k * SG:(k + 1) * SG]
        tall[k * SG:(k + 1) * SG, :HALF] = jnp.where(core == 0, some[:, :HALF], some[:, HALF:]).astype(bf16)
    back = jnp.dot(inverse_left[...], tall[:, :HALF], preferred_element_type=f32) * (1.0 / SG)
    back = back.astype(bf16)
    counter = sublanes(SG).astype(f32)
    vis_each = (parts.shape[1] - 2 * SG) // 2
    for k in range(parts.shape[0]):
        out[k, :2 * SG] = back
        first = parts[k, 2 * SG:2 * SG + vis_each].astype(f32)
        second = parts[k, 2 * SG + vis_each:].astype(f32)
        ask = vis_rows(jnp.where(core == 0, first, second))
        u_here = jnp.where(ask[0:1] == chip, ask[1:2], -1.0)
        hot = jnp.where(u_here == counter, 1.0, 0.0).astype(bf16)
        pick = ask[2:3] == counter
        line = lax.dot_general(hat[...], hot, (((0,), (0,)), ((), ())), preferred_element_type=f32)
        rows = []
        for part in range(2):
            value = jnp.sum(jnp.where(pick, line[part * SG:(part + 1) * SG], 0.0), axis=0, keepdims=True)
            rows += [value[:, i * LANES:(i + 1) * LANES] for i in range(value.shape[1] // LANES)]
        rows.append(jnp.zeros((16 - len(rows), LANES), f32))
        out[k, 2 * SG:] = jnp.concatenate(rows, 0).astype(bf16)


def back_tables_kernel(rows_count, cols_count, side, offsets_row, offsets_col, row_tab, col_tab):
    bf16 = jnp.bfloat16
    row_index, col_index = place()
    unit = sublanes(16)
    row_step = SKY // (rows_count * side)
    row_base = row_index * (SKY // rows_count)
    for r in range(NR):
        freq = offsets_row[r] + lanes(SG)
        coarse = wave((row_base + 16 * row_step * sublanes(side // 16)) * freq)
        fine = wave((row_step * unit) * freq)

        def store(at, cos, sin, r=r):
            row_tab[at:at + 16, 2 * r * SG:(2 * r + 1) * SG] = cos.astype(bf16)
            row_tab[at:at + 16, (2 * r + 1) * SG:(2 * r + 2) * SG] = sin.astype(bf16)

        spread(coarse, fine, store)
    col_step = SKY // (cols_count * side)
    pos = col_index * (SKY // cols_count) + col_step * lanes(side)
    fine = wave(unit * pos)
    for c in range(NC):
        coarse = wave((offsets_col[c] + 16 * unit) * pos)

        def store(at, cos, sin, c=c):
            left = 2 * c * SG + at
            col_tab[left:left + 16] = cos.astype(bf16)
            col_tab[left + SG:left + SG + 16] = (-sin).astype(bf16)

        spread(coarse, fine, store)


def image_kernel(scale, back, row_tab, col_tab, observed, out, residual, right, both, image, seen, sems):
    f32, bf16 = jnp.float32, jnp.bfloat16
    row_index, _ = place()
    core = row_index % 2
    fetch = pltpu.make_async_copy(observed, seen, sems.at[0])
    fetch.start()
    for c in range(NC):
        for r in range(NR):
            for half in range(2):
                real = back[half, r * NC + c, :SG]
                imag = back[half, r * NC + c, SG:2 * SG]
                top, at = 2 * r * SG, half * HALF
                right[top:top + SG, at:at + HALF] = real
                right[top:top + SG, SG + at:SG + at + HALF] = imag
                right[top + SG:top + 2 * SG, at:at + HALF] = -imag
                right[top + SG:top + 2 * SG, SG + at:SG + at + HALF] = real
        part = jnp.dot(row_tab[...], right[...], preferred_element_type=f32)
        both[:, 2 * c * SG:2 * (c + 1) * SG] = part.astype(bf16)
    chunks = sems.shape[0] - 1
    side = both.shape[0]
    step = side // chunks
    writes = []
    for n in range(chunks):
        at = slice(n * step, (n + 1) * step)
        image[at] = jnp.dot(both[at], col_tab[...], preferred_element_type=f32) * scale
        write = pltpu.make_async_copy(image.at[at], out.at[at], sems.at[1 + n])
        write.start()
        writes.append(write)
    fetch.wait()
    model = jnp.zeros((16, LANES), f32)
    for s in range(NR * NC):
        model = model + jnp.where(core == 0, back[0, s, 2 * SG:].astype(f32), back[1, s, 2 * SG:].astype(f32))
    count = observed.shape[1] // LANES
    for part in range(2):
        for i in range(count):
            at = slice(i * LANES, (i + 1) * LANES)
            residual[part:part + 1, at] = seen[part:part + 1, at] - model[part * count + i:part * count + i + 1]
    for write in writes:
        write.wait()


def call(kernel, out_shape, name, spaces, scratch=(), cost=0, outs=None, room=24):
    kinds = {"s": pltpu.SMEM, "v": pltpu.VMEM, "a": pl.ANY}
    several = isinstance(out_shape, tuple)
    outs = outs or "v" * (len(out_shape) if several else 1)
    out_specs = tuple(pl.BlockSpec(memory_space=kinds[kind]) for kind in outs)
    return pl.pallas_call(
        kernel,
        out_shape=out_shape,
        in_specs=[pl.BlockSpec(memory_space=kinds[kind]) for kind in spaces],
        out_specs=out_specs if several else out_specs[0],
        scratch_shapes=list(scratch),
        compiler_params=pltpu.CompilerParams(vmem_limit_bytes=room * 2**20),
        cost_estimate=pl.CostEstimate(flops=cost, bytes_accessed=2**20, transcendentals=0),
        name=name,
    )


def grid_tables():
    counter = np.arange(SG)
    angles = (counter[:, None] * counter[None, :] % SG).astype(np.float64) * (2.0 * math.pi / SG)
    return np.cos(angles).astype(ml_dtypes.bfloat16), np.sin(angles).astype(ml_dtypes.bfloat16)


def exchange(blocks, axes, groups):
    return lax.all_to_all(blocks, axes, 0, 0, tiled=True, axis_index_groups=groups)


def shape(*dims, dtype=jnp.bfloat16):
    return jax.ShapeDtypeStruct(dims, dtype)


def shards(facet, row_offsets, col_offsets, vis_subgrid, vis_u, vis_v, observed):
    f32, bf16 = jnp.float32, jnp.bfloat16
    rows_count, cols_count = lax.axis_size("frow"), lax.axis_size("fcol")
    side = facet.shape[0]
    n_vis = vis_u.shape[0]
    chips = rows_count // 2
    each = SG // cols_count
    x_groups = [[2 * chip + core for chip in range(chips)] for core in range(2)]
    core_groups = [[2 * chip, 2 * chip + 1] for chip in range(chips)]
    scale_in = 1.0 / (side * math.sqrt(rows_count * cols_count))
    scale_out = 1.0 / (SG * math.sqrt(NR * NC))
    line = (1, n_vis)

    halves = call(
        functools.partial(columns_kernel, cols_count), shape(2, side + 16, 4 * HALF), "columns", "saaaaa",
        scratch=[
            pltpu.VMEM((side, 8 * HALF), bf16), pltpu.VMEM((side, side), bf16), pltpu.VMEM((3,) + line, jnp.int32),
            pltpu.VMEM((2, n_vis), f32), pltpu.SemaphoreType.DMA((5,)),
        ],
        cost=10**9, room=60,
    )(col_offsets, facet, vis_subgrid.reshape(line), vis_u.reshape(line), vis_v.reshape(line), observed)
    halves = exchange(halves, "frow", core_groups)
    row_tab = call(
        functools.partial(row_tables_kernel, rows_count, side), shape(4, SG, 2 * side), "row_tables", "s", cost=10**9
    )(row_offsets)
    vis_rows_count = 8 * 2 * n_vis // LANES
    parts = call(
        functools.partial(contributions_kernel, scale_in), shape(NR * NC, 2 * SG + vis_rows_count, HALF),
        "contributions", "vv", scratch=[pltpu.VMEM((2 * side, 4 * HALF), bf16)], cost=2 * 10**9,
    )(halves, row_tab)
    parts = exchange(parts, "frow", x_groups)

    pieces = call(
        gridding_kernel, shape(cols_count, 5 * each, HALF), "gridding", "v",
        scratch=[pltpu.VMEM((5, SG, HALF), f32)], cost=10**9,
    )(parts)
    pieces = exchange(pieces, "fcol", None)
    pieces = call(pieces_sum_kernel, shape(cols_count, 5 * each, HALF), "pieces_sum", "v", cost=10**6)(pieces)
    pieces = exchange(pieces, "fcol", None)
    pieces = exchange(jnp.broadcast_to(pieces, (2,) + pieces.shape), "frow", core_groups)

    kcos, ksin = grid_tables()
    block = [np.concatenate(pair, 1) for pair in ((kcos, ksin), (-ksin, kcos), (kcos, -ksin), (ksin, kcos))]
    forward_block = np.concatenate([block[0], block[1]], 0)
    inverse_block = np.concatenate([block[2], block[3]], 0)
    back = call(
        grids_kernel, shape(chips, 2 * SG + 16, HALF), "grids", "vvvvvv",
        scratch=[
            pltpu.VMEM((5, SG, SG), f32), pltpu.VMEM((SG, 2 * SG), bf16), pltpu.VMEM((2 * SG, SG), bf16),
            pltpu.VMEM((SG, 2 * SG), bf16),
        ],
        cost=10**9,
    )(pieces, parts, inverse_block, forward_block, forward_block, inverse_block)
    back = exchange(back, "frow", x_groups)
    back = exchange(jnp.broadcast_to(back, (2,) + back.shape), "frow", core_groups)

    back_row, back_col = call(
        functools.partial(back_tables_kernel, rows_count, cols_count, side),
        (shape(side, 4 * SG), shape(4 * SG, side)), "back_tables", "ss", cost=10**9,
    )(row_offsets, col_offsets)
    chunks = 4
    return call(
        functools.partial(image_kernel, scale_out),
        (shape(side, side, dtype=f32), shape(2, n_vis, dtype=f32)), "image", "vvva", outs="av",
        scratch=[
            pltpu.VMEM((4 * SG, 2 * SG), bf16), pltpu.VMEM((side, 4 * SG), bf16), pltpu.VMEM((side, side), f32),
            pltpu.VMEM((2, n_vis), f32), pltpu.SemaphoreType.DMA((1 + chunks,)),
        ],
        cost=2 * 10**9,
    )(back, back_row, back_col, observed)


def solution(mesh):
    in_specs = (
        P("frow", "fcol"),
        P(),
        P(),
        P(("frow", "fcol")),
        P(("frow", "fcol")),
        P(("frow", "fcol")),
        P(None, ("frow", "fcol")),
    )
    out_specs = (P("frow", "fcol"), P(None, ("frow", "fcol")))
    return jax.shard_map(shards, mesh=mesh, in_specs=in_specs, out_specs=out_specs, check_vma=False)
```

time: 105 us -> 99.3 us (0.946)
  blocking collectives: 47.7 us -> 64.4 us
  waiting for transfers between devices: 19.2 us -> 8.38 us
  starting transfers between devices: 16.3 us -> 10.3 us
  local copies, waits for them, and re-layouts: 4.04 us -> 0.25 us
    all_to_all x4 -> x5, blocking collectives: 47.7 us -> 64.4 us  [exchange(): lax.all_to_all(blocks, axes, 0, 0, tiled=True, axis_index_groups=groups)]
    all_to_all x3 -> x2, waiting for transfers between devices: 19.2 us -> 8.38 us  [exchange(): lax.all_to_all(blocks, axes, 0, 0, tiled=True, axis_index_groups=groups)]
    all_to_all x3 -> x2, starting transfers between devices: 16.3 us -> 10.3 us  [exchange(): lax.all_to_all(blocks, axes, 0, 0, tiled=True, axis_index_groups=groups)]
    unnamed x20 -> x10, local copies, waits for them, and re-layouts: 3.81 us -> 0.02 us
  transfers between devices with their start and end apart: 3 -> 2, of which waited for: 3 -> 2; matrix products, arithmetic and copies ran while one was open for 0% -> 0% of each run, Pallas kernels for 3% -> 3%
where the time goes in v4:
time: 99.3 us; the launch traced here: 98.8 us
  blocking collectives  64.4 us (65%)
  Pallas kernels  14.7 us (15%)
  starting transfers between devices  10.3 us (10%)
  waiting for transfers between devices  8.38 us (8%)
    all_to_all x5, blocking collectives, exchange(): lax.all_to_all(blocks, axes, 0, 0, tiled=True, axis_index_groups=groups)  64.4 us
    all_to_all x2, starting transfers between devices, exchange(): lax.all_to_all(blocks, axes, 0, 0, tiled=True, axis_index_groups=groups)  10.3 us
    all_to_all x2, waiting for transfers between devices, exchange(): lax.all_to_all(blocks, axes, 0, 0, tiled=True, axis_index_groups=groups)  8.38 us
    pallas_call x1, Pallas kernels, shards(): call(functools.partial(columns_kernel, cols_count), shape(2, side + 16, 4...  3.47 us
    pallas_call x1, Pallas kernels, shards(): call(functools.partial(image_kernel, scale_out), (shape(side, side, dtype...  3.39 us
    pallas_call x1, Pallas kernels, shards(): call(grids_kernel, shape(chips, 2 * SG + 16, HALF), 'grids', 'vvvvvv', sc...  2.51 us
  transfers between devices with their start and end apart: 2, of which 2 were waited for; matrix products, arithmetic and copies ran while one was open for 0% of the time, Pallas kernels for 3%

profile of v4, /device:TPU:1, one launch (start us, length us, event | category | flops | bytes accessed | tf_op | source)
XLA Modules:
  0.0 98.8 jit_solution(4498033849477819636)
XLA Ops:
  0.6 3.5 %columns.1 = bf16[2,528,512]{2,1,0:T(8,128)(2,1)} custom-call(s32[2]{0:T(128)} %offsets_col.1, bf16[512,512]{1,0:T(8,128)(2,1)} %facet.1, s32[1,512]{1,0:T(1,128)} %bitcast.3, s32[1,512]{1,0:T(1,128)} %bitcast.4, s32[1,512]{1,0:T(1,128)} %bitcast.5, f32[2,512]{1,0:T(2,128)} %observed.3), custom_call_target="tpu_custom_call" | custom-call | flops 1000000000 | bytes 1048576 | tf_op jit(solution)/shard_map/columns/pallas_call | solution.py:348
  4.1 0.0 copy-start.4
  4.1 6.8 %all-to-all-start = ((bf16[2,528,512]{2,1,0:T(8,128)(2,1)}), bf16[2,528,512]{2,1,0:T(8,128)(2,1)S(1)}, u32[]{:S(2)}, u32[]{:S(2)}) async-start(bf16[2,528,512]{2,1,0:T(8,128)(2,1)} %columns.1), calls=%async_computation | async-start | bytes 2162688 | tf_op jit(solution)/shard_map/all_to_all | solution.py:328
  10.9 0.0 copy-done.4
  10.9 1.4 %row_tables.1.row_tab = bf16[4,256,1024]{2,1,0:T(8,128)(2,1)S(1)} custom-call(s32[2]{0:T(128)S(1)} %copy-done.4), custom_call_target="tpu_custom_call" | custom-call | flops 1000000000 | bytes 1048576 | tf_op jit(solution)/shard_map/row_tables/pallas_call | solution.py:357
  12.3 0.4 all-to-all-done.halves
  12.7 1.3 %contributions.1 = bf16[4,576,128]{2,1,0:T(8,128)(2,1)S(1)} custom-call(bf16[2,528,512]{2,1,0:T(8,128)(2,1)S(1)} %all-to-all-done.halves, bf16[4,256,1024]{2,1,0:T(8,128)(2,1)S(1)} %row_tables.1.row_tab), custom_call_target="tpu_custom_call" | custom-call | flops 2000000000 | bytes 1048576 | tf_op jit(solution)/shard_map/contributions/pallas_call | solution.py:361
  14.0 12.0 %all_to_all.35.parts = bf16[4,576,128]{2,1,0:T(8,128)(2,1)S(1)} all-to-all(bf16[4,576,128]{2,1,0:T(8,128)(2,1)S(1)} %contributions.1), channel_id=1, replica_groups={{0,64,128,192},{32,96,160,224},{1,65,129,193},{33,97,161,225},{2,66,130..., dimensions={0} | all-to-all | bytes 1179648 | tf_op jit(solution)/shard_map/all_to_all | solution.py:328
  26.0 1.3 %gridding.1 = bf16[32,40,128]{2,1,0:T(8,128)(2,1)S(1)} custom-call(bf16[4,576,128]{2,1,0:T(8,128)(2,1)S(1)} %all_to_all.35.parts), custom_call_target="tpu_custom_call" | custom-call | flops 1000000000 | bytes 1048576 | tf_op jit(solution)/shard_map/gridding/pallas_call | solution.py:367
  27.3 21.9 %all_to_all.36.pieces = bf16[32,40,128]{2,1,0:T(8,128)(2,1)S(1)} all-to-all(bf16[32,40,128]{2,1,0:T(8,128)(2,1)S(1)} %gridding.1), channel_id=1, replica_groups=mesh['frow'=8,'fcol'=32] {'fcol'}, dimensions={0} | all-to-all | bytes 655360 | tf_op jit(solution)/shard_map/all_to_all | solution.py:328
  49.2 0.1 pieces_sum.1
  49.2 16.4 %all_to_all.37 = bf16[32,40,128]{2,1,0:T(8,128)(2,1)S(1)} all-to-all(bf16[32,40,128]{2,1,0:T(8,128)(2,1)S(1)} %pieces_sum.1), channel_id=1, replica_groups=mesh['frow'=8,'fcol'=32] {'fcol'}, dimensions={0} | all-to-all | bytes 655360 | tf_op jit(solution)/shard_map/all_to_all | solution.py:328
  65.7 0.0 copy-start
  65.7 0.0 copy-start.1
  65.7 0.1 broadcast_in_dim.6
  65.8 8.7 %all_to_all.38.pieces = bf16[2,32,40,128]{3,2,1,0:T(8,128)(2,1)S(1)} all-to-all(bf16[2,32,40,128]{3,2,1,0:T(8,128)(2,1)S(1)} %broadcast_in_dim.6), channel_id=1, replica_groups={{0,32},{64,96},{128,160},{192,224},{1,33},{65,97},{129,161},{193,225},{..., dimensions={0} | all-to-all | bytes 1310720 | tf_op jit(solution)/shard_map/all_to_all | solution.py:328
  74.5 0.0 copy-done
  74.5 0.0 copy-done.1
  74.5 0.0 copy-start.3
  74.5 2.5 %grids.1 = bf16[4,528,128]{2,1,0:T(8,128)(2,1)} custom-call(bf16[2,32,40,128]{3,2,1,0:T(8,128)(2,1)S(1)} %all_to_all.38.pieces, bf16[4,576,128]{2,1,0:T(8,128)(2,1)S(1)} %all_to_all.35.parts, bf16[512,512]{1,0:T(8,128)(2,1)S(1)} %copy-done.1, bf16[512,512]{1,0:T(8,128)(2,1)S(1)} %copy-done, bf16[512,512]{1,0:T(8,128)(2,1)S(1)} %copy-done, ...), custom_call_target="tpu_custom_call" | custom-call | flops 1000000000 | bytes 1048576 | tf_op jit(solution)/shard_map/grids/pallas_call | solution.py:380
  77.0 3.5 %all-to-all-start.5 = ((bf16[4,528,128]{2,1,0:T(8,128)(2,1)}), bf16[4,528,128]{2,1,0:T(8,128)(2,1)S(1)}, u32[]{:S(2)}, u32[]{:S(2)}) async-start(bf16[4,528,128]{2,1,0:T(8,128)(2,1)} %grids.1), calls=%async_computation.5 | async-start | bytes 1081344 | tf_op jit(solution)/shard_map/all_to_all | solution.py:328
  80.5 0.0 copy-done.3
  80.5 1.4 %back_tables.1 = (bf16[512,1024]{1,0:T(8,128)(2,1)S(1)}, bf16[1024,512]{1,0:T(8,128)(2,1)S(1)}) custom-call(s32[2]{0:T(128)S(1)} %copy-done.4, s32[2]{0:T(128)S(1)} %copy-done.3), custom_call_target="tpu_custom_call" | custom-call | flops 1000000000 | bytes 1048576 | tf_op jit(solution)/shard_map/back_tables/pallas_call | solution.py:391
  81.9 8.0 %all-to-all-done.5 = bf16[4,528,128]{2,1,0:T(8,128)(2,1)S(1)} async-done(((bf16[4,528,128]{2,1,0:T(8,128)(2,1)}), bf16[4,528,128]{2,1,0:T(8,128)(2,1)S(1)}, u32[]{:S(2)}, u32[]{:S(2)}) %all-to-all-start.5) | async-done | bytes 540704 | tf_op jit(solution)/shard_map/all_to_all | solution.py:328
  89.8 0.1 broadcast_in_dim.7
  90.0 0.0 copy-start.2
  90.0 5.4 %all_to_all.39.back = bf16[2,4,528,128]{3,2,1,0:T(8,128)(2,1)S(1)} all-to-all(bf16[2,4,528,128]{3,2,1,0:T(8,128)(2,1)S(1)} %broadcast_in_dim.7), channel_id=1, replica_groups={{0,32},{64,96},{128,160},{192,224},{1,33},{65,97},{129,161},{193,225},{..., dimensions={0} | all-to-all | bytes 2162688 | tf_op jit(solution)/shard_map/all_to_all | solution.py:328
  95.4 0.0 copy-done.2
  95.4 3.4 %image.1 = (f32[512,512]{1,0:T(8,128)}, f32[2,512]{1,0:T(2,128)}) custom-call(bf16[2,4,528,128]{3,2,1,0:T(8,128)(2,1)S(1)} %all_to_all.39.back, bf16[512,1024]{1,0:T(8,128)(2,1)S(1)} %get-tuple-element.4.row_tab, bf16[1024,512]{1,0:T(8,128)(2,1)S(1)} %get-tuple-element.5.col_tab, f32[2,512]{1,0:T(2,128)S(1)} %copy-done.2), custom_call_target="tpu_custom_call" | custom-call | flops 2000000000 | bytes 1048576 | tf_op jit(solution)/shard_map/image/pallas_call | solution.py:396
Async XLA Ops:
  4.1 6.8 %copy-start.4 = (s32[2]{0:T(128)S(1)}, s32[2]{0:T(128)}, u32[]{:S(2)}) copy-start(s32[2]{0:T(128)} %offsets_row.1) | copy-start | bytes 28
  4.1 8.6 %all-to-all-start = ((bf16[2,528,512]{2,1,0:T(8,128)(2,1)}), bf16[2,528,512]{2,1,0:T(8,128)(2,1)S(1)}, u32[]{:S(2)}, u32[]{:S(2)}) async-start(bf16[2,528,512]{2,1,0:T(8,128)(2,1)} %columns.1), calls=%async_computation | async-start | bytes 2162688 | tf_op jit(solution)/shard_map/all_to_all | solution.py:328
  65.7 8.8 %copy-start = (bf16[512,512]{1,0:T(8,128)(2,1)S(1)}, bf16[512,512]{1,0:T(8,128)(2,1)}, u32[]{:S(2)}) copy-start(bf16[512,512]{1,0:T(8,128)(2,1)} %constant.5.clone.forward.inverse_left) | copy-start | bytes 1572868
  65.7 8.8 %copy-start.1 = (bf16[512,512]{1,0:T(8,128)(2,1)S(1)}, bf16[512,512]{1,0:T(8,128)(2,1)}, u32[]{:S(2)}) copy-start(bf16[512,512]{1,0:T(8,128)(2,1)} %constant.4.clone.grid_left.inverse) | copy-start | bytes 1572868
  74.5 6.0 %copy-start.3 = (s32[2]{0:T(128)S(1)}, s32[2]{0:T(128)}, u32[]{:S(2)}) copy-start(s32[2]{0:T(128)} %offsets_col.1) | copy-start | bytes 28
  77.0 12.9 %all-to-all-start.5 = ((bf16[4,528,128]{2,1,0:T(8,128)(2,1)}), bf16[4,528,128]{2,1,0:T(8,128)(2,1)S(1)}, u32[]{:S(2)}, u32[]{:S(2)}) async-start(bf16[4,528,128]{2,1,0:T(8,128)(2,1)} %grids.1), calls=%async_computation.5 | async-start | bytes 1081344 | tf_op jit(solution)/shard_map/all_to_all | solution.py:328
  90.0 5.4 %copy-start.2 = (f32[2,512]{1,0:T(2,128)S(1)}, f32[2,512]{1,0:T(2,128)}, u32[]{:S(2)}) copy-start(f32[2,512]{1,0:T(2,128)} %observed.3) | copy-start | bytes 12292

commit v5 on v4

--- a/solution.py
+++ b/solution.py
@@ -53,7 +53,7 @@
     return lax.axis_index("frow"), lax.axis_index("fcol")
 
 
-def columns_kernel(cols_count, offsets, facet, subgrid, u, v, observed, out, col_tab, image, indices, seen, sems):
+def columns_kernel(cols_count, offsets, facet, subgrid, u, v, observed, own, send, col_tab, image, indices, seen, sems):
     f32, bf16 = jnp.float32, jnp.bfloat16
     side = facet.shape[0]
     copies = [
@@ -65,7 +65,8 @@
     ]
     for copy in copies:
         copy.start()
-    _, col_index = place()
+    row_index, col_index = place()
+    core = row_index % 2
     unit = sublanes(16)
     col_step = SKY // (cols_count * side)
     col_base = col_index * (SKY // cols_count)
@@ -86,21 +87,20 @@
         copy.wait()
     vis = jnp.concatenate([indices[n].astype(f32) for n in range(3)] + [seen[...], jnp.zeros((3, side), f32)], 0)
     vis = jnp.concatenate([vis[:, :side // 2], vis[:, side // 2:]], 0).astype(bf16)
-    for h in range(2):
-        part = jnp.dot(image[...], col_tab[:, 2 * h * SG:2 * (h + 1) * SG], preferred_element_type=f32)
-        out[h, :side] = part.astype(bf16)
-        out[h, side:, :side // 2] = vis
-        out[h, side:, side // 2:] = vis
+    for out, half in ((send, 1 - core), (own, core)):
+        tab = col_tab[:, pl.ds(pl.multiple_of(half * 2 * SG, 2 * SG), 2 * SG)]
+        out[:side] = jnp.dot(image[...], tab, preferred_element_type=f32).astype(bf16)
+        out[side:, :side // 2] = vis
+        out[side:, side // 2:] = vis
 
 
 def row_tables_kernel(rows_count, side, offsets, row_tab):
     bf16 = jnp.bfloat16
     row_index, _ = place()
-    chip = row_index // 2
     unit = sublanes(16)
     row_step = SKY // (rows_count * side)
     for f in range(2):
-        pos = (2 * chip + f) * (SKY // rows_count) + row_step * lanes(side)
+        pos = (row_index ^ f) * (SKY // rows_count) + row_step * lanes(side)
         fine = wave(unit * pos)
         for r in range(NR):
             coarse = wave((offsets[r] + 16 * unit) * pos)
@@ -112,13 +112,13 @@
             spread(coarse, fine, store)
 
 
-def contributions_kernel(scale, halves, row_tab, out, right):
+def contributions_kernel(scale, own, other, row_tab, out, right):
     f32, bf16 = jnp.float32, jnp.bfloat16
     side = row_tab.shape[2] // 2
     vis = []
-    for f in range(2):
-        right[f * side:(f + 1) * side] = halves[f, :side]
-        some = halves[f, side:]
+    for f, half in enumerate((own, other)):
+        right[f * side:(f + 1) * side] = half[:side]
+        some = half[side:]
         vis += [some[:, k * LANES:(k + 1) * LANES] for k in range(side // 2 // LANES)]
     for s in range(NR * NC):
         for k, some in enumerate(vis):
@@ -182,18 +182,19 @@
         out[j] = total
 
 
-def grids_kernel(pieces, parts, grid_left, forward, inverse_left, inverse, out, planes, cat, tall, hat):
+def grids_kernel(own, other, parts, grid_left, forward, inverse_left, inverse, _, out, planes, cat, tall, hat):
     f32, bf16 = jnp.float32, jnp.bfloat16
     row_index, _ = place()
     core = row_index % 2
     chip = (row_index // 2).astype(f32)
-    count = pieces.shape[1]
+    count = own.shape[0]
     each = SG // count
-    for h in range(2):
+    for pieces, half in ((own, core), (other, 1 - core)):
+        at = pl.ds(pl.multiple_of(half * HALF, HALF), HALF)
         for j in range(count):
-            some = pieces[h, j].astype(f32)
+            some = pieces[j].astype(f32)
             for p in range(5):
-                planes[p, j * each:(j + 1) * each, h * HALF:(h + 1) * HALF] = some[p * each:(p + 1) * each]
+                planes[p, j * each:(j + 1) * each, at] = some[p * each:(p + 1) * each]
     cat[:, :SG] = planes[0].astype(bf16)
     cat[:, SG:] = planes[1].astype(bf16)
     wide = jnp.dot(cat[...], forward[...], preferred_element_type=f32).astype(bf16)
@@ -215,9 +216,7 @@
     vis_each = (parts.shape[1] - 2 * SG) // 2
     for k in range(parts.shape[0]):
         out[k, :2 * SG] = back
-        first = parts[k, 2 * SG:2 * SG + vis_each].astype(f32)
-        second = parts[k, 2 * SG + vis_each:].astype(f32)
-        ask = vis_rows(jnp.where(core == 0, first, second))
+        ask = vis_rows(parts[k, 2 * SG:2 * SG + vis_each].astype(f32))
         u_here = jnp.where(ask[0:1] == chip, ask[1:2], -1.0)
         hot = jnp.where(u_here == counter, 1.0, 0.0).astype(bf16)
         pick = ask[2:3] == counter
@@ -253,50 +252,57 @@
         coarse = wave((offsets_col[c] + 16 * unit) * pos)
 
         def store(at, cos, sin, c=c):
-            left = 2 * c * SG + at
+            left = (at // HALF * 2 * NC + 2 * c) * HALF + at % HALF
             col_tab[left:left + 16] = cos.astype(bf16)
-            col_tab[left + SG:left + SG + 16] = (-sin).astype(bf16)
+            col_tab[left + HALF:left + HALF + 16] = (-sin).astype(bf16)
 
         spread(coarse, fine, store)
 
 
-def image_kernel(scale, back, row_tab, col_tab, observed, out, residual, right, both, image, seen, sems):
-    f32, bf16 = jnp.float32, jnp.bfloat16
-    row_index, _ = place()
-    core = row_index % 2
-    fetch = pltpu.make_async_copy(observed, seen, sems.at[0])
-    fetch.start()
+def half_image(back, half, row_tab, col_tab, right, both):
+    f32, bf16 = jnp.float32, jnp.bfloat16
     for c in range(NC):
         for r in range(NR):
-            for half in range(2):
-                real = back[half, r * NC + c, :SG]
-                imag = back[half, r * NC + c, SG:2 * SG]
-                top, at = 2 * r * SG, half * HALF
-                right[top:top + SG, at:at + HALF] = real
-                right[top:top + SG, SG + at:SG + at + HALF] = imag
-                right[top + SG:top + 2 * SG, at:at + HALF] = -imag
-                right[top + SG:top + 2 * SG, SG + at:SG + at + HALF] = real
-        part = jnp.dot(row_tab[...], right[...], preferred_element_type=f32)
-        both[:, 2 * c * SG:2 * (c + 1) * SG] = part.astype(bf16)
-    chunks = sems.shape[0] - 1
-    side = both.shape[0]
-    step = side // chunks
-    writes = []
-    for n in range(chunks):
-        at = slice(n * step, (n + 1) * step)
-        image[at] = jnp.dot(both[at], col_tab[...], preferred_element_type=f32) * scale
-        write = pltpu.make_async_copy(image.at[at], out.at[at], sems.at[1 + n])
-        write.start()
-        writes.append(write)
-    fetch.wait()
+            real = back[r * NC + c, :SG]
+            imag = back[r * NC + c, SG:2 * SG]
+            top, at = 2 * r * SG, 2 * c * HALF
+            right[top:top + SG, at:at + HALF] = real
+            right[top:top + SG, at + HALF:at + 2 * HALF] = imag
+            right[top + SG:top + 2 * SG, at:at + HALF] = -imag
+            right[top + SG:top + 2 * SG, at + HALF:at + 2 * HALF] = real
+    both[...] = jnp.dot(row_tab[...], right[...], preferred_element_type=f32).astype(bf16)
+    depth = 2 * NC * HALF
+    rows = pl.ds(pl.multiple_of(half * depth, depth), depth)
+    return lambda at: jnp.dot(both[at], col_tab[rows], preferred_element_type=f32)
+
+
+def own_image_kernel(back, row_tab, col_tab, observed, out, residual, right, both):
+    f32 = jnp.float32
+    row_index, _ = place()
     model = jnp.zeros((16, LANES), f32)
     for s in range(NR * NC):
-        model = model + jnp.where(core == 0, back[0, s, 2 * SG:].astype(f32), back[1, s, 2 * SG:].astype(f32))
+        model = model + back[s, 2 * SG:].astype(f32)
     count = observed.shape[1] // LANES
     for part in range(2):
         for i in range(count):
             at = slice(i * LANES, (i + 1) * LANES)
-            residual[part:part + 1, at] = seen[part:part + 1, at] - model[part * count + i:part * count + i + 1]
+            residual[part:part + 1, at] = observed[part:part + 1, at] - model[part * count + i:part * count + i + 1]
+    part = half_image(back, row_index % 2, row_tab, col_tab, right, both)
+    out[...] = part(slice(0, out.shape[0]))
+
+
+def image_kernel(scale, back, first, row_tab, col_tab, out, right, both, image, sems):
+    row_index, _ = place()
+    part = half_image(back, 1 - row_index % 2, row_tab, col_tab, right, both)
+    chunks = sems.shape[0]
+    step = image.shape[0] // chunks
+    writes = []
+    for n in range(chunks):
+        at = slice(n * step, (n + 1) * step)
+        image[at] = (first[at] + part(at)) * scale
+        write = pltpu.make_async_copy(image.at[at], out.at[at], sems.at[n])
+        write.start()
+        writes.append(write)
     for write in writes:
         write.wait()
 
@@ -340,28 +346,29 @@
     chips = rows_count // 2
     each = SG // cols_count
     x_groups = [[2 * chip + core for chip in range(chips)] for core in range(2)]
-    core_groups = [[2 * chip, 2 * chip + 1] for chip in range(chips)]
+    swap = [(index, index ^ 1) for index in range(rows_count)]
     scale_in = 1.0 / (side * math.sqrt(rows_count * cols_count))
     scale_out = 1.0 / (SG * math.sqrt(NR * NC))
     line = (1, n_vis)
 
-    halves = call(
-        functools.partial(columns_kernel, cols_count), shape(2, side + 16, 4 * HALF), "columns", "saaaaa",
+    half_shape = shape(side + 16, 4 * HALF)
+    own, send = call(
+        functools.partial(columns_kernel, cols_count), (half_shape, half_shape), "columns", "saaaaa",
         scratch=[
             pltpu.VMEM((side, 8 * HALF), bf16), pltpu.VMEM((side, side), bf16), pltpu.VMEM((3,) + line, jnp.int32),
             pltpu.VMEM((2, n_vis), f32), pltpu.SemaphoreType.DMA((5,)),
         ],
         cost=10**9, room=60,
     )(col_offsets, facet, vis_subgrid.reshape(line), vis_u.reshape(line), vis_v.reshape(line), observed)
-    halves = exchange(halves, "frow", core_groups)
+    other = lax.ppermute(send, "frow", swap)
     row_tab = call(
         functools.partial(row_tables_kernel, rows_count, side), shape(4, SG, 2 * side), "row_tables", "s", cost=10**9
     )(row_offsets)
     vis_rows_count = 8 * 2 * n_vis // LANES
     parts = call(
         functools.partial(contributions_kernel, scale_in), shape(NR * NC, 2 * SG + vis_rows_count, HALF),
-        "contributions", "vv", scratch=[pltpu.VMEM((2 * side, 4 * HALF), bf16)], cost=2 * 10**9,
-    )(halves, row_tab)
+        "contributions", "vvv", scratch=[pltpu.VMEM((2 * side, 4 * HALF), bf16)], cost=2 * 10**9,
+    )(own, other, row_tab)
     parts = exchange(parts, "frow", x_groups)
 
     pieces = call(
@@ -371,37 +378,37 @@
     pieces = exchange(pieces, "fcol", None)
     pieces = call(pieces_sum_kernel, shape(cols_count, 5 * each, HALF), "pieces_sum", "v", cost=10**6)(pieces)
     pieces = exchange(pieces, "fcol", None)
-    pieces = exchange(jnp.broadcast_to(pieces, (2,) + pieces.shape), "frow", core_groups)
-
+    pieces_other = lax.ppermute(pieces, "frow", swap)
+
+    back_row, back_col = call(
+        functools.partial(back_tables_kernel, rows_count, cols_count, side),
+        (shape(side, 4 * SG), shape(4 * SG, side)), "back_tables", "ss", cost=10**9,
+    )(row_offsets, col_offsets)
     kcos, ksin = grid_tables()
     block = [np.concatenate(pair, 1) for pair in ((kcos, ksin), (-ksin, kcos), (kcos, -ksin), (ksin, kcos))]
     forward_block = np.concatenate([block[0], block[1]], 0)
     inverse_block = np.concatenate([block[2], block[3]], 0)
     back = call(
-        grids_kernel, shape(chips, 2 * SG + 16, HALF), "grids", "vvvvvv",
+        grids_kernel, shape(chips, 2 * SG + 16, HALF), "grids", "vvvvvvva",
         scratch=[
             pltpu.VMEM((5, SG, SG), f32), pltpu.VMEM((SG, 2 * SG), bf16), pltpu.VMEM((2 * SG, SG), bf16),
             pltpu.VMEM((SG, 2 * SG), bf16),
         ],
         cost=10**9,
-    )(pieces, parts, inverse_block, forward_block, forward_block, inverse_block)
+    )(pieces, pieces_other, parts, inverse_block, forward_block, forward_block, inverse_block, back_col)
     back = exchange(back, "frow", x_groups)
-    back = exchange(jnp.broadcast_to(back, (2,) + back.shape), "frow", core_groups)
-
-    back_row, back_col = call(
-        functools.partial(back_tables_kernel, rows_count, cols_count, side),
-        (shape(side, 4 * SG), shape(4 * SG, side)), "back_tables", "ss", cost=10**9,
-    )(row_offsets, col_offsets)
-    chunks = 4
-    return call(
-        functools.partial(image_kernel, scale_out),
-        (shape(side, side, dtype=f32), shape(2, n_vis, dtype=f32)), "image", "vvva", outs="av",
-        scratch=[
-            pltpu.VMEM((4 * SG, 2 * SG), bf16), pltpu.VMEM((side, 4 * SG), bf16), pltpu.VMEM((side, side), f32),
-            pltpu.VMEM((2, n_vis), f32), pltpu.SemaphoreType.DMA((1 + chunks,)),
-        ],
-        cost=2 * 10**9,
+    back_other = lax.ppermute(back, "frow", swap)
+
+    work = [pltpu.VMEM((4 * SG, 2 * SG), bf16), pltpu.VMEM((side, 2 * SG), bf16)]
+    first, residual = call(
+        own_image_kernel, (shape(side, side, dtype=f32), shape(2, n_vis, dtype=f32)), "own_image", "vvvv",
+        scratch=work, cost=10**9,
     )(back, back_row, back_col, observed)
+    image = call(
+        functools.partial(image_kernel, scale_out), shape(side, side, dtype=f32), "image", "vvvv", outs="a",
+        scratch=work + [pltpu.VMEM((side, side), f32), pltpu.SemaphoreType.DMA((4,))], cost=10**9,
+    )(back_other, first, back_row, back_col)
+    return (image, residual)
 
 
 def solution(mesh):

time: 99.3 us -> 86.9 us (0.88)
  waiting for transfers between devices: 8.38 us -> 0.42 us
  blocking collectives: 64.4 us -> 62.1 us
    all_to_all x2 -> x0, starting transfers between devices: 10.3 us -> none  [exchange(): lax.all_to_all(blocks, axes, 0, 0, tiled=True, axis_index_groups=groups)]
    ppermute x0 -> x3, starting transfers between devices: none -> 9.34 us  [the longest x1 4.7 us: shards(): pieces_other = lax.ppermute(pieces, 'frow', swap)]
    all_to_all x2 -> x0, waiting for transfers between devices: 8.38 us -> none  [exchange(): lax.all_to_all(blocks, axes, 0, 0, tiled=True, axis_index_groups=groups)]
    all_to_all x5 -> x4, blocking collectives: 64.4 us -> 62.1 us  [exchange(): lax.all_to_all(blocks, axes, 0, 0, tiled=True, axis_index_groups=groups)]
    pallas_call x3 -> x4, Pallas kernels: 9.36 us -> 8.7 us  [the longest x1 3.51 us: shards(): call(functools.partial(columns_kernel, cols_count), (half_shape, half_sha...]
  transfers between devices with their start and end apart: 2 -> 3, of which waited for: 2 -> 1; matrix products, arithmetic and copies ran while one was open for 0% -> 0% of each run, Pallas kernels for 3% -> 5%
where the time goes in v5:
time: 86.9 us; the launch traced here: 86.7 us
  blocking collectives  62.1 us (71%)
  Pallas kernels  14 us (16%)
  starting transfers between devices  9.34 us (11%)
    all_to_all x4, blocking collectives, exchange(): lax.all_to_all(blocks, axes, 0, 0, tiled=True, axis_index_groups=groups)  62.1 us
    ppermute x1, starting transfers between devices, shards(): pieces_other = lax.ppermute(pieces, 'frow', swap)  4.7 us
    pallas_call x1, Pallas kernels, shards(): call(functools.partial(columns_kernel, cols_count), (half_shape, half_sha...  3.51 us
    ppermute x1, starting transfers between devices, shards(): other = lax.ppermute(send, 'frow', swap)  3.33 us
    pallas_call x1, Pallas kernels, shards(): call(functools.partial(image_kernel, scale_out), shape(side, side, dtype=...  1.87 us
    pallas_call x1, Pallas kernels, shards(): call(grids_kernel, shape(chips, 2 * SG + 16, HALF), 'grids', 'vvvvvvva',...  1.74 us
  transfers between devices with their start and end apart: 3, of which 1 were waited for; matrix products, arithmetic and copies ran while one was open for 0% of the time, Pallas kernels for 5%

profile of v5, /device:TPU:1, one launch (start us, length us, event | category | flops | bytes accessed | tf_op | source)
XLA Modules:
  0.0 86.7 jit_solution(9751621488388422111)
XLA Ops:
  0.6 0.0 copy-start.4
  0.6 3.5 %columns.1 = (bf16[528,512]{1,0:T(8,128)(2,1)}, bf16[528,512]{1,0:T(8,128)(2,1)}) custom-call(s32[2]{0:T(128)} %offsets_col.1, bf16[512,512]{1,0:T(8,128)(2,1)} %facet.1, s32[1,512]{1,0:T(1,128)} %bitcast.3, s32[1,512]{1,0:T(1,128)} %bitcast.4, s32[1,512]{1,0:T(1,128)} %bitcast.5, f32[2,512]{1,0:T(2,128)} %observed.3), custom_call_target="tpu_custom_call" | custom-call | flops 1000000000 | bytes 1048576 | tf_op jit(solution)/shard_map/columns/pallas_call | solution.py:355
  4.2 0.0 copy-start.5
  4.2 3.3 %collective-permute-start = (bf16[528,512]{1,0:T(8,128)(2,1)}, bf16[528,512]{1,0:T(8,128)(2,1)S(1)}, u32[]{:S(2)}, u32[]{:S(2)}) collective-permute-start(bf16[528,512]{1,0:T(8,128)(2,1)} %get-tuple-element.9), channel_id=1, source_target_pairs={{0,32},{32,0},{64,96},{96,64},{128,160},{160,128},{192,224},{224,1... | collective-permute-start | bytes 1622024 | tf_op jit(solution)/shard_map/ppermute | solution.py:363
  7.5 0.0 copy-done.4
  7.5 1.3 %row_tables.1.row_tab = bf16[4,256,1024]{2,1,0:T(8,128)(2,1)S(1)} custom-call(s32[2]{0:T(128)S(1)} %copy-done.4), custom_call_target="tpu_custom_call" | custom-call | flops 1000000000 | bytes 1048576 | tf_op jit(solution)/shard_map/row_tables/pallas_call | solution.py:364
  8.9 0.4 collective-permute-done.other
  9.3 0.0 copy-done.5
  9.3 1.2 %contributions.1 = bf16[4,576,128]{2,1,0:T(8,128)(2,1)S(1)} custom-call(bf16[528,512]{1,0:T(8,128)(2,1)S(1)} %copy-done.5, bf16[528,512]{1,0:T(8,128)(2,1)S(1)} %collective-permute-done.other, bf16[4,256,1024]{2,1,0:T(8,128)(2,1)S(1)} %row_tables.1.row_tab), custom_call_target="tpu_custom_call" | custom-call | flops 2000000000 | bytes 1048576 | tf_op jit(solution)/shard_map/contributions/pallas_call | solution.py:368
  10.5 12.0 %all_to_all.20.parts = bf16[4,576,128]{2,1,0:T(8,128)(2,1)S(1)} all-to-all(bf16[4,576,128]{2,1,0:T(8,128)(2,1)S(1)} %contributions.1), channel_id=1, replica_groups={{0,64,128,192},{32,96,160,224},{1,65,129,193},{33,97,161,225},{2,66,130..., dimensions={0} | all-to-all | bytes 1179648 | tf_op jit(solution)/shard_map/all_to_all | solution.py:334
  22.5 0.0 copy-start.3
  22.5 1.3 %gridding.1 = bf16[32,40,128]{2,1,0:T(8,128)(2,1)S(1)} custom-call(bf16[4,576,128]{2,1,0:T(8,128)(2,1)S(1)} %all_to_all.20.parts), custom_call_target="tpu_custom_call" | custom-call | flops 1000000000 | bytes 1048576 | tf_op jit(solution)/shard_map/gridding/pallas_call | solution.py:374
  23.8 21.9 %all_to_all.21.pieces = bf16[32,40,128]{2,1,0:T(8,128)(2,1)S(1)} all-to-all(bf16[32,40,128]{2,1,0:T(8,128)(2,1)S(1)} %gridding.1), channel_id=1, replica_groups=mesh['frow'=8,'fcol'=32] {'fcol'}, dimensions={0} | all-to-all | bytes 655360 | tf_op jit(solution)/shard_map/all_to_all | solution.py:334
  45.7 0.1 pieces_sum.1
  45.8 0.0 copy-start
  45.8 0.0 copy-start.1
  45.8 16.6 %all_to_all.22.own = bf16[32,40,128]{2,1,0:T(8,128)(2,1)S(1)} all-to-all(bf16[32,40,128]{2,1,0:T(8,128)(2,1)S(1)} %pieces_sum.1), channel_id=1, replica_groups=mesh['frow'=8,'fcol'=32] {'fcol'}, dimensions={0} | all-to-all | bytes 655360 | tf_op jit(solution)/shard_map/all_to_all | solution.py:334
  62.4 4.7 %collective-permute-start.1 = (bf16[32,40,128]{2,1,0:T(8,128)(2,1)S(1)}, bf16[32,40,128]{2,1,0:T(8,128)(2,1)S(1)}, u32[]{:S(2)}, u32[]{:S(2)}) collective-permute-start(bf16[32,40,128]{2,1,0:T(8,128)(2,1)S(1)} %all_to_all.22.own), channel_id=1, source_target_pairs={{0,32},{32,0},{64,96},{96,64},{128,160},{160,128},{192,224},{224,1... | collective-permute-start | bytes 983048 | tf_op jit(solution)/shard_map/ppermute | solution.py:381
  67.1 0.0 copy-done.3
  67.1 1.4 %back_tables.1 = (bf16[512,1024]{1,0:T(8,128)(2,1)S(1)}, bf16[1024,512]{1,0:T(8,128)(2,1)S(1)}) custom-call(s32[2]{0:T(128)S(1)} %copy-done.4, s32[2]{0:T(128)S(1)} %copy-done.3), custom_call_target="tpu_custom_call" | custom-call | flops 1000000000 | bytes 1048576 | tf_op jit(solution)/shard_map/back_tables/pallas_call | solution.py:383
  68.4 0.0 collective-permute-done.1.other
  68.5 0.0 copy-done
  68.5 0.0 copy-done.1
  68.5 0.0 copy-start.2
  68.5 1.7 %grids.1 = bf16[4,528,128]{2,1,0:T(8,128)(2,1)S(1)} custom-call(bf16[32,40,128]{2,1,0:T(8,128)(2,1)S(1)} %all_to_all.22.own, bf16[32,40,128]{2,1,0:T(8,128)(2,1)S(1)} %collective-permute-done.1.other, bf16[4,576,128]{2,1,0:T(8,128)(2,1)S(1)} %all_to_all.20.parts, bf16[512,512]{1,0:T(8,128)(2,1)S(1)} %copy-done.1, bf16[512,512]{1,0:T(8,128)(2,1)S(1)} %copy-done, ...), custom_call_target="tpu_custom_call" | custom-call | flops 1000000000 | bytes 1048576 | tf_op jit(solution)/shard_map/grids/pallas_call | solution.py:391
  70.2 11.7 %all_to_all.23.back = bf16[4,528,128]{2,1,0:T(8,128)(2,1)S(1)} all-to-all(bf16[4,528,128]{2,1,0:T(8,128)(2,1)S(1)} %grids.1), channel_id=1, replica_groups={{0,64,128,192},{32,96,160,224},{1,65,129,193},{33,97,161,225},{2,66,130..., dimensions={0} | all-to-all | bytes 1081344 | tf_op jit(solution)/shard_map/all_to_all | solution.py:334
  81.9 1.3 %collective-permute-start.2 = (bf16[4,528,128]{2,1,0:T(8,128)(2,1)S(1)}, bf16[4,528,128]{2,1,0:T(8,128)(2,1)S(1)}, u32[]{:S(2)}, u32[]{:S(2)}) collective-permute-start(bf16[4,528,128]{2,1,0:T(8,128)(2,1)S(1)} %all_to_all.23.back), channel_id=1, source_target_pairs={{0,32},{32,0},{64,96},{96,64},{128,160},{160,128},{192,224},{224,1... | collective-permute-start | bytes 1622024 | tf_op jit(solution)/shard_map/ppermute | solution.py:400
  83.2 0.0 copy-done.2
  83.2 1.6 %own_image.1 = (f32[512,512]{1,0:T(8,128)S(1)}, f32[2,512]{1,0:T(2,128)}) custom-call(bf16[4,528,128]{2,1,0:T(8,128)(2,1)S(1)} %all_to_all.23.back, bf16[512,1024]{1,0:T(8,128)(2,1)S(1)} %get-tuple-element.11.row_tab, bf16[1024,512]{1,0:T(8,128)(2,1)S(1)} %get-tuple-element.10._.col_tab, f32[2,512]{1,0:T(2,128)S(1)} %copy-done.2), custom_call_target="tpu_custom_call" | custom-call | flops 1000000000 | bytes 1048576 | tf_op jit(solution)/shard_map/own_image/pallas_call | solution.py:403
  84.8 0.0 collective-permute-done.2.back
  84.8 1.9 %image.1 = f32[512,512]{1,0:T(8,128)} custom-call(bf16[4,528,128]{2,1,0:T(8,128)(2,1)S(1)} %collective-permute-done.2.back, f32[512,512]{1,0:T(8,128)S(1)} %get-tuple-element.12.first, bf16[512,1024]{1,0:T(8,128)(2,1)S(1)} %get-tuple-element.11.row_tab, bf16[1024,512]{1,0:T(8,128)(2,1)S(1)} %get-tuple-element.10._.col_tab), custom_call_target="tpu_custom_call" | custom-call | flops 1000000000 | bytes 1048576 | tf_op jit(solution)/shard_map/image/pallas_call | solution.py:407
Async XLA Ops:
  0.6 6.9 %copy-start.4 = (s32[2]{0:T(128)S(1)}, s32[2]{0:T(128)}, u32[]{:S(2)}) copy-start(s32[2]{0:T(128)} %offsets_row.1) | copy-start | bytes 28
  4.2 5.1 %copy-start.5 = (bf16[528,512]{1,0:T(8,128)(2,1)S(1)}, bf16[528,512]{1,0:T(8,128)(2,1)}, u32[]{:S(2)}) copy-start(bf16[528,512]{1,0:T(8,128)(2,1)} %get-tuple-element.8.own) | copy-start | bytes 1622020
  4.2 5.1 %collective-permute-start = (bf16[528,512]{1,0:T(8,128)(2,1)}, bf16[528,512]{1,0:T(8,128)(2,1)S(1)}, u32[]{:S(2)}, u32[]{:S(2)}) collective-permute-start(bf16[528,512]{1,0:T(8,128)(2,1)} %get-tuple-element.9), channel_id=1, source_target_pairs={{0,32},{32,0},{64,96},{96,64},{128,160},{160,128},{192,224},{224,1... | collective-permute-start | bytes 1622024 | tf_op jit(solution)/shard_map/ppermute | solution.py:363
  22.5 44.5 %copy-start.3 = (s32[2]{0:T(128)S(1)}, s32[2]{0:T(128)}, u32[]{:S(2)}) copy-start(s32[2]{0:T(128)} %offsets_col.1) | copy-start | bytes 28
  45.8 22.7 %copy-start = (bf16[512,512]{1,0:T(8,128)(2,1)S(1)}, bf16[512,512]{1,0:T(8,128)(2,1)}, u32[]{:S(2)}) copy-start(bf16[512,512]{1,0:T(8,128)(2,1)} %constant.5.clone.forward.inverse_left) | copy-start | bytes 1572868
  45.8 22.7 %copy-start.1 = (bf16[512,512]{1,0:T(8,128)(2,1)S(1)}, bf16[512,512]{1,0:T(8,128)(2,1)}, u32[]{:S(2)}) copy-start(bf16[512,512]{1,0:T(8,128)(2,1)} %constant.4.clone.grid_left.inverse) | copy-start | bytes 1572868
  62.4 6.1 %collective-permute-start.1 = (bf16[32,40,128]{2,1,0:T(8,128)(2,1)S(1)}, bf16[32,40,128]{2,1,0:T(8,128)(2,1)S(1)}, u32[]{:S(2)}, u32[]{:S(2)}) collective-permute-start(bf16[32,40,128]{2,1,0:T(8,128)(2,1)S(1)} %all_to_all.22.own), channel_id=1, source_target_pairs={{0,32},{32,0},{64,96},{96,64},{128,160},{160,128},{192,224},{224,1... | collective-permute-start | bytes 983048 | tf_op jit(solution)/shard_map/ppermute | solution.py:381
  68.5 14.7 %copy-start.2 = (f32[2,512]{1,0:T(2,128)S(1)}, f32[2,512]{1,0:T(2,128)}, u32[]{:S(2)}) copy-start(f32[2,512]{1,0:T(2,128)} %observed.3) | copy-start | bytes 12292
  81.9 2.9 %collective-permute-start.2 = (bf16[4,528,128]{2,1,0:T(8,128)(2,1)S(1)}, bf16[4,528,128]{2,1,0:T(8,128)(2,1)S(1)}, u32[]{:S(2)}, u32[]{:S(2)}) collective-permute-start(bf16[4,528,128]{2,1,0:T(8,128)(2,1)S(1)} %all_to_all.23.back), channel_id=1, source_target_pairs={{0,32},{32,0},{64,96},{96,64},{128,160},{160,128},{192,224},{224,1... | collective-permute-start | bytes 1622024 | tf_op jit(solution)/shard_map/ppermute | solution.py:400

commit v6 on v5

--- a/solution.py
+++ b/solution.py
@@ -112,27 +112,31 @@
             spread(coarse, fine, store)
 
 
-def contributions_kernel(scale, own, other, row_tab, out, right):
-    f32, bf16 = jnp.float32, jnp.bfloat16
+def contributions_kernel(scale, own, other, row_tab, *refs):
+    f32, bf16 = jnp.float32, jnp.bfloat16
+    outs, right = refs[:-1], refs[-1]
+    chip = place()[0] // 2
     side = row_tab.shape[2] // 2
     vis = []
     for f, half in enumerate((own, other)):
         right[f * side:(f + 1) * side] = half[:side]
         some = half[side:]
         vis += [some[:, k * LANES:(k + 1) * LANES] for k in range(side // 2 // LANES)]
-    for s in range(NR * NC):
+    for n, out in enumerate(outs):
         for k, some in enumerate(vis):
             at = 2 * SG + 16 * k
-            out[s, at:at + 16] = some
-    for r in range(NR):
-        with_cos = jnp.dot(row_tab[2 * r], right[...], preferred_element_type=f32)
-        with_sin = jnp.dot(row_tab[2 * r + 1], right[...], preferred_element_type=f32)
-        for c in range(NC):
-            at = 2 * c * HALF
-            cp, cq = with_cos[:, at:at + HALF], with_cos[:, at + HALF:at + 2 * HALF]
-            sp, sq = with_sin[:, at:at + HALF], with_sin[:, at + HALF:at + 2 * HALF]
-            out[r * NC + c, :SG] = ((cp - sq) * scale).astype(bf16)
-            out[r * NC + c, SG:2 * SG] = (-(cq + sp) * scale).astype(bf16)
+            out[at:at + 16] = some
+        r, c = split_number(chip + n)
+        some = right[:, pl.ds(pl.multiple_of(c * SG, SG), SG)]
+        with_cos = jnp.dot(row_tab[2 * r], some, preferred_element_type=f32)
+        with_sin = jnp.dot(row_tab[2 * r + 1], some, preferred_element_type=f32)
+        out[:SG] = ((with_cos[:, :HALF] - with_sin[:, HALF:]) * scale).astype(bf16)
+        out[SG:2 * SG] = (-(with_cos[:, HALF:] + with_sin[:, :HALF]) * scale).astype(bf16)
+
+
+def split_number(number):
+    number = lax.rem(number, NR * NC)
+    return number // NC, lax.rem(number, NC)
 
 
 def vis_rows(block):
@@ -142,16 +146,17 @@
     )
 
 
-def gridding_kernel(parts, pieces, planes):
-    f32, bf16 = jnp.float32, jnp.bfloat16
+def gridding_kernel(*refs):
+    f32, bf16 = jnp.float32, jnp.bfloat16
+    parts, (pieces, planes) = refs[:-2], refs[-2:]
     row_index, _ = place()
     chip = (row_index // 2).astype(f32)
     v_at = (sublanes(HALF) + (row_index % 2) * HALF).astype(f32)
     counter = sublanes(SG).astype(f32)
-    count = parts.shape[0]
+    count = len(parts)
     total = jnp.zeros((SG, 3 * HALF), f32)
     for k in range(count):
-        one = vis_rows(parts[k, 2 * SG:].astype(f32))
+        one = vis_rows(parts[k][2 * SG:].astype(f32))
         u_here = jnp.where(one[0:1] == chip, one[1:2], -1.0)
         hot = jnp.where(u_here == counter, 1.0, 0.0).astype(bf16)
         pick = one[2:3] == v_at
@@ -160,9 +165,9 @@
         ).astype(bf16)
         total = total + lax.dot_general(hot, right, (((1,), (1,)), ((), ())), preferred_element_type=f32)
     for p in range(2):
-        some = parts[0, p * SG:(p + 1) * SG].astype(f32)
+        some = parts[0][p * SG:(p + 1) * SG].astype(f32)
         for k in range(1, count):
-            some = some + parts[k, p * SG:(p + 1) * SG].astype(f32)
+            some = some + parts[k][p * SG:(p + 1) * SG].astype(f32)
         planes[p] = some
     for p in range(3):
         planes[2 + p] = total[:, p * HALF:(p + 1) * HALF]
@@ -182,8 +187,10 @@
         out[j] = total
 
 
-def grids_kernel(own, other, parts, grid_left, forward, inverse_left, inverse, _, out, planes, cat, tall, hat):
-    f32, bf16 = jnp.float32, jnp.bfloat16
+def grids_kernel(chips, own, other, *refs):
+    f32, bf16 = jnp.float32, jnp.bfloat16
+    parts, (grid_left, forward, inverse_left, inverse, _) = refs[:chips], refs[chips:chips + 5]
+    outs, rest, (planes, cat, tall, hat) = refs[chips + 5:-5], refs[-5], refs[-4:]
     row_index, _ = place()
     core = row_index % 2
     chip = (row_index // 2).astype(f32)
@@ -208,15 +215,15 @@
     hat[:, SG:] = hat_imag.astype(bf16)
     wide = jnp.dot(cat[...], inverse[...], preferred_element_type=f32)
     for k in range(2):
-        some = wide[:, k * SG:(k + 1) * SG]
-        tall[k * SG:(k + 1) * SG, :HALF] = jnp.where(core == 0, some[:, :HALF], some[:, HALF:]).astype(bf16)
-    back = jnp.dot(inverse_left[...], tall[:, :HALF], preferred_element_type=f32) * (1.0 / SG)
-    back = back.astype(bf16)
+        tall[k * SG:(k + 1) * SG] = wide[:, k * SG:(k + 1) * SG].astype(bf16)
+    back = jnp.dot(inverse_left[...], tall[...], preferred_element_type=f32) * (1.0 / SG)
+    rest[...] = jnp.where(core == 0, back[:, HALF:], back[:, :HALF]).astype(bf16)
+    back = jnp.where(core == 0, back[:, :HALF], back[:, HALF:]).astype(bf16)
     counter = sublanes(SG).astype(f32)
-    vis_each = (parts.shape[1] - 2 * SG) // 2
-    for k in range(parts.shape[0]):
-        out[k, :2 * SG] = back
-        ask = vis_rows(parts[k, 2 * SG:2 * SG + vis_each].astype(f32))
+    vis_each = (parts[0].shape[0] - 2 * SG) // 2
+    for k, out in enumerate(outs):
+        out[:2 * SG] = back
+        ask = vis_rows(parts[-k % chips][2 * SG:2 * SG + vis_each].astype(f32))
         u_here = jnp.where(ask[0:1] == chip, ask[1:2], -1.0)
         hot = jnp.where(u_here == counter, 1.0, 0.0).astype(bf16)
         pick = ask[2:3] == counter
@@ -226,7 +233,7 @@
             value = jnp.sum(jnp.where(pick, line[part * SG:(part + 1) * SG], 0.0), axis=0, keepdims=True)
             rows += [value[:, i * LANES:(i + 1) * LANES] for i in range(value.shape[1] // LANES)]
         rows.append(jnp.zeros((16 - len(rows), LANES), f32))
-        out[k, 2 * SG:] = jnp.concatenate(rows, 0).astype(bf16)
+        out[2 * SG:] = jnp.concatenate(rows, 0).astype(bf16)
 
 
 def back_tables_kernel(rows_count, cols_count, side, offsets_row, offsets_col, row_tab, col_tab):
@@ -259,41 +266,44 @@
         spread(coarse, fine, store)
 
 
-def half_image(back, half, row_tab, col_tab, right, both):
-    f32, bf16 = jnp.float32, jnp.bfloat16
-    for c in range(NC):
-        for r in range(NR):
-            real = back[r * NC + c, :SG]
-            imag = back[r * NC + c, SG:2 * SG]
-            top, at = 2 * r * SG, 2 * c * HALF
-            right[top:top + SG, at:at + HALF] = real
-            right[top:top + SG, at + HALF:at + 2 * HALF] = imag
-            right[top + SG:top + 2 * SG, at:at + HALF] = -imag
-            right[top + SG:top + 2 * SG, at + HALF:at + 2 * HALF] = real
+def half_image(blocks, half, row_tab, col_tab, right, both):
+    f32, bf16 = jnp.float32, jnp.bfloat16
+    chip = place()[0] // 2
+    for k, block in enumerate(blocks):
+        r, c = split_number(chip + len(blocks) - k)
+        real, imag = block[:SG], block[SG:2 * SG]
+        top = [pl.ds(pl.multiple_of((2 * r + n) * SG, SG), SG) for n in range(2)]
+        at = [pl.ds(pl.multiple_of((2 * c + n) * HALF, HALF), HALF) for n in range(2)]
+        right[top[0], at[0]] = real
+        right[top[0], at[1]] = imag
+        right[top[1], at[0]] = -imag
+        right[top[1], at[1]] = real
     both[...] = jnp.dot(row_tab[...], right[...], preferred_element_type=f32).astype(bf16)
     depth = 2 * NC * HALF
     rows = pl.ds(pl.multiple_of(half * depth, depth), depth)
     return lambda at: jnp.dot(both[at], col_tab[rows], preferred_element_type=f32)
 
 
-def own_image_kernel(back, row_tab, col_tab, observed, out, residual, right, both):
+def own_image_kernel(*refs):
+    blocks, (row_tab, col_tab, observed, out, residual, right, both) = refs[:-7], refs[-7:]
     f32 = jnp.float32
     row_index, _ = place()
     model = jnp.zeros((16, LANES), f32)
-    for s in range(NR * NC):
-        model = model + back[s, 2 * SG:].astype(f32)
+    for block in blocks:
+        model = model + block[2 * SG:].astype(f32)
     count = observed.shape[1] // LANES
     for part in range(2):
         for i in range(count):
             at = slice(i * LANES, (i + 1) * LANES)
             residual[part:part + 1, at] = observed[part:part + 1, at] - model[part * count + i:part * count + i + 1]
-    part = half_image(back, row_index % 2, row_tab, col_tab, right, both)
+    part = half_image(blocks, row_index % 2, row_tab, col_tab, right, both)
     out[...] = part(slice(0, out.shape[0]))
 
 
-def image_kernel(scale, back, first, row_tab, col_tab, out, right, both, image, sems):
+def image_kernel(scale, *refs):
+    blocks, (first, row_tab, col_tab, out, right, both, image, sems) = refs[:-8], refs[-8:]
     row_index, _ = place()
-    part = half_image(back, 1 - row_index % 2, row_tab, col_tab, right, both)
+    part = half_image(blocks, 1 - row_index % 2, row_tab, col_tab, right, both)
     chunks = sems.shape[0]
     step = image.shape[0] // chunks
     writes = []
@@ -345,8 +355,8 @@
     n_vis = vis_u.shape[0]
     chips = rows_count // 2
     each = SG // cols_count
-    x_groups = [[2 * chip + core for chip in range(chips)] for core in range(2)]
     swap = [(index, index ^ 1) for index in range(rows_count)]
+    turns = [[(index, (index + 2 * k) % rows_count) for index in range(rows_count)] for k in range(chips)]
     scale_in = 1.0 / (side * math.sqrt(rows_count * cols_count))
     scale_out = 1.0 / (SG * math.sqrt(NR * NC))
     line = (1, n_vis)
@@ -366,15 +376,15 @@
     )(row_offsets)
     vis_rows_count = 8 * 2 * n_vis // LANES
     parts = call(
-        functools.partial(contributions_kernel, scale_in), shape(NR * NC, 2 * SG + vis_rows_count, HALF),
+        functools.partial(contributions_kernel, scale_in), (shape(2 * SG + vis_rows_count, HALF),) * chips,
         "contributions", "vvv", scratch=[pltpu.VMEM((2 * side, 4 * HALF), bf16)], cost=2 * 10**9,
     )(own, other, row_tab)
-    parts = exchange(parts, "frow", x_groups)
+    parts = [parts[0]] + [lax.ppermute(parts[k], "frow", turns[k]) for k in range(1, chips)]
 
     pieces = call(
-        gridding_kernel, shape(cols_count, 5 * each, HALF), "gridding", "v",
+        gridding_kernel, shape(cols_count, 5 * each, HALF), "gridding", "v" * chips,
         scratch=[pltpu.VMEM((5, SG, HALF), f32)], cost=10**9,
-    )(parts)
+    )(*parts)
     pieces = exchange(pieces, "fcol", None)
     pieces = call(pieces_sum_kernel, shape(cols_count, 5 * each, HALF), "pieces_sum", "v", cost=10**6)(pieces)
     pieces = exchange(pieces, "fcol", None)
@@ -388,26 +398,27 @@
     block = [np.concatenate(pair, 1) for pair in ((kcos, ksin), (-ksin, kcos), (kcos, -ksin), (ksin, kcos))]
     forward_block = np.concatenate([block[0], block[1]], 0)
     inverse_block = np.concatenate([block[2], block[3]], 0)
-    back = call(
-        grids_kernel, shape(chips, 2 * SG + 16, HALF), "grids", "vvvvvvva",
+    *back, rest = call(
+        functools.partial(grids_kernel, chips), (shape(2 * SG + 16, HALF),) * chips + (shape(2 * SG, HALF),), "grids",
+        "v" * (6 + chips) + "a",
         scratch=[
             pltpu.VMEM((5, SG, SG), f32), pltpu.VMEM((SG, 2 * SG), bf16), pltpu.VMEM((2 * SG, SG), bf16),
             pltpu.VMEM((SG, 2 * SG), bf16),
         ],
         cost=10**9,
-    )(pieces, pieces_other, parts, inverse_block, forward_block, forward_block, inverse_block, back_col)
-    back = exchange(back, "frow", x_groups)
-    back_other = lax.ppermute(back, "frow", swap)
+    )(pieces, pieces_other, *parts, inverse_block, forward_block, forward_block, inverse_block, back_col)
+    back = [back[0]] + [lax.ppermute(back[k], "frow", turns[k]) for k in range(1, chips)]
+    back_other = [rest] + [lax.ppermute(back[k], "frow", swap) for k in range(1, chips)]
 
     work = [pltpu.VMEM((4 * SG, 2 * SG), bf16), pltpu.VMEM((side, 2 * SG), bf16)]
     first, residual = call(
-        own_image_kernel, (shape(side, side, dtype=f32), shape(2, n_vis, dtype=f32)), "own_image", "vvvv",
+        own_image_kernel, (shape(side, side, dtype=f32), shape(2, n_vis, dtype=f32)), "own_image", "vvv" + "v" * chips,
         scratch=work, cost=10**9,
-    )(back, back_row, back_col, observed)
+    )(*back, back_row, back_col, observed)
     image = call(
-        functools.partial(image_kernel, scale_out), shape(side, side, dtype=f32), "image", "vvvv", outs="a",
+        functools.partial(image_kernel, scale_out), shape(side, side, dtype=f32), "image", "vvv" + "v" * chips, outs="a",
         scratch=work + [pltpu.VMEM((side, side), f32), pltpu.SemaphoreType.DMA((4,))], cost=10**9,
-    )(back_other, first, back_row, back_col)
+    )(*back_other, first, back_row, back_col)
     return (image, residual)
 
 

time: 86.9 us -> 82.2 us (0.946)
  blocking collectives: 62.1 us -> 37.9 us
  waiting for transfers between devices: 0.42 us -> 11.7 us
  starting transfers between devices: 9.34 us -> 17.1 us
    all_to_all x4 -> x2, blocking collectives: 62.1 us -> 37.9 us  [exchange(): lax.all_to_all(blocks, axes, 0, 0, tiled=True, axis_index_groups=groups)]
    ppermute x1 -> x9, waiting for transfers between devices: 0.01 us -> 11.3 us  [the longest x3 6.64 us: shards(): lax.ppermute(parts[k], 'frow', turns[k])]
    ppermute x1 -> x9, starting transfers between devices: 1.31 us -> 9.3 us  [the longest x3 4.13 us: shards(): lax.ppermute(back[k], 'frow', turns[k])]
  transfers between devices with their start and end apart: 3 -> 11, of which waited for: 1 -> 6; matrix products, arithmetic and copies ran while one was open for 0% -> 0% of each run, Pallas kernels for 5% -> 5%
where the time goes in v6:
time: 82.2 us; the launch traced here: 82 us
  blocking collectives  37.9 us (46%)
  starting transfers between devices  17.1 us (21%)
  Pallas kernels  14.3 us (17%)
  waiting for transfers between devices  11.7 us (14%)
  between operations  0.93 us (1%)
    all_to_all x2, blocking collectives, exchange(): lax.all_to_all(blocks, axes, 0, 0, tiled=True, axis_index_groups=groups)  37.9 us
    ppermute x3, waiting for transfers between devices, shards(): lax.ppermute(parts[k], 'frow', turns[k])  6.64 us
    ppermute x3, waiting for transfers between devices, shards(): lax.ppermute(back[k], 'frow', turns[k])  4.67 us
    ppermute x1, starting transfers between devices, shards(): pieces_other = lax.ppermute(pieces, 'frow', swap)  4.51 us
    ppermute x3, starting transfers between devices, shards(): lax.ppermute(back[k], 'frow', turns[k])  4.13 us
    pallas_call x1, Pallas kernels, shards(): call(functools.partial(columns_kernel, cols_count), (half_shape, half_sha...  3.51 us
    ppermute x1, starting transfers between devices, shards(): other = lax.ppermute(send, 'frow', swap)  3.33 us
    ppermute x3, starting transfers between devices, shards(): lax.ppermute(parts[k], 'frow', turns[k])  3.15 us
  transfers between devices with their start and end apart: 11, of which 6 were waited for; matrix products, arithmetic and copies ran while one was open for 0% of the time, Pallas kernels for 5%

profile of v6, /device:TPU:1, one launch (start us, length us, event | category | flops | bytes accessed | tf_op | source)
XLA Modules:
  0.0 82.0 jit_solution(8816514083046986569)
XLA Ops:
  0.6 0.0 copy-start.4
  0.6 3.5 %columns.1 = (bf16[528,512]{1,0:T(8,128)(2,1)}, bf16[528,512]{1,0:T(8,128)(2,1)}) custom-call(s32[2]{0:T(128)} %offsets_col.1, bf16[512,512]{1,0:T(8,128)(2,1)} %facet.1, s32[1,512]{1,0:T(1,128)} %bitcast.3, s32[1,512]{1,0:T(1,128)} %bitcast.4, s32[1,512]{1,0:T(1,128)} %bitcast.5, f32[2,512]{1,0:T(2,128)} %refs_6_.2), custom_call_target="tpu_custom_call" | custom-call | flops 1000000000 | bytes 1048576 | tf_op jit(solution)/shard_map/columns/pallas_call | solution.py:365
  4.2 0.0 copy-start.5
  4.2 3.3 %collective-permute-start = (bf16[528,512]{1,0:T(8,128)(2,1)}, bf16[528,512]{1,0:T(8,128)(2,1)S(1)}, u32[]{:S(2)}, u32[]{:S(2)}) collective-permute-start(bf16[528,512]{1,0:T(8,128)(2,1)} %get-tuple-element.18), channel_id=1, source_target_pairs={{0,32},{32,0},{64,96},{96,64},{128,160},{160,128},{192,224},{224,1... | collective-permute-start | bytes 1622024 | tf_op jit(solution)/shard_map/ppermute | solution.py:373
  7.5 0.0 copy-done.4
  7.5 1.3 %row_tables.1.row_tab = bf16[4,256,1024]{2,1,0:T(8,128)(2,1)S(1)} custom-call(s32[2]{0:T(128)S(1)} %copy-done.4), custom_call_target="tpu_custom_call" | custom-call | flops 1000000000 | bytes 1048576 | tf_op jit(solution)/shard_map/row_tables/pallas_call | solution.py:374
  8.9 0.4 collective-permute-done.other
  9.3 0.0 copy-done.5
  9.3 1.3 %contributions.1 = (bf16[576,128]{1,0:T(8,128)(2,1)S(1)}, bf16[576,128]{1,0:T(8,128)(2,1)S(1)}, bf16[576,128]{1,0:T(8,128)(2,1)S(1)}, bf16[576,128]{1,0:T(8,128)(2,1)S(1)}) custom-call(bf16[528,512]{1,0:T(8,128)(2,1)S(1)} %copy-done.5, bf16[528,512]{1,0:T(8,128)(2,1)S(1)} %collective-permute-done.other, bf16[4,256,1024]{2,1,0:T(8,128)(2,1)S(1)} %row_tables.1.row_tab), custom_call_target="tpu_custom_call" | custom-call | flops 2000000000 | bytes 1048576 | tf_op jit(solution)/shard_map/contributions/pallas_call | solution.py:378
  10.6 0.1 collective-permute-start.1
  10.7 1.9 %collective-permute-start.2 = (bf16[576,128]{1,0:T(8,128)(2,1)S(1)}, bf16[576,128]{1,0:T(8,128)(2,1)S(1)}, u32[]{:S(2)}, u32[]{:S(2)}) collective-permute-start(bf16[576,128]{1,0:T(8,128)(2,1)S(1)} %get-tuple-element.21), channel_id=1, source_target_pairs={{0,128},{32,160},{64,192},{96,224},{128,0},{160,32},{192,64},{224,... | collective-permute-start | bytes 442376 | tf_op jit(solution)/shard_map/ppermute | solution.py:382
  12.6 1.2 %collective-permute-start.3 = (bf16[576,128]{1,0:T(8,128)(2,1)S(1)}, bf16[576,128]{1,0:T(8,128)(2,1)S(1)}, u32[]{:S(2)}, u32[]{:S(2)}) collective-permute-start(bf16[576,128]{1,0:T(8,128)(2,1)S(1)} %get-tuple-element.22), channel_id=1, source_target_pairs={{0,192},{32,224},{64,0},{96,32},{128,64},{160,96},{192,128},{224,1... | collective-permute-start | bytes 442376 | tf_op jit(solution)/shard_map/ppermute | solution.py:382
  13.8 3.9 %collective-permute-done.1.refs_1_ = bf16[576,128]{1,0:T(8,128)(2,1)S(1)} collective-permute-done((bf16[576,128]{1,0:T(8,128)(2,1)S(1)}, bf16[576,128]{1,0:T(8,128)(2,1)S(1)}, u32[]{:S(2)}, u32[]{:S(2)}) %collective-permute-start.1) | collective-permute-done | bytes 147488 | tf_op jit(solution)/shard_map/ppermute | solution.py:382
  17.7 1.7 %collective-permute-done.2.refs_2_ = bf16[576,128]{1,0:T(8,128)(2,1)S(1)} collective-permute-done((bf16[576,128]{1,0:T(8,128)(2,1)S(1)}, bf16[576,128]{1,0:T(8,128)(2,1)S(1)}, u32[]{:S(2)}, u32[]{:S(2)}) %collective-permute-start.2) | collective-permute-done | bytes 147488 | tf_op jit(solution)/shard_map/ppermute | solution.py:382
  19.4 1.0 %collective-permute-done.3.refs_3_ = bf16[576,128]{1,0:T(8,128)(2,1)S(1)} collective-permute-done((bf16[576,128]{1,0:T(8,128)(2,1)S(1)}, bf16[576,128]{1,0:T(8,128)(2,1)S(1)}, u32[]{:S(2)}, u32[]{:S(2)}) %collective-permute-start.3) | collective-permute-done | bytes 147488 | tf_op jit(solution)/shard_map/ppermute | solution.py:382
  20.4 0.0 copy-start.3
  20.4 1.3 %gridding.1 = bf16[32,40,128]{2,1,0:T(8,128)(2,1)S(1)} custom-call(bf16[576,128]{1,0:T(8,128)(2,1)S(1)} %get-tuple-element.19.refs_0_, bf16[576,128]{1,0:T(8,128)(2,1)S(1)} %collective-permute-done.1.refs_1_, bf16[576,128]{1,0:T(8,128)(2,1)S(1)} %collective-permute-done.2.refs_2_, bf16[576,128]{1,0:T(8,128)(2,1)S(1)} %collective-permute-done.3.refs_3_), custom_call_target="tpu_custom_call" | custom-call | flops 1000000000 | bytes 1048576 | tf_op jit(solution)/shard_map/gridding/pallas_call | solution.py:384
  21.7 21.8 %all_to_all.10.pieces = bf16[32,40,128]{2,1,0:T(8,128)(2,1)S(1)} all-to-all(bf16[32,40,128]{2,1,0:T(8,128)(2,1)S(1)} %gridding.1), channel_id=1, replica_groups=mesh['frow'=8,'fcol'=32] {'fcol'}, dimensions={0} | all-to-all | bytes 655360 | tf_op jit(solution)/shard_map/all_to_all | solution.py:344
  43.5 0.1 pieces_sum.1
  43.6 0.0 copy-start
  43.6 0.0 copy-start.1
  43.6 16.1 %all_to_all.11.own = bf16[32,40,128]{2,1,0:T(8,128)(2,1)S(1)} all-to-all(bf16[32,40,128]{2,1,0:T(8,128)(2,1)S(1)} %pieces_sum.1), channel_id=1, replica_groups=mesh['frow'=8,'fcol'=32] {'fcol'}, dimensions={0} | all-to-all | bytes 655360 | tf_op jit(solution)/shard_map/all_to_all | solution.py:344
  59.7 4.5 %collective-permute-start.4 = (bf16[32,40,128]{2,1,0:T(8,128)(2,1)S(1)}, bf16[32,40,128]{2,1,0:T(8,128)(2,1)S(1)}, u32[]{:S(2)}, u32[]{:S(2)}) collective-permute-start(bf16[32,40,128]{2,1,0:T(8,128)(2,1)S(1)} %all_to_all.11.own), channel_id=1, source_target_pairs={{0,32},{32,0},{64,96},{96,64},{128,160},{160,128},{192,224},{224,1... | collective-permute-start | bytes 983048 | tf_op jit(solution)/shard_map/ppermute | solution.py:391
  64.2 0.0 copy-done.3
  64.2 1.4 %back_tables.1 = (bf16[512,1024]{1,0:T(8,128)(2,1)S(1)}, bf16[1024,512]{1,0:T(8,128)(2,1)S(1)}) custom-call(s32[2]{0:T(128)S(1)} %copy-done.4, s32[2]{0:T(128)S(1)} %copy-done.3), custom_call_target="tpu_custom_call" | custom-call | flops 1000000000 | bytes 1048576 | tf_op jit(solution)/shard_map/back_tables/pallas_call | solution.py:393
  65.6 0.0 collective-permute-done.4.other
  65.6 0.0 copy-done
  65.6 0.0 copy-done.1
  65.6 0.0 copy-start.2
  65.7 1.7 %grids.1 = (bf16[528,128]{1,0:T(8,128)(2,1)S(1)}, bf16[528,128]{1,0:T(8,128)(2,1)S(1)}, bf16[528,128]{1,0:T(8,128)(2,1)S(1)}, bf16[528,128]{1,0:T(8,128)(2,1)S(1)}, bf16[512,128]{1,0:T(8,128)(2,1)S(1)}) custom-call(bf16[32,40,128]{2,1,0:T(8,128)(2,1)S(1)} %all_to_all.11.own, bf16[32,40,128]{2,1,0:T(8,128)(2,1)S(1)} %collective-permute-done.4.other, ...), custom_call_target="tpu_custom_call" | custom-call | flops 1000000000 | bytes 1048576 | tf_op jit(solution)/shard_map/grids/pallas_call | solution.py:401
  67.3 1.1 %collective-permute-start.5 = (bf16[528,128]{1,0:T(8,128)(2,1)S(1)}, bf16[528,128]{1,0:T(8,128)(2,1)S(1)}, u32[]{:S(2)}, u32[]{:S(2)}) collective-permute-start(bf16[528,128]{1,0:T(8,128)(2,1)S(1)} %get-tuple-element.25), channel_id=1, source_target_pairs={{0,64},{32,96},{64,128},{96,160},{128,192},{160,224},{192,0},{224,... | collective-permute-start | bytes 405512 | tf_op jit(solution)/shard_map/ppermute | solution.py:410
  68.5 2.3 %collective-permute-start.7 = (bf16[528,128]{1,0:T(8,128)(2,1)S(1)}, bf16[528,128]{1,0:T(8,128)(2,1)S(1)}, u32[]{:S(2)}, u32[]{:S(2)}) collective-permute-start(bf16[528,128]{1,0:T(8,128)(2,1)S(1)} %get-tuple-element.26), channel_id=1, source_target_pairs={{0,128},{32,160},{64,192},{96,224},{128,0},{160,32},{192,64},{224,... | collective-permute-start | bytes 405512 | tf_op jit(solution)/shard_map/ppermute | solution.py:410
  70.7 0.7 collective-permute-start.9
  71.5 2.1 %collective-permute-done.5.refs_1_ = bf16[528,128]{1,0:T(8,128)(2,1)S(1)} collective-permute-done((bf16[528,128]{1,0:T(8,128)(2,1)S(1)}, bf16[528,128]{1,0:T(8,128)(2,1)S(1)}, u32[]{:S(2)}, u32[]{:S(2)}) %collective-permute-start.5) | collective-permute-done | bytes 135200 | tf_op jit(solution)/shard_map/ppermute | solution.py:410
  73.6 1.0 %collective-permute-start.6 = (bf16[528,128]{1,0:T(8,128)(2,1)S(1)}, bf16[528,128]{1,0:T(8,128)(2,1)S(1)}, u32[]{:S(2)}, u32[]{:S(2)}) collective-permute-start(bf16[528,128]{1,0:T(8,128)(2,1)S(1)} %collective-permute-done.5.refs_1_), channel_id=1, source_target_pairs={{0,32},{32,0},{64,96},{96,64},{128,160},{160,128},{192,224},{224,1... | collective-permute-start | bytes 405512 | tf_op jit(solution)/shard_map/ppermute | solution.py:411
  74.6 2.5 %collective-permute-done.7.refs_2_ = bf16[528,128]{1,0:T(8,128)(2,1)S(1)} collective-permute-done((bf16[528,128]{1,0:T(8,128)(2,1)S(1)}, bf16[528,128]{1,0:T(8,128)(2,1)S(1)}, u32[]{:S(2)}, u32[]{:S(2)}) %collective-permute-start.7) | collective-permute-done | bytes 135200 | tf_op jit(solution)/shard_map/ppermute | solution.py:410
  77.1 1.0 %collective-permute-start.8 = (bf16[528,128]{1,0:T(8,128)(2,1)S(1)}, bf16[528,128]{1,0:T(8,128)(2,1)S(1)}, u32[]{:S(2)}, u32[]{:S(2)}) collective-permute-start(bf16[528,128]{1,0:T(8,128)(2,1)S(1)} %collective-permute-done.7.refs_2_), channel_id=1, source_target_pairs={{0,32},{32,0},{64,96},{96,64},{128,160},{160,128},{192,224},{224,1... | collective-permute-start | bytes 405512 | tf_op jit(solution)/shard_map/ppermute | solution.py:411
  78.2 0.0 collective-permute-done.9.refs_3_
  78.2 0.0 collective-permute-start.10
  78.2 0.0 copy-done.2
  78.2 1.7 %own_image.1 = (f32[512,512]{1,0:T(8,128)S(1)}, f32[2,512]{1,0:T(2,128)}) custom-call(bf16[528,128]{1,0:T(8,128)(2,1)S(1)} %get-tuple-element.28.refs_0_, bf16[528,128]{1,0:T(8,128)(2,1)S(1)} %collective-permute-done.5.refs_1_, bf16[528,128]{1,0:T(8,128)(2,1)S(1)} %collective-permute-done.7.refs_2_, bf16[528,128]{1,0:T(8,128)(2,1)S(1)} %collective-permute-done.9.refs_3_, ...), custom_call_target="tpu_custom_call" | custom-call | flops 1000000000 | bytes 1048576 | tf_op jit(solution)/shard_map/own_image/pallas_call | solution.py:414
  79.9 0.0 collective-permute-done.6.refs_1_
  79.9 0.0 collective-permute-done.8.refs_2_
  79.9 0.0 collective-permute-done.10.refs_3_
  79.9 2.0 %image.1 = f32[512,512]{1,0:T(8,128)} custom-call(bf16[512,128]{1,0:T(8,128)(2,1)S(1)} %get-tuple-element.24.refs_0_, bf16[528,128]{1,0:T(8,128)(2,1)S(1)} %collective-permute-done.6.refs_1_, bf16[528,128]{1,0:T(8,128)(2,1)S(1)} %collective-permute-done.8.refs_2_, bf16[528,128]{1,0:T(8,128)(2,1)S(1)} %collective-permute-done.10.refs_3_, ...), custom_call_target="tpu_custom_call" | custom-call | flops 1000000000 | bytes 1048576 | tf_op jit(solution)/shard_map/image/pallas_call | solution.py:418
Async XLA Ops:
  0.6 6.9 %copy-start.4 = (s32[2]{0:T(128)S(1)}, s32[2]{0:T(128)}, u32[]{:S(2)}) copy-start(s32[2]{0:T(128)} %offsets_row.1) | copy-start | bytes 28
  4.2 5.1 %copy-start.5 = (bf16[528,512]{1,0:T(8,128)(2,1)S(1)}, bf16[528,512]{1,0:T(8,128)(2,1)}, u32[]{:S(2)}) copy-start(bf16[528,512]{1,0:T(8,128)(2,1)} %get-tuple-element.17.own) | copy-start | bytes 1622020
  4.2 5.1 %collective-permute-start = (bf16[528,512]{1,0:T(8,128)(2,1)}, bf16[528,512]{1,0:T(8,128)(2,1)S(1)}, u32[]{:S(2)}, u32[]{:S(2)}) collective-permute-start(bf16[528,512]{1,0:T(8,128)(2,1)} %get-tuple-element.18), channel_id=1, source_target_pairs={{0,32},{32,0},{64,96},{96,64},{128,160},{160,128},{192,224},{224,1... | collective-permute-start | bytes 1622024 | tf_op jit(solution)/shard_map/ppermute | solution.py:373
  10.6 7.1 %collective-permute-start.1 = (bf16[576,128]{1,0:T(8,128)(2,1)S(1)}, bf16[576,128]{1,0:T(8,128)(2,1)S(1)}, u32[]{:S(2)}, u32[]{:S(2)}) collective-permute-start(bf16[576,128]{1,0:T(8,128)(2,1)S(1)} %get-tuple-element.20), channel_id=1, source_target_pairs={{0,64},{32,96},{64,128},{96,160},{128,192},{160,224},{192,0},{224,... | collective-permute-start | bytes 442376 | tf_op jit(solution)/shard_map/ppermute | solution.py:382
  10.7 8.7 %collective-permute-start.2 = (bf16[576,128]{1,0:T(8,128)(2,1)S(1)}, bf16[576,128]{1,0:T(8,128)(2,1)S(1)}, u32[]{:S(2)}, u32[]{:S(2)}) collective-permute-start(bf16[576,128]{1,0:T(8,128)(2,1)S(1)} %get-tuple-element.21), channel_id=1, source_target_pairs={{0,128},{32,160},{64,192},{96,224},{128,0},{160,32},{192,64},{224,... | collective-permute-start | bytes 442376 | tf_op jit(solution)/shard_map/ppermute | solution.py:382
  12.6 7.8 %collective-permute-start.3 = (bf16[576,128]{1,0:T(8,128)(2,1)S(1)}, bf16[576,128]{1,0:T(8,128)(2,1)S(1)}, u32[]{:S(2)}, u32[]{:S(2)}) collective-permute-start(bf16[576,128]{1,0:T(8,128)(2,1)S(1)} %get-tuple-element.22), channel_id=1, source_target_pairs={{0,192},{32,224},{64,0},{96,32},{128,64},{160,96},{192,128},{224,1... | collective-permute-start | bytes 442376 | tf_op jit(solution)/shard_map/ppermute | solution.py:382
  20.4 43.8 %copy-start.3 = (s32[2]{0:T(128)S(1)}, s32[2]{0:T(128)}, u32[]{:S(2)}) copy-start(s32[2]{0:T(128)} %offsets_col.1) | copy-start | bytes 28
  43.6 22.0 %copy-start = (bf16[512,512]{1,0:T(8,128)(2,1)S(1)}, bf16[512,512]{1,0:T(8,128)(2,1)}, u32[]{:S(2)}) copy-start(bf16[512,512]{1,0:T(8,128)(2,1)} %constant.5.clone.refs_5_.refs_6_) | copy-start | bytes 1572868
  43.6 22.0 %copy-start.1 = (bf16[512,512]{1,0:T(8,128)(2,1)S(1)}, bf16[512,512]{1,0:T(8,128)(2,1)}, u32[]{:S(2)}) copy-start(bf16[512,512]{1,0:T(8,128)(2,1)} %constant.4.clone.refs_4_.refs_7_) | copy-start | bytes 1572868
  59.7 5.9 %collective-permute-start.4 = (bf16[32,40,128]{2,1,0:T(8,128)(2,1)S(1)}, bf16[32,40,128]{2,1,0:T(8,128)(2,1)S(1)}, u32[]{:S(2)}, u32[]{:S(2)}) collective-permute-start(bf16[32,40,128]{2,1,0:T(8,128)(2,1)S(1)} %all_to_all.11.own), channel_id=1, source_target_pairs={{0,32},{32,0},{64,96},{96,64},{128,160},{160,128},{192,224},{224,1... | collective-permute-start | bytes 983048 | tf_op jit(solution)/shard_map/ppermute | solution.py:391
  65.6 12.5 %copy-start.2 = (f32[2,512]{1,0:T(2,128)S(1)}, f32[2,512]{1,0:T(2,128)}, u32[]{:S(2)}) copy-start(f32[2,512]{1,0:T(2,128)} %refs_6_.2) | copy-start | bytes 12292
  67.3 6.3 %collective-permute-start.5 = (bf16[528,128]{1,0:T(8,128)(2,1)S(1)}, bf16[528,128]{1,0:T(8,128)(2,1)S(1)}, u32[]{:S(2)}, u32[]{:S(2)}) collective-permute-start(bf16[528,128]{1,0:T(8,128)(2,1)S(1)} %get-tuple-element.25), channel_id=1, source_target_pairs={{0,64},{32,96},{64,128},{96,160},{128,192},{160,224},{192,0},{224,... | collective-permute-start | bytes 405512 | tf_op jit(solution)/shard_map/ppermute | solution.py:410
  68.5 8.7 %collective-permute-start.7 = (bf16[528,128]{1,0:T(8,128)(2,1)S(1)}, bf16[528,128]{1,0:T(8,128)(2,1)S(1)}, u32[]{:S(2)}, u32[]{:S(2)}) collective-permute-start(bf16[528,128]{1,0:T(8,128)(2,1)S(1)} %get-tuple-element.26), channel_id=1, source_target_pairs={{0,128},{32,160},{64,192},{96,224},{128,0},{160,32},{192,64},{224,... | collective-permute-start | bytes 405512 | tf_op jit(solution)/shard_map/ppermute | solution.py:410
  70.7 7.4 %collective-permute-start.9 = (bf16[528,128]{1,0:T(8,128)(2,1)S(1)}, bf16[528,128]{1,0:T(8,128)(2,1)S(1)}, u32[]{:S(2)}, u32[]{:S(2)}) collective-permute-start(bf16[528,128]{1,0:T(8,128)(2,1)S(1)} %get-tuple-element.27), channel_id=1, source_target_pairs={{0,192},{32,224},{64,0},{96,32},{128,64},{160,96},{192,128},{224,1... | collective-permute-start | bytes 405512 | tf_op jit(solution)/shard_map/ppermute | solution.py:410
  73.6 6.2 %collective-permute-start.6 = (bf16[528,128]{1,0:T(8,128)(2,1)S(1)}, bf16[528,128]{1,0:T(8,128)(2,1)S(1)}, u32[]{:S(2)}, u32[]{:S(2)}) collective-permute-start(bf16[528,128]{1,0:T(8,128)(2,1)S(1)} %collective-permute-done.5.refs_1_), channel_id=1, source_target_pairs={{0,32},{32,0},{64,96},{96,64},{128,160},{160,128},{192,224},{224,1... | collective-permute-start | bytes 405512 | tf_op jit(solution)/shard_map/ppermute | solution.py:411
  77.1 2.7 %collective-permute-start.8 = (bf16[528,128]{1,0:T(8,128)(2,1)S(1)}, bf16[528,128]{1,0:T(8,128)(2,1)S(1)}, u32[]{:S(2)}, u32[]{:S(2)}) collective-permute-start(bf16[528,128]{1,0:T(8,128)(2,1)S(1)} %collective-permute-done.7.refs_2_), channel_id=1, source_target_pairs={{0,32},{32,0},{64,96},{96,64},{128,160},{160,128},{192,224},{224,1... | collective-permute-start | bytes 405512 | tf_op jit(solution)/shard_map/ppermute | solution.py:411
  78.2 1.7 %collective-permute-start.10 = (bf16[528,128]{1,0:T(8,128)(2,1)S(1)}, bf16[528,128]{1,0:T(8,128)(2,1)S(1)}, u32[]{:S(2)}, u32[]{:S(2)}) collective-permute-start(bf16[528,128]{1,0:T(8,128)(2,1)S(1)} %collective-permute-done.9.refs_3_), channel_id=1, source_target_pairs={{0,32},{32,0},{64,96},{96,64},{128,160},{160,128},{192,224},{224,1... | collective-permute-start | bytes 405512 | tf_op jit(solution)/shard_map/ppermute | solution.py:411

commit v7 on v6

--- a/solution.py
+++ b/solution.py
@@ -53,7 +53,27 @@
     return lax.axis_index("frow"), lax.axis_index("fcol")
 
 
-def columns_kernel(cols_count, offsets, facet, subgrid, u, v, observed, own, send, col_tab, image, indices, seen, sems):
+def half_columns(cols_count, offsets, half, side, col_tab):
+    bf16 = jnp.bfloat16
+    col_index = place()[1]
+    unit = sublanes(16)
+    col_step = SKY // (cols_count * side)
+    col_base = col_index * (SKY // cols_count)
+    freq = [offsets[c] + half * HALF + lanes(HALF) for c in range(NC)]
+    freq = jnp.concatenate(freq, 1)
+    coarse = wave((col_base + 16 * col_step * sublanes(side // 16)) * freq)
+    fine = wave((col_step * unit) * freq)
+
+    def store(at, cos, sin):
+        for c in range(NC):
+            some = slice(c * HALF, (c + 1) * HALF)
+            col_tab[at:at + 16, 2 * c * HALF:(2 * c + 1) * HALF] = cos[:, some].astype(bf16)
+            col_tab[at:at + 16, (2 * c + 1) * HALF:(2 * c + 2) * HALF] = sin[:, some].astype(bf16)
+
+    spread(coarse, fine, store)
+
+
+def send_columns_kernel(cols_count, offsets, facet, subgrid, u, v, observed, send, vis, col_tab, image, indices, seen, sems):
     f32, bf16 = jnp.float32, jnp.bfloat16
     side = facet.shape[0]
     copies = [
@@ -65,33 +85,20 @@
     ]
     for copy in copies:
         copy.start()
-    row_index, col_index = place()
-    core = row_index % 2
-    unit = sublanes(16)
-    col_step = SKY // (cols_count * side)
-    col_base = col_index * (SKY // cols_count)
-    for c in range(NC):
-        freq = offsets[c] + lanes(SG)
-        coarse = wave((col_base + 16 * col_step * sublanes(side // 16)) * freq)
-        fine = wave((col_step * unit) * freq)
-
-        def store(at, cos, sin, c=c):
-            for h in range(2):
-                half = slice(h * HALF, (h + 1) * HALF)
-                left = (2 * h + c) * SG
-                col_tab[at:at + 16, left:left + HALF] = cos[:, half].astype(bf16)
-                col_tab[at:at + 16, left + HALF:left + SG] = sin[:, half].astype(bf16)
-
-        spread(coarse, fine, store)
+    half_columns(cols_count, offsets, 1 - place()[0] % 2, side, col_tab)
     for copy in copies:
         copy.wait()
-    vis = jnp.concatenate([indices[n].astype(f32) for n in range(3)] + [seen[...], jnp.zeros((3, side), f32)], 0)
-    vis = jnp.concatenate([vis[:, :side // 2], vis[:, side // 2:]], 0).astype(bf16)
-    for out, half in ((send, 1 - core), (own, core)):
-        tab = col_tab[:, pl.ds(pl.multiple_of(half * 2 * SG, 2 * SG), 2 * SG)]
-        out[:side] = jnp.dot(image[...], tab, preferred_element_type=f32).astype(bf16)
-        out[side:, :side // 2] = vis
-        out[side:, side // 2:] = vis
+    some = jnp.concatenate([indices[n].astype(f32) for n in range(3)] + [seen[...], jnp.zeros((3, side), f32)], 0)
+    some = jnp.concatenate([some[:, :side // 2], some[:, side // 2:]], 0).astype(bf16)
+    vis[...] = some
+    send[side:, :side // 2] = some
+    send[side:, side // 2:] = some
+    send[:side] = jnp.dot(image[...], col_tab[...], preferred_element_type=f32).astype(bf16)
+
+
+def own_columns_kernel(cols_count, offsets, facet, own, col_tab):
+    half_columns(cols_count, offsets, place()[0] % 2, facet.shape[0], col_tab)
+    own[...] = jnp.dot(facet[...], col_tab[...], preferred_element_type=jnp.float32).astype(jnp.bfloat16)
 
 
 def row_tables_kernel(rows_count, side, offsets, row_tab):
@@ -112,15 +119,15 @@
             spread(coarse, fine, store)
 
 
-def contributions_kernel(scale, own, other, row_tab, *refs):
+def contributions_kernel(scale, own, own_vis, other, row_tab, *refs):
     f32, bf16 = jnp.float32, jnp.bfloat16
     outs, right = refs[:-1], refs[-1]
     chip = place()[0] // 2
     side = row_tab.shape[2] // 2
     vis = []
-    for f, half in enumerate((own, other)):
-        right[f * side:(f + 1) * side] = half[:side]
-        some = half[side:]
+    right[:side] = own[...]
+    right[side:] = other[:side]
+    for some in (own_vis[...], other[side:]):
         vis += [some[:, k * LANES:(k + 1) * LANES] for k in range(side // 2 // LANES)]
     for n, out in enumerate(outs):
         for k, some in enumerate(vis):
@@ -266,28 +273,26 @@
         spread(coarse, fine, store)
 
 
-def half_image(blocks, half, row_tab, col_tab, right, both):
-    f32, bf16 = jnp.float32, jnp.bfloat16
+def block_part(block, number, row_tab):
+    r, _ = split_number(number)
+    real, imag = block[:SG], block[SG:2 * SG]
+    right = jnp.concatenate([jnp.concatenate([real, imag], 1), jnp.concatenate([-imag, real], 1)], 0)
+    left = row_tab[:, pl.ds(pl.multiple_of(2 * r * SG, 2 * SG), 2 * SG)]
+    return jnp.dot(left, right, preferred_element_type=jnp.float32)
+
+
+def first_part_kernel(number, own, rest, row_tab, out):
     chip = place()[0] // 2
-    for k, block in enumerate(blocks):
-        r, c = split_number(chip + len(blocks) - k)
-        real, imag = block[:SG], block[SG:2 * SG]
-        top = [pl.ds(pl.multiple_of((2 * r + n) * SG, SG), SG) for n in range(2)]
-        at = [pl.ds(pl.multiple_of((2 * c + n) * HALF, HALF), HALF) for n in range(2)]
-        right[top[0], at[0]] = real
-        right[top[0], at[1]] = imag
-        right[top[1], at[0]] = -imag
-        right[top[1], at[1]] = real
-    both[...] = jnp.dot(row_tab[...], right[...], preferred_element_type=f32).astype(bf16)
-    depth = 2 * NC * HALF
-    rows = pl.ds(pl.multiple_of(half * depth, depth), depth)
-    return lambda at: jnp.dot(both[at], col_tab[rows], preferred_element_type=f32)
-
-
-def own_image_kernel(*refs):
-    blocks, (row_tab, col_tab, observed, out, residual, right, both) = refs[:-7], refs[-7:]
-    f32 = jnp.float32
+    for half, block in enumerate((own, rest)):
+        out[:, half * SG:(half + 1) * SG] = block_part(block, chip + number, row_tab)
+
+
+def image_kernel(scale, chips, *refs):
+    f32, bf16 = jnp.float32, jnp.bfloat16
+    blocks, others, firsts, refs = refs[:chips], refs[chips:chips + 2], refs[chips + 2:chips + 4], refs[chips + 4:]
+    row_tab, col_tab, observed, out, residual, both, image, seen, sems = refs
     row_index, _ = place()
+    core, chip = row_index % 2, row_index // 2
     model = jnp.zeros((16, LANES), f32)
     for block in blocks:
         model = model + block[2 * SG:].astype(f32)
@@ -295,22 +300,22 @@
     for part in range(2):
         for i in range(count):
             at = slice(i * LANES, (i + 1) * LANES)
-            residual[part:part + 1, at] = observed[part:part + 1, at] - model[part * count + i:part * count + i + 1]
-    part = half_image(blocks, row_index % 2, row_tab, col_tab, right, both)
-    out[...] = part(slice(0, out.shape[0]))
-
-
-def image_kernel(scale, *refs):
-    blocks, (first, row_tab, col_tab, out, right, both, image, sems) = refs[:-8], refs[-8:]
-    row_index, _ = place()
-    part = half_image(blocks, 1 - row_index % 2, row_tab, col_tab, right, both)
-    chunks = sems.shape[0]
+            seen[part:part + 1, at] = observed[part:part + 1, at] - model[part * count + i:part * count + i + 1]
+    writes = [pltpu.make_async_copy(seen, residual, sems.at[0])]
+    writes[0].start()
+    for k in range(2, chips):
+        c = split_number(chip + chips - k)[1]
+        for n, block in enumerate((blocks[k], others[k - 2])):
+            half = core if n == 0 else 1 - core
+            at = pl.ds(pl.multiple_of((half * NC + c) * SG, SG), SG)
+            part = firsts[k - 2][:, n * SG:(n + 1) * SG] + block_part(block, chip + chips - k, row_tab)
+            both[:, at] = part.astype(bf16)
+    chunks = sems.shape[0] - 1
     step = image.shape[0] // chunks
-    writes = []
     for n in range(chunks):
         at = slice(n * step, (n + 1) * step)
-        image[at] = (first[at] + part(at)) * scale
-        write = pltpu.make_async_copy(image.at[at], out.at[at], sems.at[n])
+        image[at] = jnp.dot(both[at], col_tab[...], preferred_element_type=f32) * scale
+        write = pltpu.make_async_copy(image.at[at], out.at[at], sems.at[1 + n])
         write.start()
         writes.append(write)
     for write in writes:
@@ -357,29 +362,38 @@
     each = SG // cols_count
     swap = [(index, index ^ 1) for index in range(rows_count)]
     turns = [[(index, (index + 2 * k) % rows_count) for index in range(rows_count)] for k in range(chips)]
+
+    def turned(blocks):
+        moved = {k: lax.ppermute(blocks[k], "frow", turns[k]) for k in (2, 1, 3)}
+        return [blocks[0]] + [moved[k] for k in range(1, chips)]
+
     scale_in = 1.0 / (side * math.sqrt(rows_count * cols_count))
     scale_out = 1.0 / (SG * math.sqrt(NR * NC))
     line = (1, n_vis)
 
-    half_shape = shape(side + 16, 4 * HALF)
-    own, send = call(
-        functools.partial(columns_kernel, cols_count), (half_shape, half_shape), "columns", "saaaaa",
+    send, vis = call(
+        functools.partial(send_columns_kernel, cols_count), (shape(side + 16, 4 * HALF), shape(16, n_vis // 2)),
+        "send_columns", "saaaaa",
         scratch=[
-            pltpu.VMEM((side, 8 * HALF), bf16), pltpu.VMEM((side, side), bf16), pltpu.VMEM((3,) + line, jnp.int32),
+            pltpu.VMEM((side, 4 * HALF), bf16), pltpu.VMEM((side, side), bf16), pltpu.VMEM((3,) + line, jnp.int32),
             pltpu.VMEM((2, n_vis), f32), pltpu.SemaphoreType.DMA((5,)),
         ],
         cost=10**9, room=60,
     )(col_offsets, facet, vis_subgrid.reshape(line), vis_u.reshape(line), vis_v.reshape(line), observed)
     other = lax.ppermute(send, "frow", swap)
+    own = call(
+        functools.partial(own_columns_kernel, cols_count), shape(side, 4 * HALF), "own_columns", "sv",
+        scratch=[pltpu.VMEM((side, 4 * HALF), bf16)], cost=10**9,
+    )(col_offsets, facet)
     row_tab = call(
         functools.partial(row_tables_kernel, rows_count, side), shape(4, SG, 2 * side), "row_tables", "s", cost=10**9
     )(row_offsets)
     vis_rows_count = 8 * 2 * n_vis // LANES
     parts = call(
         functools.partial(contributions_kernel, scale_in), (shape(2 * SG + vis_rows_count, HALF),) * chips,
-        "contributions", "vvv", scratch=[pltpu.VMEM((2 * side, 4 * HALF), bf16)], cost=2 * 10**9,
-    )(own, other, row_tab)
-    parts = [parts[0]] + [lax.ppermute(parts[k], "frow", turns[k]) for k in range(1, chips)]
+        "contributions", "vvvv", scratch=[pltpu.VMEM((2 * side, 4 * HALF), bf16)], cost=2 * 10**9,
+    )(own, vis, other, row_tab)
+    parts = turned(parts)
 
     pieces = call(
         gridding_kernel, shape(cols_count, 5 * each, HALF), "gridding", "v" * chips,
@@ -407,19 +421,25 @@
         ],
         cost=10**9,
     )(pieces, pieces_other, *parts, inverse_block, forward_block, forward_block, inverse_block, back_col)
-    back = [back[0]] + [lax.ppermute(back[k], "frow", turns[k]) for k in range(1, chips)]
-    back_other = [rest] + [lax.ppermute(back[k], "frow", swap) for k in range(1, chips)]
-
-    work = [pltpu.VMEM((4 * SG, 2 * SG), bf16), pltpu.VMEM((side, 2 * SG), bf16)]
-    first, residual = call(
-        own_image_kernel, (shape(side, side, dtype=f32), shape(2, n_vis, dtype=f32)), "own_image", "vvv" + "v" * chips,
-        scratch=work, cost=10**9,
-    )(*back, back_row, back_col, observed)
-    image = call(
-        functools.partial(image_kernel, scale_out), shape(side, side, dtype=f32), "image", "vvv" + "v" * chips, outs="a",
-        scratch=work + [pltpu.VMEM((side, side), f32), pltpu.SemaphoreType.DMA((4,))], cost=10**9,
-    )(*back_other, first, back_row, back_col)
-    return (image, residual)
+    back = turned(back)
+
+    def first_part(number, mine, other):
+        kernel = functools.partial(first_part_kernel, number)
+        return call(kernel, shape(side, 2 * SG, dtype=f32), "first_part", "vvv", cost=10**9)(mine, other, back_row)
+
+    firsts = [first_part(chips, back[0], rest)]
+    back[1], firsts[0] = lax.optimization_barrier((back[1], firsts[0]))
+    rest = [lax.ppermute(block, "frow", swap) for block in back[1:]]
+    firsts.append(first_part(chips - 1, back[1], rest[0]))
+    return call(
+        functools.partial(image_kernel, scale_out, chips),
+        (shape(side, side, dtype=f32), shape(2, n_vis, dtype=f32)), "image", "v" * (chips + 7), outs="aa",
+        scratch=[
+            pltpu.VMEM((side, 4 * SG), bf16), pltpu.VMEM((side, side), f32), pltpu.VMEM((2, n_vis), f32),
+            pltpu.SemaphoreType.DMA((5,)),
+        ],
+        cost=10**9,
+    )(*back, *rest[1:], *firsts, back_row, back_col, observed)
 
 
 def solution(mesh):

time: 82.2 us -> 82.8 us (level)
    pallas_call x3 -> x5, Pallas kernels: 7.17 us -> 7.38 us  [the longest x1 3.13 us: shards(): call(functools.partial(send_columns_kernel, cols_count), (shape(side + 16...]
  transfers between devices with their start and end apart: 11 -> 11, of which waited for: 6 -> 6; matrix products, arithmetic and copies ran while one was open for 0% -> 0% of each run, Pallas kernels for 5% -> 6%
where the time goes in v7:
time: 82.8 us; the launch traced here: 82.6 us
  blocking collectives  38.4 us (46%)
  starting transfers between devices  16.9 us (20%)
  Pallas kernels  14.5 us (18%)
  waiting for transfers between devices  11.9 us (14%)
  between operations  0.97 us (1%)
    all_to_all x2, blocking collectives, exchange(): lax.all_to_all(blocks, axes, 0, 0, tiled=True, axis_index_groups=groups)  38.4 us
    ppermute x6, waiting for transfers between devices, turned(): moved = {k: lax.ppermute(blocks[k], 'frow', turns[k]) for k in (2, 1, 3)}  11 us
    ppermute x6, starting transfers between devices, turned(): moved = {k: lax.ppermute(blocks[k], 'frow', turns[k]) for k in (2, 1, 3)}  7.29 us
    ppermute x1, starting transfers between devices, shards(): pieces_other = lax.ppermute(pieces, 'frow', swap)  4.08 us
    ppermute x1, starting transfers between devices, shards(): other = lax.ppermute(send, 'frow', swap)  3.33 us
    pallas_call x1, Pallas kernels, shards(): call(functools.partial(send_columns_kernel, cols_count), (shape(side + 16...  3.13 us
    pallas_call x1, Pallas kernels, shards(): call(functools.partial(image_kernel, scale_out, chips), (shape(side, side...  2.29 us
    ppermute x3, starting transfers between devices, shards(): rest = [lax.ppermute(block, 'frow', swap) for block in back[1:]]  2.2 us
  transfers between devices with their start and end apart: 11, of which 6 were waited for; matrix products, arithmetic and copies ran while one was open for 0% of the time, Pallas kernels for 6%

profile of v7, /device:TPU:1, one launch (start us, length us, event | category | flops | bytes accessed | tf_op | source)
XLA Modules:
  0.0 82.6 jit_solution(16464452910887648031)
XLA Ops:
  0.6 0.0 copy-start.4
  0.6 0.0 copy-start.3
  0.7 3.1 %send_columns.1 = (bf16[528,512]{1,0:T(8,128)(2,1)}, bf16[16,256]{1,0:T(8,128)(2,1)}) custom-call(s32[2]{0:T(128)} %offsets_col.1, bf16[512,512]{1,0:T(8,128)(2,1)} %facet.3, s32[1,512]{1,0:T(1,128)} %bitcast.3, s32[1,512]{1,0:T(1,128)} %bitcast.4, s32[1,512]{1,0:T(1,128)} %bitcast.5, f32[2,512]{1,0:T(2,128)} %refs_10_.1), custom_call_target="tpu_custom_call" | custom-call | flops 1000000000 | bytes 1048576 | tf_op jit(solution)/shard_map/send_columns/pallas_call | solution.py:374
  3.8 0.0 copy-start.5
  3.8 3.3 %collective-permute-start = (bf16[528,512]{1,0:T(8,128)(2,1)}, bf16[528,512]{1,0:T(8,128)(2,1)S(1)}, u32[]{:S(2)}, u32[]{:S(2)}) collective-permute-start(bf16[528,512]{1,0:T(8,128)(2,1)} %get-tuple-element.18), channel_id=1, source_target_pairs={{0,32},{32,0},{64,96},{96,64},{128,160},{160,128},{192,224},{224,1... | collective-permute-start | bytes 1622024 | tf_op jit(solution)/shard_map/ppermute | solution.py:383
  7.1 0.0 copy-done.4
  7.1 0.0 copy-done.3
  7.1 1.1 %own_columns.1.own = bf16[512,512]{1,0:T(8,128)(2,1)S(1)} custom-call(s32[2]{0:T(128)S(1)} %copy-done.4, bf16[512,512]{1,0:T(8,128)(2,1)S(1)} %copy-done.3), custom_call_target="tpu_custom_call" | custom-call | flops 1000000000 | bytes 1048576 | tf_op jit(solution)/shard_map/own_columns/pallas_call | solution.py:384
  8.2 0.0 copy-done.5
  8.2 0.0 copy-start.6
  8.2 1.3 %row_tables.1.row_tab = bf16[4,256,1024]{2,1,0:T(8,128)(2,1)S(1)} custom-call(s32[2]{0:T(128)S(1)} %copy-done.5), custom_call_target="tpu_custom_call" | custom-call | flops 1000000000 | bytes 1048576 | tf_op jit(solution)/shard_map/row_tables/pallas_call | solution.py:388
  9.6 0.0 collective-permute-done.other
  9.6 0.0 copy-done.6
  9.6 1.3 %contributions.1 = (bf16[576,128]{1,0:T(8,128)(2,1)S(1)}, bf16[576,128]{1,0:T(8,128)(2,1)S(1)}, bf16[576,128]{1,0:T(8,128)(2,1)S(1)}, bf16[576,128]{1,0:T(8,128)(2,1)S(1)}) custom-call(bf16[512,512]{1,0:T(8,128)(2,1)S(1)} %own_columns.1.own, bf16[16,256]{1,0:T(8,128)(2,1)S(1)} %copy-done.6, bf16[528,512]{1,0:T(8,128)(2,1)S(1)} %collective-permute-done.other, ...), custom_call_target="tpu_custom_call" | custom-call | flops 2000000000 | bytes 1048576 | tf_op jit(solution)/shard_map/contributions/pallas_call | solution.py:392
  11.0 0.1 collective-permute-start.1
  11.0 1.9 %collective-permute-start.2 = (bf16[576,128]{1,0:T(8,128)(2,1)S(1)}, bf16[576,128]{1,0:T(8,128)(2,1)S(1)}, u32[]{:S(2)}, u32[]{:S(2)}) collective-permute-start(bf16[576,128]{1,0:T(8,128)(2,1)S(1)} %get-tuple-element.21), channel_id=1, source_target_pairs={{0,128},{32,160},{64,192},{96,224},{128,0},{160,32},{192,64},{224,... | collective-permute-start | bytes 442376 | tf_op jit(solution)/shard_map/ppermute | solution.py:367
  13.0 1.2 %collective-permute-start.3 = (bf16[576,128]{1,0:T(8,128)(2,1)S(1)}, bf16[576,128]{1,0:T(8,128)(2,1)S(1)}, u32[]{:S(2)}, u32[]{:S(2)}) collective-permute-start(bf16[576,128]{1,0:T(8,128)(2,1)S(1)} %get-tuple-element.22), channel_id=1, source_target_pairs={{0,192},{32,224},{64,0},{96,32},{128,64},{160,96},{192,128},{224,1... | collective-permute-start | bytes 442376 | tf_op jit(solution)/shard_map/ppermute | solution.py:367
  14.1 6.7 %collective-permute-done.1.refs_1_ = bf16[576,128]{1,0:T(8,128)(2,1)S(1)} collective-permute-done((bf16[576,128]{1,0:T(8,128)(2,1)S(1)}, bf16[576,128]{1,0:T(8,128)(2,1)S(1)}, u32[]{:S(2)}, u32[]{:S(2)}) %collective-permute-start.1) | collective-permute-done | bytes 147488 | tf_op jit(solution)/shard_map/ppermute | solution.py:367
  20.9 0.0 collective-permute-done.2.refs_2_
  20.9 0.3 collective-permute-done.3.refs_3_
  21.2 1.3 %gridding.1 = bf16[32,40,128]{2,1,0:T(8,128)(2,1)S(1)} custom-call(bf16[576,128]{1,0:T(8,128)(2,1)S(1)} %get-tuple-element.19.refs_0_, bf16[576,128]{1,0:T(8,128)(2,1)S(1)} %collective-permute-done.1.refs_1_, bf16[576,128]{1,0:T(8,128)(2,1)S(1)} %collective-permute-done.2.refs_2_, bf16[576,128]{1,0:T(8,128)(2,1)S(1)} %collective-permute-done.3.refs_3_), custom_call_target="tpu_custom_call" | custom-call | flops 1000000000 | bytes 1048576 | tf_op jit(solution)/shard_map/gridding/pallas_call | solution.py:398
  22.4 22.6 %all_to_all.10.pieces = bf16[32,40,128]{2,1,0:T(8,128)(2,1)S(1)} all-to-all(bf16[32,40,128]{2,1,0:T(8,128)(2,1)S(1)} %gridding.1), channel_id=1, replica_groups=mesh['frow'=8,'fcol'=32] {'fcol'}, dimensions={0} | all-to-all | bytes 655360 | tf_op jit(solution)/shard_map/all_to_all | solution.py:349
  45.0 0.1 pieces_sum.1
  45.1 0.0 copy-start
  45.1 0.0 copy-start.1
  45.1 15.8 %all_to_all.11.own = bf16[32,40,128]{2,1,0:T(8,128)(2,1)S(1)} all-to-all(bf16[32,40,128]{2,1,0:T(8,128)(2,1)S(1)} %pieces_sum.1), channel_id=1, replica_groups=mesh['frow'=8,'fcol'=32] {'fcol'}, dimensions={0} | all-to-all | bytes 655360 | tf_op jit(solution)/shard_map/all_to_all | solution.py:349
  60.9 4.1 %collective-permute-start.4 = (bf16[32,40,128]{2,1,0:T(8,128)(2,1)S(1)}, bf16[32,40,128]{2,1,0:T(8,128)(2,1)S(1)}, u32[]{:S(2)}, u32[]{:S(2)}) collective-permute-start(bf16[32,40,128]{2,1,0:T(8,128)(2,1)S(1)} %all_to_all.11.own), channel_id=1, source_target_pairs={{0,32},{32,0},{64,96},{96,64},{128,160},{160,128},{192,224},{224,1... | collective-permute-start | bytes 983048 | tf_op jit(solution)/shard_map/ppermute | solution.py:405
  65.0 1.4 %back_tables.1 = (bf16[512,1024]{1,0:T(8,128)(2,1)S(1)}, bf16[1024,512]{1,0:T(8,128)(2,1)S(1)}) custom-call(s32[2]{0:T(128)S(1)} %copy-done.5, s32[2]{0:T(128)S(1)} %copy-done.4), custom_call_target="tpu_custom_call" | custom-call | flops 1000000000 | bytes 1048576 | tf_op jit(solution)/shard_map/back_tables/pallas_call | solution.py:407
  66.4 0.0 collective-permute-done.4.other
  66.4 0.0 copy-done
  66.4 1.7 %grids.1 = (bf16[528,128]{1,0:T(8,128)(2,1)S(1)}, bf16[528,128]{1,0:T(8,128)(2,1)S(1)}, bf16[528,128]{1,0:T(8,128)(2,1)S(1)}, bf16[528,128]{1,0:T(8,128)(2,1)S(1)}, bf16[512,128]{1,0:T(8,128)(2,1)S(1)}) custom-call(bf16[32,40,128]{2,1,0:T(8,128)(2,1)S(1)} %all_to_all.11.own, bf16[32,40,128]{2,1,0:T(8,128)(2,1)S(1)} %collective-permute-done.4.other, ...), custom_call_target="tpu_custom_call" | custom-call | flops 1000000000 | bytes 1048576 | tf_op jit(solution)/shard_map/grids/pallas_call | solution.py:415
  68.1 0.7 collective-permute-start.5
  68.9 2.5 %collective-permute-start.6 = (bf16[528,128]{1,0:T(8,128)(2,1)S(1)}, bf16[528,128]{1,0:T(8,128)(2,1)S(1)}, u32[]{:S(2)}, u32[]{:S(2)}) collective-permute-start(bf16[528,128]{1,0:T(8,128)(2,1)S(1)} %get-tuple-element.29), channel_id=1, source_target_pairs={{0,128},{32,160},{64,192},{96,224},{128,0},{160,32},{192,64},{224,... | collective-permute-start | bytes 405512 | tf_op jit(solution)/shard_map/ppermute | solution.py:367
  71.4 0.9 %collective-permute-start.7 = (bf16[528,128]{1,0:T(8,128)(2,1)S(1)}, bf16[528,128]{1,0:T(8,128)(2,1)S(1)}, u32[]{:S(2)}, u32[]{:S(2)}) collective-permute-start(bf16[528,128]{1,0:T(8,128)(2,1)S(1)} %get-tuple-element.30), channel_id=1, source_target_pairs={{0,192},{32,224},{64,0},{96,32},{128,64},{160,96},{192,128},{224,1... | collective-permute-start | bytes 405512 | tf_op jit(solution)/shard_map/ppermute | solution.py:367
  72.3 0.4 first_part.2.refs_6_
  72.7 0.0 copy-start.2
  72.7 1.7 %collective-permute-done.5.own.refs_1_ = bf16[528,128]{1,0:T(8,128)(2,1)S(1)} collective-permute-done((bf16[528,128]{1,0:T(8,128)(2,1)S(1)}, bf16[528,128]{1,0:T(8,128)(2,1)S(1)}, u32[]{:S(2)}, u32[]{:S(2)}) %collective-permute-start.5) | collective-permute-done | bytes 135200 | tf_op jit(solution)/shard_map/ppermute | solution.py:367
  74.4 1.1 %collective-permute-start.10 = (bf16[528,128]{1,0:T(8,128)(2,1)S(1)}, bf16[528,128]{1,0:T(8,128)(2,1)S(1)}, u32[]{:S(2)}, u32[]{:S(2)}) collective-permute-start(bf16[528,128]{1,0:T(8,128)(2,1)S(1)} %collective-permute-done.5.own.refs_1_), channel_id=1, source_target_pairs={{0,32},{32,0},{64,96},{96,64},{128,160},{160,128},{192,224},{224,1... | collective-permute-start | bytes 405512 | tf_op jit(solution)/shard_map/ppermute | solution.py:432
  75.5 2.3 %collective-permute-done.6.refs_2_ = bf16[528,128]{1,0:T(8,128)(2,1)S(1)} collective-permute-done((bf16[528,128]{1,0:T(8,128)(2,1)S(1)}, bf16[528,128]{1,0:T(8,128)(2,1)S(1)}, u32[]{:S(2)}, u32[]{:S(2)}) %collective-permute-start.6) | collective-permute-done | bytes 135200 | tf_op jit(solution)/shard_map/ppermute | solution.py:367
  77.8 1.0 %collective-permute-start.8 = (bf16[528,128]{1,0:T(8,128)(2,1)S(1)}, bf16[528,128]{1,0:T(8,128)(2,1)S(1)}, u32[]{:S(2)}, u32[]{:S(2)}) collective-permute-start(bf16[528,128]{1,0:T(8,128)(2,1)S(1)} %collective-permute-done.6.refs_2_), channel_id=1, source_target_pairs={{0,32},{32,0},{64,96},{96,64},{128,160},{160,128},{192,224},{224,1... | collective-permute-start | bytes 405512 | tf_op jit(solution)/shard_map/ppermute | solution.py:432
  78.8 0.0 collective-permute-done.7.refs_3_
  78.8 0.1 collective-permute-start.9
  78.9 0.0 collective-permute-done.10.rest
  78.9 0.4 first_part.3.refs_7_
  79.3 0.5 collective-permute-done.8.refs_4_
  79.8 0.4 collective-permute-done.9.refs_5_
  80.2 0.0 copy-done.2
  80.2 2.3 %image.1 = (f32[512,512]{1,0:T(8,128)}, f32[2,512]{1,0:T(2,128)}) custom-call(bf16[528,128]{1,0:T(8,128)(2,1)S(1)} %get-tuple-element.24.own.refs_0_, bf16[528,128]{1,0:T(8,128)(2,1)S(1)} %collective-permute-done.5.own.refs_1_, bf16[528,128]{1,0:T(8,128)(2,1)S(1)} %collective-permute-done.6.refs_2_, bf16[528,128]{1,0:T(8,128)(2,1)S(1)} %collective-permute-done.7.refs_3_, ...), custom_call_target="tpu_custom_call" | custom-call | flops 1000000000 | bytes 1048576 | tf_op jit(solution)/shard_map/image/pallas_call | solution.py:434
  (1 shorter events, 0.0 us)
Async XLA Ops:
  0.6 6.5 %copy-start.4 = (s32[2]{0:T(128)S(1)}, s32[2]{0:T(128)}, u32[]{:S(2)}) copy-start(s32[2]{0:T(128)} %offsets_col.1) | copy-start | bytes 28
  0.6 6.5 %copy-start.3 = (bf16[512,512]{1,0:T(8,128)(2,1)S(1)}, bf16[512,512]{1,0:T(8,128)(2,1)}, u32[]{:S(2)}) copy-start(bf16[512,512]{1,0:T(8,128)(2,1)} %facet.3) | copy-start | bytes 1572868
  3.8 4.4 %copy-start.5 = (s32[2]{0:T(128)S(1)}, s32[2]{0:T(128)}, u32[]{:S(2)}) copy-start(s32[2]{0:T(128)} %offsets_row.1) | copy-start | bytes 28
  3.8 5.8 %collective-permute-start = (bf16[528,512]{1,0:T(8,128)(2,1)}, bf16[528,512]{1,0:T(8,128)(2,1)S(1)}, u32[]{:S(2)}, u32[]{:S(2)}) collective-permute-start(bf16[528,512]{1,0:T(8,128)(2,1)} %get-tuple-element.18), channel_id=1, source_target_pairs={{0,32},{32,0},{64,96},{96,64},{128,160},{160,128},{192,224},{224,1... | collective-permute-start | bytes 1622024 | tf_op jit(solution)/shard_map/ppermute | solution.py:383
  8.2 1.4 %copy-start.6 = (bf16[16,256]{1,0:T(8,128)(2,1)S(1)}, bf16[16,256]{1,0:T(8,128)(2,1)}, u32[]{:S(2)}) copy-start(bf16[16,256]{1,0:T(8,128)(2,1)} %get-tuple-element.17.own_vis) | copy-start | bytes 24580
  11.0 9.9 %collective-permute-start.1 = (bf16[576,128]{1,0:T(8,128)(2,1)S(1)}, bf16[576,128]{1,0:T(8,128)(2,1)S(1)}, u32[]{:S(2)}, u32[]{:S(2)}) collective-permute-start(bf16[576,128]{1,0:T(8,128)(2,1)S(1)} %get-tuple-element.20), channel_id=1, source_target_pairs={{0,64},{32,96},{64,128},{96,160},{128,192},{160,224},{192,0},{224,... | collective-permute-start | bytes 442376 | tf_op jit(solution)/shard_map/ppermute | solution.py:367
  11.0 9.8 %collective-permute-start.2 = (bf16[576,128]{1,0:T(8,128)(2,1)S(1)}, bf16[576,128]{1,0:T(8,128)(2,1)S(1)}, u32[]{:S(2)}, u32[]{:S(2)}) collective-permute-start(bf16[576,128]{1,0:T(8,128)(2,1)S(1)} %get-tuple-element.21), channel_id=1, source_target_pairs={{0,128},{32,160},{64,192},{96,224},{128,0},{160,32},{192,64},{224,... | collective-permute-start | bytes 442376 | tf_op jit(solution)/shard_map/ppermute | solution.py:367
  13.0 8.2 %collective-permute-start.3 = (bf16[576,128]{1,0:T(8,128)(2,1)S(1)}, bf16[576,128]{1,0:T(8,128)(2,1)S(1)}, u32[]{:S(2)}, u32[]{:S(2)}) collective-permute-start(bf16[576,128]{1,0:T(8,128)(2,1)S(1)} %get-tuple-element.22), channel_id=1, source_target_pairs={{0,192},{32,224},{64,0},{96,32},{128,64},{160,96},{192,128},{224,1... | collective-permute-start | bytes 442376 | tf_op jit(solution)/shard_map/ppermute | solution.py:367
  45.1 21.3 %copy-start = (bf16[512,512]{1,0:T(8,128)(2,1)S(1)}, bf16[512,512]{1,0:T(8,128)(2,1)}, u32[]{:S(2)}) copy-start(bf16[512,512]{1,0:T(8,128)(2,1)} %constant.5.clone.refs_5_.refs_6_) | copy-start | bytes 1572868
  45.1 21.3 %copy-start.1 = (bf16[512,512]{1,0:T(8,128)(2,1)S(1)}, bf16[512,512]{1,0:T(8,128)(2,1)}, u32[]{:S(2)}) copy-start(bf16[512,512]{1,0:T(8,128)(2,1)} %constant.4.clone.refs_4_.refs_7_) | copy-start | bytes 1572868
  60.9 5.5 %collective-permute-start.4 = (bf16[32,40,128]{2,1,0:T(8,128)(2,1)S(1)}, bf16[32,40,128]{2,1,0:T(8,128)(2,1)S(1)}, u32[]{:S(2)}, u32[]{:S(2)}) collective-permute-start(bf16[32,40,128]{2,1,0:T(8,128)(2,1)S(1)} %all_to_all.11.own), channel_id=1, source_target_pairs={{0,32},{32,0},{64,96},{96,64},{128,160},{160,128},{192,224},{224,1... | collective-permute-start | bytes 983048 | tf_op jit(solution)/shard_map/ppermute | solution.py:405
  68.1 6.3 %collective-permute-start.5 = (bf16[528,128]{1,0:T(8,128)(2,1)S(1)}, bf16[528,128]{1,0:T(8,128)(2,1)S(1)}, u32[]{:S(2)}, u32[]{:S(2)}) collective-permute-start(bf16[528,128]{1,0:T(8,128)(2,1)S(1)} %get-tuple-element.25), channel_id=1, source_target_pairs={{0,64},{32,96},{64,128},{96,160},{128,192},{160,224},{192,0},{224,... | collective-permute-start | bytes 405512 | tf_op jit(solution)/shard_map/ppermute | solution.py:367
  68.9 8.9 %collective-permute-start.6 = (bf16[528,128]{1,0:T(8,128)(2,1)S(1)}, bf16[528,128]{1,0:T(8,128)(2,1)S(1)}, u32[]{:S(2)}, u32[]{:S(2)}) collective-permute-start(bf16[528,128]{1,0:T(8,128)(2,1)S(1)} %get-tuple-element.29), channel_id=1, source_target_pairs={{0,128},{32,160},{64,192},{96,224},{128,0},{160,32},{192,64},{224,... | collective-permute-start | bytes 405512 | tf_op jit(solution)/shard_map/ppermute | solution.py:367
  71.4 7.4 %collective-permute-start.7 = (bf16[528,128]{1,0:T(8,128)(2,1)S(1)}, bf16[528,128]{1,0:T(8,128)(2,1)S(1)}, u32[]{:S(2)}, u32[]{:S(2)}) collective-permute-start(bf16[528,128]{1,0:T(8,128)(2,1)S(1)} %get-tuple-element.30), channel_id=1, source_target_pairs={{0,192},{32,224},{64,0},{96,32},{128,64},{160,96},{192,128},{224,1... | collective-permute-start | bytes 405512 | tf_op jit(solution)/shard_map/ppermute | solution.py:367
  72.7 7.5 %copy-start.2 = (f32[2,512]{1,0:T(2,128)S(1)}, f32[2,512]{1,0:T(2,128)}, u32[]{:S(2)}) copy-start(f32[2,512]{1,0:T(2,128)} %refs_10_.1) | copy-start | bytes 12292
  74.4 4.5 %collective-permute-start.10 = (bf16[528,128]{1,0:T(8,128)(2,1)S(1)}, bf16[528,128]{1,0:T(8,128)(2,1)S(1)}, u32[]{:S(2)}, u32[]{:S(2)}) collective-permute-start(bf16[528,128]{1,0:T(8,128)(2,1)S(1)} %collective-permute-done.5.own.refs_1_), channel_id=1, source_target_pairs={{0,32},{32,0},{64,96},{96,64},{128,160},{160,128},{192,224},{224,1... | collective-permute-start | bytes 405512 | tf_op jit(solution)/shard_map/ppermute | solution.py:432
  77.8 2.0 %collective-permute-start.8 = (bf16[528,128]{1,0:T(8,128)(2,1)S(1)}, bf16[528,128]{1,0:T(8,128)(2,1)S(1)}, u32[]{:S(2)}, u32[]{:S(2)}) collective-permute-start(bf16[528,128]{1,0:T(8,128)(2,1)S(1)} %collective-permute-done.6.refs_2_), channel_id=1, source_target_pairs={{0,32},{32,0},{64,96},{96,64},{128,160},{160,128},{192,224},{224,1... | collective-permute-start | bytes 405512 | tf_op jit(solution)/shard_map/ppermute | solution.py:432
  78.8 1.4 %collective-permute-start.9 = (bf16[528,128]{1,0:T(8,128)(2,1)S(1)}, bf16[528,128]{1,0:T(8,128)(2,1)S(1)}, u32[]{:S(2)}, u32[]{:S(2)}) collective-permute-start(bf16[528,128]{1,0:T(8,128)(2,1)S(1)} %collective-permute-done.7.refs_3_), channel_id=1, source_target_pairs={{0,32},{32,0},{64,96},{96,64},{128,160},{160,128},{192,224},{224,1... | collective-permute-start | bytes 405512 | tf_op jit(solution)/shard_map/ppermute | solution.py:432

commit v8 on v7

--- a/solution.py
+++ b/solution.py
@@ -73,27 +73,40 @@
     spread(coarse, fine, store)
 
 
-def send_columns_kernel(cols_count, offsets, facet, subgrid, u, v, observed, send, vis, col_tab, image, indices, seen, sems):
+def send_columns_kernel(cols_count, offsets, facet, subgrid, u, v, observed, send, vis, *scratch):
+    col_tab, image, indices, seen, first, made, tail, sems = scratch
     f32, bf16 = jnp.float32, jnp.bfloat16
     side = facet.shape[0]
-    copies = [
-        pltpu.make_async_copy(facet, image, sems.at[0]),
-        pltpu.make_async_copy(subgrid, indices.at[0], sems.at[1]),
-        pltpu.make_async_copy(u, indices.at[1], sems.at[2]),
-        pltpu.make_async_copy(v, indices.at[2], sems.at[3]),
-        pltpu.make_async_copy(observed, seen, sems.at[4]),
+    pairs = [
+        (offsets, first), (facet, image), (subgrid, indices.at[0]), (u, indices.at[1]), (v, indices.at[2]), (observed, seen),
     ]
+    copies = [pltpu.make_async_copy(source, target, sems.at[n]) for n, (source, target) in enumerate(pairs)]
     for copy in copies:
         copy.start()
-    half_columns(cols_count, offsets, 1 - place()[0] % 2, side, col_tab)
-    for copy in copies:
+    copies[0].wait()
+    half_columns(cols_count, first, 1 - place()[0] % 2, side, col_tab)
+    for copy in copies[2:]:
         copy.wait()
     some = jnp.concatenate([indices[n].astype(f32) for n in range(3)] + [seen[...], jnp.zeros((3, side), f32)], 0)
     some = jnp.concatenate([some[:, :side // 2], some[:, side // 2:]], 0).astype(bf16)
-    vis[...] = some
-    send[side:, :side // 2] = some
-    send[side:, side // 2:] = some
-    send[:side] = jnp.dot(image[...], col_tab[...], preferred_element_type=f32).astype(bf16)
+    tail[:, :side // 2] = some
+    tail[:, side // 2:] = some
+    writes = [
+        pltpu.make_async_copy(tail.at[:, pl.ds(0, side // 2)], vis, sems.at[6]),
+        pltpu.make_async_copy(tail, send.at[pl.ds(side, 16)], sems.at[7]),
+    ]
+    for write in writes:
+        write.start()
+    copies[1].wait()
+    step = side // 2
+    for n in range(2):
+        at = pl.ds(n * step, step)
+        made[at] = jnp.dot(image[at], col_tab[...], preferred_element_type=f32).astype(bf16)
+        write = pltpu.make_async_copy(made.at[at], send.at[at], sems.at[8 + n])
+        write.start()
+        writes.append(write)
+    for write in writes:
+        write.wait()
 
 
 def own_columns_kernel(cols_count, offsets, facet, own, col_tab):
@@ -153,17 +166,16 @@
     )
 
 
-def gridding_kernel(*refs):
-    f32, bf16 = jnp.float32, jnp.bfloat16
-    parts, (pieces, planes) = refs[:-2], refs[-2:]
+def grid_sums(parts):
+    f32, bf16 = jnp.float32, jnp.bfloat16
     row_index, _ = place()
     chip = (row_index // 2).astype(f32)
     v_at = (sublanes(HALF) + (row_index % 2) * HALF).astype(f32)
     counter = sublanes(SG).astype(f32)
-    count = len(parts)
     total = jnp.zeros((SG, 3 * HALF), f32)
-    for k in range(count):
-        one = vis_rows(parts[k][2 * SG:].astype(f32))
+    planes = [jnp.zeros((SG, HALF), f32)] * 2
+    for part in parts:
+        one = vis_rows(part[2 * SG:].astype(f32))
         u_here = jnp.where(one[0:1] == chip, one[1:2], -1.0)
         hot = jnp.where(u_here == counter, 1.0, 0.0).astype(bf16)
         pick = one[2:3] == v_at
@@ -171,17 +183,23 @@
             [jnp.where(pick, one[3:4], 0.0), jnp.where(pick, one[4:5], 0.0), jnp.where(pick, 1.0, 0.0)], 0
         ).astype(bf16)
         total = total + lax.dot_general(hot, right, (((1,), (1,)), ((), ())), preferred_element_type=f32)
-    for p in range(2):
-        some = parts[0][p * SG:(p + 1) * SG].astype(f32)
-        for k in range(1, count):
-            some = some + parts[k][p * SG:(p + 1) * SG].astype(f32)
-        planes[p] = some
-    for p in range(3):
-        planes[2 + p] = total[:, p * HALF:(p + 1) * HALF]
+        planes = [planes[p] + part[p * SG:(p + 1) * SG].astype(f32) for p in range(2)]
+    return planes + [total[:, p * HALF:(p + 1) * HALF] for p in range(3)]
+
+
+def first_sums_kernel(*refs):
+    for p, plane in enumerate(grid_sums(refs[:-1])):
+        refs[-1][p] = plane
+
+
+def gridding_kernel(*refs):
+    parts, (first, pieces, planes) = refs[:-3], refs[-3:]
+    for p, plane in enumerate(grid_sums(parts)):
+        planes[p] = first[p] + plane
     each = SG // pieces.shape[0]
     for j in range(pieces.shape[0]):
         rows = [planes[p, j * each:(j + 1) * each] for p in range(5)]
-        pieces[j] = jnp.concatenate(rows, 0).astype(bf16)
+        pieces[j] = jnp.concatenate(rows, 0).astype(jnp.bfloat16)
 
 
 def pieces_sum_kernel(pieces, out):
@@ -194,21 +212,25 @@
         out[j] = total
 
 
-def grids_kernel(chips, own, other, *refs):
-    f32, bf16 = jnp.float32, jnp.bfloat16
+def grids_kernel(chips, near, *refs):
+    f32, bf16 = jnp.float32, jnp.bfloat16
+    own, other, refs = refs[:near], refs[near:2 * near], refs[2 * near:]
     parts, (grid_left, forward, inverse_left, inverse, _) = refs[:chips], refs[chips:chips + 5]
     outs, rest, (planes, cat, tall, hat) = refs[chips + 5:-5], refs[-5], refs[-4:]
-    row_index, _ = place()
+    row_index, col_index = place()
     core = row_index % 2
     chip = (row_index // 2).astype(f32)
-    count = own.shape[0]
-    each = SG // count
-    for pieces, half in ((own, core), (other, 1 - core)):
+    count = own[0].shape[0]
+    each = SG // (count * near)
+    for blocks, half in ((own, core), (other, 1 - core)):
         at = pl.ds(pl.multiple_of(half * HALF, HALF), HALF)
-        for j in range(count):
-            some = pieces[j].astype(f32)
-            for p in range(5):
-                planes[p, j * each:(j + 1) * each, at] = some[p * each:(p + 1) * each]
+        for k, pieces in enumerate(blocks):
+            line = lax.rem(col_index + near - k, near)
+            for j in range(count):
+                some = pieces[j].astype(f32)
+                rows = pl.ds(pl.multiple_of((j * near + line) * each, each), each)
+                for p in range(5):
+                    planes[p, rows, at] = some[p * each:(p + 1) * each]
     cat[:, :SG] = planes[0].astype(bf16)
     cat[:, SG:] = planes[1].astype(bf16)
     wide = jnp.dot(cat[...], forward[...], preferred_element_type=f32).astype(bf16)
@@ -369,16 +391,18 @@
 
     scale_in = 1.0 / (side * math.sqrt(rows_count * cols_count))
     scale_out = 1.0 / (SG * math.sqrt(NR * NC))
+    near = 4
     line = (1, n_vis)
 
     send, vis = call(
         functools.partial(send_columns_kernel, cols_count), (shape(side + 16, 4 * HALF), shape(16, n_vis // 2)),
-        "send_columns", "saaaaa",
+        "send_columns", "aaaaaa",
         scratch=[
             pltpu.VMEM((side, 4 * HALF), bf16), pltpu.VMEM((side, side), bf16), pltpu.VMEM((3,) + line, jnp.int32),
-            pltpu.VMEM((2, n_vis), f32), pltpu.SemaphoreType.DMA((5,)),
+            pltpu.VMEM((2, n_vis), f32), pltpu.SMEM((NC,), jnp.int32), pltpu.VMEM((side, 4 * HALF), bf16),
+            pltpu.VMEM((16, n_vis), bf16), pltpu.SemaphoreType.DMA((10,)),
         ],
-        cost=10**9, room=60,
+        cost=10**9, room=60, outs="aa",
     )(col_offsets, facet, vis_subgrid.reshape(line), vis_u.reshape(line), vis_v.reshape(line), observed)
     other = lax.ppermute(send, "frow", swap)
     own = call(
@@ -395,14 +419,18 @@
     )(own, vis, other, row_tab)
     parts = turned(parts)
 
+    sums = call(first_sums_kernel, shape(5, SG, HALF, dtype=f32), "first_sums", "vv", cost=10**9)(*parts[:2])
     pieces = call(
-        gridding_kernel, shape(cols_count, 5 * each, HALF), "gridding", "v" * chips,
+        gridding_kernel, shape(cols_count, 5 * each, HALF), "gridding", "v" * (chips - 1),
         scratch=[pltpu.VMEM((5, SG, HALF), f32)], cost=10**9,
-    )(*parts)
+    )(*parts[2:], sums)
     pieces = exchange(pieces, "fcol", None)
-    pieces = call(pieces_sum_kernel, shape(cols_count, 5 * each, HALF), "pieces_sum", "v", cost=10**6)(pieces)
-    pieces = exchange(pieces, "fcol", None)
-    pieces_other = lax.ppermute(pieces, "frow", swap)
+    far = cols_count // near
+    pieces = call(pieces_sum_kernel, shape(far, 5 * each, HALF), "pieces_sum", "v", cost=10**6)(pieces)
+    pieces = exchange(pieces, "fcol", [[near * step + line for step in range(far)] for line in range(near)])
+    lines = [[(index, index // near * near + (index + k) % near) for index in range(cols_count)] for k in range(near)]
+    pieces = [pieces] + [lax.ppermute(pieces, "fcol", lines[k]) for k in range(1, near)]
+    pieces_other = [lax.ppermute(block, "frow", swap) for block in pieces]
 
     back_row, back_col = call(
         functools.partial(back_tables_kernel, rows_count, cols_count, side),
@@ -413,14 +441,14 @@
     forward_block = np.concatenate([block[0], block[1]], 0)
     inverse_block = np.concatenate([block[2], block[3]], 0)
     *back, rest = call(
-        functools.partial(grids_kernel, chips), (shape(2 * SG + 16, HALF),) * chips + (shape(2 * SG, HALF),), "grids",
-        "v" * (6 + chips) + "a",
+        functools.partial(grids_kernel, chips, near), (shape(2 * SG + 16, HALF),) * chips + (shape(2 * SG, HALF),), "grids",
+        "v" * (4 + chips + 2 * near) + "a",
         scratch=[
             pltpu.VMEM((5, SG, SG), f32), pltpu.VMEM((SG, 2 * SG), bf16), pltpu.VMEM((2 * SG, SG), bf16),
             pltpu.VMEM((SG, 2 * SG), bf16),
         ],
         cost=10**9,
-    )(pieces, pieces_other, *parts, inverse_block, forward_block, forward_block, inverse_block, back_col)
+    )(*pieces, *pieces_other, *parts, inverse_block, forward_block, forward_block, inverse_block, back_col)
     back = turned(back)
 
     def first_part(number, mine, other):

time: 82.8 us -> 83.9 us (1.013)
  starting transfers between devices: 16.9 us -> 23.9 us
  blocking collectives: 38.4 us -> 32.3 us
    ppermute x1 -> x7, starting transfers between devices: 4.08 us -> 11.7 us  [the longest x4 9.09 us: shards(): pieces_other = [lax.ppermute(block, 'frow', swap) for block in pieces]]
    all_to_all x2, blocking collectives: 38.4 us -> 32.3 us  [exchange(): lax.all_to_all(blocks, axes, 0, 0, tiled=True, axis_index_groups=groups)]
    pallas_call x2 -> x3, Pallas kernels: 1.75 us -> 2.68 us  [the longest x1 1.83 us: shards(): call(functools.partial(grids_kernel, chips, near), (shape(2 * SG + 16, HA...]
  transfers between devices with their start and end apart: 11 -> 17, of which waited for: 6 -> 5; matrix products, arithmetic and copies ran while one was open for 0% -> 0% of each run, Pallas kernels for 6% -> 7%
where the time goes in v8:
time: 83.9 us; the launch traced here: 83.7 us
  blocking collectives  32.3 us (38%)
  starting transfers between devices  23.9 us (28%)
  Pallas kernels  14.1 us (17%)
  waiting for transfers between devices  12.4 us (15%)
  between operations  1.01 us (1%)
    all_to_all x2, blocking collectives, exchange(): lax.all_to_all(blocks, axes, 0, 0, tiled=True, axis_index_groups=groups)  32.3 us
    ppermute x6, waiting for transfers between devices, turned(): moved = {k: lax.ppermute(blocks[k], 'frow', turns[k]) for k in (2, 1, 3)}  11.4 us
    ppermute x4, starting transfers between devices, shards(): pieces_other = [lax.ppermute(block, 'frow', swap) for block in pieces]  9.09 us
    ppermute x6, starting transfers between devices, turned(): moved = {k: lax.ppermute(blocks[k], 'frow', turns[k]) for k in (2, 1, 3)}  7.33 us
    ppermute x1, starting transfers between devices, shards(): other = lax.ppermute(send, 'frow', swap)  3.33 us
    ppermute x3, starting transfers between devices, shards(): lax.ppermute(pieces, 'fcol', lines[k])  2.62 us
    pallas_call x1, Pallas kernels, shards(): call(functools.partial(send_columns_kernel, cols_count), (shape(side + 16...  2.34 us
    pallas_call x1, Pallas kernels, shards(): call(functools.partial(image_kernel, scale_out, chips), (shape(side, side...  2.29 us
  transfers between devices with their start and end apart: 17, of which 5 were waited for; matrix products, arithmetic and copies ran while one was open for 0% of the time, Pallas kernels for 7%

profile of v8, /device:TPU:1, one launch (start us, length us, event | category | flops | bytes accessed | tf_op | source)
XLA Modules:
  0.0 83.7 jit_solution(18149615893833024546)
XLA Ops:
  0.7 2.3 %send_columns.1 = (bf16[528,512]{1,0:T(8,128)(2,1)}, bf16[16,256]{1,0:T(8,128)(2,1)}) custom-call(s32[2]{0:T(128)} %offsets_col.1, bf16[512,512]{1,0:T(8,128)(2,1)} %facet.3, s32[1,512]{1,0:T(1,128)} %bitcast.3, s32[1,512]{1,0:T(1,128)} %bitcast.4, s32[1,512]{1,0:T(1,128)} %bitcast.5, f32[2,512]{1,0:T(2,128)} %refs_10_.1), custom_call_target="tpu_custom_call" | custom-call | flops 1000000000 | bytes 1048576 | tf_op jit(solution)/shard_map/send_columns/pallas_call | solution.py:397
  3.0 0.0 copy-start.5
  3.0 3.3 %collective-permute-start = (bf16[528,512]{1,0:T(8,128)(2,1)}, bf16[528,512]{1,0:T(8,128)(2,1)S(1)}, u32[]{:S(2)}, u32[]{:S(2)}) collective-permute-start(bf16[528,512]{1,0:T(8,128)(2,1)} %get-tuple-element.18), channel_id=1, source_target_pairs={{0,32},{32,0},{64,96},{96,64},{128,160},{160,128},{192,224},{224,1... | collective-permute-start | bytes 1622024 | tf_op jit(solution)/shard_map/ppermute | solution.py:407
  6.4 1.1 %own_columns.1.own = bf16[512,512]{1,0:T(8,128)(2,1)S(1)} custom-call(s32[2]{0:T(128)S(1)} %copy-done.4, bf16[512,512]{1,0:T(8,128)(2,1)S(1)} %copy-done.3), custom_call_target="tpu_custom_call" | custom-call | flops 1000000000 | bytes 1048576 | tf_op jit(solution)/shard_map/own_columns/pallas_call | solution.py:408
  7.5 1.3 %row_tables.1.row_tab = bf16[4,256,1024]{2,1,0:T(8,128)(2,1)S(1)} custom-call(s32[2]{0:T(128)S(1)} %copy-done.5), custom_call_target="tpu_custom_call" | custom-call | flops 1000000000 | bytes 1048576 | tf_op jit(solution)/shard_map/row_tables/pallas_call | solution.py:412
  8.8 0.0 collective-permute-done.other
  8.8 1.3 %contributions.1 = (bf16[576,128]{1,0:T(8,128)(2,1)S(1)}, bf16[576,128]{1,0:T(8,128)(2,1)S(1)}, bf16[576,128]{1,0:T(8,128)(2,1)S(1)}, bf16[576,128]{1,0:T(8,128)(2,1)S(1)}) custom-call(bf16[512,512]{1,0:T(8,128)(2,1)S(1)} %own_columns.1.own, bf16[16,256]{1,0:T(8,128)(2,1)S(1)} %copy-done.6, bf16[528,512]{1,0:T(8,128)(2,1)S(1)} %collective-permute-done.other, ...), custom_call_target="tpu_custom_call" | custom-call | flops 2000000000 | bytes 1048576 | tf_op jit(solution)/shard_map/contributions/pallas_call | solution.py:416
  10.2 0.1 collective-permute-start.3
  10.3 1.9 %collective-permute-start.1 = (bf16[576,128]{1,0:T(8,128)(2,1)S(1)}, bf16[576,128]{1,0:T(8,128)(2,1)S(1)}, u32[]{:S(2)}, u32[]{:S(2)}) collective-permute-start(bf16[576,128]{1,0:T(8,128)(2,1)S(1)} %get-tuple-element.19), channel_id=1, source_target_pairs={{0,128},{32,160},{64,192},{96,224},{128,0},{160,32},{192,64},{224,... | collective-permute-start | bytes 442376 | tf_op jit(solution)/shard_map/ppermute | solution.py:389
  12.2 1.1 %collective-permute-start.2 = (bf16[576,128]{1,0:T(8,128)(2,1)S(1)}, bf16[576,128]{1,0:T(8,128)(2,1)S(1)}, u32[]{:S(2)}, u32[]{:S(2)}) collective-permute-start(bf16[576,128]{1,0:T(8,128)(2,1)S(1)} %get-tuple-element.20), channel_id=1, source_target_pairs={{0,192},{32,224},{64,0},{96,32},{128,64},{160,96},{192,128},{224,1... | collective-permute-start | bytes 442376 | tf_op jit(solution)/shard_map/ppermute | solution.py:389
  13.3 6.8 %collective-permute-done.3.refs_1_.refs_9_ = bf16[576,128]{1,0:T(8,128)(2,1)S(1)} collective-permute-done((bf16[576,128]{1,0:T(8,128)(2,1)S(1)}, bf16[576,128]{1,0:T(8,128)(2,1)S(1)}, u32[]{:S(2)}, u32[]{:S(2)}) %collective-permute-start.3) | collective-permute-done | bytes 147488 | tf_op jit(solution)/shard_map/ppermute | solution.py:389
  20.1 0.8 first_sums.1.refs_2_
  20.9 0.0 collective-permute-done.1.refs_0_.refs_10_
  20.9 0.0 collective-permute-done.2.refs_1_.refs_11_
  20.9 0.8 gridding.1
  21.7 22.1 %all_to_all.10.pieces = bf16[32,40,128]{2,1,0:T(8,128)(2,1)S(1)} all-to-all(bf16[32,40,128]{2,1,0:T(8,128)(2,1)S(1)} %gridding.1), channel_id=1, replica_groups=mesh['frow'=8,'fcol'=32] {'fcol'}, dimensions={0} | all-to-all | bytes 655360 | tf_op jit(solution)/shard_map/all_to_all | solution.py:371
  43.7 0.1 pieces_sum.1
  43.8 10.3 %all_to_all.11.refs_0_ = bf16[8,40,128]{2,1,0:T(8,128)(2,1)S(1)} all-to-all(bf16[8,40,128]{2,1,0:T(8,128)(2,1)S(1)} %pieces_sum.1), channel_id=1, replica_groups={{0,4,8,12,16,20,24,28},{1,5,9,13,17,21,25,29},{2,6,10,14,18,22,26,30},{..., dimensions={0} | all-to-all | bytes 163840 | tf_op jit(solution)/shard_map/all_to_all | solution.py:371
  54.0 1.4 %collective-permute-start.6 = (bf16[8,40,128]{2,1,0:T(8,128)(2,1)S(1)}, bf16[8,40,128]{2,1,0:T(8,128)(2,1)S(1)}, u32[]{:S(2)}, u32[]{:S(2)}) collective-permute-start(bf16[8,40,128]{2,1,0:T(8,128)(2,1)S(1)} %all_to_all.11.refs_0_), channel_id=1, source_target_pairs={{0,3},{1,0},{2,1},{3,2},{4,7},{5,4},{6,5},{7,6},{8,11},{9,8},{10,9... | collective-permute-start | bytes 245768 | tf_op jit(solution)/shard_map/ppermute | solution.py:432
  55.4 0.4 collective-permute-start.5
  55.8 0.9 %collective-permute-start.4 = (bf16[8,40,128]{2,1,0:T(8,128)(2,1)S(1)}, bf16[8,40,128]{2,1,0:T(8,128)(2,1)S(1)}, u32[]{:S(2)}, u32[]{:S(2)}) collective-permute-start(bf16[8,40,128]{2,1,0:T(8,128)(2,1)S(1)} %all_to_all.11.refs_0_), channel_id=1, source_target_pairs={{0,1},{1,2},{2,3},{3,0},{4,5},{5,6},{6,7},{7,4},{8,9},{9,10},{10,1... | collective-permute-start | bytes 245768 | tf_op jit(solution)/shard_map/ppermute | solution.py:432
  56.7 3.8 %collective-permute-start.7 = (bf16[8,40,128]{2,1,0:T(8,128)(2,1)S(1)}, bf16[8,40,128]{2,1,0:T(8,128)(2,1)S(1)}, u32[]{:S(2)}, u32[]{:S(2)}) collective-permute-start(bf16[8,40,128]{2,1,0:T(8,128)(2,1)S(1)} %all_to_all.11.refs_0_), channel_id=1, source_target_pairs={{0,32},{32,0},{64,96},{96,64},{128,160},{160,128},{192,224},{224,1... | collective-permute-start | bytes 245768 | tf_op jit(solution)/shard_map/ppermute | solution.py:433
  60.5 0.0 collective-permute-done.6.refs_3_
  60.5 1.3 %collective-permute-start.10 = (bf16[8,40,128]{2,1,0:T(8,128)(2,1)S(1)}, bf16[8,40,128]{2,1,0:T(8,128)(2,1)S(1)}, u32[]{:S(2)}, u32[]{:S(2)}) collective-permute-start(bf16[8,40,128]{2,1,0:T(8,128)(2,1)S(1)} %collective-permute-done.6.refs_3_), channel_id=1, source_target_pairs={{0,32},{32,0},{64,96},{96,64},{128,160},{160,128},{192,224},{224,1... | collective-permute-start | bytes 245768 | tf_op jit(solution)/shard_map/ppermute | solution.py:433
  61.9 0.0 collective-permute-done.5.refs_2_
  61.9 2.9 %collective-permute-start.9 = (bf16[8,40,128]{2,1,0:T(8,128)(2,1)S(1)}, bf16[8,40,128]{2,1,0:T(8,128)(2,1)S(1)}, u32[]{:S(2)}, u32[]{:S(2)}) collective-permute-start(bf16[8,40,128]{2,1,0:T(8,128)(2,1)S(1)} %collective-permute-done.5.refs_2_), channel_id=1, source_target_pairs={{0,32},{32,0},{64,96},{96,64},{128,160},{160,128},{192,224},{224,1... | collective-permute-start | bytes 245768 | tf_op jit(solution)/shard_map/ppermute | solution.py:433
  64.7 0.0 collective-permute-done.4.refs_1_
  64.7 1.0 %collective-permute-start.8 = (bf16[8,40,128]{2,1,0:T(8,128)(2,1)S(1)}, bf16[8,40,128]{2,1,0:T(8,128)(2,1)S(1)}, u32[]{:S(2)}, u32[]{:S(2)}) collective-permute-start(bf16[8,40,128]{2,1,0:T(8,128)(2,1)S(1)} %collective-permute-done.4.refs_1_), channel_id=1, source_target_pairs={{0,32},{32,0},{64,96},{96,64},{128,160},{160,128},{192,224},{224,1... | collective-permute-start | bytes 245768 | tf_op jit(solution)/shard_map/ppermute | solution.py:433
  65.8 1.4 %back_tables.1 = (bf16[512,1024]{1,0:T(8,128)(2,1)S(1)}, bf16[1024,512]{1,0:T(8,128)(2,1)S(1)}) custom-call(s32[2]{0:T(128)S(1)} %copy-done.5, s32[2]{0:T(128)S(1)} %copy-done.4), custom_call_target="tpu_custom_call" | custom-call | flops 1000000000 | bytes 1048576 | tf_op jit(solution)/shard_map/back_tables/pallas_call | solution.py:435
  67.2 0.0 collective-permute-done.7.refs_4_
  67.2 0.0 collective-permute-done.10.refs_7_
  67.2 0.0 collective-permute-done.9.refs_6_
  67.2 1.8 %grids.1 = (bf16[528,128]{1,0:T(8,128)(2,1)S(1)}, bf16[528,128]{1,0:T(8,128)(2,1)S(1)}, bf16[528,128]{1,0:T(8,128)(2,1)S(1)}, bf16[528,128]{1,0:T(8,128)(2,1)S(1)}, bf16[512,128]{1,0:T(8,128)(2,1)S(1)}) custom-call(bf16[8,40,128]{2,1,0:T(8,128)(2,1)S(1)} %all_to_all.11.refs_0_, bf16[8,40,128]{2,1,0:T(8,128)(2,1)S(1)} %collective-permute-done.4.refs_1_, ...), custom_call_target="tpu_custom_call" | custom-call | flops 1000000000 | bytes 1048576 | tf_op jit(solution)/shard_map/grids/pallas_call | solution.py:443
  69.1 0.8 collective-permute-start.11
  69.8 2.7 %collective-permute-start.12 = (bf16[528,128]{1,0:T(8,128)(2,1)S(1)}, bf16[528,128]{1,0:T(8,128)(2,1)S(1)}, u32[]{:S(2)}, u32[]{:S(2)}) collective-permute-start(bf16[528,128]{1,0:T(8,128)(2,1)S(1)} %get-tuple-element.29), channel_id=1, source_target_pairs={{0,128},{32,160},{64,192},{96,224},{128,0},{160,32},{192,64},{224,... | collective-permute-start | bytes 405512 | tf_op jit(solution)/shard_map/ppermute | solution.py:389
  72.5 0.8 collective-permute-start.13
  73.3 0.4 first_part.2.refs_6_
  73.7 0.0 copy-start.2
  73.7 1.9 %collective-permute-done.11.own.refs_1_ = bf16[528,128]{1,0:T(8,128)(2,1)S(1)} collective-permute-done((bf16[528,128]{1,0:T(8,128)(2,1)S(1)}, bf16[528,128]{1,0:T(8,128)(2,1)S(1)}, u32[]{:S(2)}, u32[]{:S(2)}) %collective-permute-start.11) | collective-permute-done | bytes 135200 | tf_op jit(solution)/shard_map/ppermute | solution.py:389
  75.6 0.8 collective-permute-start.16
  76.3 2.8 %collective-permute-done.12.refs_2_ = bf16[528,128]{1,0:T(8,128)(2,1)S(1)} collective-permute-done((bf16[528,128]{1,0:T(8,128)(2,1)S(1)}, bf16[528,128]{1,0:T(8,128)(2,1)S(1)}, u32[]{:S(2)}, u32[]{:S(2)}) %collective-permute-start.12) | collective-permute-done | bytes 135200 | tf_op jit(solution)/shard_map/ppermute | solution.py:389
  79.2 0.8 collective-permute-start.14
  79.9 0.0 collective-permute-done.13.refs_3_
  79.9 0.0 collective-permute-start.15
  80.0 0.4 first_part.3.refs_7_
  80.4 0.5 collective-permute-done.14.refs_4_
  80.9 0.4 collective-permute-done.15.refs_5_
  81.3 2.3 %image.1 = (f32[512,512]{1,0:T(8,128)}, f32[2,512]{1,0:T(2,128)}) custom-call(bf16[528,128]{1,0:T(8,128)(2,1)S(1)} %get-tuple-element.24.own.refs_0_, bf16[528,128]{1,0:T(8,128)(2,1)S(1)} %collective-permute-done.11.own.refs_1_, bf16[528,128]{1,0:T(8,128)(2,1)S(1)} %collective-permute-done.12.refs_2_, bf16[528,128]{1,0:T(8,128)(2,1)S(1)} %collective-permute-done.13.refs_3_, ...), custom_call_target="tpu_custom_call" | custom-call | flops 1000000000 | bytes 1048576 | tf_op jit(solution)/shard_map/image/pallas_call | solution.py:462
  (14 shorter events, 0.0 us)
Async XLA Ops:
  0.6 5.7 %copy-start.4 = (s32[2]{0:T(128)S(1)}, s32[2]{0:T(128)}, u32[]{:S(2)}) copy-start(s32[2]{0:T(128)} %offsets_col.1) | copy-start | bytes 28
  0.6 5.7 %copy-start.3 = (bf16[512,512]{1,0:T(8,128)(2,1)S(1)}, bf16[512,512]{1,0:T(8,128)(2,1)}, u32[]{:S(2)}) copy-start(bf16[512,512]{1,0:T(8,128)(2,1)} %facet.3) | copy-start | bytes 1572868
  3.0 4.4 %copy-start.5 = (s32[2]{0:T(128)S(1)}, s32[2]{0:T(128)}, u32[]{:S(2)}) copy-start(s32[2]{0:T(128)} %offsets_row.1) | copy-start | bytes 28
  3.0 5.8 %collective-permute-start = (bf16[528,512]{1,0:T(8,128)(2,1)}, bf16[528,512]{1,0:T(8,128)(2,1)S(1)}, u32[]{:S(2)}, u32[]{:S(2)}) collective-permute-start(bf16[528,512]{1,0:T(8,128)(2,1)} %get-tuple-element.18), channel_id=1, source_target_pairs={{0,32},{32,0},{64,96},{96,64},{128,160},{160,128},{192,224},{224,1... | collective-permute-start | bytes 1622024 | tf_op jit(solution)/shard_map/ppermute | solution.py:407
  7.5 1.4 %copy-start.6 = (bf16[16,256]{1,0:T(8,128)(2,1)S(1)}, bf16[16,256]{1,0:T(8,128)(2,1)}, u32[]{:S(2)}) copy-start(bf16[16,256]{1,0:T(8,128)(2,1)} %get-tuple-element.17.own_vis) | copy-start | bytes 24580
  10.2 9.9 %collective-permute-start.3 = (bf16[576,128]{1,0:T(8,128)(2,1)S(1)}, bf16[576,128]{1,0:T(8,128)(2,1)S(1)}, u32[]{:S(2)}, u32[]{:S(2)}) collective-permute-start(bf16[576,128]{1,0:T(8,128)(2,1)S(1)} %get-tuple-element.22), channel_id=1, source_target_pairs={{0,64},{32,96},{64,128},{96,160},{128,192},{160,224},{192,0},{224,... | collective-permute-start | bytes 442376 | tf_op jit(solution)/shard_map/ppermute | solution.py:389
  10.3 10.6 %collective-permute-start.1 = (bf16[576,128]{1,0:T(8,128)(2,1)S(1)}, bf16[576,128]{1,0:T(8,128)(2,1)S(1)}, u32[]{:S(2)}, u32[]{:S(2)}) collective-permute-start(bf16[576,128]{1,0:T(8,128)(2,1)S(1)} %get-tuple-element.19), channel_id=1, source_target_pairs={{0,128},{32,160},{64,192},{96,224},{128,0},{160,32},{192,64},{224,... | collective-permute-start | bytes 442376 | tf_op jit(solution)/shard_map/ppermute | solution.py:389
  12.2 8.7 %collective-permute-start.2 = (bf16[576,128]{1,0:T(8,128)(2,1)S(1)}, bf16[576,128]{1,0:T(8,128)(2,1)S(1)}, u32[]{:S(2)}, u32[]{:S(2)}) collective-permute-start(bf16[576,128]{1,0:T(8,128)(2,1)S(1)} %get-tuple-element.20), channel_id=1, source_target_pairs={{0,192},{32,224},{64,0},{96,32},{128,64},{160,96},{192,128},{224,1... | collective-permute-start | bytes 442376 | tf_op jit(solution)/shard_map/ppermute | solution.py:389
  43.7 23.5 %copy-start = (bf16[512,512]{1,0:T(8,128)(2,1)S(1)}, bf16[512,512]{1,0:T(8,128)(2,1)}, u32[]{:S(2)}) copy-start(bf16[512,512]{1,0:T(8,128)(2,1)} %constant.5.clone.refs_13_.refs_14_) | copy-start | bytes 1572868
  43.7 23.5 %copy-start.1 = (bf16[512,512]{1,0:T(8,128)(2,1)S(1)}, bf16[512,512]{1,0:T(8,128)(2,1)}, u32[]{:S(2)}) copy-start(bf16[512,512]{1,0:T(8,128)(2,1)} %constant.4.clone.refs_12_.refs_15_) | copy-start | bytes 1572868
  54.0 6.5 %collective-permute-start.6 = (bf16[8,40,128]{2,1,0:T(8,128)(2,1)S(1)}, bf16[8,40,128]{2,1,0:T(8,128)(2,1)S(1)}, u32[]{:S(2)}, u32[]{:S(2)}) collective-permute-start(bf16[8,40,128]{2,1,0:T(8,128)(2,1)S(1)} %all_to_all.11.refs_0_), channel_id=1, source_target_pairs={{0,3},{1,0},{2,1},{3,2},{4,7},{5,4},{6,5},{7,6},{8,11},{9,8},{10,9... | collective-permute-start | bytes 245768 | tf_op jit(solution)/shard_map/ppermute | solution.py:432
  55.4 6.4 %collective-permute-start.5 = (bf16[8,40,128]{2,1,0:T(8,128)(2,1)S(1)}, bf16[8,40,128]{2,1,0:T(8,128)(2,1)S(1)}, u32[]{:S(2)}, u32[]{:S(2)}) collective-permute-start(bf16[8,40,128]{2,1,0:T(8,128)(2,1)S(1)} %all_to_all.11.refs_0_), channel_id=1, source_target_pairs={{0,2},{1,3},{2,0},{3,1},{4,6},{5,7},{6,4},{7,5},{8,10},{9,11},{10,... | collective-permute-start | bytes 245768 | tf_op jit(solution)/shard_map/ppermute | solution.py:432
  55.8 8.9 %collective-permute-start.4 = (bf16[8,40,128]{2,1,0:T(8,128)(2,1)S(1)}, bf16[8,40,128]{2,1,0:T(8,128)(2,1)S(1)}, u32[]{:S(2)}, u32[]{:S(2)}) collective-permute-start(bf16[8,40,128]{2,1,0:T(8,128)(2,1)S(1)} %all_to_all.11.refs_0_), channel_id=1, source_target_pairs={{0,1},{1,2},{2,3},{3,0},{4,5},{5,6},{6,7},{7,4},{8,9},{9,10},{10,1... | collective-permute-start | bytes 245768 | tf_op jit(solution)/shard_map/ppermute | solution.py:432
  56.7 10.5 %collective-permute-start.7 = (bf16[8,40,128]{2,1,0:T(8,128)(2,1)S(1)}, bf16[8,40,128]{2,1,0:T(8,128)(2,1)S(1)}, u32[]{:S(2)}, u32[]{:S(2)}) collective-permute-start(bf16[8,40,128]{2,1,0:T(8,128)(2,1)S(1)} %all_to_all.11.refs_0_), channel_id=1, source_target_pairs={{0,32},{32,0},{64,96},{96,64},{128,160},{160,128},{192,224},{224,1... | collective-permute-start | bytes 245768 | tf_op jit(solution)/shard_map/ppermute | solution.py:433
  60.5 6.7 %collective-permute-start.10 = (bf16[8,40,128]{2,1,0:T(8,128)(2,1)S(1)}, bf16[8,40,128]{2,1,0:T(8,128)(2,1)S(1)}, u32[]{:S(2)}, u32[]{:S(2)}) collective-permute-start(bf16[8,40,128]{2,1,0:T(8,128)(2,1)S(1)} %collective-permute-done.6.refs_3_), channel_id=1, source_target_pairs={{0,32},{32,0},{64,96},{96,64},{128,160},{160,128},{192,224},{224,1... | collective-permute-start | bytes 245768 | tf_op jit(solution)/shard_map/ppermute | solution.py:433
  61.9 5.3 %collective-permute-start.9 = (bf16[8,40,128]{2,1,0:T(8,128)(2,1)S(1)}, bf16[8,40,128]{2,1,0:T(8,128)(2,1)S(1)}, u32[]{:S(2)}, u32[]{:S(2)}) collective-permute-start(bf16[8,40,128]{2,1,0:T(8,128)(2,1)S(1)} %collective-permute-done.5.refs_2_), channel_id=1, source_target_pairs={{0,32},{32,0},{64,96},{96,64},{128,160},{160,128},{192,224},{224,1... | collective-permute-start | bytes 245768 | tf_op jit(solution)/shard_map/ppermute | solution.py:433
  64.7 2.4 %collective-permute-start.8 = (bf16[8,40,128]{2,1,0:T(8,128)(2,1)S(1)}, bf16[8,40,128]{2,1,0:T(8,128)(2,1)S(1)}, u32[]{:S(2)}, u32[]{:S(2)}) collective-permute-start(bf16[8,40,128]{2,1,0:T(8,128)(2,1)S(1)} %collective-permute-done.4.refs_1_), channel_id=1, source_target_pairs={{0,32},{32,0},{64,96},{96,64},{128,160},{160,128},{192,224},{224,1... | collective-permute-start | bytes 245768 | tf_op jit(solution)/shard_map/ppermute | solution.py:433
  69.1 6.5 %collective-permute-start.11 = (bf16[528,128]{1,0:T(8,128)(2,1)S(1)}, bf16[528,128]{1,0:T(8,128)(2,1)S(1)}, u32[]{:S(2)}, u32[]{:S(2)}) collective-permute-start(bf16[528,128]{1,0:T(8,128)(2,1)S(1)} %get-tuple-element.25), channel_id=1, source_target_pairs={{0,64},{32,96},{64,128},{96,160},{128,192},{160,224},{192,0},{224,... | collective-permute-start | bytes 405512 | tf_op jit(solution)/shard_map/ppermute | solution.py:389
  69.8 9.3 %collective-permute-start.12 = (bf16[528,128]{1,0:T(8,128)(2,1)S(1)}, bf16[528,128]{1,0:T(8,128)(2,1)S(1)}, u32[]{:S(2)}, u32[]{:S(2)}) collective-permute-start(bf16[528,128]{1,0:T(8,128)(2,1)S(1)} %get-tuple-element.29), channel_id=1, source_target_pairs={{0,128},{32,160},{64,192},{96,224},{128,0},{160,32},{192,64},{224,... | collective-permute-start | bytes 405512 | tf_op jit(solution)/shard_map/ppermute | solution.py:389
  72.5 7.4 %collective-permute-start.13 = (bf16[528,128]{1,0:T(8,128)(2,1)S(1)}, bf16[528,128]{1,0:T(8,128)(2,1)S(1)}, u32[]{:S(2)}, u32[]{:S(2)}) collective-permute-start(bf16[528,128]{1,0:T(8,128)(2,1)S(1)} %get-tuple-element.30), channel_id=1, source_target_pairs={{0,192},{32,224},{64,0},{96,32},{128,64},{160,96},{192,128},{224,1... | collective-permute-start | bytes 405512 | tf_op jit(solution)/shard_map/ppermute | solution.py:389
  73.7 7.6 %copy-start.2 = (f32[2,512]{1,0:T(2,128)S(1)}, f32[2,512]{1,0:T(2,128)}, u32[]{:S(2)}) copy-start(f32[2,512]{1,0:T(2,128)} %refs_10_.1) | copy-start | bytes 12292
  75.6 4.4 %collective-permute-start.16 = (bf16[528,128]{1,0:T(8,128)(2,1)S(1)}, bf16[528,128]{1,0:T(8,128)(2,1)S(1)}, u32[]{:S(2)}, u32[]{:S(2)}) collective-permute-start(bf16[528,128]{1,0:T(8,128)(2,1)S(1)} %collective-permute-done.11.own.refs_1_), channel_id=1, source_target_pairs={{0,32},{32,0},{64,96},{96,64},{128,160},{160,128},{192,224},{224,1... | collective-permute-start | bytes 405512 | tf_op jit(solution)/shard_map/ppermute | solution.py:460
  79.2 1.8 %collective-permute-start.14 = (bf16[528,128]{1,0:T(8,128)(2,1)S(1)}, bf16[528,128]{1,0:T(8,128)(2,1)S(1)}, u32[]{:S(2)}, u32[]{:S(2)}) collective-permute-start(bf16[528,128]{1,0:T(8,128)(2,1)S(1)} %collective-permute-done.12.refs_2_), channel_id=1, source_target_pairs={{0,32},{32,0},{64,96},{96,64},{128,160},{160,128},{192,224},{224,1... | collective-permute-start | bytes 405512 | tf_op jit(solution)/shard_map/ppermute | solution.py:460
  79.9 1.4 %collective-permute-start.15 = (bf16[528,128]{1,0:T(8,128)(2,1)S(1)}, bf16[528,128]{1,0:T(8,128)(2,1)S(1)}, u32[]{:S(2)}, u32[]{:S(2)}) collective-permute-start(bf16[528,128]{1,0:T(8,128)(2,1)S(1)} %collective-permute-done.13.refs_3_), channel_id=1, source_target_pairs={{0,32},{32,0},{64,96},{96,64},{128,160},{160,128},{192,224},{224,1... | collective-permute-start | bytes 405512 | tf_op jit(solution)/shard_map/ppermute | solution.py:460

commit v9 on v8

--- a/solution.py
+++ b/solution.py
@@ -109,14 +109,12 @@
         write.wait()
 
 
-def own_columns_kernel(cols_count, offsets, facet, own, col_tab):
-    half_columns(cols_count, offsets, place()[0] % 2, facet.shape[0], col_tab)
-    own[...] = jnp.dot(facet[...], col_tab[...], preferred_element_type=jnp.float32).astype(jnp.bfloat16)
-
-
-def row_tables_kernel(rows_count, side, offsets, row_tab):
+def own_tables_kernel(rows_count, cols_count, offsets, col_offsets, facet, own, row_tab, col_tab):
     bf16 = jnp.bfloat16
     row_index, _ = place()
+    side = facet.shape[0]
+    half_columns(cols_count, col_offsets, row_index % 2, side, col_tab)
+    own[...] = jnp.dot(facet[...], col_tab[...], preferred_element_type=jnp.float32).astype(bf16)
     unit = sublanes(16)
     row_step = SKY // (rows_count * side)
     for f in range(2):
@@ -193,7 +191,7 @@
 
 
 def gridding_kernel(*refs):
-    parts, (first, pieces, planes) = refs[:-3], refs[-3:]
+    parts, (first, _, pieces, planes) = refs[:-4], refs[-4:]
     for p, plane in enumerate(grid_sums(parts)):
         planes[p] = first[p] + plane
     each = SG // pieces.shape[0]
@@ -212,25 +210,21 @@
         out[j] = total
 
 
-def grids_kernel(chips, near, *refs):
-    f32, bf16 = jnp.float32, jnp.bfloat16
-    own, other, refs = refs[:near], refs[near:2 * near], refs[2 * near:]
-    parts, (grid_left, forward, inverse_left, inverse, _) = refs[:chips], refs[chips:chips + 5]
-    outs, rest, (planes, cat, tall, hat) = refs[chips + 5:-5], refs[-5], refs[-4:]
-    row_index, col_index = place()
+def grids_kernel(chips, own, other, *refs):
+    f32, bf16 = jnp.float32, jnp.bfloat16
+    parts, (grid_left, forward, inverse_left, inverse) = refs[:chips], refs[chips:chips + 4]
+    outs, rest, (planes, cat, tall, hat) = refs[chips + 4:-5], refs[-5], refs[-4:]
+    row_index, _ = place()
     core = row_index % 2
     chip = (row_index // 2).astype(f32)
-    count = own[0].shape[0]
-    each = SG // (count * near)
-    for blocks, half in ((own, core), (other, 1 - core)):
+    count = own.shape[0]
+    each = SG // count
+    for pieces, half in ((own, core), (other, 1 - core)):
         at = pl.ds(pl.multiple_of(half * HALF, HALF), HALF)
-        for k, pieces in enumerate(blocks):
-            line = lax.rem(col_index + near - k, near)
-            for j in range(count):
-                some = pieces[j].astype(f32)
-                rows = pl.ds(pl.multiple_of((j * near + line) * each, each), each)
-                for p in range(5):
-                    planes[p, rows, at] = some[p * each:(p + 1) * each]
+        for j in range(count):
+            some = pieces[j].astype(f32)
+            for p in range(5):
+                planes[p, j * each:(j + 1) * each, at] = some[p * each:(p + 1) * each]
     cat[:, :SG] = planes[0].astype(bf16)
     cat[:, SG:] = planes[1].astype(bf16)
     wide = jnp.dot(cat[...], forward[...], preferred_element_type=f32).astype(bf16)
@@ -391,7 +385,6 @@
 
     scale_in = 1.0 / (side * math.sqrt(rows_count * cols_count))
     scale_out = 1.0 / (SG * math.sqrt(NR * NC))
-    near = 4
     line = (1, n_vis)
 
     send, vis = call(
@@ -405,13 +398,11 @@
         cost=10**9, room=60, outs="aa",
     )(col_offsets, facet, vis_subgrid.reshape(line), vis_u.reshape(line), vis_v.reshape(line), observed)
     other = lax.ppermute(send, "frow", swap)
-    own = call(
-        functools.partial(own_columns_kernel, cols_count), shape(side, 4 * HALF), "own_columns", "sv",
+    own, row_tab = call(
+        functools.partial(own_tables_kernel, rows_count, cols_count),
+        (shape(side, 4 * HALF), shape(4, SG, 2 * side)), "own_tables", "ssv",
         scratch=[pltpu.VMEM((side, 4 * HALF), bf16)], cost=10**9,
-    )(col_offsets, facet)
-    row_tab = call(
-        functools.partial(row_tables_kernel, rows_count, side), shape(4, SG, 2 * side), "row_tables", "s", cost=10**9
-    )(row_offsets)
+    )(row_offsets, col_offsets, facet)
     vis_rows_count = 8 * 2 * n_vis // LANES
     parts = call(
         functools.partial(contributions_kernel, scale_in), (shape(2 * SG + vis_rows_count, HALF),) * chips,
@@ -420,35 +411,32 @@
     parts = turned(parts)
 
     sums = call(first_sums_kernel, shape(5, SG, HALF, dtype=f32), "first_sums", "vv", cost=10**9)(*parts[:2])
-    pieces = call(
-        gridding_kernel, shape(cols_count, 5 * each, HALF), "gridding", "v" * (chips - 1),
-        scratch=[pltpu.VMEM((5, SG, HALF), f32)], cost=10**9,
-    )(*parts[2:], sums)
-    pieces = exchange(pieces, "fcol", None)
-    far = cols_count // near
-    pieces = call(pieces_sum_kernel, shape(far, 5 * each, HALF), "pieces_sum", "v", cost=10**6)(pieces)
-    pieces = exchange(pieces, "fcol", [[near * step + line for step in range(far)] for line in range(near)])
-    lines = [[(index, index // near * near + (index + k) % near) for index in range(cols_count)] for k in range(near)]
-    pieces = [pieces] + [lax.ppermute(pieces, "fcol", lines[k]) for k in range(1, near)]
-    pieces_other = [lax.ppermute(block, "frow", swap) for block in pieces]
-
     back_row, back_col = call(
         functools.partial(back_tables_kernel, rows_count, cols_count, side),
         (shape(side, 4 * SG), shape(4 * SG, side)), "back_tables", "ss", cost=10**9,
     )(row_offsets, col_offsets)
+    pieces = call(
+        gridding_kernel, shape(cols_count, 5 * each, HALF), "gridding", "v" * (chips - 1) + "a",
+        scratch=[pltpu.VMEM((5, SG, HALF), f32)], cost=10**9,
+    )(*parts[2:], sums, back_col)
+    pieces = exchange(pieces, "fcol", None)
+    pieces = call(pieces_sum_kernel, shape(cols_count, 5 * each, HALF), "pieces_sum", "v", cost=10**6)(pieces)
+    pieces = exchange(pieces, "fcol", None)
+    pieces_other = lax.ppermute(pieces, "frow", swap)
+
     kcos, ksin = grid_tables()
     block = [np.concatenate(pair, 1) for pair in ((kcos, ksin), (-ksin, kcos), (kcos, -ksin), (ksin, kcos))]
     forward_block = np.concatenate([block[0], block[1]], 0)
     inverse_block = np.concatenate([block[2], block[3]], 0)
     *back, rest = call(
-        functools.partial(grids_kernel, chips, near), (shape(2 * SG + 16, HALF),) * chips + (shape(2 * SG, HALF),), "grids",
-        "v" * (4 + chips + 2 * near) + "a",
+        functools.partial(grids_kernel, chips), (shape(2 * SG + 16, HALF),) * chips + (shape(2 * SG, HALF),), "grids",
+        "v" * (6 + chips),
         scratch=[
             pltpu.VMEM((5, SG, SG), f32), pltpu.VMEM((SG, 2 * SG), bf16), pltpu.VMEM((2 * SG, SG), bf16),
             pltpu.VMEM((SG, 2 * SG), bf16),
         ],
         cost=10**9,
-    )(*pieces, *pieces_other, *parts, inverse_block, forward_block, forward_block, inverse_block, back_col)
+    )(pieces, pieces_other, *parts, inverse_block, forward_block, forward_block, inverse_block)
     back = turned(back)
 
     def first_part(number, mine, other):

time: 83.9 us -> 80.6 us (0.961)
  starting transfers between devices: 23.9 us -> 17.6 us
  blocking collectives: 32.3 us -> 37.2 us
  waiting for transfers between devices: 12.4 us -> 11.1 us
    ppermute x7 -> x1, starting transfers between devices: 11.7 us -> 4.51 us  [shards(): pieces_other = lax.ppermute(pieces, 'frow', swap)]
    all_to_all x2, blocking collectives: 32.3 us -> 37.2 us  [exchange(): lax.all_to_all(blocks, axes, 0, 0, tiled=True, axis_index_groups=groups)]
    ppermute x6, waiting for transfers between devices: 11.4 us -> 8.93 us  [turned(): moved = {k: lax.ppermute(blocks[k], 'frow', turns[k]) for k in (2, 1, 3)}]
    ppermute x7 -> x1, waiting for transfers between devices: 0.02 us -> 1.26 us  [shards(): pieces_other = lax.ppermute(pieces, 'frow', swap)]
    ppermute x3, starting transfers between devices: 1.57 us -> 2.52 us  [shards(): rest = [lax.ppermute(block, 'frow', swap) for block in back[1:]]]
    pallas_call x4 -> x3, Pallas kernels: 4.33 us -> 3.64 us  [the longest x1 1.9 us: shards(): call(functools.partial(own_tables_kernel, rows_count, cols_count), (shape...]
  transfers between devices with their start and end apart: 17 -> 11, of which waited for: 5 -> 6; matrix products, arithmetic and copies ran while one was open for 0% -> 0% of each run, Pallas kernels for 7% -> 6%
where the time goes in v9:
time: 80.6 us; the launch traced here: 80.4 us
  blocking collectives  37.2 us (46%)
  starting transfers between devices  17.6 us (22%)
  Pallas kernels  13.4 us (17%)
  waiting for transfers between devices  11.1 us (14%)
  between operations  0.96 us (1%)
    all_to_all x2, blocking collectives, exchange(): lax.all_to_all(blocks, axes, 0, 0, tiled=True, axis_index_groups=groups)  37.2 us
    ppermute x6, waiting for transfers between devices, turned(): moved = {k: lax.ppermute(blocks[k], 'frow', turns[k]) for k in (2, 1, 3)}  8.93 us
    ppermute x6, starting transfers between devices, turned(): moved = {k: lax.ppermute(blocks[k], 'frow', turns[k]) for k in (2, 1, 3)}  7.28 us
    ppermute x1, starting transfers between devices, shards(): pieces_other = lax.ppermute(pieces, 'frow', swap)  4.51 us
    ppermute x1, starting transfers between devices, shards(): other = lax.ppermute(send, 'frow', swap)  3.32 us
    ppermute x3, starting transfers between devices, shards(): rest = [lax.ppermute(block, 'frow', swap) for block in back[1:]]  2.52 us
    pallas_call x1, Pallas kernels, shards(): call(functools.partial(send_columns_kernel, cols_count), (shape(side + 16...  2.34 us
    pallas_call x1, Pallas kernels, shards(): call(functools.partial(image_kernel, scale_out, chips), (shape(side, side...  2.29 us
  transfers between devices with their start and end apart: 11, of which 6 were waited for; matrix products, arithmetic and copies ran while one was open for 0% of the time, Pallas kernels for 6%

profile of v9, /device:TPU:1, one launch (start us, length us, event | category | flops | bytes accessed | tf_op | source)
XLA Modules:
  0.0 80.4 jit_solution(14538757949055196696)
XLA Ops:
  0.6 0.0 copy-start.3
  0.6 0.0 copy-start.1
  0.7 0.0 copy-start.2
  0.7 2.3 %send_columns.1 = (bf16[528,512]{1,0:T(8,128)(2,1)}, bf16[16,256]{1,0:T(8,128)(2,1)}) custom-call(s32[2]{0:T(128)} %offsets_col.1, bf16[512,512]{1,0:T(8,128)(2,1)} %facet.3, s32[1,512]{1,0:T(1,128)} %bitcast.3, s32[1,512]{1,0:T(1,128)} %bitcast.4, s32[1,512]{1,0:T(1,128)} %bitcast.5, f32[2,512]{1,0:T(2,128)} %refs_10_.1), custom_call_target="tpu_custom_call" | custom-call | flops 1000000000 | bytes 1048576 | tf_op jit(solution)/shard_map/send_columns/pallas_call | solution.py:390
  3.0 0.0 copy-start.6
  3.0 3.3 %collective-permute-start = (bf16[528,512]{1,0:T(8,128)(2,1)}, bf16[528,512]{1,0:T(8,128)(2,1)S(1)}, u32[]{:S(2)}, u32[]{:S(2)}) collective-permute-start(bf16[528,512]{1,0:T(8,128)(2,1)} %get-tuple-element.21), channel_id=1, source_target_pairs={{0,32},{32,0},{64,96},{96,64},{128,160},{160,128},{192,224},{224,1... | collective-permute-start | bytes 1622024 | tf_op jit(solution)/shard_map/ppermute | solution.py:400
  6.3 0.0 copy-done.3
  6.3 0.0 copy-done.1
  6.3 0.0 copy-done.2
  6.3 1.9 %own_tables.1 = (bf16[512,512]{1,0:T(8,128)(2,1)S(1)}, bf16[4,256,1024]{2,1,0:T(8,128)(2,1)S(1)}) custom-call(s32[2]{0:T(128)S(1)} %copy-done.2, s32[2]{0:T(128)S(1)} %copy-done.3, bf16[512,512]{1,0:T(8,128)(2,1)S(1)} %copy-done.1), custom_call_target="tpu_custom_call" | custom-call | flops 1000000000 | bytes 1048576 | tf_op jit(solution)/shard_map/own_tables/pallas_call | solution.py:401
  8.3 0.0 collective-permute-done.other
  8.3 0.0 copy-done.6
  8.3 1.3 %contributions.1 = (bf16[576,128]{1,0:T(8,128)(2,1)S(1)}, bf16[576,128]{1,0:T(8,128)(2,1)S(1)}, bf16[576,128]{1,0:T(8,128)(2,1)S(1)}, bf16[576,128]{1,0:T(8,128)(2,1)S(1)}) custom-call(bf16[512,512]{1,0:T(8,128)(2,1)S(1)} %get-tuple-element.19.own, bf16[16,256]{1,0:T(8,128)(2,1)S(1)} %copy-done.6, bf16[528,512]{1,0:T(8,128)(2,1)S(1)} %collective-permute-done.other, ...), custom_call_target="tpu_custom_call" | custom-call | flops 2000000000 | bytes 1048576 | tf_op jit(solution)/shard_map/contributions/pallas_call | solution.py:407
  9.6 0.1 collective-permute-start.3
  9.7 1.9 %collective-permute-start.1 = (bf16[576,128]{1,0:T(8,128)(2,1)S(1)}, bf16[576,128]{1,0:T(8,128)(2,1)S(1)}, u32[]{:S(2)}, u32[]{:S(2)}) collective-permute-start(bf16[576,128]{1,0:T(8,128)(2,1)S(1)} %get-tuple-element.23), channel_id=1, source_target_pairs={{0,128},{32,160},{64,192},{96,224},{128,0},{160,32},{192,64},{224,... | collective-permute-start | bytes 442376 | tf_op jit(solution)/shard_map/ppermute | solution.py:383
  11.6 1.2 %collective-permute-start.2 = (bf16[576,128]{1,0:T(8,128)(2,1)S(1)}, bf16[576,128]{1,0:T(8,128)(2,1)S(1)}, u32[]{:S(2)}, u32[]{:S(2)}) collective-permute-start(bf16[576,128]{1,0:T(8,128)(2,1)S(1)} %get-tuple-element.24), channel_id=1, source_target_pairs={{0,192},{32,224},{64,0},{96,32},{128,64},{160,96},{192,128},{224,1... | collective-permute-start | bytes 442376 | tf_op jit(solution)/shard_map/ppermute | solution.py:383
  12.8 1.4 %back_tables.1 = (bf16[512,1024]{1,0:T(8,128)(2,1)S(1)}, bf16[1024,512]{1,0:T(8,128)(2,1)S(1)}) custom-call(s32[2]{0:T(128)S(1)} %copy-done.2, s32[2]{0:T(128)S(1)} %copy-done.3), custom_call_target="tpu_custom_call" | custom-call | flops 1000000000 | bytes 1048576 | tf_op jit(solution)/shard_map/back_tables/pallas_call | solution.py:414
  14.2 5.2 %collective-permute-done.3.refs_1_ = bf16[576,128]{1,0:T(8,128)(2,1)S(1)} collective-permute-done((bf16[576,128]{1,0:T(8,128)(2,1)S(1)}, bf16[576,128]{1,0:T(8,128)(2,1)S(1)}, u32[]{:S(2)}, u32[]{:S(2)}) %collective-permute-start.3) | collective-permute-done | bytes 147488 | tf_op jit(solution)/shard_map/ppermute | solution.py:383
  19.3 0.8 first_sums.1.refs_2_
  20.1 0.0 collective-permute-done.1.refs_0_.refs_2_
  20.1 0.0 collective-permute-done.2.refs_1_.refs_3_
  20.1 0.0 copy-start.4
  20.1 0.0 copy-start.5
  20.1 0.8 gridding.1
  20.9 21.5 %all_to_all.10.pieces = bf16[32,40,128]{2,1,0:T(8,128)(2,1)S(1)} all-to-all(bf16[32,40,128]{2,1,0:T(8,128)(2,1)S(1)} %gridding.1), channel_id=1, replica_groups=mesh['frow'=8,'fcol'=32] {'fcol'}, dimensions={0} | all-to-all | bytes 655360 | tf_op jit(solution)/shard_map/all_to_all | solution.py:365
  42.4 0.1 pieces_sum.1
  42.5 15.7 %all_to_all.11.own = bf16[32,40,128]{2,1,0:T(8,128)(2,1)S(1)} all-to-all(bf16[32,40,128]{2,1,0:T(8,128)(2,1)S(1)} %pieces_sum.1), channel_id=1, replica_groups=mesh['frow'=8,'fcol'=32] {'fcol'}, dimensions={0} | all-to-all | bytes 655360 | tf_op jit(solution)/shard_map/all_to_all | solution.py:365
  58.2 4.5 %collective-permute-start.4 = (bf16[32,40,128]{2,1,0:T(8,128)(2,1)S(1)}, bf16[32,40,128]{2,1,0:T(8,128)(2,1)S(1)}, u32[]{:S(2)}, u32[]{:S(2)}) collective-permute-start(bf16[32,40,128]{2,1,0:T(8,128)(2,1)S(1)} %all_to_all.11.own), channel_id=1, source_target_pairs={{0,32},{32,0},{64,96},{96,64},{128,160},{160,128},{192,224},{224,1... | collective-permute-start | bytes 983048 | tf_op jit(solution)/shard_map/ppermute | solution.py:425
  62.7 1.3 %collective-permute-done.4.other = bf16[32,40,128]{2,1,0:T(8,128)(2,1)S(1)} collective-permute-done((bf16[32,40,128]{2,1,0:T(8,128)(2,1)S(1)}, bf16[32,40,128]{2,1,0:T(8,128)(2,1)S(1)}, u32[]{:S(2)}, u32[]{:S(2)}) %collective-permute-start.4) | collective-permute-done | bytes 327712 | tf_op jit(solution)/shard_map/ppermute | solution.py:425
  64.0 0.0 copy-done.4
  64.0 0.0 copy-done.5
  64.0 1.7 %grids.1 = (bf16[528,128]{1,0:T(8,128)(2,1)S(1)}, bf16[528,128]{1,0:T(8,128)(2,1)S(1)}, bf16[528,128]{1,0:T(8,128)(2,1)S(1)}, bf16[528,128]{1,0:T(8,128)(2,1)S(1)}, bf16[512,128]{1,0:T(8,128)(2,1)S(1)}) custom-call(bf16[32,40,128]{2,1,0:T(8,128)(2,1)S(1)} %all_to_all.11.own, bf16[32,40,128]{2,1,0:T(8,128)(2,1)S(1)} %collective-permute-done.4.other, ...), custom_call_target="tpu_custom_call" | custom-call | flops 1000000000 | bytes 1048576 | tf_op jit(solution)/shard_map/grids/pallas_call | solution.py:431
  65.7 1.0 %collective-permute-start.5 = (bf16[528,128]{1,0:T(8,128)(2,1)S(1)}, bf16[528,128]{1,0:T(8,128)(2,1)S(1)}, u32[]{:S(2)}, u32[]{:S(2)}) collective-permute-start(bf16[528,128]{1,0:T(8,128)(2,1)S(1)} %get-tuple-element.29), channel_id=1, source_target_pairs={{0,64},{32,96},{64,128},{96,160},{128,192},{160,224},{192,0},{224,... | collective-permute-start | bytes 405512 | tf_op jit(solution)/shard_map/ppermute | solution.py:383
  66.6 2.5 %collective-permute-start.6 = (bf16[528,128]{1,0:T(8,128)(2,1)S(1)}, bf16[528,128]{1,0:T(8,128)(2,1)S(1)}, u32[]{:S(2)}, u32[]{:S(2)}) collective-permute-start(bf16[528,128]{1,0:T(8,128)(2,1)S(1)} %get-tuple-element.33), channel_id=1, source_target_pairs={{0,128},{32,160},{64,192},{96,224},{128,0},{160,32},{192,64},{224,... | collective-permute-start | bytes 405512 | tf_op jit(solution)/shard_map/ppermute | solution.py:383
  69.1 0.7 collective-permute-start.7
  69.8 0.4 first_part.2.refs_6_
  70.2 0.0 copy-start
  70.3 1.5 %collective-permute-done.5.own.refs_1_ = bf16[528,128]{1,0:T(8,128)(2,1)S(1)} collective-permute-done((bf16[528,128]{1,0:T(8,128)(2,1)S(1)}, bf16[528,128]{1,0:T(8,128)(2,1)S(1)}, u32[]{:S(2)}, u32[]{:S(2)}) %collective-permute-start.5) | collective-permute-done | bytes 135200 | tf_op jit(solution)/shard_map/ppermute | solution.py:383
  71.8 1.3 %collective-permute-start.10 = (bf16[528,128]{1,0:T(8,128)(2,1)S(1)}, bf16[528,128]{1,0:T(8,128)(2,1)S(1)}, u32[]{:S(2)}, u32[]{:S(2)}) collective-permute-start(bf16[528,128]{1,0:T(8,128)(2,1)S(1)} %collective-permute-done.5.own.refs_1_), channel_id=1, source_target_pairs={{0,32},{32,0},{64,96},{96,64},{128,160},{160,128},{192,224},{224,1... | collective-permute-start | bytes 405512 | tf_op jit(solution)/shard_map/ppermute | solution.py:448
  73.1 2.3 %collective-permute-done.6.refs_2_ = bf16[528,128]{1,0:T(8,128)(2,1)S(1)} collective-permute-done((bf16[528,128]{1,0:T(8,128)(2,1)S(1)}, bf16[528,128]{1,0:T(8,128)(2,1)S(1)}, u32[]{:S(2)}, u32[]{:S(2)}) %collective-permute-start.6) | collective-permute-done | bytes 135200 | tf_op jit(solution)/shard_map/ppermute | solution.py:383
  75.3 1.2 %collective-permute-start.8 = (bf16[528,128]{1,0:T(8,128)(2,1)S(1)}, bf16[528,128]{1,0:T(8,128)(2,1)S(1)}, u32[]{:S(2)}, u32[]{:S(2)}) collective-permute-start(bf16[528,128]{1,0:T(8,128)(2,1)S(1)} %collective-permute-done.6.refs_2_), channel_id=1, source_target_pairs={{0,32},{32,0},{64,96},{96,64},{128,160},{160,128},{192,224},{224,1... | collective-permute-start | bytes 405512 | tf_op jit(solution)/shard_map/ppermute | solution.py:448
  76.5 0.0 collective-permute-done.7.refs_3_
  76.5 0.0 collective-permute-start.9
  76.6 0.0 collective-permute-done.10.rest
  76.6 0.4 first_part.3.refs_7_
  77.0 0.5 collective-permute-done.8.refs_4_
  77.5 0.4 collective-permute-done.9.refs_5_
  77.9 2.3 %image.1 = (f32[512,512]{1,0:T(8,128)}, f32[2,512]{1,0:T(2,128)}) custom-call(bf16[528,128]{1,0:T(8,128)(2,1)S(1)} %get-tuple-element.28.own.refs_0_, bf16[528,128]{1,0:T(8,128)(2,1)S(1)} %collective-permute-done.5.own.refs_1_, bf16[528,128]{1,0:T(8,128)(2,1)S(1)} %collective-permute-done.6.refs_2_, bf16[528,128]{1,0:T(8,128)(2,1)S(1)} %collective-permute-done.7.refs_3_, ...), custom_call_target="tpu_custom_call" | custom-call | flops 1000000000 | bytes 1048576 | tf_op jit(solution)/shard_map/image/pallas_call | solution.py:450
  (1 shorter events, 0.0 us)
Async XLA Ops:
  0.6 5.7 %copy-start.3 = (s32[2]{0:T(128)S(1)}, s32[2]{0:T(128)}, u32[]{:S(2)}) copy-start(s32[2]{0:T(128)} %offsets_col.1) | copy-start | bytes 28
  0.6 5.7 %copy-start.1 = (bf16[512,512]{1,0:T(8,128)(2,1)S(1)}, bf16[512,512]{1,0:T(8,128)(2,1)}, u32[]{:S(2)}) copy-start(bf16[512,512]{1,0:T(8,128)(2,1)} %facet.3) | copy-start | bytes 1572868
  0.7 5.7 %copy-start.2 = (s32[2]{0:T(128)S(1)}, s32[2]{0:T(128)}, u32[]{:S(2)}) copy-start(s32[2]{0:T(128)} %offsets_row.1) | copy-start | bytes 28
  3.0 5.3 %copy-start.6 = (bf16[16,256]{1,0:T(8,128)(2,1)S(1)}, bf16[16,256]{1,0:T(8,128)(2,1)}, u32[]{:S(2)}) copy-start(bf16[16,256]{1,0:T(8,128)(2,1)} %get-tuple-element.20.own_vis) | copy-start | bytes 24580
  3.0 5.2 %collective-permute-start = (bf16[528,512]{1,0:T(8,128)(2,1)}, bf16[528,512]{1,0:T(8,128)(2,1)S(1)}, u32[]{:S(2)}, u32[]{:S(2)}) collective-permute-start(bf16[528,512]{1,0:T(8,128)(2,1)} %get-tuple-element.21), channel_id=1, source_target_pairs={{0,32},{32,0},{64,96},{96,64},{128,160},{160,128},{192,224},{224,1... | collective-permute-start | bytes 1622024 | tf_op jit(solution)/shard_map/ppermute | solution.py:400
  9.6 9.7 %collective-permute-start.3 = (bf16[576,128]{1,0:T(8,128)(2,1)S(1)}, bf16[576,128]{1,0:T(8,128)(2,1)S(1)}, u32[]{:S(2)}, u32[]{:S(2)}) collective-permute-start(bf16[576,128]{1,0:T(8,128)(2,1)S(1)} %get-tuple-element.26), channel_id=1, source_target_pairs={{0,64},{32,96},{64,128},{96,160},{128,192},{160,224},{192,0},{224,... | collective-permute-start | bytes 442376 | tf_op jit(solution)/shard_map/ppermute | solution.py:383
  9.7 10.4 %collective-permute-start.1 = (bf16[576,128]{1,0:T(8,128)(2,1)S(1)}, bf16[576,128]{1,0:T(8,128)(2,1)S(1)}, u32[]{:S(2)}, u32[]{:S(2)}) collective-permute-start(bf16[576,128]{1,0:T(8,128)(2,1)S(1)} %get-tuple-element.23), channel_id=1, source_target_pairs={{0,128},{32,160},{64,192},{96,224},{128,0},{160,32},{192,64},{224,... | collective-permute-start | bytes 442376 | tf_op jit(solution)/shard_map/ppermute | solution.py:383
  11.6 8.5 %collective-permute-start.2 = (bf16[576,128]{1,0:T(8,128)(2,1)S(1)}, bf16[576,128]{1,0:T(8,128)(2,1)S(1)}, u32[]{:S(2)}, u32[]{:S(2)}) collective-permute-start(bf16[576,128]{1,0:T(8,128)(2,1)S(1)} %get-tuple-element.24), channel_id=1, source_target_pairs={{0,192},{32,224},{64,0},{96,32},{128,64},{160,96},{192,128},{224,1... | collective-permute-start | bytes 442376 | tf_op jit(solution)/shard_map/ppermute | solution.py:383
  20.1 43.9 %copy-start.4 = (bf16[512,512]{1,0:T(8,128)(2,1)S(1)}, bf16[512,512]{1,0:T(8,128)(2,1)}, u32[]{:S(2)}) copy-start(bf16[512,512]{1,0:T(8,128)(2,1)} %constant.5.clone.refs_5_.refs_6_) | copy-start | bytes 1572868
  20.1 43.9 %copy-start.5 = (bf16[512,512]{1,0:T(8,128)(2,1)S(1)}, bf16[512,512]{1,0:T(8,128)(2,1)}, u32[]{:S(2)}) copy-start(bf16[512,512]{1,0:T(8,128)(2,1)} %constant.4.clone.refs_4_.refs_7_) | copy-start | bytes 1572868
  58.2 5.8 %collective-permute-start.4 = (bf16[32,40,128]{2,1,0:T(8,128)(2,1)S(1)}, bf16[32,40,128]{2,1,0:T(8,128)(2,1)S(1)}, u32[]{:S(2)}, u32[]{:S(2)}) collective-permute-start(bf16[32,40,128]{2,1,0:T(8,128)(2,1)S(1)} %all_to_all.11.own), channel_id=1, source_target_pairs={{0,32},{32,0},{64,96},{96,64},{128,160},{160,128},{192,224},{224,1... | collective-permute-start | bytes 983048 | tf_op jit(solution)/shard_map/ppermute | solution.py:425
  65.7 6.1 %collective-permute-start.5 = (bf16[528,128]{1,0:T(8,128)(2,1)S(1)}, bf16[528,128]{1,0:T(8,128)(2,1)S(1)}, u32[]{:S(2)}, u32[]{:S(2)}) collective-permute-start(bf16[528,128]{1,0:T(8,128)(2,1)S(1)} %get-tuple-element.29), channel_id=1, source_target_pairs={{0,64},{32,96},{64,128},{96,160},{128,192},{160,224},{192,0},{224,... | collective-permute-start | bytes 405512 | tf_op jit(solution)/shard_map/ppermute | solution.py:383
  66.6 8.7 %collective-permute-start.6 = (bf16[528,128]{1,0:T(8,128)(2,1)S(1)}, bf16[528,128]{1,0:T(8,128)(2,1)S(1)}, u32[]{:S(2)}, u32[]{:S(2)}) collective-permute-start(bf16[528,128]{1,0:T(8,128)(2,1)S(1)} %get-tuple-element.33), channel_id=1, source_target_pairs={{0,128},{32,160},{64,192},{96,224},{128,0},{160,32},{192,64},{224,... | collective-permute-start | bytes 405512 | tf_op jit(solution)/shard_map/ppermute | solution.py:383
  69.1 7.4 %collective-permute-start.7 = (bf16[528,128]{1,0:T(8,128)(2,1)S(1)}, bf16[528,128]{1,0:T(8,128)(2,1)S(1)}, u32[]{:S(2)}, u32[]{:S(2)}) collective-permute-start(bf16[528,128]{1,0:T(8,128)(2,1)S(1)} %get-tuple-element.34), channel_id=1, source_target_pairs={{0,192},{32,224},{64,0},{96,32},{128,64},{160,96},{192,128},{224,1... | collective-permute-start | bytes 405512 | tf_op jit(solution)/shard_map/ppermute | solution.py:383
  70.2 7.7 %copy-start = (f32[2,512]{1,0:T(2,128)S(1)}, f32[2,512]{1,0:T(2,128)}, u32[]{:S(2)}) copy-start(f32[2,512]{1,0:T(2,128)} %refs_10_.1) | copy-start | bytes 12292
  71.8 4.8 %collective-permute-start.10 = (bf16[528,128]{1,0:T(8,128)(2,1)S(1)}, bf16[528,128]{1,0:T(8,128)(2,1)S(1)}, u32[]{:S(2)}, u32[]{:S(2)}) collective-permute-start(bf16[528,128]{1,0:T(8,128)(2,1)S(1)} %collective-permute-done.5.own.refs_1_), channel_id=1, source_target_pairs={{0,32},{32,0},{64,96},{96,64},{128,160},{160,128},{192,224},{224,1... | collective-permute-start | bytes 405512 | tf_op jit(solution)/shard_map/ppermute | solution.py:448
  75.3 2.2 %collective-permute-start.8 = (bf16[528,128]{1,0:T(8,128)(2,1)S(1)}, bf16[528,128]{1,0:T(8,128)(2,1)S(1)}, u32[]{:S(2)}, u32[]{:S(2)}) collective-permute-start(bf16[528,128]{1,0:T(8,128)(2,1)S(1)} %collective-permute-done.6.refs_2_), channel_id=1, source_target_pairs={{0,32},{32,0},{64,96},{96,64},{128,160},{160,128},{192,224},{224,1... | collective-permute-start | bytes 405512 | tf_op jit(solution)/shard_map/ppermute | solution.py:448
  76.5 1.4 %collective-permute-start.9 = (bf16[528,128]{1,0:T(8,128)(2,1)S(1)}, bf16[528,128]{1,0:T(8,128)(2,1)S(1)}, u32[]{:S(2)}, u32[]{:S(2)}) collective-permute-start(bf16[528,128]{1,0:T(8,128)(2,1)S(1)} %collective-permute-done.7.refs_3_), channel_id=1, source_target_pairs={{0,32},{32,0},{64,96},{96,64},{128,160},{160,128},{192,224},{224,1... | collective-permute-start | bytes 405512 | tf_op jit(solution)/shard_map/ppermute | solution.py:448

commit v10 on v9

--- a/solution.py
+++ b/solution.py
@@ -282,7 +282,7 @@
         coarse = wave((offsets_col[c] + 16 * unit) * pos)
 
         def store(at, cos, sin, c=c):
-            left = (at // HALF * 2 * NC + 2 * c) * HALF + at % HALF
+            left = (2 * c + at // HALF) * 2 * HALF + at % HALF
             col_tab[left:left + 16] = cos.astype(bf16)
             col_tab[left + HALF:left + HALF + 16] = (-sin).astype(bf16)
 
@@ -297,18 +297,35 @@
     return jnp.dot(left, right, preferred_element_type=jnp.float32)
 
 
-def first_part_kernel(number, own, rest, row_tab, out):
+def first_part_kernel(own, rest, row_tab, out):
     chip = place()[0] // 2
-    for half, block in enumerate((own, rest)):
-        out[:, half * SG:(half + 1) * SG] = block_part(block, chip + number, row_tab)
+    for n, block in enumerate((own, rest)):
+        out[:, n * SG:(n + 1) * SG] = block_part(block, chip, row_tab)
+
+
+def column_rows(number):
+    depth = 2 * SG
+    return pl.ds(pl.multiple_of(split_number(number)[1] * depth, depth), depth)
+
+
+def half_lanes(n):
+    half = place()[0] % 2
+    return pl.ds(pl.multiple_of((half if n == 0 else 1 - half) * SG, SG), SG)
+
+
+def own_column_kernel(chips, opposite, own, rest, first, row_tab, col_tab, out, both):
+    chip = place()[0] // 2
+    for n, block in enumerate((own, rest)):
+        part = first[:, n * SG:(n + 1) * SG] + block_part(block, chip + chips - opposite, row_tab)
+        both[:, half_lanes(n)] = part.astype(jnp.bfloat16)
+    out[...] = jnp.dot(both[...], col_tab[column_rows(chip)], preferred_element_type=jnp.float32)
 
 
 def image_kernel(scale, chips, *refs):
     f32, bf16 = jnp.float32, jnp.bfloat16
-    blocks, others, firsts, refs = refs[:chips], refs[chips:chips + 2], refs[chips + 2:chips + 4], refs[chips + 4:]
-    row_tab, col_tab, observed, out, residual, both, image, seen, sems = refs
-    row_index, _ = place()
-    core, chip = row_index % 2, row_index // 2
+    blocks, others, refs = refs[:chips], refs[chips:chips + 2], refs[chips + 2:]
+    first, row_tab, col_tab, observed, out, residual, both, image, seen, sems = refs
+    chip = place()[0] // 2
     model = jnp.zeros((16, LANES), f32)
     for block in blocks:
         model = model + block[2 * SG:].astype(f32)
@@ -319,18 +336,15 @@
             seen[part:part + 1, at] = observed[part:part + 1, at] - model[part * count + i:part * count + i + 1]
     writes = [pltpu.make_async_copy(seen, residual, sems.at[0])]
     writes[0].start()
-    for k in range(2, chips):
-        c = split_number(chip + chips - k)[1]
-        for n, block in enumerate((blocks[k], others[k - 2])):
-            half = core if n == 0 else 1 - core
-            at = pl.ds(pl.multiple_of((half * NC + c) * SG, SG), SG)
-            part = firsts[k - 2][:, n * SG:(n + 1) * SG] + block_part(block, chip + chips - k, row_tab)
-            both[:, at] = part.astype(bf16)
+    for n, pair in enumerate(((blocks[1], blocks[3]), others)):
+        part = block_part(pair[0], chip + chips - 1, row_tab) + block_part(pair[1], chip + chips - 3, row_tab)
+        both[:, half_lanes(n)] = part.astype(bf16)
     chunks = sems.shape[0] - 1
     step = image.shape[0] // chunks
     for n in range(chunks):
         at = slice(n * step, (n + 1) * step)
-        image[at] = jnp.dot(both[at], col_tab[...], preferred_element_type=f32) * scale
+        part = jnp.dot(both[at], col_tab[column_rows(chip + 1)], preferred_element_type=f32)
+        image[at] = (first[at] + part) * scale
         write = pltpu.make_async_copy(image.at[at], out.at[at], sems.at[1 + n])
         write.start()
         writes.append(write)
@@ -410,7 +424,7 @@
     )(own, vis, other, row_tab)
     parts = turned(parts)
 
-    sums = call(first_sums_kernel, shape(5, SG, HALF, dtype=f32), "first_sums", "vv", cost=10**9)(*parts[:2])
+    sums = call(first_sums_kernel, shape(5, SG, HALF, dtype=f32), "first_sums", "vv", cost=10**9)(parts[0], parts[2])
     back_row, back_col = call(
         functools.partial(back_tables_kernel, rows_count, cols_count, side),
         (shape(side, 4 * SG), shape(4 * SG, side)), "back_tables", "ss", cost=10**9,
@@ -418,7 +432,7 @@
     pieces = call(
         gridding_kernel, shape(cols_count, 5 * each, HALF), "gridding", "v" * (chips - 1) + "a",
         scratch=[pltpu.VMEM((5, SG, HALF), f32)], cost=10**9,
-    )(*parts[2:], sums, back_col)
+    )(parts[1], parts[3], sums, back_col)
     pieces = exchange(pieces, "fcol", None)
     pieces = call(pieces_sum_kernel, shape(cols_count, 5 * each, HALF), "pieces_sum", "v", cost=10**6)(pieces)
     pieces = exchange(pieces, "fcol", None)
@@ -439,23 +453,20 @@
     )(pieces, pieces_other, *parts, inverse_block, forward_block, forward_block, inverse_block)
     back = turned(back)
 
-    def first_part(number, mine, other):
-        kernel = functools.partial(first_part_kernel, number)
-        return call(kernel, shape(side, 2 * SG, dtype=f32), "first_part", "vvv", cost=10**9)(mine, other, back_row)
-
-    firsts = [first_part(chips, back[0], rest)]
-    back[1], firsts[0] = lax.optimization_barrier((back[1], firsts[0]))
-    rest = [lax.ppermute(block, "frow", swap) for block in back[1:]]
-    firsts.append(first_part(chips - 1, back[1], rest[0]))
+    both = pltpu.VMEM((side, 2 * SG), bf16)
+    square = shape(side, side, dtype=f32)
+    first = call(first_part_kernel, square, "first_part", "vvv", cost=10**9)(back[0], rest, back_row)
+    back[2], first = lax.optimization_barrier((back[2], first))
+    rest = {k: lax.ppermute(back[k], "frow", swap) for k in (2, 1, 3)}
+    first = call(
+        functools.partial(own_column_kernel, chips, 2), square, "own_column", "v" * 5, scratch=[both], cost=10**9
+    )(back[2], rest[2], first, back_row, back_col)
     return call(
-        functools.partial(image_kernel, scale_out, chips),
-        (shape(side, side, dtype=f32), shape(2, n_vis, dtype=f32)), "image", "v" * (chips + 7), outs="aa",
-        scratch=[
-            pltpu.VMEM((side, 4 * SG), bf16), pltpu.VMEM((side, side), f32), pltpu.VMEM((2, n_vis), f32),
-            pltpu.SemaphoreType.DMA((5,)),
-        ],
+        functools.partial(image_kernel, scale_out, chips), (square, shape(2, n_vis, dtype=f32)), "image",
+        "v" * (chips + 6), outs="aa",
+        scratch=[both, pltpu.VMEM((side, side), f32), pltpu.VMEM((2, n_vis), f32), pltpu.SemaphoreType.DMA((5,))],
         cost=10**9,
-    )(*back, *rest[1:], *firsts, back_row, back_col, observed)
+    )(*back, rest[1], rest[3], first, back_row, back_col, observed)
 
 
 def solution(mesh):

time: 80.6 us -> 79.3 us (0.984)
  waiting for transfers between devices: 11.1 us -> 9.41 us
  starting transfers between devices: 17.6 us -> 18.7 us
    ppermute x6, waiting for transfers between devices: 8.93 us -> 7.55 us  [turned(): moved = {k: lax.ppermute(blocks[k], 'frow', turns[k]) for k in (2, 1, 3)}]
    ppermute x6, starting transfers between devices: 7.28 us -> 8.23 us  [turned(): moved = {k: lax.ppermute(blocks[k], 'frow', turns[k]) for k in (2, 1, 3)}]
  transfers between devices with their start and end apart: 11 -> 11, of which waited for: 6 -> 7; matrix products, arithmetic and copies ran while one was open for 0% -> 0% of each run, Pallas kernels for 6% -> 7%
where the time goes in v10:
time: 79.3 us; the launch traced here: 79.1 us
  blocking collectives  36.8 us (46%)
  starting transfers between devices  18.7 us (24%)
  Pallas kernels  13.3 us (17%)
  waiting for transfers between devices  9.41 us (12%)
  between operations  0.92 us (1%)
    all_to_all x2, blocking collectives, exchange(): lax.all_to_all(blocks, axes, 0, 0, tiled=True, axis_index_groups=groups)  36.8 us
    ppermute x6, starting transfers between devices, turned(): moved = {k: lax.ppermute(blocks[k], 'frow', turns[k]) for k in (2, 1, 3)}  8.23 us
    ppermute x6, waiting for transfers between devices, turned(): moved = {k: lax.ppermute(blocks[k], 'frow', turns[k]) for k in (2, 1, 3)}  7.55 us
    ppermute x1, starting transfers between devices, shards(): pieces_other = lax.ppermute(pieces, 'frow', swap)  4.51 us
    ppermute x1, starting transfers between devices, shards(): other = lax.ppermute(send, 'frow', swap)  3.32 us
    ppermute x3, starting transfers between devices, shards(): rest = {k: lax.ppermute(back[k], 'frow', swap) for k in (2, 1, 3)}  2.62 us
    pallas_call x1, Pallas kernels, shards(): call(functools.partial(send_columns_kernel, cols_count), (shape(side + 16...  2.34 us
    pallas_call x1, Pallas kernels, shards(): call(functools.partial(own_tables_kernel, rows_count, cols_count), (shape...  1.9 us
  transfers between devices with their start and end apart: 11, of which 7 were waited for; matrix products, arithmetic and copies ran while one was open for 0% of the time, Pallas kernels for 7%

profile of v10, /device:TPU:1, one launch (start us, length us, event | category | flops | bytes accessed | tf_op | source)
XLA Modules:
  0.0 79.1 jit_solution(16545047207514749296)
XLA Ops:
  0.6 0.0 copy-start.3
  0.6 0.0 copy-start.1
  0.7 0.0 copy-start.2
  0.7 2.3 %send_columns.1 = (bf16[528,512]{1,0:T(8,128)(2,1)}, bf16[16,256]{1,0:T(8,128)(2,1)}) custom-call(s32[2]{0:T(128)} %offsets_col.1, bf16[512,512]{1,0:T(8,128)(2,1)} %facet.3, s32[1,512]{1,0:T(1,128)} %bitcast.3, s32[1,512]{1,0:T(1,128)} %bitcast.4, s32[1,512]{1,0:T(1,128)} %bitcast.5, f32[2,512]{1,0:T(2,128)} %refs_9_.1), custom_call_target="tpu_custom_call" | custom-call | flops 1000000000 | bytes 1048576 | tf_op jit(solution)/shard_map/send_columns/pallas_call | solution.py:404
  3.0 0.0 copy-start.6
  3.0 3.3 %collective-permute-start = (bf16[528,512]{1,0:T(8,128)(2,1)}, bf16[528,512]{1,0:T(8,128)(2,1)S(1)}, u32[]{:S(2)}, u32[]{:S(2)}) collective-permute-start(bf16[528,512]{1,0:T(8,128)(2,1)} %get-tuple-element.21), channel_id=1, source_target_pairs={{0,32},{32,0},{64,96},{96,64},{128,160},{160,128},{192,224},{224,1... | collective-permute-start | bytes 1622024 | tf_op jit(solution)/shard_map/ppermute | solution.py:414
  6.3 0.0 copy-done.3
  6.3 0.0 copy-done.1
  6.3 0.0 copy-done.2
  6.3 1.9 %own_tables.1 = (bf16[512,512]{1,0:T(8,128)(2,1)S(1)}, bf16[4,256,1024]{2,1,0:T(8,128)(2,1)S(1)}) custom-call(s32[2]{0:T(128)S(1)} %copy-done.2, s32[2]{0:T(128)S(1)} %copy-done.3, bf16[512,512]{1,0:T(8,128)(2,1)S(1)} %copy-done.1), custom_call_target="tpu_custom_call" | custom-call | flops 1000000000 | bytes 1048576 | tf_op jit(solution)/shard_map/own_tables/pallas_call | solution.py:415
  8.3 0.0 collective-permute-done.other
  8.3 0.0 copy-done.6
  8.3 1.3 %contributions.1 = (bf16[576,128]{1,0:T(8,128)(2,1)S(1)}, bf16[576,128]{1,0:T(8,128)(2,1)S(1)}, bf16[576,128]{1,0:T(8,128)(2,1)S(1)}, bf16[576,128]{1,0:T(8,128)(2,1)S(1)}) custom-call(bf16[512,512]{1,0:T(8,128)(2,1)S(1)} %get-tuple-element.19.own, bf16[16,256]{1,0:T(8,128)(2,1)S(1)} %copy-done.6, bf16[528,512]{1,0:T(8,128)(2,1)S(1)} %collective-permute-done.other, ...), custom_call_target="tpu_custom_call" | custom-call | flops 2000000000 | bytes 1048576 | tf_op jit(solution)/shard_map/contributions/pallas_call | solution.py:421
  9.6 1.1 %collective-permute-start.3 = (bf16[576,128]{1,0:T(8,128)(2,1)S(1)}, bf16[576,128]{1,0:T(8,128)(2,1)S(1)}, u32[]{:S(2)}, u32[]{:S(2)}) collective-permute-start(bf16[576,128]{1,0:T(8,128)(2,1)S(1)} %get-tuple-element.26), channel_id=1, source_target_pairs={{0,128},{32,160},{64,192},{96,224},{128,0},{160,32},{192,64},{224,... | collective-permute-start | bytes 442376 | tf_op jit(solution)/shard_map/ppermute | solution.py:397
  10.7 0.3 collective-permute-start.1
  11.0 2.4 %collective-permute-start.2 = (bf16[576,128]{1,0:T(8,128)(2,1)S(1)}, bf16[576,128]{1,0:T(8,128)(2,1)S(1)}, u32[]{:S(2)}, u32[]{:S(2)}) collective-permute-start(bf16[576,128]{1,0:T(8,128)(2,1)S(1)} %get-tuple-element.24), channel_id=1, source_target_pairs={{0,192},{32,224},{64,0},{96,32},{128,64},{160,96},{192,128},{224,1... | collective-permute-start | bytes 442376 | tf_op jit(solution)/shard_map/ppermute | solution.py:397
  13.4 1.4 %back_tables.1 = (bf16[512,1024]{1,0:T(8,128)(2,1)S(1)}, bf16[1024,512]{1,0:T(8,128)(2,1)S(1)}) custom-call(s32[2]{0:T(128)S(1)} %copy-done.2, s32[2]{0:T(128)S(1)} %copy-done.3), custom_call_target="tpu_custom_call" | custom-call | flops 1000000000 | bytes 1048576 | tf_op jit(solution)/shard_map/back_tables/pallas_call | solution.py:428
  14.8 1.7 %collective-permute-done.3.refs_1_.refs_2_ = bf16[576,128]{1,0:T(8,128)(2,1)S(1)} collective-permute-done((bf16[576,128]{1,0:T(8,128)(2,1)S(1)}, bf16[576,128]{1,0:T(8,128)(2,1)S(1)}, u32[]{:S(2)}, u32[]{:S(2)}) %collective-permute-start.3) | collective-permute-done | bytes 147488 | tf_op jit(solution)/shard_map/ppermute | solution.py:397
  16.5 0.8 first_sums.1.refs_2_
  17.3 2.9 %collective-permute-done.1.refs_0_.refs_1_ = bf16[576,128]{1,0:T(8,128)(2,1)S(1)} collective-permute-done((bf16[576,128]{1,0:T(8,128)(2,1)S(1)}, bf16[576,128]{1,0:T(8,128)(2,1)S(1)}, u32[]{:S(2)}, u32[]{:S(2)}) %collective-permute-start.1) | collective-permute-done | bytes 147488 | tf_op jit(solution)/shard_map/ppermute | solution.py:397
  20.1 0.0 collective-permute-done.2.refs_1_.refs_3_
  20.1 0.0 copy-start.4
  20.1 0.8 gridding.1
  20.9 21.1 %all_to_all.10.pieces = bf16[32,40,128]{2,1,0:T(8,128)(2,1)S(1)} all-to-all(bf16[32,40,128]{2,1,0:T(8,128)(2,1)S(1)} %gridding.1), channel_id=1, replica_groups=mesh['frow'=8,'fcol'=32] {'fcol'}, dimensions={0} | all-to-all | bytes 655360 | tf_op jit(solution)/shard_map/all_to_all | solution.py:379
  42.0 0.1 pieces_sum.1
  42.1 15.6 %all_to_all.11.own = bf16[32,40,128]{2,1,0:T(8,128)(2,1)S(1)} all-to-all(bf16[32,40,128]{2,1,0:T(8,128)(2,1)S(1)} %pieces_sum.1), channel_id=1, replica_groups=mesh['frow'=8,'fcol'=32] {'fcol'}, dimensions={0} | all-to-all | bytes 655360 | tf_op jit(solution)/shard_map/all_to_all | solution.py:379
  57.7 4.5 %collective-permute-start.4 = (bf16[32,40,128]{2,1,0:T(8,128)(2,1)S(1)}, bf16[32,40,128]{2,1,0:T(8,128)(2,1)S(1)}, u32[]{:S(2)}, u32[]{:S(2)}) collective-permute-start(bf16[32,40,128]{2,1,0:T(8,128)(2,1)S(1)} %all_to_all.11.own), channel_id=1, source_target_pairs={{0,32},{32,0},{64,96},{96,64},{128,160},{160,128},{192,224},{224,1... | collective-permute-start | bytes 983048 | tf_op jit(solution)/shard_map/ppermute | solution.py:439
  62.2 1.3 %collective-permute-done.4.other = bf16[32,40,128]{2,1,0:T(8,128)(2,1)S(1)} collective-permute-done((bf16[32,40,128]{2,1,0:T(8,128)(2,1)S(1)}, bf16[32,40,128]{2,1,0:T(8,128)(2,1)S(1)}, u32[]{:S(2)}, u32[]{:S(2)}) %collective-permute-start.4) | collective-permute-done | bytes 327712 | tf_op jit(solution)/shard_map/ppermute | solution.py:439
  63.5 0.0 copy-done.4
  63.5 0.0 copy-done.5
  63.5 1.7 %grids.1 = (bf16[528,128]{1,0:T(8,128)(2,1)S(1)}, bf16[528,128]{1,0:T(8,128)(2,1)S(1)}, bf16[528,128]{1,0:T(8,128)(2,1)S(1)}, bf16[528,128]{1,0:T(8,128)(2,1)S(1)}, bf16[512,128]{1,0:T(8,128)(2,1)S(1)}) custom-call(bf16[32,40,128]{2,1,0:T(8,128)(2,1)S(1)} %all_to_all.11.own, bf16[32,40,128]{2,1,0:T(8,128)(2,1)S(1)} %collective-permute-done.4.other, ...), custom_call_target="tpu_custom_call" | custom-call | flops 1000000000 | bytes 1048576 | tf_op jit(solution)/shard_map/grids/pallas_call | solution.py:445
  65.2 1.8 %collective-permute-start.6 = (bf16[528,128]{1,0:T(8,128)(2,1)S(1)}, bf16[528,128]{1,0:T(8,128)(2,1)S(1)}, u32[]{:S(2)}, u32[]{:S(2)}) collective-permute-start(bf16[528,128]{1,0:T(8,128)(2,1)S(1)} %get-tuple-element.30), channel_id=1, source_target_pairs={{0,128},{32,160},{64,192},{96,224},{128,0},{160,32},{192,64},{224,... | collective-permute-start | bytes 405512 | tf_op jit(solution)/shard_map/ppermute | solution.py:397
  67.0 1.1 %collective-permute-start.5 = (bf16[528,128]{1,0:T(8,128)(2,1)S(1)}, bf16[528,128]{1,0:T(8,128)(2,1)S(1)}, u32[]{:S(2)}, u32[]{:S(2)}) collective-permute-start(bf16[528,128]{1,0:T(8,128)(2,1)S(1)} %get-tuple-element.29), channel_id=1, source_target_pairs={{0,64},{32,96},{64,128},{96,160},{128,192},{160,224},{192,0},{224,... | collective-permute-start | bytes 405512 | tf_op jit(solution)/shard_map/ppermute | solution.py:397
  68.1 1.6 %collective-permute-start.7 = (bf16[528,128]{1,0:T(8,128)(2,1)S(1)}, bf16[528,128]{1,0:T(8,128)(2,1)S(1)}, u32[]{:S(2)}, u32[]{:S(2)}) collective-permute-start(bf16[528,128]{1,0:T(8,128)(2,1)S(1)} %get-tuple-element.34), channel_id=1, source_target_pairs={{0,192},{32,224},{64,0},{96,32},{128,64},{160,96},{192,128},{224,1... | collective-permute-start | bytes 405512 | tf_op jit(solution)/shard_map/ppermute | solution.py:397
  69.6 0.4 first_part.1.first
  70.1 0.0 copy-start
  70.1 1.5 %collective-permute-done.6.own.refs_2_ = bf16[528,128]{1,0:T(8,128)(2,1)S(1)} collective-permute-done((bf16[528,128]{1,0:T(8,128)(2,1)S(1)}, bf16[528,128]{1,0:T(8,128)(2,1)S(1)}, u32[]{:S(2)}, u32[]{:S(2)}) %collective-permute-start.6) | collective-permute-done | bytes 135200 | tf_op jit(solution)/shard_map/ppermute | solution.py:397
  71.6 2.0 %collective-permute-start.10 = (bf16[528,128]{1,0:T(8,128)(2,1)S(1)}, bf16[528,128]{1,0:T(8,128)(2,1)S(1)}, u32[]{:S(2)}, u32[]{:S(2)}) collective-permute-start(bf16[528,128]{1,0:T(8,128)(2,1)S(1)} %collective-permute-done.6.own.refs_2_), channel_id=1, source_target_pairs={{0,32},{32,0},{64,96},{96,64},{128,160},{160,128},{192,224},{224,1... | collective-permute-start | bytes 405512 | tf_op jit(solution)/shard_map/ppermute | solution.py:460
  73.6 1.5 %collective-permute-done.5.refs_1_ = bf16[528,128]{1,0:T(8,128)(2,1)S(1)} collective-permute-done((bf16[528,128]{1,0:T(8,128)(2,1)S(1)}, bf16[528,128]{1,0:T(8,128)(2,1)S(1)}, u32[]{:S(2)}, u32[]{:S(2)}) %collective-permute-start.5) | collective-permute-done | bytes 135200 | tf_op jit(solution)/shard_map/ppermute | solution.py:397
  75.1 0.6 collective-permute-start.8
  75.7 0.0 collective-permute-done.7.refs_3_
  75.7 0.0 collective-permute-start.9
  75.7 0.0 collective-permute-done.10.rest
  75.7 0.7 own_column.1.refs_6_
  76.4 0.2 collective-permute-done.8.refs_4_
  76.7 0.4 collective-permute-done.9.refs_5_
  77.0 0.0 copy-done
  77.0 1.9 %image.1 = (f32[512,512]{1,0:T(8,128)}, f32[2,512]{1,0:T(2,128)}) custom-call(bf16[528,128]{1,0:T(8,128)(2,1)S(1)} %get-tuple-element.28.own.refs_0_, bf16[528,128]{1,0:T(8,128)(2,1)S(1)} %collective-permute-done.5.refs_1_, bf16[528,128]{1,0:T(8,128)(2,1)S(1)} %collective-permute-done.6.own.refs_2_, bf16[528,128]{1,0:T(8,128)(2,1)S(1)} %collective-permute-done.7.refs_3_, ...), custom_call_target="tpu_custom_call" | custom-call | flops 1000000000 | bytes 1048576 | tf_op jit(solution)/shard_map/image/pallas_call | solution.py:464
  (1 shorter events, 0.0 us)
Async XLA Ops:
  0.6 5.7 %copy-start.3 = (s32[2]{0:T(128)S(1)}, s32[2]{0:T(128)}, u32[]{:S(2)}) copy-start(s32[2]{0:T(128)} %offsets_col.1) | copy-start | bytes 28
  0.6 5.7 %copy-start.1 = (bf16[512,512]{1,0:T(8,128)(2,1)S(1)}, bf16[512,512]{1,0:T(8,128)(2,1)}, u32[]{:S(2)}) copy-start(bf16[512,512]{1,0:T(8,128)(2,1)} %facet.3) | copy-start | bytes 1572868
  0.7 5.7 %copy-start.2 = (s32[2]{0:T(128)S(1)}, s32[2]{0:T(128)}, u32[]{:S(2)}) copy-start(s32[2]{0:T(128)} %offsets_row.1) | copy-start | bytes 28
  3.0 5.3 %copy-start.6 = (bf16[16,256]{1,0:T(8,128)(2,1)S(1)}, bf16[16,256]{1,0:T(8,128)(2,1)}, u32[]{:S(2)}) copy-start(bf16[16,256]{1,0:T(8,128)(2,1)} %get-tuple-element.20.own_vis) | copy-start | bytes 24580
  3.0 5.2 %collective-permute-start = (bf16[528,512]{1,0:T(8,128)(2,1)}, bf16[528,512]{1,0:T(8,128)(2,1)S(1)}, u32[]{:S(2)}, u32[]{:S(2)}) collective-permute-start(bf16[528,512]{1,0:T(8,128)(2,1)} %get-tuple-element.21), channel_id=1, source_target_pairs={{0,32},{32,0},{64,96},{96,64},{128,160},{160,128},{192,224},{224,1... | collective-permute-start | bytes 1622024 | tf_op jit(solution)/shard_map/ppermute | solution.py:414
  9.6 6.9 %collective-permute-start.3 = (bf16[576,128]{1,0:T(8,128)(2,1)S(1)}, bf16[576,128]{1,0:T(8,128)(2,1)S(1)}, u32[]{:S(2)}, u32[]{:S(2)}) collective-permute-start(bf16[576,128]{1,0:T(8,128)(2,1)S(1)} %get-tuple-element.26), channel_id=1, source_target_pairs={{0,128},{32,160},{64,192},{96,224},{128,0},{160,32},{192,64},{224,... | collective-permute-start | bytes 442376 | tf_op jit(solution)/shard_map/ppermute | solution.py:397
  10.7 9.4 %collective-permute-start.1 = (bf16[576,128]{1,0:T(8,128)(2,1)S(1)}, bf16[576,128]{1,0:T(8,128)(2,1)S(1)}, u32[]{:S(2)}, u32[]{:S(2)}) collective-permute-start(bf16[576,128]{1,0:T(8,128)(2,1)S(1)} %get-tuple-element.23), channel_id=1, source_target_pairs={{0,64},{32,96},{64,128},{96,160},{128,192},{160,224},{192,0},{224,... | collective-permute-start | bytes 442376 | tf_op jit(solution)/shard_map/ppermute | solution.py:397
  11.0 9.1 %collective-permute-start.2 = (bf16[576,128]{1,0:T(8,128)(2,1)S(1)}, bf16[576,128]{1,0:T(8,128)(2,1)S(1)}, u32[]{:S(2)}, u32[]{:S(2)}) collective-permute-start(bf16[576,128]{1,0:T(8,128)(2,1)S(1)} %get-tuple-element.24), channel_id=1, source_target_pairs={{0,192},{32,224},{64,0},{96,32},{128,64},{160,96},{192,128},{224,1... | collective-permute-start | bytes 442376 | tf_op jit(solution)/shard_map/ppermute | solution.py:397
  20.1 43.4 %copy-start.4 = (bf16[512,512]{1,0:T(8,128)(2,1)S(1)}, bf16[512,512]{1,0:T(8,128)(2,1)}, u32[]{:S(2)}) copy-start(bf16[512,512]{1,0:T(8,128)(2,1)} %constant.4.clone.refs_4_.refs_7_) | copy-start | bytes 1572868
  20.1 43.4 %copy-start.5 = (bf16[512,512]{1,0:T(8,128)(2,1)S(1)}, bf16[512,512]{1,0:T(8,128)(2,1)}, u32[]{:S(2)}) copy-start(bf16[512,512]{1,0:T(8,128)(2,1)} %constant.5.clone.refs_5_.refs_6_) | copy-start | bytes 1572868
  57.7 5.8 %collective-permute-start.4 = (bf16[32,40,128]{2,1,0:T(8,128)(2,1)S(1)}, bf16[32,40,128]{2,1,0:T(8,128)(2,1)S(1)}, u32[]{:S(2)}, u32[]{:S(2)}) collective-permute-start(bf16[32,40,128]{2,1,0:T(8,128)(2,1)S(1)} %all_to_all.11.own), channel_id=1, source_target_pairs={{0,32},{32,0},{64,96},{96,64},{128,160},{160,128},{192,224},{224,1... | collective-permute-start | bytes 983048 | tf_op jit(solution)/shard_map/ppermute | solution.py:439
  65.2 6.4 %collective-permute-start.6 = (bf16[528,128]{1,0:T(8,128)(2,1)S(1)}, bf16[528,128]{1,0:T(8,128)(2,1)S(1)}, u32[]{:S(2)}, u32[]{:S(2)}) collective-permute-start(bf16[528,128]{1,0:T(8,128)(2,1)S(1)} %get-tuple-element.30), channel_id=1, source_target_pairs={{0,128},{32,160},{64,192},{96,224},{128,0},{160,32},{192,64},{224,... | collective-permute-start | bytes 405512 | tf_op jit(solution)/shard_map/ppermute | solution.py:397
  67.0 8.1 %collective-permute-start.5 = (bf16[528,128]{1,0:T(8,128)(2,1)S(1)}, bf16[528,128]{1,0:T(8,128)(2,1)S(1)}, u32[]{:S(2)}, u32[]{:S(2)}) collective-permute-start(bf16[528,128]{1,0:T(8,128)(2,1)S(1)} %get-tuple-element.29), channel_id=1, source_target_pairs={{0,64},{32,96},{64,128},{96,160},{128,192},{160,224},{192,0},{224,... | collective-permute-start | bytes 405512 | tf_op jit(solution)/shard_map/ppermute | solution.py:397
  68.1 7.6 %collective-permute-start.7 = (bf16[528,128]{1,0:T(8,128)(2,1)S(1)}, bf16[528,128]{1,0:T(8,128)(2,1)S(1)}, u32[]{:S(2)}, u32[]{:S(2)}) collective-permute-start(bf16[528,128]{1,0:T(8,128)(2,1)S(1)} %get-tuple-element.34), channel_id=1, source_target_pairs={{0,192},{32,224},{64,0},{96,32},{128,64},{160,96},{192,128},{224,1... | collective-permute-start | bytes 405512 | tf_op jit(solution)/shard_map/ppermute | solution.py:397
  70.1 6.9 %copy-start = (f32[2,512]{1,0:T(2,128)S(1)}, f32[2,512]{1,0:T(2,128)}, u32[]{:S(2)}) copy-start(f32[2,512]{1,0:T(2,128)} %refs_9_.1) | copy-start | bytes 12292
  71.6 4.1 %collective-permute-start.10 = (bf16[528,128]{1,0:T(8,128)(2,1)S(1)}, bf16[528,128]{1,0:T(8,128)(2,1)S(1)}, u32[]{:S(2)}, u32[]{:S(2)}) collective-permute-start(bf16[528,128]{1,0:T(8,128)(2,1)S(1)} %collective-permute-done.6.own.refs_2_), channel_id=1, source_target_pairs={{0,32},{32,0},{64,96},{96,64},{128,160},{160,128},{192,224},{224,1... | collective-permute-start | bytes 405512 | tf_op jit(solution)/shard_map/ppermute | solution.py:460
  75.1 1.6 %collective-permute-start.8 = (bf16[528,128]{1,0:T(8,128)(2,1)S(1)}, bf16[528,128]{1,0:T(8,128)(2,1)S(1)}, u32[]{:S(2)}, u32[]{:S(2)}) collective-permute-start(bf16[528,128]{1,0:T(8,128)(2,1)S(1)} %collective-permute-done.5.refs_1_), channel_id=1, source_target_pairs={{0,32},{32,0},{64,96},{96,64},{128,160},{160,128},{192,224},{224,1... | collective-permute-start | bytes 405512 | tf_op jit(solution)/shard_map/ppermute | solution.py:460
  75.7 1.4 %collective-permute-start.9 = (bf16[528,128]{1,0:T(8,128)(2,1)S(1)}, bf16[528,128]{1,0:T(8,128)(2,1)S(1)}, u32[]{:S(2)}, u32[]{:S(2)}) collective-permute-start(bf16[528,128]{1,0:T(8,128)(2,1)S(1)} %collective-permute-done.7.refs_3_), channel_id=1, source_target_pairs={{0,32},{32,0},{64,96},{96,64},{128,160},{160,128},{192,224},{224,1... | collective-permute-start | bytes 405512 | tf_op jit(solution)/shard_map/ppermute | solution.py:460

commit v11 on v10

--- a/solution.py
+++ b/solution.py
@@ -130,26 +130,22 @@
             spread(coarse, fine, store)
 
 
-def contributions_kernel(scale, own, own_vis, other, row_tab, *refs):
-    f32, bf16 = jnp.float32, jnp.bfloat16
-    outs, right = refs[:-1], refs[-1]
-    chip = place()[0] // 2
-    side = row_tab.shape[2] // 2
+def contribution_kernel(scale, number, own, own_vis, other, row_tab, out):
+    f32, bf16 = jnp.float32, jnp.bfloat16
+    side = own.shape[0]
     vis = []
-    right[:side] = own[...]
-    right[side:] = other[:side]
     for some in (own_vis[...], other[side:]):
         vis += [some[:, k * LANES:(k + 1) * LANES] for k in range(side // 2 // LANES)]
-    for n, out in enumerate(outs):
-        for k, some in enumerate(vis):
-            at = 2 * SG + 16 * k
-            out[at:at + 16] = some
-        r, c = split_number(chip + n)
-        some = right[:, pl.ds(pl.multiple_of(c * SG, SG), SG)]
-        with_cos = jnp.dot(row_tab[2 * r], some, preferred_element_type=f32)
-        with_sin = jnp.dot(row_tab[2 * r + 1], some, preferred_element_type=f32)
-        out[:SG] = ((with_cos[:, :HALF] - with_sin[:, HALF:]) * scale).astype(bf16)
-        out[SG:2 * SG] = (-(with_cos[:, HALF:] + with_sin[:, :HALF]) * scale).astype(bf16)
+    for k, some in enumerate(vis):
+        at = 2 * SG + 16 * k
+        out[at:at + 16] = some
+    r, c = split_number(place()[0] // 2 + number)
+    at = pl.ds(pl.multiple_of(c * SG, SG), SG)
+    right = jnp.concatenate([own[:, at], other[:side, at]], 0)
+    with_cos = jnp.dot(row_tab[2 * r], right, preferred_element_type=f32)
+    with_sin = jnp.dot(row_tab[2 * r + 1], right, preferred_element_type=f32)
+    out[:SG] = ((with_cos[:, :HALF] - with_sin[:, HALF:]) * scale).astype(bf16)
+    out[SG:2 * SG] = (-(with_cos[:, HALF:] + with_sin[:, :HALF]) * scale).astype(bf16)
 
 
 def split_number(number):
@@ -210,24 +206,39 @@
         out[j] = total
 
 
-def grids_kernel(chips, own, other, *refs):
+def lay_out(pieces, half, planes, lanes_at):
+    f32, bf16 = jnp.float32, jnp.bfloat16
+    each = SG // pieces.shape[0]
+    for j in range(pieces.shape[0]):
+        some = pieces[j].astype(f32)
+        for p in range(5):
+            planes[p, j * each:(j + 1) * each, lanes_at] = some[p * each:(p + 1) * each]
+
+    def step(forward):
+        rows = [pl.ds(pl.multiple_of(p * SG + half * HALF, HALF), HALF) for p in range(2)]
+        left = jnp.concatenate([planes[p, :, lanes_at].astype(bf16) for p in range(2)], 1)
+        right = jnp.concatenate([forward[at] for at in rows], 0)
+        return jnp.dot(left, right, preferred_element_type=f32)
+
+    return step
+
+
+def own_half_kernel(pieces, forward, out, wide, planes):
+    wide[...] = lay_out(pieces, place()[0] % 2, planes, slice(0, HALF))(forward)
+    out[...] = planes[2:]
+
+
+def grids_kernel(chips, own, own_wide, other, *refs):
     f32, bf16 = jnp.float32, jnp.bfloat16
     parts, (grid_left, forward, inverse_left, inverse) = refs[:chips], refs[chips:chips + 4]
     outs, rest, (planes, cat, tall, hat) = refs[chips + 4:-5], refs[-5], refs[-4:]
     row_index, _ = place()
     core = row_index % 2
     chip = (row_index // 2).astype(f32)
-    count = own.shape[0]
-    each = SG // count
-    for pieces, half in ((own, core), (other, 1 - core)):
-        at = pl.ds(pl.multiple_of(half * HALF, HALF), HALF)
-        for j in range(count):
-            some = pieces[j].astype(f32)
-            for p in range(5):
-                planes[p, j * each:(j + 1) * each, at] = some[p * each:(p + 1) * each]
-    cat[:, :SG] = planes[0].astype(bf16)
-    cat[:, SG:] = planes[1].astype(bf16)
-    wide = jnp.dot(cat[...], forward[...], preferred_element_type=f32).astype(bf16)
+    at = [pl.ds(pl.multiple_of(half * HALF, HALF), HALF) for half in (core, 1 - core)]
+    wide = (own_wide[...] + lay_out(other, 1 - core, planes, at[1])(forward)).astype(bf16)
+    for p in range(3):
+        planes[2 + p, :, at[0]] = own[p]
     tall[:SG] = wide[:, :SG]
     tall[SG:] = wide[:, SG:]
     model = jnp.dot(grid_left[...], tall[...], preferred_element_type=f32) * (1.0 / SG)
@@ -418,10 +429,13 @@
         scratch=[pltpu.VMEM((side, 4 * HALF), bf16)], cost=10**9,
     )(row_offsets, col_offsets, facet)
     vis_rows_count = 8 * 2 * n_vis // LANES
-    parts = call(
-        functools.partial(contributions_kernel, scale_in), (shape(2 * SG + vis_rows_count, HALF),) * chips,
-        "contributions", "vvvv", scratch=[pltpu.VMEM((2 * side, 4 * HALF), bf16)], cost=2 * 10**9,
-    )(own, vis, other, row_tab)
+    parts = {}
+    for k in (2, 1, 3, 0):
+        parts[k] = call(
+            functools.partial(contribution_kernel, scale_in, k), shape(2 * SG + vis_rows_count, HALF), "contribution",
+            "vvvv", cost=5 * 10**8,
+        )(own, vis, other, row_tab)
+        own, parts[k] = lax.optimization_barrier((own, parts[k]))
     parts = turned(parts)
 
     sums = call(first_sums_kernel, shape(5, SG, HALF, dtype=f32), "first_sums", "vv", cost=10**9)(parts[0], parts[2])
@@ -442,15 +456,19 @@
     block = [np.concatenate(pair, 1) for pair in ((kcos, ksin), (-ksin, kcos), (kcos, -ksin), (ksin, kcos))]
     forward_block = np.concatenate([block[0], block[1]], 0)
     inverse_block = np.concatenate([block[2], block[3]], 0)
+    own_planes, own_wide = call(
+        own_half_kernel, (shape(3, SG, HALF, dtype=f32), shape(SG, 2 * SG, dtype=f32)), "own_half", "vv",
+        scratch=[pltpu.VMEM((5, SG, HALF), f32)], cost=10**9,
+    )(pieces, forward_block)
     *back, rest = call(
         functools.partial(grids_kernel, chips), (shape(2 * SG + 16, HALF),) * chips + (shape(2 * SG, HALF),), "grids",
-        "v" * (6 + chips),
+        "v" * (7 + chips),
         scratch=[
             pltpu.VMEM((5, SG, SG), f32), pltpu.VMEM((SG, 2 * SG), bf16), pltpu.VMEM((2 * SG, SG), bf16),
             pltpu.VMEM((SG, 2 * SG), bf16),
         ],
         cost=10**9,
-    )(pieces, pieces_other, *parts, inverse_block, forward_block, forward_block, inverse_block)
+    )(own_planes, own_wide, pieces_other, *parts, inverse_block, forward_block, forward_block, inverse_block)
     back = turned(back)
 
     both = pltpu.VMEM((side, 2 * SG), bf16)

time: 79.3 us -> 79.2 us (level)
  waiting for transfers between devices: 9.41 us -> 7.77 us
    ppermute x6, waiting for transfers between devices: 7.55 us -> 6.26 us  [turned(): moved = {k: lax.ppermute(blocks[k], 'frow', turns[k]) for k in (2, 1, 3)}]
    pallas_call x1 -> x5, Pallas kernels: 1.33 us -> 2.06 us  [the longest x4 1.82 us: shards(): call(functools.partial(contribution_kernel, scale_in, k), shape(2 * SG +...]
  transfers between devices with their start and end apart: 11 -> 11, of which waited for: 7 -> 8; matrix products, arithmetic and copies ran while one was open for 0% -> 0% of each run, Pallas kernels for 7% -> 8%
where the time goes in v11:
time: 79.2 us; the launch traced here: 79 us
  blocking collectives  36.8 us (46%)
  starting transfers between devices  19.4 us (24%)
  Pallas kernels  14 us (18%)
  waiting for transfers between devices  7.77 us (10%)
  between operations  0.95 us (1%)
    all_to_all x2, blocking collectives, exchange(): lax.all_to_all(blocks, axes, 0, 0, tiled=True, axis_index_groups=groups)  36.8 us
    ppermute x6, starting transfers between devices, turned(): moved = {k: lax.ppermute(blocks[k], 'frow', turns[k]) for k in (2, 1, 3)}  8.54 us
    ppermute x6, waiting for transfers between devices, turned(): moved = {k: lax.ppermute(blocks[k], 'frow', turns[k]) for k in (2, 1, 3)}  6.26 us
    ppermute x1, starting transfers between devices, shards(): pieces_other = lax.ppermute(pieces, 'frow', swap)  4.7 us
    ppermute x1, starting transfers between devices, shards(): other = lax.ppermute(send, 'frow', swap)  3.32 us
    ppermute x3, starting transfers between devices, shards(): rest = {k: lax.ppermute(back[k], 'frow', swap) for k in (2, 1, 3)}  2.86 us
    pallas_call x1, Pallas kernels, shards(): call(functools.partial(send_columns_kernel, cols_count), (shape(side + 16...  2.34 us
    pallas_call x1, Pallas kernels, shards(): call(functools.partial(own_tables_kernel, rows_count, cols_count), (shape...  1.9 us
  transfers between devices with their start and end apart: 11, of which 8 were waited for; matrix products, arithmetic and copies ran while one was open for 0% of the time, Pallas kernels for 8%

profile of v11, /device:TPU:1, one launch (start us, length us, event | category | flops | bytes accessed | tf_op | source)
XLA Modules:
  0.0 79.0 jit_solution(7276717205254251749)
XLA Ops:
  0.6 0.0 copy-start.6
  0.6 0.0 copy-start.4
  0.7 0.0 copy-start.5
  0.7 2.3 %send_columns.1 = (bf16[528,512]{1,0:T(8,128)(2,1)}, bf16[16,256]{1,0:T(8,128)(2,1)}) custom-call(s32[2]{0:T(128)} %offsets_col.1, bf16[512,512]{1,0:T(8,128)(2,1)} %facet.3, s32[1,512]{1,0:T(1,128)} %bitcast.3, s32[1,512]{1,0:T(1,128)} %bitcast.4, s32[1,512]{1,0:T(1,128)} %bitcast.5, f32[2,512]{1,0:T(2,128)} %refs_9_.1), custom_call_target="tpu_custom_call" | custom-call | flops 1000000000 | bytes 1048576 | tf_op jit(solution)/shard_map/send_columns/pallas_call | solution.py:415
  3.0 0.0 copy-start.2
  3.0 3.3 %collective-permute-start = (bf16[528,512]{1,0:T(8,128)(2,1)}, bf16[528,512]{1,0:T(8,128)(2,1)S(1)}, u32[]{:S(2)}, u32[]{:S(2)}) collective-permute-start(bf16[528,512]{1,0:T(8,128)(2,1)} %get-tuple-element.26), channel_id=1, source_target_pairs={{0,32},{32,0},{64,96},{96,64},{128,160},{160,128},{192,224},{224,1... | collective-permute-start | bytes 1622024 | tf_op jit(solution)/shard_map/ppermute | solution.py:425
  6.3 0.0 copy-done.6
  6.3 0.0 copy-done.4
  6.3 0.0 copy-done.5
  6.3 1.9 %own_tables.1 = (bf16[512,512]{1,0:T(8,128)(2,1)S(1)}, bf16[4,256,1024]{2,1,0:T(8,128)(2,1)S(1)}) custom-call(s32[2]{0:T(128)S(1)} %copy-done.5, s32[2]{0:T(128)S(1)} %copy-done.6, bf16[512,512]{1,0:T(8,128)(2,1)S(1)} %copy-done.4), custom_call_target="tpu_custom_call" | custom-call | flops 1000000000 | bytes 1048576 | tf_op jit(solution)/shard_map/own_tables/pallas_call | solution.py:426
  8.3 0.0 collective-permute-done.other
  8.3 0.5 contribution.4
  8.7 0.5 contribution.5
  9.2 1.1 %collective-permute-start.3 = (bf16[576,128]{1,0:T(8,128)(2,1)S(1)}, bf16[576,128]{1,0:T(8,128)(2,1)S(1)}, u32[]{:S(2)}, u32[]{:S(2)}) collective-permute-start(bf16[576,128]{1,0:T(8,128)(2,1)S(1)} %contribution.4), channel_id=1, source_target_pairs={{0,128},{32,160},{64,192},{96,224},{128,0},{160,32},{192,64},{224,... | collective-permute-start | bytes 442376 | tf_op jit(solution)/shard_map/ppermute | solution.py:408
  10.3 0.4 contribution.6
  10.7 0.9 %collective-permute-start.2 = (bf16[576,128]{1,0:T(8,128)(2,1)S(1)}, bf16[576,128]{1,0:T(8,128)(2,1)S(1)}, u32[]{:S(2)}, u32[]{:S(2)}) collective-permute-start(bf16[576,128]{1,0:T(8,128)(2,1)S(1)} %contribution.6), channel_id=1, source_target_pairs={{0,192},{32,224},{64,0},{96,32},{128,64},{160,96},{192,128},{224,1... | collective-permute-start | bytes 442376 | tf_op jit(solution)/shard_map/ppermute | solution.py:408
  11.7 0.6 collective-permute-start.1
  12.3 1.4 %back_tables.1 = (bf16[512,1024]{1,0:T(8,128)(2,1)S(1)}, bf16[1024,512]{1,0:T(8,128)(2,1)S(1)}) custom-call(s32[2]{0:T(128)S(1)} %copy-done.5, s32[2]{0:T(128)S(1)} %copy-done.6), custom_call_target="tpu_custom_call" | custom-call | flops 1000000000 | bytes 1048576 | tf_op jit(solution)/shard_map/back_tables/pallas_call | solution.py:442
  13.7 0.5 contribution.7.refs_0_
  14.1 1.9 %collective-permute-done.3.refs_1_.refs_2_ = bf16[576,128]{1,0:T(8,128)(2,1)S(1)} collective-permute-done((bf16[576,128]{1,0:T(8,128)(2,1)S(1)}, bf16[576,128]{1,0:T(8,128)(2,1)S(1)}, u32[]{:S(2)}, u32[]{:S(2)}) %collective-permute-start.3) | collective-permute-done | bytes 147488 | tf_op jit(solution)/shard_map/ppermute | solution.py:408
  16.1 0.8 first_sums.1.refs_2_
  16.8 0.7 collective-permute-done.2.refs_1_.refs_3_
  17.6 1.9 %collective-permute-done.1.refs_0_.refs_1_ = bf16[576,128]{1,0:T(8,128)(2,1)S(1)} collective-permute-done((bf16[576,128]{1,0:T(8,128)(2,1)S(1)}, bf16[576,128]{1,0:T(8,128)(2,1)S(1)}, u32[]{:S(2)}, u32[]{:S(2)}) %collective-permute-start.1) | collective-permute-done | bytes 147488 | tf_op jit(solution)/shard_map/ppermute | solution.py:408
  19.4 0.8 gridding.1
  20.2 20.3 %all_to_all.10.pieces = bf16[32,40,128]{2,1,0:T(8,128)(2,1)S(1)} all-to-all(bf16[32,40,128]{2,1,0:T(8,128)(2,1)S(1)} %gridding.1), channel_id=1, replica_groups=mesh['frow'=8,'fcol'=32] {'fcol'}, dimensions={0} | all-to-all | bytes 655360 | tf_op jit(solution)/shard_map/all_to_all | solution.py:390
  40.5 0.1 pieces_sum.1
  40.6 0.0 copy-start.1
  40.6 16.5 %all_to_all.11.pieces = bf16[32,40,128]{2,1,0:T(8,128)(2,1)S(1)} all-to-all(bf16[32,40,128]{2,1,0:T(8,128)(2,1)S(1)} %pieces_sum.1), channel_id=1, replica_groups=mesh['frow'=8,'fcol'=32] {'fcol'}, dimensions={0} | all-to-all | bytes 655360 | tf_op jit(solution)/shard_map/all_to_all | solution.py:390
  57.1 4.7 %collective-permute-start.4 = (bf16[32,40,128]{2,1,0:T(8,128)(2,1)S(1)}, bf16[32,40,128]{2,1,0:T(8,128)(2,1)S(1)}, u32[]{:S(2)}, u32[]{:S(2)}) collective-permute-start(bf16[32,40,128]{2,1,0:T(8,128)(2,1)S(1)} %all_to_all.11.pieces), channel_id=1, source_target_pairs={{0,32},{32,0},{64,96},{96,64},{128,160},{160,128},{192,224},{224,1... | collective-permute-start | bytes 983048 | tf_op jit(solution)/shard_map/ppermute | solution.py:453
  61.8 0.2 own_half.1
  62.1 1.0 %collective-permute-done.4.other = bf16[32,40,128]{2,1,0:T(8,128)(2,1)S(1)} collective-permute-done((bf16[32,40,128]{2,1,0:T(8,128)(2,1)S(1)}, bf16[32,40,128]{2,1,0:T(8,128)(2,1)S(1)}, u32[]{:S(2)}, u32[]{:S(2)}) %collective-permute-start.4) | collective-permute-done | bytes 327712 | tf_op jit(solution)/shard_map/ppermute | solution.py:453
  63.1 1.6 %grids.1 = (bf16[528,128]{1,0:T(8,128)(2,1)S(1)}, bf16[528,128]{1,0:T(8,128)(2,1)S(1)}, bf16[528,128]{1,0:T(8,128)(2,1)S(1)}, bf16[528,128]{1,0:T(8,128)(2,1)S(1)}, bf16[512,128]{1,0:T(8,128)(2,1)S(1)}) custom-call(f32[3,256,128]{2,1,0:T(8,128)S(1)} %get-tuple-element.36.own, f32[256,512]{1,0:T(8,128)S(1)} %get-tuple-element.37.own_wide, ...), custom_call_target="tpu_custom_call" | custom-call | flops 1000000000 | bytes 1048576 | tf_op jit(solution)/shard_map/grids/pallas_call | solution.py:463
  64.7 3.2 %collective-permute-start.6 = (bf16[528,128]{1,0:T(8,128)(2,1)S(1)}, bf16[528,128]{1,0:T(8,128)(2,1)S(1)}, u32[]{:S(2)}, u32[]{:S(2)}) collective-permute-start(bf16[528,128]{1,0:T(8,128)(2,1)S(1)} %get-tuple-element.40), channel_id=1, source_target_pairs={{0,128},{32,160},{64,192},{96,224},{128,0},{160,32},{192,64},{224,... | collective-permute-start | bytes 405512 | tf_op jit(solution)/shard_map/ppermute | solution.py:408
  67.9 0.3 collective-permute-start.5
  68.2 2.4 %collective-permute-start.7 = (bf16[528,128]{1,0:T(8,128)(2,1)S(1)}, bf16[528,128]{1,0:T(8,128)(2,1)S(1)}, u32[]{:S(2)}, u32[]{:S(2)}) collective-permute-start(bf16[528,128]{1,0:T(8,128)(2,1)S(1)} %get-tuple-element.44), channel_id=1, source_target_pairs={{0,192},{32,224},{64,0},{96,32},{128,64},{160,96},{192,128},{224,1... | collective-permute-start | bytes 405512 | tf_op jit(solution)/shard_map/ppermute | solution.py:408
  70.6 0.4 first_part.1.first
  71.0 0.0 copy-start.3
  71.1 0.4 collective-permute-done.6.own.refs_2_
  71.5 1.6 %collective-permute-start.10 = (bf16[528,128]{1,0:T(8,128)(2,1)S(1)}, bf16[528,128]{1,0:T(8,128)(2,1)S(1)}, u32[]{:S(2)}, u32[]{:S(2)}) collective-permute-start(bf16[528,128]{1,0:T(8,128)(2,1)S(1)} %collective-permute-done.6.own.refs_2_), channel_id=1, source_target_pairs={{0,32},{32,0},{64,96},{96,64},{128,160},{160,128},{192,224},{224,1... | collective-permute-start | bytes 405512 | tf_op jit(solution)/shard_map/ppermute | solution.py:478
  73.1 1.4 %collective-permute-done.5.refs_1_ = bf16[528,128]{1,0:T(8,128)(2,1)S(1)} collective-permute-done((bf16[528,128]{1,0:T(8,128)(2,1)S(1)}, bf16[528,128]{1,0:T(8,128)(2,1)S(1)}, u32[]{:S(2)}, u32[]{:S(2)}) %collective-permute-start.5) | collective-permute-done | bytes 135200 | tf_op jit(solution)/shard_map/ppermute | solution.py:408
  74.5 1.1 %collective-permute-start.8 = (bf16[528,128]{1,0:T(8,128)(2,1)S(1)}, bf16[528,128]{1,0:T(8,128)(2,1)S(1)}, u32[]{:S(2)}, u32[]{:S(2)}) collective-permute-start(bf16[528,128]{1,0:T(8,128)(2,1)S(1)} %collective-permute-done.5.refs_1_), channel_id=1, source_target_pairs={{0,32},{32,0},{64,96},{96,64},{128,160},{160,128},{192,224},{224,1... | collective-permute-start | bytes 405512 | tf_op jit(solution)/shard_map/ppermute | solution.py:478
  75.6 0.0 collective-permute-done.7.refs_3_
  75.6 0.1 collective-permute-start.9
  75.7 0.0 collective-permute-done.10.rest
  75.7 0.7 own_column.1.refs_6_
  76.4 0.1 collective-permute-done.8.refs_4_
  76.6 0.4 collective-permute-done.9.refs_5_
  76.9 1.9 %image.1 = (f32[512,512]{1,0:T(8,128)}, f32[2,512]{1,0:T(2,128)}) custom-call(bf16[528,128]{1,0:T(8,128)(2,1)S(1)} %get-tuple-element.38.own.refs_0_, bf16[528,128]{1,0:T(8,128)(2,1)S(1)} %collective-permute-done.5.refs_1_, bf16[528,128]{1,0:T(8,128)(2,1)S(1)} %collective-permute-done.6.own.refs_2_, bf16[528,128]{1,0:T(8,128)(2,1)S(1)} %collective-permute-done.7.refs_3_, ...), custom_call_target="tpu_custom_call" | custom-call | flops 1000000000 | bytes 1048576 | tf_op jit(solution)/shard_map/image/pallas_call | solution.py:482
  (5 shorter events, 0.0 us)
Async XLA Ops:
  0.6 5.7 %copy-start.6 = (s32[2]{0:T(128)S(1)}, s32[2]{0:T(128)}, u32[]{:S(2)}) copy-start(s32[2]{0:T(128)} %offsets_col.1) | copy-start | bytes 28
  0.6 5.7 %copy-start.4 = (bf16[512,512]{1,0:T(8,128)(2,1)S(1)}, bf16[512,512]{1,0:T(8,128)(2,1)}, u32[]{:S(2)}) copy-start(bf16[512,512]{1,0:T(8,128)(2,1)} %facet.3) | copy-start | bytes 1572868
  0.7 5.7 %copy-start.5 = (s32[2]{0:T(128)S(1)}, s32[2]{0:T(128)}, u32[]{:S(2)}) copy-start(s32[2]{0:T(128)} %offsets_row.1) | copy-start | bytes 28
  3.0 5.3 %copy-start.2 = (bf16[16,256]{1,0:T(8,128)(2,1)S(1)}, bf16[16,256]{1,0:T(8,128)(2,1)}, u32[]{:S(2)}) copy-start(bf16[16,256]{1,0:T(8,128)(2,1)} %get-tuple-element.25.own_vis) | copy-start | bytes 24580
  3.0 5.2 %collective-permute-start = (bf16[528,512]{1,0:T(8,128)(2,1)}, bf16[528,512]{1,0:T(8,128)(2,1)S(1)}, u32[]{:S(2)}, u32[]{:S(2)}) collective-permute-start(bf16[528,512]{1,0:T(8,128)(2,1)} %get-tuple-element.26), channel_id=1, source_target_pairs={{0,32},{32,0},{64,96},{96,64},{128,160},{160,128},{192,224},{224,1... | collective-permute-start | bytes 1622024 | tf_op jit(solution)/shard_map/ppermute | solution.py:425
  9.2 6.9 %collective-permute-start.3 = (bf16[576,128]{1,0:T(8,128)(2,1)S(1)}, bf16[576,128]{1,0:T(8,128)(2,1)S(1)}, u32[]{:S(2)}, u32[]{:S(2)}) collective-permute-start(bf16[576,128]{1,0:T(8,128)(2,1)S(1)} %contribution.4), channel_id=1, source_target_pairs={{0,128},{32,160},{64,192},{96,224},{128,0},{160,32},{192,64},{224,... | collective-permute-start | bytes 442376 | tf_op jit(solution)/shard_map/ppermute | solution.py:408
  10.7 6.8 %collective-permute-start.2 = (bf16[576,128]{1,0:T(8,128)(2,1)S(1)}, bf16[576,128]{1,0:T(8,128)(2,1)S(1)}, u32[]{:S(2)}, u32[]{:S(2)}) collective-permute-start(bf16[576,128]{1,0:T(8,128)(2,1)S(1)} %contribution.6), channel_id=1, source_target_pairs={{0,192},{32,224},{64,0},{96,32},{128,64},{160,96},{192,128},{224,1... | collective-permute-start | bytes 442376 | tf_op jit(solution)/shard_map/ppermute | solution.py:408
  11.7 7.7 %collective-permute-start.1 = (bf16[576,128]{1,0:T(8,128)(2,1)S(1)}, bf16[576,128]{1,0:T(8,128)(2,1)S(1)}, u32[]{:S(2)}, u32[]{:S(2)}) collective-permute-start(bf16[576,128]{1,0:T(8,128)(2,1)S(1)} %contribution.5), channel_id=1, source_target_pairs={{0,64},{32,96},{64,128},{96,160},{128,192},{160,224},{192,0},{224,... | collective-permute-start | bytes 442376 | tf_op jit(solution)/shard_map/ppermute | solution.py:408
  19.4 42.4 %copy-start = (bf16[512,512]{1,0:T(8,128)(2,1)S(1)}, bf16[512,512]{1,0:T(8,128)(2,1)}, u32[]{:S(2)}) copy-start(bf16[512,512]{1,0:T(8,128)(2,1)} %constant.4.clone.forward.refs_5_.refs_6_) | copy-start | bytes 1572868
  40.6 22.5 %copy-start.1 = (bf16[512,512]{1,0:T(8,128)(2,1)S(1)}, bf16[512,512]{1,0:T(8,128)(2,1)}, u32[]{:S(2)}) copy-start(bf16[512,512]{1,0:T(8,128)(2,1)} %constant.5.clone.refs_4_.refs_7_) | copy-start | bytes 1572868
  57.1 6.0 %collective-permute-start.4 = (bf16[32,40,128]{2,1,0:T(8,128)(2,1)S(1)}, bf16[32,40,128]{2,1,0:T(8,128)(2,1)S(1)}, u32[]{:S(2)}, u32[]{:S(2)}) collective-permute-start(bf16[32,40,128]{2,1,0:T(8,128)(2,1)S(1)} %all_to_all.11.pieces), channel_id=1, source_target_pairs={{0,32},{32,0},{64,96},{96,64},{128,160},{160,128},{192,224},{224,1... | collective-permute-start | bytes 983048 | tf_op jit(solution)/shard_map/ppermute | solution.py:453
  64.7 6.7 %collective-permute-start.6 = (bf16[528,128]{1,0:T(8,128)(2,1)S(1)}, bf16[528,128]{1,0:T(8,128)(2,1)S(1)}, u32[]{:S(2)}, u32[]{:S(2)}) collective-permute-start(bf16[528,128]{1,0:T(8,128)(2,1)S(1)} %get-tuple-element.40), channel_id=1, source_target_pairs={{0,128},{32,160},{64,192},{96,224},{128,0},{160,32},{192,64},{224,... | collective-permute-start | bytes 405512 | tf_op jit(solution)/shard_map/ppermute | solution.py:408
  67.9 6.5 %collective-permute-start.5 = (bf16[528,128]{1,0:T(8,128)(2,1)S(1)}, bf16[528,128]{1,0:T(8,128)(2,1)S(1)}, u32[]{:S(2)}, u32[]{:S(2)}) collective-permute-start(bf16[528,128]{1,0:T(8,128)(2,1)S(1)} %get-tuple-element.39), channel_id=1, source_target_pairs={{0,64},{32,96},{64,128},{96,160},{128,192},{160,224},{192,0},{224,... | collective-permute-start | bytes 405512 | tf_op jit(solution)/shard_map/ppermute | solution.py:408
  68.2 7.3 %collective-permute-start.7 = (bf16[528,128]{1,0:T(8,128)(2,1)S(1)}, bf16[528,128]{1,0:T(8,128)(2,1)S(1)}, u32[]{:S(2)}, u32[]{:S(2)}) collective-permute-start(bf16[528,128]{1,0:T(8,128)(2,1)S(1)} %get-tuple-element.44), channel_id=1, source_target_pairs={{0,192},{32,224},{64,0},{96,32},{128,64},{160,96},{192,128},{224,1... | collective-permute-start | bytes 405512 | tf_op jit(solution)/shard_map/ppermute | solution.py:408
  71.0 5.9 %copy-start.3 = (f32[2,512]{1,0:T(2,128)S(1)}, f32[2,512]{1,0:T(2,128)}, u32[]{:S(2)}) copy-start(f32[2,512]{1,0:T(2,128)} %refs_9_.1) | copy-start | bytes 12292
  71.5 4.2 %collective-permute-start.10 = (bf16[528,128]{1,0:T(8,128)(2,1)S(1)}, bf16[528,128]{1,0:T(8,128)(2,1)S(1)}, u32[]{:S(2)}, u32[]{:S(2)}) collective-permute-start(bf16[528,128]{1,0:T(8,128)(2,1)S(1)} %collective-permute-done.6.own.refs_2_), channel_id=1, source_target_pairs={{0,32},{32,0},{64,96},{96,64},{128,160},{160,128},{192,224},{224,1... | collective-permute-start | bytes 405512 | tf_op jit(solution)/shard_map/ppermute | solution.py:478
  74.5 2.1 %collective-permute-start.8 = (bf16[528,128]{1,0:T(8,128)(2,1)S(1)}, bf16[528,128]{1,0:T(8,128)(2,1)S(1)}, u32[]{:S(2)}, u32[]{:S(2)}) collective-permute-start(bf16[528,128]{1,0:T(8,128)(2,1)S(1)} %collective-permute-done.5.refs_1_), channel_id=1, source_target_pairs={{0,32},{32,0},{64,96},{96,64},{128,160},{160,128},{192,224},{224,1... | collective-permute-start | bytes 405512 | tf_op jit(solution)/shard_map/ppermute | solution.py:478
  75.6 1.4 %collective-permute-start.9 = (bf16[528,128]{1,0:T(8,128)(2,1)S(1)}, bf16[528,128]{1,0:T(8,128)(2,1)S(1)}, u32[]{:S(2)}, u32[]{:S(2)}) collective-permute-start(bf16[528,128]{1,0:T(8,128)(2,1)S(1)} %collective-permute-done.7.refs_3_), channel_id=1, source_target_pairs={{0,32},{32,0},{64,96},{96,64},{128,160},{160,128},{192,224},{224,1... | collective-permute-start | bytes 405512 | tf_op jit(solution)/shard_map/ppermute | solution.py:478

commit v12 on v11

--- a/solution.py
+++ b/solution.py
@@ -16,6 +16,7 @@
 NC = 2
 HALF = SG // 2
 LANES = 128
+BOTH = ("frow", "fcol")
 
 
 def wave(count):
@@ -51,6 +52,11 @@
 
 def place():
     return lax.axis_index("frow"), lax.axis_index("fcol")
+
+
+def served():
+    row_index, col_index = place()
+    return lax.rem(row_index // 2 + col_index, NR * NC)
 
 
 def half_columns(cols_count, offsets, half, side, col_tab):
@@ -139,7 +145,7 @@
     for k, some in enumerate(vis):
         at = 2 * SG + 16 * k
         out[at:at + 16] = some
-    r, c = split_number(place()[0] // 2 + number)
+    r, c = split_number(served() + number)
     at = pl.ds(pl.multiple_of(c * SG, SG), SG)
     right = jnp.concatenate([own[:, at], other[:side, at]], 0)
     with_cos = jnp.dot(row_tab[2 * r], right, preferred_element_type=f32)
@@ -163,7 +169,7 @@
 def grid_sums(parts):
     f32, bf16 = jnp.float32, jnp.bfloat16
     row_index, _ = place()
-    chip = (row_index // 2).astype(f32)
+    chip = served().astype(f32)
     v_at = (sublanes(HALF) + (row_index % 2) * HALF).astype(f32)
     counter = sublanes(SG).astype(f32)
     total = jnp.zeros((SG, 3 * HALF), f32)
@@ -234,7 +240,7 @@
     outs, rest, (planes, cat, tall, hat) = refs[chips + 4:-5], refs[-5], refs[-4:]
     row_index, _ = place()
     core = row_index % 2
-    chip = (row_index // 2).astype(f32)
+    chip = served().astype(f32)
     at = [pl.ds(pl.multiple_of(half * HALF, HALF), HALF) for half in (core, 1 - core)]
     wide = (own_wide[...] + lay_out(other, 1 - core, planes, at[1])(forward)).astype(bf16)
     for p in range(3):
@@ -309,7 +315,7 @@
 
 
 def first_part_kernel(own, rest, row_tab, out):
-    chip = place()[0] // 2
+    chip = served()
     for n, block in enumerate((own, rest)):
         out[:, n * SG:(n + 1) * SG] = block_part(block, chip, row_tab)
 
@@ -325,7 +331,7 @@
 
 
 def own_column_kernel(chips, opposite, own, rest, first, row_tab, col_tab, out, both):
-    chip = place()[0] // 2
+    chip = served()
     for n, block in enumerate((own, rest)):
         part = first[:, n * SG:(n + 1) * SG] + block_part(block, chip + chips - opposite, row_tab)
         both[:, half_lanes(n)] = part.astype(jnp.bfloat16)
@@ -336,7 +342,7 @@
     f32, bf16 = jnp.float32, jnp.bfloat16
     blocks, others, refs = refs[:chips], refs[chips:chips + 2], refs[chips + 2:]
     first, row_tab, col_tab, observed, out, residual, both, image, seen, sems = refs
-    chip = place()[0] // 2
+    chip = served()
     model = jnp.zeros((16, LANES), f32)
     for block in blocks:
         model = model + block[2 * SG:].astype(f32)
@@ -402,26 +408,40 @@
     chips = rows_count // 2
     each = SG // cols_count
     swap = [(index, index ^ 1) for index in range(rows_count)]
-    turns = [[(index, (index + 2 * k) % rows_count) for index in range(rows_count)] for k in range(chips)]
+    line = NR * NC
+
+    def turn(index, k):
+        row, col = index // cols_count, index % cols_count
+        if row % 2 == 0:
+            row = (row + 2 * k) % rows_count
+        else:
+            col = col // line * line + (col + k) % line
+        return row * cols_count + col
+
+    turns = [[(index, turn(index, k)) for index in range(rows_count * cols_count)] for k in range(chips)]
+    groups = [
+        [((number - col) % line * 2 + core) * cols_count + col for col in range(cols_count)]
+        for number in range(line) for core in range(2)
+    ]
 
     def turned(blocks):
-        moved = {k: lax.ppermute(blocks[k], "frow", turns[k]) for k in (2, 1, 3)}
+        moved = {k: lax.ppermute(blocks[k], BOTH, turns[k]) for k in (2, 1, 3)}
         return [blocks[0]] + [moved[k] for k in range(1, chips)]
 
     scale_in = 1.0 / (side * math.sqrt(rows_count * cols_count))
     scale_out = 1.0 / (SG * math.sqrt(NR * NC))
-    line = (1, n_vis)
+    flat = (1, n_vis)
 
     send, vis = call(
         functools.partial(send_columns_kernel, cols_count), (shape(side + 16, 4 * HALF), shape(16, n_vis // 2)),
         "send_columns", "aaaaaa",
         scratch=[
-            pltpu.VMEM((side, 4 * HALF), bf16), pltpu.VMEM((side, side), bf16), pltpu.VMEM((3,) + line, jnp.int32),
+            pltpu.VMEM((side, 4 * HALF), bf16), pltpu.VMEM((side, side), bf16), pltpu.VMEM((3,) + flat, jnp.int32),
             pltpu.VMEM((2, n_vis), f32), pltpu.SMEM((NC,), jnp.int32), pltpu.VMEM((side, 4 * HALF), bf16),
             pltpu.VMEM((16, n_vis), bf16), pltpu.SemaphoreType.DMA((10,)),
         ],
         cost=10**9, room=60, outs="aa",
-    )(col_offsets, facet, vis_subgrid.reshape(line), vis_u.reshape(line), vis_v.reshape(line), observed)
+    )(col_offsets, facet, vis_subgrid.reshape(flat), vis_u.reshape(flat), vis_v.reshape(flat), observed)
     other = lax.ppermute(send, "frow", swap)
     own, row_tab = call(
         functools.partial(own_tables_kernel, rows_count, cols_count),
@@ -447,9 +467,9 @@
         gridding_kernel, shape(cols_count, 5 * each, HALF), "gridding", "v" * (chips - 1) + "a",
         scratch=[pltpu.VMEM((5, SG, HALF), f32)], cost=10**9,
     )(parts[1], parts[3], sums, back_col)
-    pieces = exchange(pieces, "fcol", None)
+    pieces = exchange(pieces, BOTH, groups)
     pieces = call(pieces_sum_kernel, shape(cols_count, 5 * each, HALF), "pieces_sum", "v", cost=10**6)(pieces)
-    pieces = exchange(pieces, "fcol", None)
+    pieces = exchange(pieces, BOTH, groups)
     pieces_other = lax.ppermute(pieces, "frow", swap)
 
     kcos, ksin = grid_tables()

time: 79.2 us -> 79.9 us (level)
  blocking collectives: 36.8 us -> 42.4 us
  starting transfers between devices: 19.4 us -> 16.2 us
  waiting for transfers between devices: 7.77 us -> 6.17 us
    all_to_all x2, blocking collectives: 36.8 us -> 42.4 us  [exchange(): lax.all_to_all(blocks, axes, 0, 0, tiled=True, axis_index_groups=groups)]
    ppermute x6, starting transfers between devices: 8.54 us -> 5.86 us  [turned(): moved = {k: lax.ppermute(blocks[k], BOTH, turns[k]) for k in (2, 1, 3)}]
    ppermute x6, waiting for transfers between devices: 6.26 us -> 4.56 us  [turned(): moved = {k: lax.ppermute(blocks[k], BOTH, turns[k]) for k in (2, 1, 3)}]
  transfers between devices with their start and end apart: 11 -> 11, of which waited for: 8 -> 7; matrix products, arithmetic and copies ran while one was open for 0% -> 0% of each run, Pallas kernels for 8% -> 8%
where the time goes in v12:
time: 79.9 us; the launch traced here: 79.8 us
  blocking collectives  42.4 us (53%)
  starting transfers between devices  16.2 us (20%)
  Pallas kernels  14 us (18%)
  waiting for transfers between devices  6.17 us (8%)
  between operations  0.96 us (1%)
    all_to_all x2, blocking collectives, exchange(): lax.all_to_all(blocks, axes, 0, 0, tiled=True, axis_index_groups=groups)  42.4 us
    ppermute x6, starting transfers between devices, turned(): moved = {k: lax.ppermute(blocks[k], BOTH, turns[k]) for k in (2, 1, 3)}  5.86 us
    ppermute x6, waiting for transfers between devices, turned(): moved = {k: lax.ppermute(blocks[k], BOTH, turns[k]) for k in (2, 1, 3)}  4.56 us
    ppermute x1, starting transfers between devices, shards(): pieces_other = lax.ppermute(pieces, 'frow', swap)  4.49 us
    ppermute x1, starting transfers between devices, shards(): other = lax.ppermute(send, 'frow', swap)  3.32 us
    ppermute x3, starting transfers between devices, shards(): rest = {k: lax.ppermute(back[k], 'frow', swap) for k in (2, 1, 3)}  2.52 us
    pallas_call x1, Pallas kernels, shards(): call(functools.partial(send_columns_kernel, cols_count), (shape(side + 16...  2.34 us
    pallas_call x1, Pallas kernels, shards(): call(functools.partial(own_tables_kernel, rows_count, cols_count), (shape...  1.9 us
  transfers between devices with their start and end apart: 11, of which 7 were waited for; matrix products, arithmetic and copies ran while one was open for 0% of the time, Pallas kernels for 8%

profile of v12, /device:TPU:1, one launch (start us, length us, event | category | flops | bytes accessed | tf_op | source)
XLA Modules:
  0.0 79.8 jit_solution(8630671131897003510)
XLA Ops:
  0.6 0.0 copy-start.6
  0.6 0.0 copy-start.4
  0.7 0.0 copy-start.5
  0.7 2.3 %send_columns.1 = (bf16[528,512]{1,0:T(8,128)(2,1)}, bf16[16,256]{1,0:T(8,128)(2,1)}) custom-call(s32[2]{0:T(128)} %offsets_col.1, bf16[512,512]{1,0:T(8,128)(2,1)} %facet.3, s32[1,512]{1,0:T(1,128)} %bitcast.3, s32[1,512]{1,0:T(1,128)} %bitcast.4, s32[1,512]{1,0:T(1,128)} %bitcast.5, f32[2,512]{1,0:T(2,128)} %refs_9_.1), custom_call_target="tpu_custom_call" | custom-call | flops 1000000000 | bytes 1048576 | tf_op jit(solution)/shard_map/send_columns/pallas_call | solution.py:435
  3.0 0.0 copy-start.2
  3.0 3.3 %collective-permute-start = (bf16[528,512]{1,0:T(8,128)(2,1)}, bf16[528,512]{1,0:T(8,128)(2,1)S(1)}, u32[]{:S(2)}, u32[]{:S(2)}) collective-permute-start(bf16[528,512]{1,0:T(8,128)(2,1)} %get-tuple-element.26), channel_id=1, source_target_pairs={{0,32},{32,0},{64,96},{96,64},{128,160},{160,128},{192,224},{224,1... | collective-permute-start | bytes 1622024 | tf_op jit(solution)/shard_map/ppermute | solution.py:445
  6.3 0.0 copy-done.6
  6.3 0.0 copy-done.4
  6.3 1.9 %own_tables.1 = (bf16[512,512]{1,0:T(8,128)(2,1)S(1)}, bf16[4,256,1024]{2,1,0:T(8,128)(2,1)S(1)}) custom-call(s32[2]{0:T(128)S(1)} %copy-done.5, s32[2]{0:T(128)S(1)} %copy-done.6, bf16[512,512]{1,0:T(8,128)(2,1)S(1)} %copy-done.4), custom_call_target="tpu_custom_call" | custom-call | flops 1000000000 | bytes 1048576 | tf_op jit(solution)/shard_map/own_tables/pallas_call | solution.py:446
  8.3 0.0 collective-permute-done.other
  8.3 0.5 contribution.4
  8.7 0.5 contribution.5
  9.2 1.3 %collective-permute-start.3 = (bf16[576,128]{1,0:T(8,128)(2,1)S(1)}, bf16[576,128]{1,0:T(8,128)(2,1)S(1)}, u32[]{:S(2)}, u32[]{:S(2)}) collective-permute-start(bf16[576,128]{1,0:T(8,128)(2,1)S(1)} %contribution.4), channel_id=1, source_target_pairs={{0,128},{1,129},{2,130},{3,131},{4,132},{5,133},{6,134},{7,135},{8... | collective-permute-start | bytes 442376 | tf_op jit(solution)/shard_map/ppermute | solution.py:428
  10.5 0.4 contribution.6
  10.9 0.9 %collective-permute-start.2 = (bf16[576,128]{1,0:T(8,128)(2,1)S(1)}, bf16[576,128]{1,0:T(8,128)(2,1)S(1)}, u32[]{:S(2)}, u32[]{:S(2)}) collective-permute-start(bf16[576,128]{1,0:T(8,128)(2,1)S(1)} %contribution.6), channel_id=1, source_target_pairs={{0,192},{1,193},{2,194},{3,195},{4,196},{5,197},{6,198},{7,199},{8... | collective-permute-start | bytes 442376 | tf_op jit(solution)/shard_map/ppermute | solution.py:428
  11.8 0.7 collective-permute-start.1
  12.5 1.4 %back_tables.1 = (bf16[512,1024]{1,0:T(8,128)(2,1)S(1)}, bf16[1024,512]{1,0:T(8,128)(2,1)S(1)}) custom-call(s32[2]{0:T(128)S(1)} %copy-done.5, s32[2]{0:T(128)S(1)} %copy-done.6), custom_call_target="tpu_custom_call" | custom-call | flops 1000000000 | bytes 1048576 | tf_op jit(solution)/shard_map/back_tables/pallas_call | solution.py:462
  13.9 0.5 contribution.7.refs_0_
  14.3 0.8 collective-permute-done.3.refs_1_.refs_2_
  15.1 0.8 first_sums.1.refs_2_
  15.9 0.0 collective-permute-done.2.refs_1_.refs_3_
  15.9 1.4 %collective-permute-done.1.refs_0_.refs_1_ = bf16[576,128]{1,0:T(8,128)(2,1)S(1)} collective-permute-done((bf16[576,128]{1,0:T(8,128)(2,1)S(1)}, bf16[576,128]{1,0:T(8,128)(2,1)S(1)}, u32[]{:S(2)}, u32[]{:S(2)}) %collective-permute-start.1) | collective-permute-done | bytes 147488 | tf_op jit(solution)/shard_map/ppermute | solution.py:428
  17.3 0.8 gridding.1
  18.0 24.2 %all_to_all.10.pieces = bf16[32,40,128]{2,1,0:T(8,128)(2,1)S(1)} all-to-all(bf16[32,40,128]{2,1,0:T(8,128)(2,1)S(1)} %gridding.1), channel_id=1, replica_groups={{0,193,130,67,4,197,134,71,8,201,138,75,12,205,142,79,16,209,146,83,20,..., dimensions={0} | all-to-all | bytes 655360 | tf_op jit(solution)/shard_map/all_to_all | solution.py:396
  42.2 0.1 pieces_sum.1
  42.3 0.0 copy-start.1
  42.3 18.2 %all_to_all.11.pieces = bf16[32,40,128]{2,1,0:T(8,128)(2,1)S(1)} all-to-all(bf16[32,40,128]{2,1,0:T(8,128)(2,1)S(1)} %pieces_sum.1), channel_id=1, replica_groups={{0,193,130,67,4,197,134,71,8,201,138,75,12,205,142,79,16,209,146,83,20,..., dimensions={0} | all-to-all | bytes 655360 | tf_op jit(solution)/shard_map/all_to_all | solution.py:396
  60.5 4.5 %collective-permute-start.4 = (bf16[32,40,128]{2,1,0:T(8,128)(2,1)S(1)}, bf16[32,40,128]{2,1,0:T(8,128)(2,1)S(1)}, u32[]{:S(2)}, u32[]{:S(2)}) collective-permute-start(bf16[32,40,128]{2,1,0:T(8,128)(2,1)S(1)} %all_to_all.11.pieces), channel_id=1, source_target_pairs={{0,32},{32,0},{64,96},{96,64},{128,160},{160,128},{192,224},{224,1... | collective-permute-start | bytes 983048 | tf_op jit(solution)/shard_map/ppermute | solution.py:473
  65.0 0.2 own_half.1
  65.3 1.0 %collective-permute-done.4.other = bf16[32,40,128]{2,1,0:T(8,128)(2,1)S(1)} collective-permute-done((bf16[32,40,128]{2,1,0:T(8,128)(2,1)S(1)}, bf16[32,40,128]{2,1,0:T(8,128)(2,1)S(1)}, u32[]{:S(2)}, u32[]{:S(2)}) %collective-permute-start.4) | collective-permute-done | bytes 327712 | tf_op jit(solution)/shard_map/ppermute | solution.py:473
  66.3 0.0 copy-done.1
  66.3 1.6 %grids.1 = (bf16[528,128]{1,0:T(8,128)(2,1)S(1)}, bf16[528,128]{1,0:T(8,128)(2,1)S(1)}, bf16[528,128]{1,0:T(8,128)(2,1)S(1)}, bf16[528,128]{1,0:T(8,128)(2,1)S(1)}, bf16[512,128]{1,0:T(8,128)(2,1)S(1)}) custom-call(f32[3,256,128]{2,1,0:T(8,128)S(1)} %get-tuple-element.36.own, f32[256,512]{1,0:T(8,128)S(1)} %get-tuple-element.37.own_wide, ...), custom_call_target="tpu_custom_call" | custom-call | flops 1000000000 | bytes 1048576 | tf_op jit(solution)/shard_map/grids/pallas_call | solution.py:483
  67.9 0.4 collective-permute-start.6
  68.3 1.2 %collective-permute-start.5 = (bf16[528,128]{1,0:T(8,128)(2,1)S(1)}, bf16[528,128]{1,0:T(8,128)(2,1)S(1)}, u32[]{:S(2)}, u32[]{:S(2)}) collective-permute-start(bf16[528,128]{1,0:T(8,128)(2,1)S(1)} %get-tuple-element.39), channel_id=1, source_target_pairs={{0,64},{1,65},{2,66},{3,67},{4,68},{5,69},{6,70},{7,71},{8,72},{9,... | collective-permute-start | bytes 405512 | tf_op jit(solution)/shard_map/ppermute | solution.py:428
  69.5 1.4 %collective-permute-start.7 = (bf16[528,128]{1,0:T(8,128)(2,1)S(1)}, bf16[528,128]{1,0:T(8,128)(2,1)S(1)}, u32[]{:S(2)}, u32[]{:S(2)}) collective-permute-start(bf16[528,128]{1,0:T(8,128)(2,1)S(1)} %get-tuple-element.44), channel_id=1, source_target_pairs={{0,192},{1,193},{2,194},{3,195},{4,196},{5,197},{6,198},{7,199},{8... | collective-permute-start | bytes 405512 | tf_op jit(solution)/shard_map/ppermute | solution.py:428
  71.0 0.4 first_part.1.first
  71.4 0.0 copy-start.3
  71.4 2.3 %collective-permute-done.6.own.refs_2_ = bf16[528,128]{1,0:T(8,128)(2,1)S(1)} collective-permute-done((bf16[528,128]{1,0:T(8,128)(2,1)S(1)}, bf16[528,128]{1,0:T(8,128)(2,1)S(1)}, u32[]{:S(2)}, u32[]{:S(2)}) %collective-permute-start.6) | collective-permute-done | bytes 135200 | tf_op jit(solution)/shard_map/ppermute | solution.py:428
  73.7 1.3 %collective-permute-start.10 = (bf16[528,128]{1,0:T(8,128)(2,1)S(1)}, bf16[528,128]{1,0:T(8,128)(2,1)S(1)}, u32[]{:S(2)}, u32[]{:S(2)}) collective-permute-start(bf16[528,128]{1,0:T(8,128)(2,1)S(1)} %collective-permute-done.6.own.refs_2_), channel_id=1, source_target_pairs={{0,32},{32,0},{64,96},{96,64},{128,160},{160,128},{192,224},{224,1... | collective-permute-start | bytes 405512 | tf_op jit(solution)/shard_map/ppermute | solution.py:498
  75.0 0.1 collective-permute-done.5.refs_1_
  75.1 1.2 %collective-permute-start.8 = (bf16[528,128]{1,0:T(8,128)(2,1)S(1)}, bf16[528,128]{1,0:T(8,128)(2,1)S(1)}, u32[]{:S(2)}, u32[]{:S(2)}) collective-permute-start(bf16[528,128]{1,0:T(8,128)(2,1)S(1)} %collective-permute-done.5.refs_1_), channel_id=1, source_target_pairs={{0,32},{32,0},{64,96},{96,64},{128,160},{160,128},{192,224},{224,1... | collective-permute-start | bytes 405512 | tf_op jit(solution)/shard_map/ppermute | solution.py:498
  76.3 0.0 collective-permute-done.7.refs_3_
  76.3 0.0 collective-permute-start.9
  76.3 0.0 collective-permute-done.10.rest
  76.4 0.7 own_column.1.refs_6_
  77.1 0.2 collective-permute-done.8.refs_4_
  77.3 0.4 collective-permute-done.9.refs_5_
  77.7 1.9 %image.1 = (f32[512,512]{1,0:T(8,128)}, f32[2,512]{1,0:T(2,128)}) custom-call(bf16[528,128]{1,0:T(8,128)(2,1)S(1)} %get-tuple-element.38.own.refs_0_, bf16[528,128]{1,0:T(8,128)(2,1)S(1)} %collective-permute-done.5.refs_1_, bf16[528,128]{1,0:T(8,128)(2,1)S(1)} %collective-permute-done.6.own.refs_2_, bf16[528,128]{1,0:T(8,128)(2,1)S(1)} %collective-permute-done.7.refs_3_, ...), custom_call_target="tpu_custom_call" | custom-call | flops 1000000000 | bytes 1048576 | tf_op jit(solution)/shard_map/image/pallas_call | solution.py:502
  (5 shorter events, 0.0 us)
Async XLA Ops:
  0.6 5.7 %copy-start.6 = (s32[2]{0:T(128)S(1)}, s32[2]{0:T(128)}, u32[]{:S(2)}) copy-start(s32[2]{0:T(128)} %offsets_col.1) | copy-start | bytes 28
  0.6 5.7 %copy-start.4 = (bf16[512,512]{1,0:T(8,128)(2,1)S(1)}, bf16[512,512]{1,0:T(8,128)(2,1)}, u32[]{:S(2)}) copy-start(bf16[512,512]{1,0:T(8,128)(2,1)} %facet.3) | copy-start | bytes 1572868
  0.7 5.7 %copy-start.5 = (s32[2]{0:T(128)S(1)}, s32[2]{0:T(128)}, u32[]{:S(2)}) copy-start(s32[2]{0:T(128)} %offsets_row.1) | copy-start | bytes 28
  3.0 5.3 %copy-start.2 = (bf16[16,256]{1,0:T(8,128)(2,1)S(1)}, bf16[16,256]{1,0:T(8,128)(2,1)}, u32[]{:S(2)}) copy-start(bf16[16,256]{1,0:T(8,128)(2,1)} %get-tuple-element.25.own_vis) | copy-start | bytes 24580
  3.0 5.2 %collective-permute-start = (bf16[528,512]{1,0:T(8,128)(2,1)}, bf16[528,512]{1,0:T(8,128)(2,1)S(1)}, u32[]{:S(2)}, u32[]{:S(2)}) collective-permute-start(bf16[528,512]{1,0:T(8,128)(2,1)} %get-tuple-element.26), channel_id=1, source_target_pairs={{0,32},{32,0},{64,96},{96,64},{128,160},{160,128},{192,224},{224,1... | collective-permute-start | bytes 1622024 | tf_op jit(solution)/shard_map/ppermute | solution.py:445
  9.2 5.9 %collective-permute-start.3 = (bf16[576,128]{1,0:T(8,128)(2,1)S(1)}, bf16[576,128]{1,0:T(8,128)(2,1)S(1)}, u32[]{:S(2)}, u32[]{:S(2)}) collective-permute-start(bf16[576,128]{1,0:T(8,128)(2,1)S(1)} %contribution.4), channel_id=1, source_target_pairs={{0,128},{1,129},{2,130},{3,131},{4,132},{5,133},{6,134},{7,135},{8... | collective-permute-start | bytes 442376 | tf_op jit(solution)/shard_map/ppermute | solution.py:428
  10.9 5.0 %collective-permute-start.2 = (bf16[576,128]{1,0:T(8,128)(2,1)S(1)}, bf16[576,128]{1,0:T(8,128)(2,1)S(1)}, u32[]{:S(2)}, u32[]{:S(2)}) collective-permute-start(bf16[576,128]{1,0:T(8,128)(2,1)S(1)} %contribution.6), channel_id=1, source_target_pairs={{0,192},{1,193},{2,194},{3,195},{4,196},{5,197},{6,198},{7,199},{8... | collective-permute-start | bytes 442376 | tf_op jit(solution)/shard_map/ppermute | solution.py:428
  11.8 5.5 %collective-permute-start.1 = (bf16[576,128]{1,0:T(8,128)(2,1)S(1)}, bf16[576,128]{1,0:T(8,128)(2,1)S(1)}, u32[]{:S(2)}, u32[]{:S(2)}) collective-permute-start(bf16[576,128]{1,0:T(8,128)(2,1)S(1)} %contribution.5), channel_id=1, source_target_pairs={{0,64},{1,65},{2,66},{3,67},{4,68},{5,69},{6,70},{7,71},{8,72},{9,... | collective-permute-start | bytes 442376 | tf_op jit(solution)/shard_map/ppermute | solution.py:428
  17.3 47.8 %copy-start = (bf16[512,512]{1,0:T(8,128)(2,1)S(1)}, bf16[512,512]{1,0:T(8,128)(2,1)}, u32[]{:S(2)}) copy-start(bf16[512,512]{1,0:T(8,128)(2,1)} %constant.4.clone.forward.refs_5_.refs_6_) | copy-start | bytes 1572868
  42.3 24.0 %copy-start.1 = (bf16[512,512]{1,0:T(8,128)(2,1)S(1)}, bf16[512,512]{1,0:T(8,128)(2,1)}, u32[]{:S(2)}) copy-start(bf16[512,512]{1,0:T(8,128)(2,1)} %constant.5.clone.refs_4_.refs_7_) | copy-start | bytes 1572868
  60.5 5.7 %collective-permute-start.4 = (bf16[32,40,128]{2,1,0:T(8,128)(2,1)S(1)}, bf16[32,40,128]{2,1,0:T(8,128)(2,1)S(1)}, u32[]{:S(2)}, u32[]{:S(2)}) collective-permute-start(bf16[32,40,128]{2,1,0:T(8,128)(2,1)S(1)} %all_to_all.11.pieces), channel_id=1, source_target_pairs={{0,32},{32,0},{64,96},{96,64},{128,160},{160,128},{192,224},{224,1... | collective-permute-start | bytes 983048 | tf_op jit(solution)/shard_map/ppermute | solution.py:473
  67.9 5.8 %collective-permute-start.6 = (bf16[528,128]{1,0:T(8,128)(2,1)S(1)}, bf16[528,128]{1,0:T(8,128)(2,1)S(1)}, u32[]{:S(2)}, u32[]{:S(2)}) collective-permute-start(bf16[528,128]{1,0:T(8,128)(2,1)S(1)} %get-tuple-element.40), channel_id=1, source_target_pairs={{0,128},{1,129},{2,130},{3,131},{4,132},{5,133},{6,134},{7,135},{8... | collective-permute-start | bytes 405512 | tf_op jit(solution)/shard_map/ppermute | solution.py:428
  68.3 6.8 %collective-permute-start.5 = (bf16[528,128]{1,0:T(8,128)(2,1)S(1)}, bf16[528,128]{1,0:T(8,128)(2,1)S(1)}, u32[]{:S(2)}, u32[]{:S(2)}) collective-permute-start(bf16[528,128]{1,0:T(8,128)(2,1)S(1)} %get-tuple-element.39), channel_id=1, source_target_pairs={{0,64},{1,65},{2,66},{3,67},{4,68},{5,69},{6,70},{7,71},{8,72},{9,... | collective-permute-start | bytes 405512 | tf_op jit(solution)/shard_map/ppermute | solution.py:428
  69.5 6.8 %collective-permute-start.7 = (bf16[528,128]{1,0:T(8,128)(2,1)S(1)}, bf16[528,128]{1,0:T(8,128)(2,1)S(1)}, u32[]{:S(2)}, u32[]{:S(2)}) collective-permute-start(bf16[528,128]{1,0:T(8,128)(2,1)S(1)} %get-tuple-element.44), channel_id=1, source_target_pairs={{0,192},{1,193},{2,194},{3,195},{4,196},{5,197},{6,198},{7,199},{8... | collective-permute-start | bytes 405512 | tf_op jit(solution)/shard_map/ppermute | solution.py:428
  71.4 6.3 %copy-start.3 = (f32[2,512]{1,0:T(2,128)S(1)}, f32[2,512]{1,0:T(2,128)}, u32[]{:S(2)}) copy-start(f32[2,512]{1,0:T(2,128)} %refs_9_.1) | copy-start | bytes 12292
  73.7 2.6 %collective-permute-start.10 = (bf16[528,128]{1,0:T(8,128)(2,1)S(1)}, bf16[528,128]{1,0:T(8,128)(2,1)S(1)}, u32[]{:S(2)}, u32[]{:S(2)}) collective-permute-start(bf16[528,128]{1,0:T(8,128)(2,1)S(1)} %collective-permute-done.6.own.refs_2_), channel_id=1, source_target_pairs={{0,32},{32,0},{64,96},{96,64},{128,160},{160,128},{192,224},{224,1... | collective-permute-start | bytes 405512 | tf_op jit(solution)/shard_map/ppermute | solution.py:498
  75.1 2.2 %collective-permute-start.8 = (bf16[528,128]{1,0:T(8,128)(2,1)S(1)}, bf16[528,128]{1,0:T(8,128)(2,1)S(1)}, u32[]{:S(2)}, u32[]{:S(2)}) collective-permute-start(bf16[528,128]{1,0:T(8,128)(2,1)S(1)} %collective-permute-done.5.refs_1_), channel_id=1, source_target_pairs={{0,32},{32,0},{64,96},{96,64},{128,160},{160,128},{192,224},{224,1... | collective-permute-start | bytes 405512 | tf_op jit(solution)/shard_map/ppermute | solution.py:498
  76.3 1.4 %collective-permute-start.9 = (bf16[528,128]{1,0:T(8,128)(2,1)S(1)}, bf16[528,128]{1,0:T(8,128)(2,1)S(1)}, u32[]{:S(2)}, u32[]{:S(2)}) collective-permute-start(bf16[528,128]{1,0:T(8,128)(2,1)S(1)} %collective-permute-done.7.refs_3_), channel_id=1, source_target_pairs={{0,32},{32,0},{64,96},{96,64},{128,160},{160,128},{192,224},{224,1... | collective-permute-start | bytes 405512 | tf_op jit(solution)/shard_map/ppermute | solution.py:498

commit v13 on v11

--- a/solution.py
+++ b/solution.py
@@ -228,13 +228,9 @@
     out[...] = planes[2:]
 
 
-def grids_kernel(chips, own, own_wide, other, *refs):
-    f32, bf16 = jnp.float32, jnp.bfloat16
-    parts, (grid_left, forward, inverse_left, inverse) = refs[:chips], refs[chips:chips + 4]
-    outs, rest, (planes, cat, tall, hat) = refs[chips + 4:-5], refs[-5], refs[-4:]
-    row_index, _ = place()
-    core = row_index % 2
-    chip = (row_index // 2).astype(f32)
+def grids_kernel(own, own_wide, other, grid_left, forward, inverse_left, inverse, mine, rest, hat, planes, cat, tall):
+    f32, bf16 = jnp.float32, jnp.bfloat16
+    core = place()[0] % 2
     at = [pl.ds(pl.multiple_of(half * HALF, HALF), HALF) for half in (core, 1 - core)]
     wide = (own_wide[...] + lay_out(other, 1 - core, planes, at[1])(forward)).astype(bf16)
     for p in range(3):
@@ -252,11 +248,16 @@
         tall[k * SG:(k + 1) * SG] = wide[:, k * SG:(k + 1) * SG].astype(bf16)
     back = jnp.dot(inverse_left[...], tall[...], preferred_element_type=f32) * (1.0 / SG)
     rest[...] = jnp.where(core == 0, back[:, HALF:], back[:, :HALF]).astype(bf16)
-    back = jnp.where(core == 0, back[:, :HALF], back[:, HALF:]).astype(bf16)
+    mine[...] = jnp.where(core == 0, back[:, :HALF], back[:, HALF:]).astype(bf16)
+
+
+def answers_kernel(chips, hat, *refs):
+    f32, bf16 = jnp.float32, jnp.bfloat16
+    parts, outs = refs[:chips], refs[chips:]
+    chip = (place()[0] // 2).astype(f32)
     counter = sublanes(SG).astype(f32)
     vis_each = (parts[0].shape[0] - 2 * SG) // 2
     for k, out in enumerate(outs):
-        out[:2 * SG] = back
         ask = vis_rows(parts[-k % chips][2 * SG:2 * SG + vis_each].astype(f32))
         u_here = jnp.where(ask[0:1] == chip, ask[1:2], -1.0)
         hot = jnp.where(u_here == counter, 1.0, 0.0).astype(bf16)
@@ -267,7 +268,7 @@
             value = jnp.sum(jnp.where(pick, line[part * SG:(part + 1) * SG], 0.0), axis=0, keepdims=True)
             rows += [value[:, i * LANES:(i + 1) * LANES] for i in range(value.shape[1] // LANES)]
         rows.append(jnp.zeros((16 - len(rows), LANES), f32))
-        out[2 * SG:] = jnp.concatenate(rows, 0).astype(bf16)
+        out[...] = jnp.concatenate(rows, 0).astype(bf16)
 
 
 def back_tables_kernel(rows_count, cols_count, side, offsets_row, offsets_col, row_tab, col_tab):
@@ -334,12 +335,12 @@
 
 def image_kernel(scale, chips, *refs):
     f32, bf16 = jnp.float32, jnp.bfloat16
-    blocks, others, refs = refs[:chips], refs[chips:chips + 2], refs[chips + 2:]
+    answers, blocks, others, refs = refs[:chips], refs[chips:chips + 2], refs[chips + 2:chips + 4], refs[chips + 4:]
     first, row_tab, col_tab, observed, out, residual, both, image, seen, sems = refs
     chip = place()[0] // 2
     model = jnp.zeros((16, LANES), f32)
-    for block in blocks:
-        model = model + block[2 * SG:].astype(f32)
+    for answer in answers:
+        model = model + answer[...].astype(f32)
     count = observed.shape[1] // LANES
     for part in range(2):
         for i in range(count):
@@ -347,7 +348,7 @@
             seen[part:part + 1, at] = observed[part:part + 1, at] - model[part * count + i:part * count + i + 1]
     writes = [pltpu.make_async_copy(seen, residual, sems.at[0])]
     writes[0].start()
-    for n, pair in enumerate(((blocks[1], blocks[3]), others)):
+    for n, pair in enumerate((blocks, others)):
         part = block_part(pair[0], chip + chips - 1, row_tab) + block_part(pair[1], chip + chips - 3, row_tab)
         both[:, half_lanes(n)] = part.astype(bf16)
     chunks = sems.shape[0] - 1
@@ -460,31 +461,34 @@
         own_half_kernel, (shape(3, SG, HALF, dtype=f32), shape(SG, 2 * SG, dtype=f32)), "own_half", "vv",
         scratch=[pltpu.VMEM((5, SG, HALF), f32)], cost=10**9,
     )(pieces, forward_block)
-    *back, rest = call(
-        functools.partial(grids_kernel, chips), (shape(2 * SG + 16, HALF),) * chips + (shape(2 * SG, HALF),), "grids",
-        "v" * (7 + chips),
+    mine, rest, hat = call(
+        grids_kernel, (shape(2 * SG, HALF), shape(2 * SG, HALF), shape(SG, 2 * SG)), "grids", "v" * 7,
         scratch=[
             pltpu.VMEM((5, SG, SG), f32), pltpu.VMEM((SG, 2 * SG), bf16), pltpu.VMEM((2 * SG, SG), bf16),
-            pltpu.VMEM((SG, 2 * SG), bf16),
         ],
         cost=10**9,
-    )(own_planes, own_wide, pieces_other, *parts, inverse_block, forward_block, forward_block, inverse_block)
-    back = turned(back)
+    )(own_planes, own_wide, pieces_other, inverse_block, forward_block, forward_block, inverse_block)
+    back = turned([mine] * chips)
 
     both = pltpu.VMEM((side, 2 * SG), bf16)
     square = shape(side, side, dtype=f32)
     first = call(first_part_kernel, square, "first_part", "vvv", cost=10**9)(back[0], rest, back_row)
-    back[2], first = lax.optimization_barrier((back[2], first))
+    first, hat = lax.optimization_barrier((first, hat))
+    *answers, = call(
+        functools.partial(answers_kernel, chips), (shape(16, LANES),) * chips, "answers", "v" * (1 + chips), cost=10**9
+    )(hat, *parts)
+    answers = turned(answers)
+    back[2], *answers = lax.optimization_barrier((back[2], *answers))
     rest = {k: lax.ppermute(back[k], "frow", swap) for k in (2, 1, 3)}
     first = call(
         functools.partial(own_column_kernel, chips, 2), square, "own_column", "v" * 5, scratch=[both], cost=10**9
     )(back[2], rest[2], first, back_row, back_col)
     return call(
         functools.partial(image_kernel, scale_out, chips), (square, shape(2, n_vis, dtype=f32)), "image",
-        "v" * (chips + 6), outs="aa",
+        "v" * (chips + 8), outs="aa",
         scratch=[both, pltpu.VMEM((side, side), f32), pltpu.VMEM((2, n_vis), f32), pltpu.SemaphoreType.DMA((5,))],
         cost=10**9,
-    )(*back, rest[1], rest[3], first, back_row, back_col, observed)
+    )(*answers, back[1], back[3], rest[1], rest[3], first, back_row, back_col, observed)
 
 
 def solution(mesh):

time: 79.2 us -> 85 us (1.073)
  waiting for transfers between devices: 7.77 us -> 10.9 us
  starting transfers between devices: 19.4 us -> 21.8 us
    ppermute x6 -> x9, waiting for transfers between devices: 6.26 us -> 9.45 us  [turned(): moved = {k: lax.ppermute(blocks[k], 'frow', turns[k]) for k in (2, 1, 3)}]
    ppermute x6 -> x9, starting transfers between devices: 8.54 us -> 9.78 us  [turned(): moved = {k: lax.ppermute(blocks[k], 'frow', turns[k]) for k in (2, 1, 3)}]
    ppermute x3, starting transfers between devices: 2.86 us -> 4.04 us  [shards(): rest = {k: lax.ppermute(back[k], 'frow', swap) for k in (2, 1, 3)}]
    pallas_call x1 -> x2, Pallas kernels: 1.62 us -> 1.82 us  [the longest x1 1.06 us: shards(): call(grids_kernel, (shape(2 * SG, HALF), shape(2 * SG, HALF), shape(SG, 2...]
  transfers between devices with their start and end apart: 11 -> 14, of which waited for: 8 -> 8; matrix products, arithmetic and copies ran while one was open for 0% -> 0% of each run, Pallas kernels for 8% -> 8%
where the time goes in v13:
time: 85 us; the launch traced here: 84.8 us
  blocking collectives  36.8 us (43%)
  starting transfers between devices  21.8 us (26%)
  Pallas kernels  14.2 us (17%)
  waiting for transfers between devices  10.9 us (13%)
  between operations  0.98 us (1%)
    all_to_all x2, blocking collectives, exchange(): lax.all_to_all(blocks, axes, 0, 0, tiled=True, axis_index_groups=groups)  36.8 us
    ppermute x9, starting transfers between devices, turned(): moved = {k: lax.ppermute(blocks[k], 'frow', turns[k]) for k in (2, 1, 3)}  9.78 us
    ppermute x9, waiting for transfers between devices, turned(): moved = {k: lax.ppermute(blocks[k], 'frow', turns[k]) for k in (2, 1, 3)}  9.45 us
    ppermute x1, starting transfers between devices, shards(): pieces_other = lax.ppermute(pieces, 'frow', swap)  4.7 us
    ppermute x3, starting transfers between devices, shards(): rest = {k: lax.ppermute(back[k], 'frow', swap) for k in (2, 1, 3)}  4.04 us
    ppermute x1, starting transfers between devices, shards(): other = lax.ppermute(send, 'frow', swap)  3.32 us
    pallas_call x1, Pallas kernels, shards(): call(functools.partial(send_columns_kernel, cols_count), (shape(side + 16...  2.34 us
    pallas_call x1, Pallas kernels, shards(): call(functools.partial(image_kernel, scale_out, chips), (square, shape(2,...  1.9 us
  transfers between devices with their start and end apart: 14, of which 8 were waited for; matrix products, arithmetic and copies ran while one was open for 0% of the time, Pallas kernels for 8%

profile of v13, /device:TPU:1, one launch (start us, length us, event | category | flops | bytes accessed | tf_op | source)
XLA Modules:
  0.0 84.8 jit_solution(8040256960343095853)
XLA Ops:
  0.6 0.0 copy-start.4
  0.7 2.3 %send_columns.1 = (bf16[528,512]{1,0:T(8,128)(2,1)}, bf16[16,256]{1,0:T(8,128)(2,1)}) custom-call(s32[2]{0:T(128)} %offsets_col.1, bf16[512,512]{1,0:T(8,128)(2,1)} %facet.3, s32[1,512]{1,0:T(1,128)} %bitcast.3, s32[1,512]{1,0:T(1,128)} %bitcast.4, s32[1,512]{1,0:T(1,128)} %bitcast.5, f32[2,512]{1,0:T(2,128)} %refs_11_.1), custom_call_target="tpu_custom_call" | custom-call | flops 1000000000 | bytes 1048576 | tf_op jit(solution)/shard_map/send_columns/pallas_call | solution.py:416
  3.0 3.3 %collective-permute-start = (bf16[528,512]{1,0:T(8,128)(2,1)}, bf16[528,512]{1,0:T(8,128)(2,1)S(1)}, u32[]{:S(2)}, u32[]{:S(2)}) collective-permute-start(bf16[528,512]{1,0:T(8,128)(2,1)} %get-tuple-element.33), channel_id=1, source_target_pairs={{0,32},{32,0},{64,96},{96,64},{128,160},{160,128},{192,224},{224,1... | collective-permute-start | bytes 1622024 | tf_op jit(solution)/shard_map/ppermute | solution.py:426
  6.3 1.9 %own_tables.1 = (bf16[512,512]{1,0:T(8,128)(2,1)S(1)}, bf16[4,256,1024]{2,1,0:T(8,128)(2,1)S(1)}) custom-call(s32[2]{0:T(128)S(1)} %copy-done.3, s32[2]{0:T(128)S(1)} %copy-done.4, bf16[512,512]{1,0:T(8,128)(2,1)S(1)} %copy-done.1), custom_call_target="tpu_custom_call" | custom-call | flops 1000000000 | bytes 1048576 | tf_op jit(solution)/shard_map/own_tables/pallas_call | solution.py:427
  8.3 0.0 collective-permute-done.other
  8.3 0.5 contribution.4
  8.7 0.5 contribution.5
  9.2 1.1 %collective-permute-start.3 = (bf16[576,128]{1,0:T(8,128)(2,1)S(1)}, bf16[576,128]{1,0:T(8,128)(2,1)S(1)}, u32[]{:S(2)}, u32[]{:S(2)}) collective-permute-start(bf16[576,128]{1,0:T(8,128)(2,1)S(1)} %contribution.4), channel_id=1, source_target_pairs={{0,128},{32,160},{64,192},{96,224},{128,0},{160,32},{192,64},{224,... | collective-permute-start | bytes 442376 | tf_op jit(solution)/shard_map/ppermute | solution.py:409
  10.3 0.4 contribution.6
  10.7 0.9 %collective-permute-start.2 = (bf16[576,128]{1,0:T(8,128)(2,1)S(1)}, bf16[576,128]{1,0:T(8,128)(2,1)S(1)}, u32[]{:S(2)}, u32[]{:S(2)}) collective-permute-start(bf16[576,128]{1,0:T(8,128)(2,1)S(1)} %contribution.6), channel_id=1, source_target_pairs={{0,192},{32,224},{64,0},{96,32},{128,64},{160,96},{192,128},{224,1... | collective-permute-start | bytes 442376 | tf_op jit(solution)/shard_map/ppermute | solution.py:409
  11.7 0.6 collective-permute-start.1
  12.3 1.4 %back_tables.1 = (bf16[512,1024]{1,0:T(8,128)(2,1)S(1)}, bf16[1024,512]{1,0:T(8,128)(2,1)S(1)}) custom-call(s32[2]{0:T(128)S(1)} %copy-done.3, s32[2]{0:T(128)S(1)} %copy-done.4), custom_call_target="tpu_custom_call" | custom-call | flops 1000000000 | bytes 1048576 | tf_op jit(solution)/shard_map/back_tables/pallas_call | solution.py:443
  13.7 0.5 contribution.7.refs_0_
  14.1 1.9 %collective-permute-done.3.refs_1_.refs_2_ = bf16[576,128]{1,0:T(8,128)(2,1)S(1)} collective-permute-done((bf16[576,128]{1,0:T(8,128)(2,1)S(1)}, bf16[576,128]{1,0:T(8,128)(2,1)S(1)}, u32[]{:S(2)}, u32[]{:S(2)}) %collective-permute-start.3) | collective-permute-done | bytes 147488 | tf_op jit(solution)/shard_map/ppermute | solution.py:409
  16.1 0.8 first_sums.1.refs_2_
  16.8 0.7 collective-permute-done.2.refs_1_.refs_3_
  17.6 1.9 %collective-permute-done.1.refs_0_.refs_1_ = bf16[576,128]{1,0:T(8,128)(2,1)S(1)} collective-permute-done((bf16[576,128]{1,0:T(8,128)(2,1)S(1)}, bf16[576,128]{1,0:T(8,128)(2,1)S(1)}, u32[]{:S(2)}, u32[]{:S(2)}) %collective-permute-start.1) | collective-permute-done | bytes 147488 | tf_op jit(solution)/shard_map/ppermute | solution.py:409
  19.4 0.8 gridding.1
  20.2 20.3 %all_to_all.10.pieces = bf16[32,40,128]{2,1,0:T(8,128)(2,1)S(1)} all-to-all(bf16[32,40,128]{2,1,0:T(8,128)(2,1)S(1)} %gridding.1), channel_id=1, replica_groups=mesh['frow'=8,'fcol'=32] {'fcol'}, dimensions={0} | all-to-all | bytes 655360 | tf_op jit(solution)/shard_map/all_to_all | solution.py:391
  40.5 0.1 pieces_sum.1
  40.6 0.0 copy-start.6
  40.6 16.5 %all_to_all.11.pieces = bf16[32,40,128]{2,1,0:T(8,128)(2,1)S(1)} all-to-all(bf16[32,40,128]{2,1,0:T(8,128)(2,1)S(1)} %pieces_sum.1), channel_id=1, replica_groups=mesh['frow'=8,'fcol'=32] {'fcol'}, dimensions={0} | all-to-all | bytes 655360 | tf_op jit(solution)/shard_map/all_to_all | solution.py:391
  57.1 4.7 %collective-permute-start.4 = (bf16[32,40,128]{2,1,0:T(8,128)(2,1)S(1)}, bf16[32,40,128]{2,1,0:T(8,128)(2,1)S(1)}, u32[]{:S(2)}, u32[]{:S(2)}) collective-permute-start(bf16[32,40,128]{2,1,0:T(8,128)(2,1)S(1)} %all_to_all.11.pieces), channel_id=1, source_target_pairs={{0,32},{32,0},{64,96},{96,64},{128,160},{160,128},{192,224},{224,1... | collective-permute-start | bytes 983048 | tf_op jit(solution)/shard_map/ppermute | solution.py:454
  61.8 0.2 own_half.1
  62.1 1.0 %collective-permute-done.4.other = bf16[32,40,128]{2,1,0:T(8,128)(2,1)S(1)} collective-permute-done((bf16[32,40,128]{2,1,0:T(8,128)(2,1)S(1)}, bf16[32,40,128]{2,1,0:T(8,128)(2,1)S(1)}, u32[]{:S(2)}, u32[]{:S(2)}) %collective-permute-start.4) | collective-permute-done | bytes 327712 | tf_op jit(solution)/shard_map/ppermute | solution.py:454
  63.1 1.1 %grids.1 = (bf16[512,128]{1,0:T(8,128)(2,1)S(1)}, bf16[512,128]{1,0:T(8,128)(2,1)S(1)}, bf16[256,512]{1,0:T(8,128)(2,1)S(1)}) custom-call(f32[3,256,128]{2,1,0:T(8,128)S(1)} %get-tuple-element.43.own, f32[256,512]{1,0:T(8,128)S(1)} %get-tuple-element.44.own_wide, bf16[32,40,128]{2,1,0:T(8,128)(2,1)S(1)} %collective-permute-done.4.other, ...), custom_call_target="tpu_custom_call" | custom-call | flops 1000000000 | bytes 1048576 | tf_op jit(solution)/shard_map/grids/pallas_call | solution.py:464
  64.1 3.2 %collective-permute-start.5 = (bf16[512,128]{1,0:T(8,128)(2,1)S(1)}, bf16[512,128]{1,0:T(8,128)(2,1)S(1)}, u32[]{:S(2)}, u32[]{:S(2)}) collective-permute-start(bf16[512,128]{1,0:T(8,128)(2,1)S(1)} %get-tuple-element.45.own), channel_id=1, source_target_pairs={{0,128},{32,160},{64,192},{96,224},{128,0},{160,32},{192,64},{224,... | collective-permute-start | bytes 393224 | tf_op jit(solution)/shard_map/ppermute | solution.py:409
  67.4 0.3 collective-permute-start.9
  67.7 2.4 %collective-permute-start.10 = (bf16[512,128]{1,0:T(8,128)(2,1)S(1)}, bf16[512,128]{1,0:T(8,128)(2,1)S(1)}, u32[]{:S(2)}, u32[]{:S(2)}) collective-permute-start(bf16[512,128]{1,0:T(8,128)(2,1)S(1)} %get-tuple-element.45.own), channel_id=1, source_target_pairs={{0,192},{32,224},{64,0},{96,32},{128,64},{160,96},{192,128},{224,1... | collective-permute-start | bytes 393224 | tf_op jit(solution)/shard_map/ppermute | solution.py:409
  70.0 0.4 first_part.1.first
  70.5 0.8 answers.1
  71.2 0.1 collective-permute-start.6
  71.3 1.2 %collective-permute-start.7 = (bf16[16,128]{1,0:T(8,128)(2,1)S(1)}, bf16[16,128]{1,0:T(8,128)(2,1)S(1)}, u32[]{:S(2)}, u32[]{:S(2)}) collective-permute-start(bf16[16,128]{1,0:T(8,128)(2,1)S(1)} %get-tuple-element.52), channel_id=1, source_target_pairs={{0,128},{32,160},{64,192},{96,224},{128,0},{160,32},{192,64},{224,... | collective-permute-start | bytes 12296 | tf_op jit(solution)/shard_map/ppermute | solution.py:409
  72.5 2.5 %collective-permute-done.6.refs_1_ = bf16[16,128]{1,0:T(8,128)(2,1)S(1)} collective-permute-done((bf16[16,128]{1,0:T(8,128)(2,1)S(1)}, bf16[16,128]{1,0:T(8,128)(2,1)S(1)}, u32[]{:S(2)}, u32[]{:S(2)}) %collective-permute-start.6) | collective-permute-done | bytes 4128 | tf_op jit(solution)/shard_map/ppermute | solution.py:409
  75.0 0.0 collective-permute-start.8
  75.0 0.4 collective-permute-done.7.refs_2_
  75.4 2.1 %collective-permute-done.8.refs_3_ = bf16[16,128]{1,0:T(8,128)(2,1)S(1)} collective-permute-done((bf16[16,128]{1,0:T(8,128)(2,1)S(1)}, bf16[16,128]{1,0:T(8,128)(2,1)S(1)}, u32[]{:S(2)}, u32[]{:S(2)}) %collective-permute-start.8) | collective-permute-done | bytes 4128 | tf_op jit(solution)/shard_map/ppermute | solution.py:409
  77.4 0.0 collective-permute-done.5.own
  77.5 3.5 %collective-permute-start.13 = (bf16[512,128]{1,0:T(8,128)(2,1)S(1)}, bf16[512,128]{1,0:T(8,128)(2,1)S(1)}, u32[]{:S(2)}, u32[]{:S(2)}) collective-permute-start(bf16[512,128]{1,0:T(8,128)(2,1)S(1)} %collective-permute-done.5.own), channel_id=1, source_target_pairs={{0,32},{32,0},{64,96},{96,64},{128,160},{160,128},{192,224},{224,1... | collective-permute-start | bytes 393224 | tf_op jit(solution)/shard_map/ppermute | solution.py:482
  81.0 0.0 collective-permute-done.9.refs_4_
  81.0 0.1 collective-permute-start.11
  81.1 0.0 collective-permute-done.10.refs_5_
  81.1 0.4 collective-permute-start.12
  81.5 0.5 collective-permute-done.13.rest
  82.0 0.7 own_column.1.refs_8_
  82.7 0.0 collective-permute-done.11.refs_6_
  82.7 0.0 collective-permute-done.12.refs_7_
  82.7 1.9 %image.1 = (f32[512,512]{1,0:T(8,128)}, f32[2,512]{1,0:T(2,128)}) custom-call(bf16[16,128]{1,0:T(8,128)(2,1)S(1)} %get-tuple-element.54.refs_0_, bf16[16,128]{1,0:T(8,128)(2,1)S(1)} %collective-permute-done.6.refs_1_, bf16[16,128]{1,0:T(8,128)(2,1)S(1)} %collective-permute-done.7.refs_2_, bf16[16,128]{1,0:T(8,128)(2,1)S(1)} %collective-permute-done.8.refs_3_, ...), custom_call_target="tpu_custom_call" | custom-call | flops 1000000000 | bytes 1048576 | tf_op jit(solution)/shard_map/image/pallas_call | solution.py:486
  (12 shorter events, 0.0 us)
Async XLA Ops:
  0.6 5.7 %copy-start.4 = (s32[2]{0:T(128)S(1)}, s32[2]{0:T(128)}, u32[]{:S(2)}) copy-start(s32[2]{0:T(128)} %offsets_col.1) | copy-start | bytes 28
  0.6 5.7 %copy-start.1 = (bf16[512,512]{1,0:T(8,128)(2,1)S(1)}, bf16[512,512]{1,0:T(8,128)(2,1)}, u32[]{:S(2)}) copy-start(bf16[512,512]{1,0:T(8,128)(2,1)} %facet.3) | copy-start | bytes 1572868
  0.7 5.7 %copy-start.3 = (s32[2]{0:T(128)S(1)}, s32[2]{0:T(128)}, u32[]{:S(2)}) copy-start(s32[2]{0:T(128)} %offsets_row.1) | copy-start | bytes 28
  3.0 5.3 %copy-start = (bf16[16,256]{1,0:T(8,128)(2,1)S(1)}, bf16[16,256]{1,0:T(8,128)(2,1)}, u32[]{:S(2)}) copy-start(bf16[16,256]{1,0:T(8,128)(2,1)} %get-tuple-element.32.own_vis) | copy-start | bytes 24580
  3.0 5.2 %collective-permute-start = (bf16[528,512]{1,0:T(8,128)(2,1)}, bf16[528,512]{1,0:T(8,128)(2,1)S(1)}, u32[]{:S(2)}, u32[]{:S(2)}) collective-permute-start(bf16[528,512]{1,0:T(8,128)(2,1)} %get-tuple-element.33), channel_id=1, source_target_pairs={{0,32},{32,0},{64,96},{96,64},{128,160},{160,128},{192,224},{224,1... | collective-permute-start | bytes 1622024 | tf_op jit(solution)/shard_map/ppermute | solution.py:426
  9.2 6.9 %collective-permute-start.3 = (bf16[576,128]{1,0:T(8,128)(2,1)S(1)}, bf16[576,128]{1,0:T(8,128)(2,1)S(1)}, u32[]{:S(2)}, u32[]{:S(2)}) collective-permute-start(bf16[576,128]{1,0:T(8,128)(2,1)S(1)} %contribution.4), channel_id=1, source_target_pairs={{0,128},{32,160},{64,192},{96,224},{128,0},{160,32},{192,64},{224,... | collective-permute-start | bytes 442376 | tf_op jit(solution)/shard_map/ppermute | solution.py:409
  10.7 6.8 %collective-permute-start.2 = (bf16[576,128]{1,0:T(8,128)(2,1)S(1)}, bf16[576,128]{1,0:T(8,128)(2,1)S(1)}, u32[]{:S(2)}, u32[]{:S(2)}) collective-permute-start(bf16[576,128]{1,0:T(8,128)(2,1)S(1)} %contribution.6), channel_id=1, source_target_pairs={{0,192},{32,224},{64,0},{96,32},{128,64},{160,96},{192,128},{224,1... | collective-permute-start | bytes 442376 | tf_op jit(solution)/shard_map/ppermute | solution.py:409
  11.7 7.7 %collective-permute-start.1 = (bf16[576,128]{1,0:T(8,128)(2,1)S(1)}, bf16[576,128]{1,0:T(8,128)(2,1)S(1)}, u32[]{:S(2)}, u32[]{:S(2)}) collective-permute-start(bf16[576,128]{1,0:T(8,128)(2,1)S(1)} %contribution.5), channel_id=1, source_target_pairs={{0,64},{32,96},{64,128},{96,160},{128,192},{160,224},{192,0},{224,... | collective-permute-start | bytes 442376 | tf_op jit(solution)/shard_map/ppermute | solution.py:409
  19.4 42.4 %copy-start.5 = (bf16[512,512]{1,0:T(8,128)(2,1)S(1)}, bf16[512,512]{1,0:T(8,128)(2,1)}, u32[]{:S(2)}) copy-start(bf16[512,512]{1,0:T(8,128)(2,1)} %constant.4.clone.forward.inverse_left) | copy-start | bytes 1572868
  40.6 22.5 %copy-start.6 = (bf16[512,512]{1,0:T(8,128)(2,1)S(1)}, bf16[512,512]{1,0:T(8,128)(2,1)}, u32[]{:S(2)}) copy-start(bf16[512,512]{1,0:T(8,128)(2,1)} %constant.5.clone.grid_left.inverse) | copy-start | bytes 1572868
  57.1 6.0 %collective-permute-start.4 = (bf16[32,40,128]{2,1,0:T(8,128)(2,1)S(1)}, bf16[32,40,128]{2,1,0:T(8,128)(2,1)S(1)}, u32[]{:S(2)}, u32[]{:S(2)}) collective-permute-start(bf16[32,40,128]{2,1,0:T(8,128)(2,1)S(1)} %all_to_all.11.pieces), channel_id=1, source_target_pairs={{0,32},{32,0},{64,96},{96,64},{128,160},{160,128},{192,224},{224,1... | collective-permute-start | bytes 983048 | tf_op jit(solution)/shard_map/ppermute | solution.py:454
  64.1 13.3 %collective-permute-start.5 = (bf16[512,128]{1,0:T(8,128)(2,1)S(1)}, bf16[512,128]{1,0:T(8,128)(2,1)S(1)}, u32[]{:S(2)}, u32[]{:S(2)}) collective-permute-start(bf16[512,128]{1,0:T(8,128)(2,1)S(1)} %get-tuple-element.45.own), channel_id=1, source_target_pairs={{0,128},{32,160},{64,192},{96,224},{128,0},{160,32},{192,64},{224,... | collective-permute-start | bytes 393224 | tf_op jit(solution)/shard_map/ppermute | solution.py:409
  67.4 13.6 %collective-permute-start.9 = (bf16[512,128]{1,0:T(8,128)(2,1)S(1)}, bf16[512,128]{1,0:T(8,128)(2,1)S(1)}, u32[]{:S(2)}, u32[]{:S(2)}) collective-permute-start(bf16[512,128]{1,0:T(8,128)(2,1)S(1)} %get-tuple-element.45.own), channel_id=1, source_target_pairs={{0,64},{32,96},{64,128},{96,160},{128,192},{160,224},{192,0},{224,... | collective-permute-start | bytes 393224 | tf_op jit(solution)/shard_map/ppermute | solution.py:409
  67.7 13.4 %collective-permute-start.10 = (bf16[512,128]{1,0:T(8,128)(2,1)S(1)}, bf16[512,128]{1,0:T(8,128)(2,1)S(1)}, u32[]{:S(2)}, u32[]{:S(2)}) collective-permute-start(bf16[512,128]{1,0:T(8,128)(2,1)S(1)} %get-tuple-element.45.own), channel_id=1, source_target_pairs={{0,192},{32,224},{64,0},{96,32},{128,64},{160,96},{192,128},{224,1... | collective-permute-start | bytes 393224 | tf_op jit(solution)/shard_map/ppermute | solution.py:409
  71.2 3.7 %collective-permute-start.6 = (bf16[16,128]{1,0:T(8,128)(2,1)S(1)}, bf16[16,128]{1,0:T(8,128)(2,1)S(1)}, u32[]{:S(2)}, u32[]{:S(2)}) collective-permute-start(bf16[16,128]{1,0:T(8,128)(2,1)S(1)} %get-tuple-element.51), channel_id=1, source_target_pairs={{0,64},{32,96},{64,128},{96,160},{128,192},{160,224},{192,0},{224,... | collective-permute-start | bytes 12296 | tf_op jit(solution)/shard_map/ppermute | solution.py:409
  71.3 4.0 %collective-permute-start.7 = (bf16[16,128]{1,0:T(8,128)(2,1)S(1)}, bf16[16,128]{1,0:T(8,128)(2,1)S(1)}, u32[]{:S(2)}, u32[]{:S(2)}) collective-permute-start(bf16[16,128]{1,0:T(8,128)(2,1)S(1)} %get-tuple-element.52), channel_id=1, source_target_pairs={{0,128},{32,160},{64,192},{96,224},{128,0},{160,32},{192,64},{224,... | collective-permute-start | bytes 12296 | tf_op jit(solution)/shard_map/ppermute | solution.py:409
  75.0 2.5 %collective-permute-start.8 = (bf16[16,128]{1,0:T(8,128)(2,1)S(1)}, bf16[16,128]{1,0:T(8,128)(2,1)S(1)}, u32[]{:S(2)}, u32[]{:S(2)}) collective-permute-start(bf16[16,128]{1,0:T(8,128)(2,1)S(1)} %get-tuple-element.53), channel_id=1, source_target_pairs={{0,192},{32,224},{64,0},{96,32},{128,64},{160,96},{192,128},{224,1... | collective-permute-start | bytes 12296 | tf_op jit(solution)/shard_map/ppermute | solution.py:409
  77.5 5.3 %copy-start.2 = (f32[2,512]{1,0:T(2,128)S(1)}, f32[2,512]{1,0:T(2,128)}, u32[]{:S(2)}) copy-start(f32[2,512]{1,0:T(2,128)} %refs_11_.1) | copy-start | bytes 12292
  77.5 4.5 %collective-permute-start.13 = (bf16[512,128]{1,0:T(8,128)(2,1)S(1)}, bf16[512,128]{1,0:T(8,128)(2,1)S(1)}, u32[]{:S(2)}, u32[]{:S(2)}) collective-permute-start(bf16[512,128]{1,0:T(8,128)(2,1)S(1)} %collective-permute-done.5.own), channel_id=1, source_target_pairs={{0,32},{32,0},{64,96},{96,64},{128,160},{160,128},{192,224},{224,1... | collective-permute-start | bytes 393224 | tf_op jit(solution)/shard_map/ppermute | solution.py:482
  81.0 1.7 %collective-permute-start.11 = (bf16[512,128]{1,0:T(8,128)(2,1)S(1)}, bf16[512,128]{1,0:T(8,128)(2,1)S(1)}, u32[]{:S(2)}, u32[]{:S(2)}) collective-permute-start(bf16[512,128]{1,0:T(8,128)(2,1)S(1)} %collective-permute-done.9.refs_4_), channel_id=1, source_target_pairs={{0,32},{32,0},{64,96},{96,64},{128,160},{160,128},{192,224},{224,1... | collective-permute-start | bytes 393224 | tf_op jit(solution)/shard_map/ppermute | solution.py:482
  81.1 1.6 %collective-permute-start.12 = (bf16[512,128]{1,0:T(8,128)(2,1)S(1)}, bf16[512,128]{1,0:T(8,128)(2,1)S(1)}, u32[]{:S(2)}, u32[]{:S(2)}) collective-permute-start(bf16[512,128]{1,0:T(8,128)(2,1)S(1)} %collective-permute-done.10.refs_5_), channel_id=1, source_target_pairs={{0,32},{32,0},{64,96},{96,64},{128,160},{160,128},{192,224},{224,1... | collective-permute-start | bytes 393224 | tf_op jit(solution)/shard_map/ppermute | solution.py:482

commit v14 on v12

--- a/solution.py
+++ b/solution.py
@@ -55,8 +55,7 @@
 
 
 def served():
-    row_index, col_index = place()
-    return lax.rem(row_index // 2 + col_index, NR * NC)
+    return lax.rem(place()[1], NR * NC)
 
 
 def half_columns(cols_count, offsets, half, side, col_tab):
@@ -410,22 +409,16 @@
     swap = [(index, index ^ 1) for index in range(rows_count)]
     line = NR * NC
 
-    def turn(index, k):
-        row, col = index // cols_count, index % cols_count
-        if row % 2 == 0:
-            row = (row + 2 * k) % rows_count
-        else:
-            col = col // line * line + (col + k) % line
-        return row * cols_count + col
-
-    turns = [[(index, turn(index, k)) for index in range(rows_count * cols_count)] for k in range(chips)]
+    turns = [
+        [(col, col // line * line + (col + k) % line) for col in range(cols_count)] for k in range(line)
+    ]
     groups = [
-        [((number - col) % line * 2 + core) * cols_count + col for col in range(cols_count)]
+        [(2 * chip + core) * cols_count + far * line + number for far in range(cols_count // line) for chip in range(chips)]
         for number in range(line) for core in range(2)
     ]
 
     def turned(blocks):
-        moved = {k: lax.ppermute(blocks[k], BOTH, turns[k]) for k in (2, 1, 3)}
+        moved = {k: lax.ppermute(blocks[k], "fcol", turns[k]) for k in (2, 1, 3)}
         return [blocks[0]] + [moved[k] for k in range(1, chips)]
 
     scale_in = 1.0 / (side * math.sqrt(rows_count * cols_count))

time: 79.9 us -> 79.2 us (level)
  blocking collectives: 42.4 us -> 37.1 us
  starting transfers between devices: 16.2 us -> 19.6 us
  waiting for transfers between devices: 6.17 us -> 7.41 us
    all_to_all x2, blocking collectives: 42.4 us -> 37.1 us  [exchange(): lax.all_to_all(blocks, axes, 0, 0, tiled=True, axis_index_groups=groups)]
    ppermute x6, starting transfers between devices: 5.86 us -> 8.61 us  [turned(): moved = {k: lax.ppermute(blocks[k], 'fcol', turns[k]) for k in (2, 1, 3)}]
    ppermute x6, waiting for transfers between devices: 4.56 us -> 5.93 us  [turned(): moved = {k: lax.ppermute(blocks[k], 'fcol', turns[k]) for k in (2, 1, 3)}]
  transfers between devices with their start and end apart: 11 -> 11, of which waited for: 7 -> 8; matrix products, arithmetic and copies ran while one was open for 0% -> 0% of each run, Pallas kernels for 8% -> 8%
where the time goes in v14:
time: 79.2 us; the launch traced here: 79 us
  blocking collectives  37.1 us (47%)
  starting transfers between devices  19.6 us (25%)
  Pallas kernels  13.9 us (18%)
  waiting for transfers between devices  7.41 us (9%)
  between operations  0.95 us (1%)
    all_to_all x2, blocking collectives, exchange(): lax.all_to_all(blocks, axes, 0, 0, tiled=True, axis_index_groups=groups)  37.1 us
    ppermute x6, starting transfers between devices, turned(): moved = {k: lax.ppermute(blocks[k], 'fcol', turns[k]) for k in (2, 1, 3)}  8.61 us
    ppermute x6, waiting for transfers between devices, turned(): moved = {k: lax.ppermute(blocks[k], 'fcol', turns[k]) for k in (2, 1, 3)}  5.93 us
    ppermute x1, starting transfers between devices, shards(): pieces_other = lax.ppermute(pieces, 'frow', swap)  4.59 us
    ppermute x1, starting transfers between devices, shards(): other = lax.ppermute(send, 'frow', swap)  3.32 us
    ppermute x3, starting transfers between devices, shards(): rest = {k: lax.ppermute(back[k], 'frow', swap) for k in (2, 1, 3)}  3.07 us
    pallas_call x1, Pallas kernels, shards(): call(functools.partial(send_columns_kernel, cols_count), (shape(side + 16...  2.34 us
    pallas_call x1, Pallas kernels, shards(): call(functools.partial(own_tables_kernel, rows_count, cols_count), (shape...  1.9 us
  transfers between devices with their start and end apart: 11, of which 8 were waited for; matrix products, arithmetic and copies ran while one was open for 0% of the time, Pallas kernels for 8%

profile of v14, /device:TPU:1, one launch (start us, length us, event | category | flops | bytes accessed | tf_op | source)
XLA Modules:
  0.0 79.0 jit_solution(443655335432489337)
XLA Ops:
  0.6 0.0 copy-start.6
  0.6 0.0 copy-start.4
  0.7 0.0 copy-start.5
  0.7 2.3 %send_columns.1 = (bf16[528,512]{1,0:T(8,128)(2,1)}, bf16[16,256]{1,0:T(8,128)(2,1)}) custom-call(s32[2]{0:T(128)} %offsets_col.1, bf16[512,512]{1,0:T(8,128)(2,1)} %facet.3, s32[1,512]{1,0:T(1,128)} %bitcast.3, s32[1,512]{1,0:T(1,128)} %bitcast.4, s32[1,512]{1,0:T(1,128)} %bitcast.5, f32[2,512]{1,0:T(2,128)} %refs_9_.1), custom_call_target="tpu_custom_call" | custom-call | flops 1000000000 | bytes 1048576 | tf_op jit(solution)/shard_map/send_columns/pallas_call | solution.py:428
  3.0 0.0 copy-start.2
  3.0 3.3 %collective-permute-start = (bf16[528,512]{1,0:T(8,128)(2,1)}, bf16[528,512]{1,0:T(8,128)(2,1)S(1)}, u32[]{:S(2)}, u32[]{:S(2)}) collective-permute-start(bf16[528,512]{1,0:T(8,128)(2,1)} %get-tuple-element.26), channel_id=1, source_target_pairs={{0,32},{32,0},{64,96},{96,64},{128,160},{160,128},{192,224},{224,1... | collective-permute-start | bytes 1622024 | tf_op jit(solution)/shard_map/ppermute | solution.py:438
  6.3 0.0 copy-done.5
  6.3 1.9 %own_tables.1 = (bf16[512,512]{1,0:T(8,128)(2,1)S(1)}, bf16[4,256,1024]{2,1,0:T(8,128)(2,1)S(1)}) custom-call(s32[2]{0:T(128)S(1)} %copy-done.5, s32[2]{0:T(128)S(1)} %copy-done.6, bf16[512,512]{1,0:T(8,128)(2,1)S(1)} %copy-done.4), custom_call_target="tpu_custom_call" | custom-call | flops 1000000000 | bytes 1048576 | tf_op jit(solution)/shard_map/own_tables/pallas_call | solution.py:439
  8.3 0.0 collective-permute-done.other
  8.3 0.0 copy-done.2
  8.3 0.5 contribution.4
  8.7 0.5 contribution.5
  9.2 1.3 %collective-permute-start.3 = (bf16[576,128]{1,0:T(8,128)(2,1)S(1)}, bf16[576,128]{1,0:T(8,128)(2,1)S(1)}, u32[]{:S(2)}, u32[]{:S(2)}) collective-permute-start(bf16[576,128]{1,0:T(8,128)(2,1)S(1)} %contribution.4), channel_id=1, source_target_pairs={{0,2},{1,3},{2,0},{3,1},{4,6},{5,7},{6,4},{7,5},{8,10},{9,11},{10,... | collective-permute-start | bytes 442376 | tf_op jit(solution)/shard_map/ppermute | solution.py:421
  10.5 0.4 contribution.6
  10.9 0.8 %collective-permute-start.2 = (bf16[576,128]{1,0:T(8,128)(2,1)S(1)}, bf16[576,128]{1,0:T(8,128)(2,1)S(1)}, u32[]{:S(2)}, u32[]{:S(2)}) collective-permute-start(bf16[576,128]{1,0:T(8,128)(2,1)S(1)} %contribution.6), channel_id=1, source_target_pairs={{0,3},{1,0},{2,1},{3,2},{4,7},{5,4},{6,5},{7,6},{8,11},{9,8},{10,9... | collective-permute-start | bytes 442376 | tf_op jit(solution)/shard_map/ppermute | solution.py:421
  11.8 0.7 collective-permute-start.1
  12.5 1.4 %back_tables.1 = (bf16[512,1024]{1,0:T(8,128)(2,1)S(1)}, bf16[1024,512]{1,0:T(8,128)(2,1)S(1)}) custom-call(s32[2]{0:T(128)S(1)} %copy-done.5, s32[2]{0:T(128)S(1)} %copy-done.6), custom_call_target="tpu_custom_call" | custom-call | flops 1000000000 | bytes 1048576 | tf_op jit(solution)/shard_map/back_tables/pallas_call | solution.py:455
  13.8 0.5 contribution.7.refs_0_
  14.3 1.8 %collective-permute-done.3.refs_1_.refs_2_ = bf16[576,128]{1,0:T(8,128)(2,1)S(1)} collective-permute-done((bf16[576,128]{1,0:T(8,128)(2,1)S(1)}, bf16[576,128]{1,0:T(8,128)(2,1)S(1)}, u32[]{:S(2)}, u32[]{:S(2)}) %collective-permute-start.3) | collective-permute-done | bytes 147488 | tf_op jit(solution)/shard_map/ppermute | solution.py:421
  16.0 0.8 first_sums.1.refs_2_
  16.8 1.0 %collective-permute-done.2.refs_1_.refs_3_ = bf16[576,128]{1,0:T(8,128)(2,1)S(1)} collective-permute-done((bf16[576,128]{1,0:T(8,128)(2,1)S(1)}, bf16[576,128]{1,0:T(8,128)(2,1)S(1)}, u32[]{:S(2)}, u32[]{:S(2)}) %collective-permute-start.2) | collective-permute-done | bytes 147488 | tf_op jit(solution)/shard_map/ppermute | solution.py:421
  17.8 1.6 %collective-permute-done.1.refs_0_.refs_1_ = bf16[576,128]{1,0:T(8,128)(2,1)S(1)} collective-permute-done((bf16[576,128]{1,0:T(8,128)(2,1)S(1)}, bf16[576,128]{1,0:T(8,128)(2,1)S(1)}, u32[]{:S(2)}, u32[]{:S(2)}) %collective-permute-start.1) | collective-permute-done | bytes 147488 | tf_op jit(solution)/shard_map/ppermute | solution.py:421
  19.4 0.8 gridding.1
  20.1 20.5 %all_to_all.10.pieces = bf16[32,40,128]{2,1,0:T(8,128)(2,1)S(1)} all-to-all(bf16[32,40,128]{2,1,0:T(8,128)(2,1)S(1)} %gridding.1), channel_id=1, replica_groups={{0,64,128,192,4,68,132,196,8,72,136,200,12,76,140,204,16,80,144,208,20,..., dimensions={0} | all-to-all | bytes 655360 | tf_op jit(solution)/shard_map/all_to_all | solution.py:395
  40.6 0.1 pieces_sum.1
  40.7 0.0 copy-start.1
  40.7 16.6 %all_to_all.11.pieces = bf16[32,40,128]{2,1,0:T(8,128)(2,1)S(1)} all-to-all(bf16[32,40,128]{2,1,0:T(8,128)(2,1)S(1)} %pieces_sum.1), channel_id=1, replica_groups={{0,64,128,192,4,68,132,196,8,72,136,200,12,76,140,204,16,80,144,208,20,..., dimensions={0} | all-to-all | bytes 655360 | tf_op jit(solution)/shard_map/all_to_all | solution.py:395
  57.3 4.6 %collective-permute-start.4 = (bf16[32,40,128]{2,1,0:T(8,128)(2,1)S(1)}, bf16[32,40,128]{2,1,0:T(8,128)(2,1)S(1)}, u32[]{:S(2)}, u32[]{:S(2)}) collective-permute-start(bf16[32,40,128]{2,1,0:T(8,128)(2,1)S(1)} %all_to_all.11.pieces), channel_id=1, source_target_pairs={{0,32},{32,0},{64,96},{96,64},{128,160},{160,128},{192,224},{224,1... | collective-permute-start | bytes 983048 | tf_op jit(solution)/shard_map/ppermute | solution.py:466
  61.9 0.2 own_half.1
  62.2 1.0 %collective-permute-done.4.other = bf16[32,40,128]{2,1,0:T(8,128)(2,1)S(1)} collective-permute-done((bf16[32,40,128]{2,1,0:T(8,128)(2,1)S(1)}, bf16[32,40,128]{2,1,0:T(8,128)(2,1)S(1)}, u32[]{:S(2)}, u32[]{:S(2)}) %collective-permute-start.4) | collective-permute-done | bytes 327712 | tf_op jit(solution)/shard_map/ppermute | solution.py:466
  63.2 0.0 copy-done.1
  63.2 1.6 %grids.1 = (bf16[528,128]{1,0:T(8,128)(2,1)S(1)}, bf16[528,128]{1,0:T(8,128)(2,1)S(1)}, bf16[528,128]{1,0:T(8,128)(2,1)S(1)}, bf16[528,128]{1,0:T(8,128)(2,1)S(1)}, bf16[512,128]{1,0:T(8,128)(2,1)S(1)}) custom-call(f32[3,256,128]{2,1,0:T(8,128)S(1)} %get-tuple-element.36.own, f32[256,512]{1,0:T(8,128)S(1)} %get-tuple-element.37.own_wide, ...), custom_call_target="tpu_custom_call" | custom-call | flops 1000000000 | bytes 1048576 | tf_op jit(solution)/shard_map/grids/pallas_call | solution.py:476
  64.8 3.1 %collective-permute-start.6 = (bf16[528,128]{1,0:T(8,128)(2,1)S(1)}, bf16[528,128]{1,0:T(8,128)(2,1)S(1)}, u32[]{:S(2)}, u32[]{:S(2)}) collective-permute-start(bf16[528,128]{1,0:T(8,128)(2,1)S(1)} %get-tuple-element.40), channel_id=1, source_target_pairs={{0,2},{1,3},{2,0},{3,1},{4,6},{5,7},{6,4},{7,5},{8,10},{9,11},{10,... | collective-permute-start | bytes 405512 | tf_op jit(solution)/shard_map/ppermute | solution.py:421
  67.9 0.4 collective-permute-start.5
  68.3 2.3 %collective-permute-start.7 = (bf16[528,128]{1,0:T(8,128)(2,1)S(1)}, bf16[528,128]{1,0:T(8,128)(2,1)S(1)}, u32[]{:S(2)}, u32[]{:S(2)}) collective-permute-start(bf16[528,128]{1,0:T(8,128)(2,1)S(1)} %get-tuple-element.44), channel_id=1, source_target_pairs={{0,3},{1,0},{2,1},{3,2},{4,7},{5,4},{6,5},{7,6},{8,11},{9,8},{10,9... | collective-permute-start | bytes 405512 | tf_op jit(solution)/shard_map/ppermute | solution.py:421
  70.6 0.4 first_part.1.first
  71.0 0.0 copy-start.3
  71.0 0.3 collective-permute-done.6.own.refs_2_
  71.3 1.9 %collective-permute-start.10 = (bf16[528,128]{1,0:T(8,128)(2,1)S(1)}, bf16[528,128]{1,0:T(8,128)(2,1)S(1)}, u32[]{:S(2)}, u32[]{:S(2)}) collective-permute-start(bf16[528,128]{1,0:T(8,128)(2,1)S(1)} %collective-permute-done.6.own.refs_2_), channel_id=1, source_target_pairs={{0,32},{32,0},{64,96},{96,64},{128,160},{160,128},{192,224},{224,1... | collective-permute-start | bytes 405512 | tf_op jit(solution)/shard_map/ppermute | solution.py:491
  73.2 1.4 %collective-permute-done.5.refs_1_ = bf16[528,128]{1,0:T(8,128)(2,1)S(1)} collective-permute-done((bf16[528,128]{1,0:T(8,128)(2,1)S(1)}, bf16[528,128]{1,0:T(8,128)(2,1)S(1)}, u32[]{:S(2)}, u32[]{:S(2)}) %collective-permute-start.5) | collective-permute-done | bytes 135200 | tf_op jit(solution)/shard_map/ppermute | solution.py:421
  74.5 1.1 %collective-permute-start.8 = (bf16[528,128]{1,0:T(8,128)(2,1)S(1)}, bf16[528,128]{1,0:T(8,128)(2,1)S(1)}, u32[]{:S(2)}, u32[]{:S(2)}) collective-permute-start(bf16[528,128]{1,0:T(8,128)(2,1)S(1)} %collective-permute-done.5.refs_1_), channel_id=1, source_target_pairs={{0,32},{32,0},{64,96},{96,64},{128,160},{160,128},{192,224},{224,1... | collective-permute-start | bytes 405512 | tf_op jit(solution)/shard_map/ppermute | solution.py:491
  75.6 0.0 collective-permute-done.7.refs_3_
  75.6 0.1 collective-permute-start.9
  75.7 0.0 collective-permute-done.10.rest
  75.7 0.7 own_column.1.refs_6_
  76.5 0.1 collective-permute-done.8.refs_4_
  76.6 0.4 collective-permute-done.9.refs_5_
  77.0 1.9 %image.1 = (f32[512,512]{1,0:T(8,128)}, f32[2,512]{1,0:T(2,128)}) custom-call(bf16[528,128]{1,0:T(8,128)(2,1)S(1)} %get-tuple-element.38.own.refs_0_, bf16[528,128]{1,0:T(8,128)(2,1)S(1)} %collective-permute-done.5.refs_1_, bf16[528,128]{1,0:T(8,128)(2,1)S(1)} %collective-permute-done.6.own.refs_2_, bf16[528,128]{1,0:T(8,128)(2,1)S(1)} %collective-permute-done.7.refs_3_, ...), custom_call_target="tpu_custom_call" | custom-call | flops 1000000000 | bytes 1048576 | tf_op jit(solution)/shard_map/image/pallas_call | solution.py:495
  (5 shorter events, 0.0 us)
Async XLA Ops:
  0.6 5.7 %copy-start.6 = (s32[2]{0:T(128)S(1)}, s32[2]{0:T(128)}, u32[]{:S(2)}) copy-start(s32[2]{0:T(128)} %offsets_col.1) | copy-start | bytes 28
  0.6 5.7 %copy-start.4 = (bf16[512,512]{1,0:T(8,128)(2,1)S(1)}, bf16[512,512]{1,0:T(8,128)(2,1)}, u32[]{:S(2)}) copy-start(bf16[512,512]{1,0:T(8,128)(2,1)} %facet.3) | copy-start | bytes 1572868
  0.7 5.7 %copy-start.5 = (s32[2]{0:T(128)S(1)}, s32[2]{0:T(128)}, u32[]{:S(2)}) copy-start(s32[2]{0:T(128)} %offsets_row.1) | copy-start | bytes 28
  3.0 5.3 %copy-start.2 = (bf16[16,256]{1,0:T(8,128)(2,1)S(1)}, bf16[16,256]{1,0:T(8,128)(2,1)}, u32[]{:S(2)}) copy-start(bf16[16,256]{1,0:T(8,128)(2,1)} %get-tuple-element.25.own_vis) | copy-start | bytes 24580
  3.0 5.2 %collective-permute-start = (bf16[528,512]{1,0:T(8,128)(2,1)}, bf16[528,512]{1,0:T(8,128)(2,1)S(1)}, u32[]{:S(2)}, u32[]{:S(2)}) collective-permute-start(bf16[528,512]{1,0:T(8,128)(2,1)} %get-tuple-element.26), channel_id=1, source_target_pairs={{0,32},{32,0},{64,96},{96,64},{128,160},{160,128},{192,224},{224,1... | collective-permute-start | bytes 1622024 | tf_op jit(solution)/shard_map/ppermute | solution.py:438
  9.2 6.9 %collective-permute-start.3 = (bf16[576,128]{1,0:T(8,128)(2,1)S(1)}, bf16[576,128]{1,0:T(8,128)(2,1)S(1)}, u32[]{:S(2)}, u32[]{:S(2)}) collective-permute-start(bf16[576,128]{1,0:T(8,128)(2,1)S(1)} %contribution.4), channel_id=1, source_target_pairs={{0,2},{1,3},{2,0},{3,1},{4,6},{5,7},{6,4},{7,5},{8,10},{9,11},{10,... | collective-permute-start | bytes 442376 | tf_op jit(solution)/shard_map/ppermute | solution.py:421
  10.9 6.9 %collective-permute-start.2 = (bf16[576,128]{1,0:T(8,128)(2,1)S(1)}, bf16[576,128]{1,0:T(8,128)(2,1)S(1)}, u32[]{:S(2)}, u32[]{:S(2)}) collective-permute-start(bf16[576,128]{1,0:T(8,128)(2,1)S(1)} %contribution.6), channel_id=1, source_target_pairs={{0,3},{1,0},{2,1},{3,2},{4,7},{5,4},{6,5},{7,6},{8,11},{9,8},{10,9... | collective-permute-start | bytes 442376 | tf_op jit(solution)/shard_map/ppermute | solution.py:421
  11.8 7.6 %collective-permute-start.1 = (bf16[576,128]{1,0:T(8,128)(2,1)S(1)}, bf16[576,128]{1,0:T(8,128)(2,1)S(1)}, u32[]{:S(2)}, u32[]{:S(2)}) collective-permute-start(bf16[576,128]{1,0:T(8,128)(2,1)S(1)} %contribution.5), channel_id=1, source_target_pairs={{0,1},{1,2},{2,3},{3,0},{4,5},{5,6},{6,7},{7,4},{8,9},{9,10},{10,1... | collective-permute-start | bytes 442376 | tf_op jit(solution)/shard_map/ppermute | solution.py:421
  19.4 42.5 %copy-start = (bf16[512,512]{1,0:T(8,128)(2,1)S(1)}, bf16[512,512]{1,0:T(8,128)(2,1)}, u32[]{:S(2)}) copy-start(bf16[512,512]{1,0:T(8,128)(2,1)} %constant.4.clone.forward.refs_5_.refs_6_) | copy-start | bytes 1572868
  40.7 22.5 %copy-start.1 = (bf16[512,512]{1,0:T(8,128)(2,1)S(1)}, bf16[512,512]{1,0:T(8,128)(2,1)}, u32[]{:S(2)}) copy-start(bf16[512,512]{1,0:T(8,128)(2,1)} %constant.5.clone.refs_4_.refs_7_) | copy-start | bytes 1572868
  57.3 5.8 %collective-permute-start.4 = (bf16[32,40,128]{2,1,0:T(8,128)(2,1)S(1)}, bf16[32,40,128]{2,1,0:T(8,128)(2,1)S(1)}, u32[]{:S(2)}, u32[]{:S(2)}) collective-permute-start(bf16[32,40,128]{2,1,0:T(8,128)(2,1)S(1)} %all_to_all.11.pieces), channel_id=1, source_target_pairs={{0,32},{32,0},{64,96},{96,64},{128,160},{160,128},{192,224},{224,1... | collective-permute-start | bytes 983048 | tf_op jit(solution)/shard_map/ppermute | solution.py:466
  64.8 6.5 %collective-permute-start.6 = (bf16[528,128]{1,0:T(8,128)(2,1)S(1)}, bf16[528,128]{1,0:T(8,128)(2,1)S(1)}, u32[]{:S(2)}, u32[]{:S(2)}) collective-permute-start(bf16[528,128]{1,0:T(8,128)(2,1)S(1)} %get-tuple-element.40), channel_id=1, source_target_pairs={{0,2},{1,3},{2,0},{3,1},{4,6},{5,7},{6,4},{7,5},{8,10},{9,11},{10,... | collective-permute-start | bytes 405512 | tf_op jit(solution)/shard_map/ppermute | solution.py:421
  67.9 6.6 %collective-permute-start.5 = (bf16[528,128]{1,0:T(8,128)(2,1)S(1)}, bf16[528,128]{1,0:T(8,128)(2,1)S(1)}, u32[]{:S(2)}, u32[]{:S(2)}) collective-permute-start(bf16[528,128]{1,0:T(8,128)(2,1)S(1)} %get-tuple-element.39), channel_id=1, source_target_pairs={{0,1},{1,2},{2,3},{3,0},{4,5},{5,6},{6,7},{7,4},{8,9},{9,10},{10,1... | collective-permute-start | bytes 405512 | tf_op jit(solution)/shard_map/ppermute | solution.py:421
  68.3 7.3 %collective-permute-start.7 = (bf16[528,128]{1,0:T(8,128)(2,1)S(1)}, bf16[528,128]{1,0:T(8,128)(2,1)S(1)}, u32[]{:S(2)}, u32[]{:S(2)}) collective-permute-start(bf16[528,128]{1,0:T(8,128)(2,1)S(1)} %get-tuple-element.44), channel_id=1, source_target_pairs={{0,3},{1,0},{2,1},{3,2},{4,7},{5,4},{6,5},{7,6},{8,11},{9,8},{10,9... | collective-permute-start | bytes 405512 | tf_op jit(solution)/shard_map/ppermute | solution.py:421
  71.0 5.9 %copy-start.3 = (f32[2,512]{1,0:T(2,128)S(1)}, f32[2,512]{1,0:T(2,128)}, u32[]{:S(2)}) copy-start(f32[2,512]{1,0:T(2,128)} %refs_9_.1) | copy-start | bytes 12292
  71.3 4.4 %collective-permute-start.10 = (bf16[528,128]{1,0:T(8,128)(2,1)S(1)}, bf16[528,128]{1,0:T(8,128)(2,1)S(1)}, u32[]{:S(2)}, u32[]{:S(2)}) collective-permute-start(bf16[528,128]{1,0:T(8,128)(2,1)S(1)} %collective-permute-done.6.own.refs_2_), channel_id=1, source_target_pairs={{0,32},{32,0},{64,96},{96,64},{128,160},{160,128},{192,224},{224,1... | collective-permute-start | bytes 405512 | tf_op jit(solution)/shard_map/ppermute | solution.py:491
  74.5 2.1 %collective-permute-start.8 = (bf16[528,128]{1,0:T(8,128)(2,1)S(1)}, bf16[528,128]{1,0:T(8,128)(2,1)S(1)}, u32[]{:S(2)}, u32[]{:S(2)}) collective-permute-start(bf16[528,128]{1,0:T(8,128)(2,1)S(1)} %collective-permute-done.5.refs_1_), channel_id=1, source_target_pairs={{0,32},{32,0},{64,96},{96,64},{128,160},{160,128},{192,224},{224,1... | collective-permute-start | bytes 405512 | tf_op jit(solution)/shard_map/ppermute | solution.py:491
  75.6 1.4 %collective-permute-start.9 = (bf16[528,128]{1,0:T(8,128)(2,1)S(1)}, bf16[528,128]{1,0:T(8,128)(2,1)S(1)}, u32[]{:S(2)}, u32[]{:S(2)}) collective-permute-start(bf16[528,128]{1,0:T(8,128)(2,1)S(1)} %collective-permute-done.7.refs_3_), channel_id=1, source_target_pairs={{0,32},{32,0},{64,96},{96,64},{128,160},{160,128},{192,224},{224,1... | collective-permute-start | bytes 405512 | tf_op jit(solution)/shard_map/ppermute | solution.py:491

commit v15 on v11

--- a/solution.py
+++ b/solution.py
@@ -223,18 +223,29 @@
     return step
 
 
-def own_half_kernel(pieces, forward, out, wide, planes):
+def asked(part):
+    each = (part.shape[0] - 2 * SG) // 2
+    return vis_rows(part[2 * SG:2 * SG + each].astype(jnp.float32))
+
+
+def own_half_kernel(chips, pieces, forward, *refs):
+    parts, (out, wide, hots, planes) = refs[:chips], refs[chips:]
+    chip = (place()[0] // 2).astype(jnp.float32)
+    counter = sublanes(SG).astype(jnp.float32)
+    for k in range(chips):
+        ask = asked(parts[-k % chips])
+        u_here = jnp.where(ask[0:1] == chip, ask[1:2], -1.0)
+        hots[k] = jnp.where(u_here == counter, 1.0, 0.0).astype(jnp.bfloat16)
     wide[...] = lay_out(pieces, place()[0] % 2, planes, slice(0, HALF))(forward)
     out[...] = planes[2:]
 
 
-def grids_kernel(chips, own, own_wide, other, *refs):
+def grids_kernel(chips, own, own_wide, hots, other, *refs):
     f32, bf16 = jnp.float32, jnp.bfloat16
     parts, (grid_left, forward, inverse_left, inverse) = refs[:chips], refs[chips:chips + 4]
     outs, rest, (planes, cat, tall, hat) = refs[chips + 4:-5], refs[-5], refs[-4:]
     row_index, _ = place()
     core = row_index % 2
-    chip = (row_index // 2).astype(f32)
     at = [pl.ds(pl.multiple_of(half * HALF, HALF), HALF) for half in (core, 1 - core)]
     wide = (own_wide[...] + lay_out(other, 1 - core, planes, at[1])(forward)).astype(bf16)
     for p in range(3):
@@ -254,14 +265,11 @@
     rest[...] = jnp.where(core == 0, back[:, HALF:], back[:, :HALF]).astype(bf16)
     back = jnp.where(core == 0, back[:, :HALF], back[:, HALF:]).astype(bf16)
     counter = sublanes(SG).astype(f32)
-    vis_each = (parts[0].shape[0] - 2 * SG) // 2
     for k, out in enumerate(outs):
         out[:2 * SG] = back
-        ask = vis_rows(parts[-k % chips][2 * SG:2 * SG + vis_each].astype(f32))
-        u_here = jnp.where(ask[0:1] == chip, ask[1:2], -1.0)
-        hot = jnp.where(u_here == counter, 1.0, 0.0).astype(bf16)
+        ask = asked(parts[-k % chips])
         pick = ask[2:3] == counter
-        line = lax.dot_general(hat[...], hot, (((0,), (0,)), ((), ())), preferred_element_type=f32)
+        line = lax.dot_general(hat[...], hots[k], (((0,), (0,)), ((), ())), preferred_element_type=f32)
         rows = []
         for part in range(2):
             value = jnp.sum(jnp.where(pick, line[part * SG:(part + 1) * SG], 0.0), axis=0, keepdims=True)
@@ -435,7 +443,6 @@
             functools.partial(contribution_kernel, scale_in, k), shape(2 * SG + vis_rows_count, HALF), "contribution",
             "vvvv", cost=5 * 10**8,
         )(own, vis, other, row_tab)
-        own, parts[k] = lax.optimization_barrier((own, parts[k]))
     parts = turned(parts)
 
     sums = call(first_sums_kernel, shape(5, SG, HALF, dtype=f32), "first_sums", "vv", cost=10**9)(parts[0], parts[2])
@@ -456,19 +463,20 @@
     block = [np.concatenate(pair, 1) for pair in ((kcos, ksin), (-ksin, kcos), (kcos, -ksin), (ksin, kcos))]
     forward_block = np.concatenate([block[0], block[1]], 0)
     inverse_block = np.concatenate([block[2], block[3]], 0)
-    own_planes, own_wide = call(
-        own_half_kernel, (shape(3, SG, HALF, dtype=f32), shape(SG, 2 * SG, dtype=f32)), "own_half", "vv",
+    own_planes, own_wide, hots = call(
+        functools.partial(own_half_kernel, chips),
+        (shape(3, SG, HALF, dtype=f32), shape(SG, 2 * SG, dtype=f32), shape(chips, SG, n_vis)), "own_half", "vv" + "v" * chips,
         scratch=[pltpu.VMEM((5, SG, HALF), f32)], cost=10**9,
-    )(pieces, forward_block)
+    )(pieces, forward_block, *parts)
     *back, rest = call(
         functools.partial(grids_kernel, chips), (shape(2 * SG + 16, HALF),) * chips + (shape(2 * SG, HALF),), "grids",
-        "v" * (7 + chips),
+        "v" * (8 + chips),
         scratch=[
             pltpu.VMEM((5, SG, SG), f32), pltpu.VMEM((SG, 2 * SG), bf16), pltpu.VMEM((2 * SG, SG), bf16),
             pltpu.VMEM((SG, 2 * SG), bf16),
         ],
         cost=10**9,
-    )(own_planes, own_wide, pieces_other, *parts, inverse_block, forward_block, forward_block, inverse_block)
+    )(own_planes, own_wide, hots, pieces_other, *parts, inverse_block, forward_block, forward_block, inverse_block)
     back = turned(back)
 
     both = pltpu.VMEM((side, 2 * SG), bf16)

time: 79.2 us -> 78.9 us (level)
  waiting for transfers between devices: 7.77 us -> 6.93 us
  transfers between devices with their start and end apart: 11 -> 11, of which waited for: 8 -> 8; matrix products, arithmetic and copies ran while one was open for 0% -> 0% of each run, Pallas kernels for 8% -> 9%
where the time goes in v15:
time: 78.9 us; the launch traced here: 78.7 us
  blocking collectives  37.5 us (48%)
  starting transfers between devices  19.1 us (24%)
  Pallas kernels  14.1 us (18%)
  waiting for transfers between devices  6.93 us (9%)
  between operations  0.96 us (1%)
    all_to_all x2, blocking collectives, exchange(): lax.all_to_all(blocks, axes, 0, 0, tiled=True, axis_index_groups=groups)  37.5 us
    ppermute x6, starting transfers between devices, turned(): moved = {k: lax.ppermute(blocks[k], 'frow', turns[k]) for k in (2, 1, 3)}  8.16 us
    ppermute x6, waiting for transfers between devices, turned(): moved = {k: lax.ppermute(blocks[k], 'frow', turns[k]) for k in (2, 1, 3)}  5.51 us
    ppermute x1, starting transfers between devices, shards(): pieces_other = lax.ppermute(pieces, 'frow', swap)  4.69 us
    ppermute x1, starting transfers between devices, shards(): other = lax.ppermute(send, 'frow', swap)  3.32 us
    ppermute x3, starting transfers between devices, shards(): rest = {k: lax.ppermute(back[k], 'frow', swap) for k in (2, 1, 3)}  2.97 us
    pallas_call x1, Pallas kernels, shards(): call(functools.partial(send_columns_kernel, cols_count), (shape(side + 16...  2.34 us
    pallas_call x1, Pallas kernels, shards(): call(functools.partial(own_tables_kernel, rows_count, cols_count), (shape...  1.9 us
  transfers between devices with their start and end apart: 11, of which 8 were waited for; matrix products, arithmetic and copies ran while one was open for 0% of the time, Pallas kernels for 9%

profile of v15, /device:TPU:1, one launch (start us, length us, event | category | flops | bytes accessed | tf_op | source)
XLA Modules:
  0.0 78.7 jit_solution(12807837147516386151)
XLA Ops:
  0.6 0.0 copy-start.6
  0.6 0.0 copy-start.4
  0.7 0.0 copy-start.5
  0.7 2.3 %send_columns.1 = (bf16[528,512]{1,0:T(8,128)(2,1)}, bf16[16,256]{1,0:T(8,128)(2,1)}) custom-call(s32[2]{0:T(128)} %offsets_col.1, bf16[512,512]{1,0:T(8,128)(2,1)} %facet.3, s32[1,512]{1,0:T(1,128)} %bitcast.3, s32[1,512]{1,0:T(1,128)} %bitcast.4, s32[1,512]{1,0:T(1,128)} %bitcast.5, f32[2,512]{1,0:T(2,128)} %refs_9_.1), custom_call_target="tpu_custom_call" | custom-call | flops 1000000000 | bytes 1048576 | tf_op jit(solution)/shard_map/send_columns/pallas_call | solution.py:423
  3.0 0.0 copy-start.2
  3.0 3.3 %collective-permute-start = (bf16[528,512]{1,0:T(8,128)(2,1)}, bf16[528,512]{1,0:T(8,128)(2,1)S(1)}, u32[]{:S(2)}, u32[]{:S(2)}) collective-permute-start(bf16[528,512]{1,0:T(8,128)(2,1)} %get-tuple-element.20), channel_id=1, source_target_pairs={{0,32},{32,0},{64,96},{96,64},{128,160},{160,128},{192,224},{224,1... | collective-permute-start | bytes 1622024 | tf_op jit(solution)/shard_map/ppermute | solution.py:433
  6.3 0.0 copy-done.6
  6.3 0.0 copy-done.4
  6.3 0.0 copy-done.5
  6.3 1.9 %own_tables.1 = (bf16[512,512]{1,0:T(8,128)(2,1)S(1)}, bf16[4,256,1024]{2,1,0:T(8,128)(2,1)S(1)}) custom-call(s32[2]{0:T(128)S(1)} %copy-done.5, s32[2]{0:T(128)S(1)} %copy-done.6, bf16[512,512]{1,0:T(8,128)(2,1)S(1)} %copy-done.4), custom_call_target="tpu_custom_call" | custom-call | flops 1000000000 | bytes 1048576 | tf_op jit(solution)/shard_map/own_tables/pallas_call | solution.py:434
  8.3 0.0 collective-permute-done.other
  8.3 0.5 contribution.7
  8.7 1.1 %collective-permute-start.3 = (bf16[576,128]{1,0:T(8,128)(2,1)S(1)}, bf16[576,128]{1,0:T(8,128)(2,1)S(1)}, u32[]{:S(2)}, u32[]{:S(2)}) collective-permute-start(bf16[576,128]{1,0:T(8,128)(2,1)S(1)} %contribution.7), channel_id=1, source_target_pairs={{0,128},{32,160},{64,192},{96,224},{128,0},{160,32},{192,64},{224,... | collective-permute-start | bytes 442376 | tf_op jit(solution)/shard_map/ppermute | solution.py:416
  9.8 0.4 contribution.5
  10.3 0.9 %collective-permute-start.2 = (bf16[576,128]{1,0:T(8,128)(2,1)S(1)}, bf16[576,128]{1,0:T(8,128)(2,1)S(1)}, u32[]{:S(2)}, u32[]{:S(2)}) collective-permute-start(bf16[576,128]{1,0:T(8,128)(2,1)S(1)} %contribution.5), channel_id=1, source_target_pairs={{0,192},{32,224},{64,0},{96,32},{128,64},{160,96},{192,128},{224,1... | collective-permute-start | bytes 442376 | tf_op jit(solution)/shard_map/ppermute | solution.py:416
  11.2 0.4 contribution.4
  11.7 0.7 collective-permute-start.1
  12.3 1.4 %back_tables.1 = (bf16[512,1024]{1,0:T(8,128)(2,1)S(1)}, bf16[1024,512]{1,0:T(8,128)(2,1)S(1)}) custom-call(s32[2]{0:T(128)S(1)} %copy-done.5, s32[2]{0:T(128)S(1)} %copy-done.6), custom_call_target="tpu_custom_call" | custom-call | flops 1000000000 | bytes 1048576 | tf_op jit(solution)/shard_map/back_tables/pallas_call | solution.py:449
  13.7 0.5 contribution.6.refs_0_
  14.2 1.4 %collective-permute-done.3.refs_1_.refs_2_ = bf16[576,128]{1,0:T(8,128)(2,1)S(1)} collective-permute-done((bf16[576,128]{1,0:T(8,128)(2,1)S(1)}, bf16[576,128]{1,0:T(8,128)(2,1)S(1)}, u32[]{:S(2)}, u32[]{:S(2)}) %collective-permute-start.3) | collective-permute-done | bytes 147488 | tf_op jit(solution)/shard_map/ppermute | solution.py:416
  15.6 0.8 first_sums.1.refs_2_
  16.4 0.7 collective-permute-done.2.refs_1_.refs_3_
  17.1 1.6 %collective-permute-done.1.refs_0_.refs_1_ = bf16[576,128]{1,0:T(8,128)(2,1)S(1)} collective-permute-done((bf16[576,128]{1,0:T(8,128)(2,1)S(1)}, bf16[576,128]{1,0:T(8,128)(2,1)S(1)}, u32[]{:S(2)}, u32[]{:S(2)}) %collective-permute-start.1) | collective-permute-done | bytes 147488 | tf_op jit(solution)/shard_map/ppermute | solution.py:416
  18.7 0.8 gridding.1
  19.5 20.6 %all_to_all.10.pieces = bf16[32,40,128]{2,1,0:T(8,128)(2,1)S(1)} all-to-all(bf16[32,40,128]{2,1,0:T(8,128)(2,1)S(1)} %gridding.1), channel_id=1, replica_groups=mesh['frow'=8,'fcol'=32] {'fcol'}, dimensions={0} | all-to-all | bytes 655360 | tf_op jit(solution)/shard_map/all_to_all | solution.py:398
  40.1 0.1 pieces_sum.1
  40.2 0.0 copy-start.1
  40.2 16.9 %all_to_all.11.pieces = bf16[32,40,128]{2,1,0:T(8,128)(2,1)S(1)} all-to-all(bf16[32,40,128]{2,1,0:T(8,128)(2,1)S(1)} %pieces_sum.1), channel_id=1, replica_groups=mesh['frow'=8,'fcol'=32] {'fcol'}, dimensions={0} | all-to-all | bytes 655360 | tf_op jit(solution)/shard_map/all_to_all | solution.py:398
  57.1 4.7 %collective-permute-start.4 = (bf16[32,40,128]{2,1,0:T(8,128)(2,1)S(1)}, bf16[32,40,128]{2,1,0:T(8,128)(2,1)S(1)}, u32[]{:S(2)}, u32[]{:S(2)}) collective-permute-start(bf16[32,40,128]{2,1,0:T(8,128)(2,1)S(1)} %all_to_all.11.pieces), channel_id=1, source_target_pairs={{0,32},{32,0},{64,96},{96,64},{128,160},{160,128},{192,224},{224,1... | collective-permute-start | bytes 983048 | tf_op jit(solution)/shard_map/ppermute | solution.py:460
  61.8 0.4 own_half.1
  62.2 0.8 %collective-permute-done.4.other = bf16[32,40,128]{2,1,0:T(8,128)(2,1)S(1)} collective-permute-done((bf16[32,40,128]{2,1,0:T(8,128)(2,1)S(1)}, bf16[32,40,128]{2,1,0:T(8,128)(2,1)S(1)}, u32[]{:S(2)}, u32[]{:S(2)}) %collective-permute-start.4) | collective-permute-done | bytes 327712 | tf_op jit(solution)/shard_map/ppermute | solution.py:460
  63.0 1.6 %grids.1 = (bf16[528,128]{1,0:T(8,128)(2,1)S(1)}, bf16[528,128]{1,0:T(8,128)(2,1)S(1)}, bf16[528,128]{1,0:T(8,128)(2,1)S(1)}, bf16[528,128]{1,0:T(8,128)(2,1)S(1)}, bf16[512,128]{1,0:T(8,128)(2,1)S(1)}) custom-call(f32[3,256,128]{2,1,0:T(8,128)S(1)} %get-tuple-element.23.own, f32[256,512]{1,0:T(8,128)S(1)} %get-tuple-element.24.own_wide, ...), custom_call_target="tpu_custom_call" | custom-call | flops 1000000000 | bytes 1048576 | tf_op jit(solution)/shard_map/grids/pallas_call | solution.py:471
  64.6 2.8 %collective-permute-start.6 = (bf16[528,128]{1,0:T(8,128)(2,1)S(1)}, bf16[528,128]{1,0:T(8,128)(2,1)S(1)}, u32[]{:S(2)}, u32[]{:S(2)}) collective-permute-start(bf16[528,128]{1,0:T(8,128)(2,1)S(1)} %get-tuple-element.28), channel_id=1, source_target_pairs={{0,128},{32,160},{64,192},{96,224},{128,0},{160,32},{192,64},{224,... | collective-permute-start | bytes 405512 | tf_op jit(solution)/shard_map/ppermute | solution.py:416
  67.4 0.4 collective-permute-start.5
  67.8 2.3 %collective-permute-start.7 = (bf16[528,128]{1,0:T(8,128)(2,1)S(1)}, bf16[528,128]{1,0:T(8,128)(2,1)S(1)}, u32[]{:S(2)}, u32[]{:S(2)}) collective-permute-start(bf16[528,128]{1,0:T(8,128)(2,1)S(1)} %get-tuple-element.32), channel_id=1, source_target_pairs={{0,192},{32,224},{64,0},{96,32},{128,64},{160,96},{192,128},{224,1... | collective-permute-start | bytes 405512 | tf_op jit(solution)/shard_map/ppermute | solution.py:416
  70.1 0.4 first_part.1.first
  70.5 0.0 copy-start.3
  70.5 0.5 collective-permute-done.6.own.refs_2_
  71.0 2.0 %collective-permute-start.10 = (bf16[528,128]{1,0:T(8,128)(2,1)S(1)}, bf16[528,128]{1,0:T(8,128)(2,1)S(1)}, u32[]{:S(2)}, u32[]{:S(2)}) collective-permute-start(bf16[528,128]{1,0:T(8,128)(2,1)S(1)} %collective-permute-done.6.own.refs_2_), channel_id=1, source_target_pairs={{0,32},{32,0},{64,96},{96,64},{128,160},{160,128},{192,224},{224,1... | collective-permute-start | bytes 405512 | tf_op jit(solution)/shard_map/ppermute | solution.py:486
  73.0 1.3 %collective-permute-done.5.refs_1_ = bf16[528,128]{1,0:T(8,128)(2,1)S(1)} collective-permute-done((bf16[528,128]{1,0:T(8,128)(2,1)S(1)}, bf16[528,128]{1,0:T(8,128)(2,1)S(1)}, u32[]{:S(2)}, u32[]{:S(2)}) %collective-permute-start.5) | collective-permute-done | bytes 135200 | tf_op jit(solution)/shard_map/ppermute | solution.py:416
  74.3 1.0 %collective-permute-start.8 = (bf16[528,128]{1,0:T(8,128)(2,1)S(1)}, bf16[528,128]{1,0:T(8,128)(2,1)S(1)}, u32[]{:S(2)}, u32[]{:S(2)}) collective-permute-start(bf16[528,128]{1,0:T(8,128)(2,1)S(1)} %collective-permute-done.5.refs_1_), channel_id=1, source_target_pairs={{0,32},{32,0},{64,96},{96,64},{128,160},{160,128},{192,224},{224,1... | collective-permute-start | bytes 405512 | tf_op jit(solution)/shard_map/ppermute | solution.py:486
  75.3 0.0 collective-permute-done.7.refs_3_
  75.3 0.0 collective-permute-start.9
  75.3 0.0 collective-permute-done.10.rest
  75.3 0.7 own_column.1.refs_6_
  76.0 0.2 collective-permute-done.8.refs_4_
  76.3 0.4 collective-permute-done.9.refs_5_
  76.6 1.9 %image.1 = (f32[512,512]{1,0:T(8,128)}, f32[2,512]{1,0:T(2,128)}) custom-call(bf16[528,128]{1,0:T(8,128)(2,1)S(1)} %get-tuple-element.26.own.refs_0_, bf16[528,128]{1,0:T(8,128)(2,1)S(1)} %collective-permute-done.5.refs_1_, bf16[528,128]{1,0:T(8,128)(2,1)S(1)} %collective-permute-done.6.own.refs_2_, bf16[528,128]{1,0:T(8,128)(2,1)S(1)} %collective-permute-done.7.refs_3_, ...), custom_call_target="tpu_custom_call" | custom-call | flops 1000000000 | bytes 1048576 | tf_op jit(solution)/shard_map/image/pallas_call | solution.py:490
  (5 shorter events, 0.0 us)
Async XLA Ops:
  0.6 5.7 %copy-start.6 = (s32[2]{0:T(128)S(1)}, s32[2]{0:T(128)}, u32[]{:S(2)}) copy-start(s32[2]{0:T(128)} %offsets_col.1) | copy-start | bytes 28
  0.6 5.7 %copy-start.4 = (bf16[512,512]{1,0:T(8,128)(2,1)S(1)}, bf16[512,512]{1,0:T(8,128)(2,1)}, u32[]{:S(2)}) copy-start(bf16[512,512]{1,0:T(8,128)(2,1)} %facet.3) | copy-start | bytes 1572868
  0.7 5.7 %copy-start.5 = (s32[2]{0:T(128)S(1)}, s32[2]{0:T(128)}, u32[]{:S(2)}) copy-start(s32[2]{0:T(128)} %offsets_row.1) | copy-start | bytes 28
  3.0 5.3 %copy-start.2 = (bf16[16,256]{1,0:T(8,128)(2,1)S(1)}, bf16[16,256]{1,0:T(8,128)(2,1)}, u32[]{:S(2)}) copy-start(bf16[16,256]{1,0:T(8,128)(2,1)} %get-tuple-element.19.own_vis) | copy-start | bytes 24580
  3.0 5.2 %collective-permute-start = (bf16[528,512]{1,0:T(8,128)(2,1)}, bf16[528,512]{1,0:T(8,128)(2,1)S(1)}, u32[]{:S(2)}, u32[]{:S(2)}) collective-permute-start(bf16[528,512]{1,0:T(8,128)(2,1)} %get-tuple-element.20), channel_id=1, source_target_pairs={{0,32},{32,0},{64,96},{96,64},{128,160},{160,128},{192,224},{224,1... | collective-permute-start | bytes 1622024 | tf_op jit(solution)/shard_map/ppermute | solution.py:433
  8.7 6.9 %collective-permute-start.3 = (bf16[576,128]{1,0:T(8,128)(2,1)S(1)}, bf16[576,128]{1,0:T(8,128)(2,1)S(1)}, u32[]{:S(2)}, u32[]{:S(2)}) collective-permute-start(bf16[576,128]{1,0:T(8,128)(2,1)S(1)} %contribution.7), channel_id=1, source_target_pairs={{0,128},{32,160},{64,192},{96,224},{128,0},{160,32},{192,64},{224,... | collective-permute-start | bytes 442376 | tf_op jit(solution)/shard_map/ppermute | solution.py:416
  10.3 6.8 %collective-permute-start.2 = (bf16[576,128]{1,0:T(8,128)(2,1)S(1)}, bf16[576,128]{1,0:T(8,128)(2,1)S(1)}, u32[]{:S(2)}, u32[]{:S(2)}) collective-permute-start(bf16[576,128]{1,0:T(8,128)(2,1)S(1)} %contribution.5), channel_id=1, source_target_pairs={{0,192},{32,224},{64,0},{96,32},{128,64},{160,96},{192,128},{224,1... | collective-permute-start | bytes 442376 | tf_op jit(solution)/shard_map/ppermute | solution.py:416
  11.7 7.1 %collective-permute-start.1 = (bf16[576,128]{1,0:T(8,128)(2,1)S(1)}, bf16[576,128]{1,0:T(8,128)(2,1)S(1)}, u32[]{:S(2)}, u32[]{:S(2)}) collective-permute-start(bf16[576,128]{1,0:T(8,128)(2,1)S(1)} %contribution.4), channel_id=1, source_target_pairs={{0,64},{32,96},{64,128},{96,160},{128,192},{160,224},{192,0},{224,... | collective-permute-start | bytes 442376 | tf_op jit(solution)/shard_map/ppermute | solution.py:416
  18.7 43.0 %copy-start = (bf16[512,512]{1,0:T(8,128)(2,1)S(1)}, bf16[512,512]{1,0:T(8,128)(2,1)}, u32[]{:S(2)}) copy-start(bf16[512,512]{1,0:T(8,128)(2,1)} %constant.4.clone.forward.refs_5_.refs_6_) | copy-start | bytes 1572868
  40.2 22.8 %copy-start.1 = (bf16[512,512]{1,0:T(8,128)(2,1)S(1)}, bf16[512,512]{1,0:T(8,128)(2,1)}, u32[]{:S(2)}) copy-start(bf16[512,512]{1,0:T(8,128)(2,1)} %constant.5.clone.refs_4_.refs_7_) | copy-start | bytes 1572868
  57.1 5.9 %collective-permute-start.4 = (bf16[32,40,128]{2,1,0:T(8,128)(2,1)S(1)}, bf16[32,40,128]{2,1,0:T(8,128)(2,1)S(1)}, u32[]{:S(2)}, u32[]{:S(2)}) collective-permute-start(bf16[32,40,128]{2,1,0:T(8,128)(2,1)S(1)} %all_to_all.11.pieces), channel_id=1, source_target_pairs={{0,32},{32,0},{64,96},{96,64},{128,160},{160,128},{192,224},{224,1... | collective-permute-start | bytes 983048 | tf_op jit(solution)/shard_map/ppermute | solution.py:460
  64.6 6.4 %collective-permute-start.6 = (bf16[528,128]{1,0:T(8,128)(2,1)S(1)}, bf16[528,128]{1,0:T(8,128)(2,1)S(1)}, u32[]{:S(2)}, u32[]{:S(2)}) collective-permute-start(bf16[528,128]{1,0:T(8,128)(2,1)S(1)} %get-tuple-element.28), channel_id=1, source_target_pairs={{0,128},{32,160},{64,192},{96,224},{128,0},{160,32},{192,64},{224,... | collective-permute-start | bytes 405512 | tf_op jit(solution)/shard_map/ppermute | solution.py:416
  67.4 6.9 %collective-permute-start.5 = (bf16[528,128]{1,0:T(8,128)(2,1)S(1)}, bf16[528,128]{1,0:T(8,128)(2,1)S(1)}, u32[]{:S(2)}, u32[]{:S(2)}) collective-permute-start(bf16[528,128]{1,0:T(8,128)(2,1)S(1)} %get-tuple-element.27), channel_id=1, source_target_pairs={{0,64},{32,96},{64,128},{96,160},{128,192},{160,224},{192,0},{224,... | collective-permute-start | bytes 405512 | tf_op jit(solution)/shard_map/ppermute | solution.py:416
  67.8 7.5 %collective-permute-start.7 = (bf16[528,128]{1,0:T(8,128)(2,1)S(1)}, bf16[528,128]{1,0:T(8,128)(2,1)S(1)}, u32[]{:S(2)}, u32[]{:S(2)}) collective-permute-start(bf16[528,128]{1,0:T(8,128)(2,1)S(1)} %get-tuple-element.32), channel_id=1, source_target_pairs={{0,192},{32,224},{64,0},{96,32},{128,64},{160,96},{192,128},{224,1... | collective-permute-start | bytes 405512 | tf_op jit(solution)/shard_map/ppermute | solution.py:416
  70.5 6.1 %copy-start.3 = (f32[2,512]{1,0:T(2,128)S(1)}, f32[2,512]{1,0:T(2,128)}, u32[]{:S(2)}) copy-start(f32[2,512]{1,0:T(2,128)} %refs_9_.1) | copy-start | bytes 12292
  71.0 4.3 %collective-permute-start.10 = (bf16[528,128]{1,0:T(8,128)(2,1)S(1)}, bf16[528,128]{1,0:T(8,128)(2,1)S(1)}, u32[]{:S(2)}, u32[]{:S(2)}) collective-permute-start(bf16[528,128]{1,0:T(8,128)(2,1)S(1)} %collective-permute-done.6.own.refs_2_), channel_id=1, source_target_pairs={{0,32},{32,0},{64,96},{96,64},{128,160},{160,128},{192,224},{224,1... | collective-permute-start | bytes 405512 | tf_op jit(solution)/shard_map/ppermute | solution.py:486
  74.3 2.0 %collective-permute-start.8 = (bf16[528,128]{1,0:T(8,128)(2,1)S(1)}, bf16[528,128]{1,0:T(8,128)(2,1)S(1)}, u32[]{:S(2)}, u32[]{:S(2)}) collective-permute-start(bf16[528,128]{1,0:T(8,128)(2,1)S(1)} %collective-permute-done.5.refs_1_), channel_id=1, source_target_pairs={{0,32},{32,0},{64,96},{96,64},{128,160},{160,128},{192,224},{224,1... | collective-permute-start | bytes 405512 | tf_op jit(solution)/shard_map/ppermute | solution.py:486
  75.3 1.4 %collective-permute-start.9 = (bf16[528,128]{1,0:T(8,128)(2,1)S(1)}, bf16[528,128]{1,0:T(8,128)(2,1)S(1)}, u32[]{:S(2)}, u32[]{:S(2)}) collective-permute-start(bf16[528,128]{1,0:T(8,128)(2,1)S(1)} %collective-permute-done.7.refs_3_), channel_id=1, source_target_pairs={{0,32},{32,0},{64,96},{96,64},{128,160},{160,128},{192,224},{224,1... | collective-permute-start | bytes 405512 | tf_op jit(solution)/shard_map/ppermute | solution.py:486

commit v16 on v15

--- a/solution.py
+++ b/solution.py
@@ -256,8 +256,8 @@
     hat_real, hat_imag = model[:SG], model[SG:]
     cat[:, :SG] = (planes[2] - planes[4] * hat_real).astype(bf16)
     cat[:, SG:] = (planes[3] - planes[4] * hat_imag).astype(bf16)
-    hat[:, :SG] = hat_real.astype(bf16)
-    hat[:, SG:] = hat_imag.astype(bf16)
+    hat[:SG] = hat_real.T.astype(bf16)
+    hat[SG:] = hat_imag.T.astype(bf16)
     wide = jnp.dot(cat[...], inverse[...], preferred_element_type=f32)
     for k in range(2):
         tall[k * SG:(k + 1) * SG] = wide[:, k * SG:(k + 1) * SG].astype(bf16)
@@ -269,7 +269,7 @@
         out[:2 * SG] = back
         ask = asked(parts[-k % chips])
         pick = ask[2:3] == counter
-        line = lax.dot_general(hat[...], hots[k], (((0,), (0,)), ((), ())), preferred_element_type=f32)
+        line = jnp.dot(hat[...], hots[k], preferred_element_type=f32)
         rows = []
         for part in range(2):
             value = jnp.sum(jnp.where(pick, line[part * SG:(part + 1) * SG], 0.0), axis=0, keepdims=True)
@@ -473,7 +473,7 @@
         "v" * (8 + chips),
         scratch=[
             pltpu.VMEM((5, SG, SG), f32), pltpu.VMEM((SG, 2 * SG), bf16), pltpu.VMEM((2 * SG, SG), bf16),
-            pltpu.VMEM((SG, 2 * SG), bf16),
+            pltpu.VMEM((2 * SG, SG), bf16),
         ],
         cost=10**9,
     )(own_planes, own_wide, hots, pieces_other, *parts, inverse_block, forward_block, forward_block, inverse_block)

time: 78.9 us -> 78.9 us (level)
  no operation moved by 1% of the time
where the time goes in v16:
time: 78.9 us; the launch traced here: 78.7 us
  blocking collectives  37.5 us (48%)
  starting transfers between devices  19.1 us (24%)
  Pallas kernels  14.1 us (18%)
  waiting for transfers between devices  6.93 us (9%)
  between operations  0.96 us (1%)
    all_to_all x2, blocking collectives, exchange(): lax.all_to_all(blocks, axes, 0, 0, tiled=True, axis_index_groups=groups)  37.5 us
    ppermute x6, starting transfers between devices, turned(): moved = {k: lax.ppermute(blocks[k], 'frow', turns[k]) for k in (2, 1, 3)}  8.16 us
    ppermute x6, waiting for transfers between devices, turned(): moved = {k: lax.ppermute(blocks[k], 'frow', turns[k]) for k in (2, 1, 3)}  5.52 us
    ppermute x1, starting transfers between devices, shards(): pieces_other = lax.ppermute(pieces, 'frow', swap)  4.69 us
    ppermute x1, starting transfers between devices, shards(): other = lax.ppermute(send, 'frow', swap)  3.32 us
    ppermute x3, starting transfers between devices, shards(): rest = {k: lax.ppermute(back[k], 'frow', swap) for k in (2, 1, 3)}  2.97 us
    pallas_call x1, Pallas kernels, shards(): call(functools.partial(send_columns_kernel, cols_count), (shape(side + 16...  2.34 us
    pallas_call x1, Pallas kernels, shards(): call(functools.partial(own_tables_kernel, rows_count, cols_count), (shape...  1.9 us
  transfers between devices with their start and end apart: 11, of which 8 were waited for; matrix products, arithmetic and copies ran while one was open for 0% of the time, Pallas kernels for 9%

profile of v16, /device:TPU:1, one launch (start us, length us, event | category | flops | bytes accessed | tf_op | source)
XLA Modules:
  0.0 78.7 jit_solution(13777203928468752505)
XLA Ops:
  0.6 0.0 copy-start.6
  0.6 0.0 copy-start.4
  0.7 0.0 copy-start.5
  0.7 2.3 %send_columns.1 = (bf16[528,512]{1,0:T(8,128)(2,1)}, bf16[16,256]{1,0:T(8,128)(2,1)}) custom-call(s32[2]{0:T(128)} %offsets_col.1, bf16[512,512]{1,0:T(8,128)(2,1)} %facet.3, s32[1,512]{1,0:T(1,128)} %bitcast.3, s32[1,512]{1,0:T(1,128)} %bitcast.4, s32[1,512]{1,0:T(1,128)} %bitcast.5, f32[2,512]{1,0:T(2,128)} %refs_9_.1), custom_call_target="tpu_custom_call" | custom-call | flops 1000000000 | bytes 1048576 | tf_op jit(solution)/shard_map/send_columns/pallas_call | solution.py:423
  3.0 0.0 copy-start.2
  3.0 3.3 %collective-permute-start = (bf16[528,512]{1,0:T(8,128)(2,1)}, bf16[528,512]{1,0:T(8,128)(2,1)S(1)}, u32[]{:S(2)}, u32[]{:S(2)}) collective-permute-start(bf16[528,512]{1,0:T(8,128)(2,1)} %get-tuple-element.20), channel_id=1, source_target_pairs={{0,32},{32,0},{64,96},{96,64},{128,160},{160,128},{192,224},{224,1... | collective-permute-start | bytes 1622024 | tf_op jit(solution)/shard_map/ppermute | solution.py:433
  6.3 0.0 copy-done.5
  6.3 1.9 %own_tables.1 = (bf16[512,512]{1,0:T(8,128)(2,1)S(1)}, bf16[4,256,1024]{2,1,0:T(8,128)(2,1)S(1)}) custom-call(s32[2]{0:T(128)S(1)} %copy-done.5, s32[2]{0:T(128)S(1)} %copy-done.6, bf16[512,512]{1,0:T(8,128)(2,1)S(1)} %copy-done.4), custom_call_target="tpu_custom_call" | custom-call | flops 1000000000 | bytes 1048576 | tf_op jit(solution)/shard_map/own_tables/pallas_call | solution.py:434
  8.3 0.0 collective-permute-done.other
  8.3 0.0 copy-done.2
  8.3 0.5 contribution.7
  8.7 1.1 %collective-permute-start.3 = (bf16[576,128]{1,0:T(8,128)(2,1)S(1)}, bf16[576,128]{1,0:T(8,128)(2,1)S(1)}, u32[]{:S(2)}, u32[]{:S(2)}) collective-permute-start(bf16[576,128]{1,0:T(8,128)(2,1)S(1)} %contribution.7), channel_id=1, source_target_pairs={{0,128},{32,160},{64,192},{96,224},{128,0},{160,32},{192,64},{224,... | collective-permute-start | bytes 442376 | tf_op jit(solution)/shard_map/ppermute | solution.py:416
  9.8 0.4 contribution.5
  10.3 0.9 %collective-permute-start.2 = (bf16[576,128]{1,0:T(8,128)(2,1)S(1)}, bf16[576,128]{1,0:T(8,128)(2,1)S(1)}, u32[]{:S(2)}, u32[]{:S(2)}) collective-permute-start(bf16[576,128]{1,0:T(8,128)(2,1)S(1)} %contribution.5), channel_id=1, source_target_pairs={{0,192},{32,224},{64,0},{96,32},{128,64},{160,96},{192,128},{224,1... | collective-permute-start | bytes 442376 | tf_op jit(solution)/shard_map/ppermute | solution.py:416
  11.2 0.4 contribution.4
  11.7 0.7 collective-permute-start.1
  12.3 1.4 %back_tables.1 = (bf16[512,1024]{1,0:T(8,128)(2,1)S(1)}, bf16[1024,512]{1,0:T(8,128)(2,1)S(1)}) custom-call(s32[2]{0:T(128)S(1)} %copy-done.5, s32[2]{0:T(128)S(1)} %copy-done.6), custom_call_target="tpu_custom_call" | custom-call | flops 1000000000 | bytes 1048576 | tf_op jit(solution)/shard_map/back_tables/pallas_call | solution.py:449
  13.7 0.5 contribution.6.refs_0_
  14.2 1.4 %collective-permute-done.3.refs_1_.refs_2_ = bf16[576,128]{1,0:T(8,128)(2,1)S(1)} collective-permute-done((bf16[576,128]{1,0:T(8,128)(2,1)S(1)}, bf16[576,128]{1,0:T(8,128)(2,1)S(1)}, u32[]{:S(2)}, u32[]{:S(2)}) %collective-permute-start.3) | collective-permute-done | bytes 147488 | tf_op jit(solution)/shard_map/ppermute | solution.py:416
  15.6 0.8 first_sums.1.refs_2_
  16.4 0.7 collective-permute-done.2.refs_1_.refs_3_
  17.1 1.6 %collective-permute-done.1.refs_0_.refs_1_ = bf16[576,128]{1,0:T(8,128)(2,1)S(1)} collective-permute-done((bf16[576,128]{1,0:T(8,128)(2,1)S(1)}, bf16[576,128]{1,0:T(8,128)(2,1)S(1)}, u32[]{:S(2)}, u32[]{:S(2)}) %collective-permute-start.1) | collective-permute-done | bytes 147488 | tf_op jit(solution)/shard_map/ppermute | solution.py:416
  18.7 0.8 gridding.1
  19.5 20.6 %all_to_all.10.pieces = bf16[32,40,128]{2,1,0:T(8,128)(2,1)S(1)} all-to-all(bf16[32,40,128]{2,1,0:T(8,128)(2,1)S(1)} %gridding.1), channel_id=1, replica_groups=mesh['frow'=8,'fcol'=32] {'fcol'}, dimensions={0} | all-to-all | bytes 655360 | tf_op jit(solution)/shard_map/all_to_all | solution.py:398
  40.1 0.1 pieces_sum.1
  40.2 0.0 copy-start.1
  40.2 16.9 %all_to_all.11.pieces = bf16[32,40,128]{2,1,0:T(8,128)(2,1)S(1)} all-to-all(bf16[32,40,128]{2,1,0:T(8,128)(2,1)S(1)} %pieces_sum.1), channel_id=1, replica_groups=mesh['frow'=8,'fcol'=32] {'fcol'}, dimensions={0} | all-to-all | bytes 655360 | tf_op jit(solution)/shard_map/all_to_all | solution.py:398
  57.1 4.7 %collective-permute-start.4 = (bf16[32,40,128]{2,1,0:T(8,128)(2,1)S(1)}, bf16[32,40,128]{2,1,0:T(8,128)(2,1)S(1)}, u32[]{:S(2)}, u32[]{:S(2)}) collective-permute-start(bf16[32,40,128]{2,1,0:T(8,128)(2,1)S(1)} %all_to_all.11.pieces), channel_id=1, source_target_pairs={{0,32},{32,0},{64,96},{96,64},{128,160},{160,128},{192,224},{224,1... | collective-permute-start | bytes 983048 | tf_op jit(solution)/shard_map/ppermute | solution.py:460
  61.7 0.0 copy-done
  61.8 0.4 own_half.1
  62.2 0.8 %collective-permute-done.4.other = bf16[32,40,128]{2,1,0:T(8,128)(2,1)S(1)} collective-permute-done((bf16[32,40,128]{2,1,0:T(8,128)(2,1)S(1)}, bf16[32,40,128]{2,1,0:T(8,128)(2,1)S(1)}, u32[]{:S(2)}, u32[]{:S(2)}) %collective-permute-start.4) | collective-permute-done | bytes 327712 | tf_op jit(solution)/shard_map/ppermute | solution.py:460
  63.0 1.6 %grids.1 = (bf16[528,128]{1,0:T(8,128)(2,1)S(1)}, bf16[528,128]{1,0:T(8,128)(2,1)S(1)}, bf16[528,128]{1,0:T(8,128)(2,1)S(1)}, bf16[528,128]{1,0:T(8,128)(2,1)S(1)}, bf16[512,128]{1,0:T(8,128)(2,1)S(1)}) custom-call(f32[3,256,128]{2,1,0:T(8,128)S(1)} %get-tuple-element.23.own, f32[256,512]{1,0:T(8,128)S(1)} %get-tuple-element.24.own_wide, ...), custom_call_target="tpu_custom_call" | custom-call | flops 1000000000 | bytes 1048576 | tf_op jit(solution)/shard_map/grids/pallas_call | solution.py:471
  64.6 2.8 %collective-permute-start.6 = (bf16[528,128]{1,0:T(8,128)(2,1)S(1)}, bf16[528,128]{1,0:T(8,128)(2,1)S(1)}, u32[]{:S(2)}, u32[]{:S(2)}) collective-permute-start(bf16[528,128]{1,0:T(8,128)(2,1)S(1)} %get-tuple-element.28), channel_id=1, source_target_pairs={{0,128},{32,160},{64,192},{96,224},{128,0},{160,32},{192,64},{224,... | collective-permute-start | bytes 405512 | tf_op jit(solution)/shard_map/ppermute | solution.py:416
  67.4 0.4 collective-permute-start.5
  67.8 2.3 %collective-permute-start.7 = (bf16[528,128]{1,0:T(8,128)(2,1)S(1)}, bf16[528,128]{1,0:T(8,128)(2,1)S(1)}, u32[]{:S(2)}, u32[]{:S(2)}) collective-permute-start(bf16[528,128]{1,0:T(8,128)(2,1)S(1)} %get-tuple-element.32), channel_id=1, source_target_pairs={{0,192},{32,224},{64,0},{96,32},{128,64},{160,96},{192,128},{224,1... | collective-permute-start | bytes 405512 | tf_op jit(solution)/shard_map/ppermute | solution.py:416
  70.1 0.4 first_part.1.first
  70.5 0.0 copy-start.3
  70.5 0.5 collective-permute-done.6.own.refs_2_
  71.0 2.0 %collective-permute-start.10 = (bf16[528,128]{1,0:T(8,128)(2,1)S(1)}, bf16[528,128]{1,0:T(8,128)(2,1)S(1)}, u32[]{:S(2)}, u32[]{:S(2)}) collective-permute-start(bf16[528,128]{1,0:T(8,128)(2,1)S(1)} %collective-permute-done.6.own.refs_2_), channel_id=1, source_target_pairs={{0,32},{32,0},{64,96},{96,64},{128,160},{160,128},{192,224},{224,1... | collective-permute-start | bytes 405512 | tf_op jit(solution)/shard_map/ppermute | solution.py:486
  73.0 1.3 %collective-permute-done.5.refs_1_ = bf16[528,128]{1,0:T(8,128)(2,1)S(1)} collective-permute-done((bf16[528,128]{1,0:T(8,128)(2,1)S(1)}, bf16[528,128]{1,0:T(8,128)(2,1)S(1)}, u32[]{:S(2)}, u32[]{:S(2)}) %collective-permute-start.5) | collective-permute-done | bytes 135200 | tf_op jit(solution)/shard_map/ppermute | solution.py:416
  74.3 1.0 %collective-permute-start.8 = (bf16[528,128]{1,0:T(8,128)(2,1)S(1)}, bf16[528,128]{1,0:T(8,128)(2,1)S(1)}, u32[]{:S(2)}, u32[]{:S(2)}) collective-permute-start(bf16[528,128]{1,0:T(8,128)(2,1)S(1)} %collective-permute-done.5.refs_1_), channel_id=1, source_target_pairs={{0,32},{32,0},{64,96},{96,64},{128,160},{160,128},{192,224},{224,1... | collective-permute-start | bytes 405512 | tf_op jit(solution)/shard_map/ppermute | solution.py:486
  75.3 0.0 collective-permute-done.7.refs_3_
  75.3 0.0 collective-permute-start.9
  75.3 0.0 collective-permute-done.10.rest
  75.3 0.7 own_column.1.refs_6_
  76.0 0.2 collective-permute-done.8.refs_4_
  76.3 0.4 collective-permute-done.9.refs_5_
  76.6 1.9 %image.1 = (f32[512,512]{1,0:T(8,128)}, f32[2,512]{1,0:T(2,128)}) custom-call(bf16[528,128]{1,0:T(8,128)(2,1)S(1)} %get-tuple-element.26.own.refs_0_, bf16[528,128]{1,0:T(8,128)(2,1)S(1)} %collective-permute-done.5.refs_1_, bf16[528,128]{1,0:T(8,128)(2,1)S(1)} %collective-permute-done.6.own.refs_2_, bf16[528,128]{1,0:T(8,128)(2,1)S(1)} %collective-permute-done.7.refs_3_, ...), custom_call_target="tpu_custom_call" | custom-call | flops 1000000000 | bytes 1048576 | tf_op jit(solution)/shard_map/image/pallas_call | solution.py:490
  (5 shorter events, 0.0 us)
Async XLA Ops:
  0.6 5.7 %copy-start.6 = (s32[2]{0:T(128)S(1)}, s32[2]{0:T(128)}, u32[]{:S(2)}) copy-start(s32[2]{0:T(128)} %offsets_col.1) | copy-start | bytes 28
  0.6 5.7 %copy-start.4 = (bf16[512,512]{1,0:T(8,128)(2,1)S(1)}, bf16[512,512]{1,0:T(8,128)(2,1)}, u32[]{:S(2)}) copy-start(bf16[512,512]{1,0:T(8,128)(2,1)} %facet.3) | copy-start | bytes 1572868
  0.7 5.7 %copy-start.5 = (s32[2]{0:T(128)S(1)}, s32[2]{0:T(128)}, u32[]{:S(2)}) copy-start(s32[2]{0:T(128)} %offsets_row.1) | copy-start | bytes 28
  3.0 5.3 %copy-start.2 = (bf16[16,256]{1,0:T(8,128)(2,1)S(1)}, bf16[16,256]{1,0:T(8,128)(2,1)}, u32[]{:S(2)}) copy-start(bf16[16,256]{1,0:T(8,128)(2,1)} %get-tuple-element.19.own_vis) | copy-start | bytes 24580
  3.0 5.2 %collective-permute-start = (bf16[528,512]{1,0:T(8,128)(2,1)}, bf16[528,512]{1,0:T(8,128)(2,1)S(1)}, u32[]{:S(2)}, u32[]{:S(2)}) collective-permute-start(bf16[528,512]{1,0:T(8,128)(2,1)} %get-tuple-element.20), channel_id=1, source_target_pairs={{0,32},{32,0},{64,96},{96,64},{128,160},{160,128},{192,224},{224,1... | collective-permute-start | bytes 1622024 | tf_op jit(solution)/shard_map/ppermute | solution.py:433
  8.7 6.9 %collective-permute-start.3 = (bf16[576,128]{1,0:T(8,128)(2,1)S(1)}, bf16[576,128]{1,0:T(8,128)(2,1)S(1)}, u32[]{:S(2)}, u32[]{:S(2)}) collective-permute-start(bf16[576,128]{1,0:T(8,128)(2,1)S(1)} %contribution.7), channel_id=1, source_target_pairs={{0,128},{32,160},{64,192},{96,224},{128,0},{160,32},{192,64},{224,... | collective-permute-start | bytes 442376 | tf_op jit(solution)/shard_map/ppermute | solution.py:416
  10.3 6.8 %collective-permute-start.2 = (bf16[576,128]{1,0:T(8,128)(2,1)S(1)}, bf16[576,128]{1,0:T(8,128)(2,1)S(1)}, u32[]{:S(2)}, u32[]{:S(2)}) collective-permute-start(bf16[576,128]{1,0:T(8,128)(2,1)S(1)} %contribution.5), channel_id=1, source_target_pairs={{0,192},{32,224},{64,0},{96,32},{128,64},{160,96},{192,128},{224,1... | collective-permute-start | bytes 442376 | tf_op jit(solution)/shard_map/ppermute | solution.py:416
  11.7 7.1 %collective-permute-start.1 = (bf16[576,128]{1,0:T(8,128)(2,1)S(1)}, bf16[576,128]{1,0:T(8,128)(2,1)S(1)}, u32[]{:S(2)}, u32[]{:S(2)}) collective-permute-start(bf16[576,128]{1,0:T(8,128)(2,1)S(1)} %contribution.4), channel_id=1, source_target_pairs={{0,64},{32,96},{64,128},{96,160},{128,192},{160,224},{192,0},{224,... | collective-permute-start | bytes 442376 | tf_op jit(solution)/shard_map/ppermute | solution.py:416
  18.7 43.0 %copy-start = (bf16[512,512]{1,0:T(8,128)(2,1)S(1)}, bf16[512,512]{1,0:T(8,128)(2,1)}, u32[]{:S(2)}) copy-start(bf16[512,512]{1,0:T(8,128)(2,1)} %constant.4.clone.forward.refs_5_.refs_6_) | copy-start | bytes 1572868
  40.2 22.8 %copy-start.1 = (bf16[512,512]{1,0:T(8,128)(2,1)S(1)}, bf16[512,512]{1,0:T(8,128)(2,1)}, u32[]{:S(2)}) copy-start(bf16[512,512]{1,0:T(8,128)(2,1)} %constant.5.clone.refs_4_.refs_7_) | copy-start | bytes 1572868
  57.1 5.9 %collective-permute-start.4 = (bf16[32,40,128]{2,1,0:T(8,128)(2,1)S(1)}, bf16[32,40,128]{2,1,0:T(8,128)(2,1)S(1)}, u32[]{:S(2)}, u32[]{:S(2)}) collective-permute-start(bf16[32,40,128]{2,1,0:T(8,128)(2,1)S(1)} %all_to_all.11.pieces), channel_id=1, source_target_pairs={{0,32},{32,0},{64,96},{96,64},{128,160},{160,128},{192,224},{224,1... | collective-permute-start | bytes 983048 | tf_op jit(solution)/shard_map/ppermute | solution.py:460
  64.6 6.4 %collective-permute-start.6 = (bf16[528,128]{1,0:T(8,128)(2,1)S(1)}, bf16[528,128]{1,0:T(8,128)(2,1)S(1)}, u32[]{:S(2)}, u32[]{:S(2)}) collective-permute-start(bf16[528,128]{1,0:T(8,128)(2,1)S(1)} %get-tuple-element.28), channel_id=1, source_target_pairs={{0,128},{32,160},{64,192},{96,224},{128,0},{160,32},{192,64},{224,... | collective-permute-start | bytes 405512 | tf_op jit(solution)/shard_map/ppermute | solution.py:416
  67.4 6.9 %collective-permute-start.5 = (bf16[528,128]{1,0:T(8,128)(2,1)S(1)}, bf16[528,128]{1,0:T(8,128)(2,1)S(1)}, u32[]{:S(2)}, u32[]{:S(2)}) collective-permute-start(bf16[528,128]{1,0:T(8,128)(2,1)S(1)} %get-tuple-element.27), channel_id=1, source_target_pairs={{0,64},{32,96},{64,128},{96,160},{128,192},{160,224},{192,0},{224,... | collective-permute-start | bytes 405512 | tf_op jit(solution)/shard_map/ppermute | solution.py:416
  67.8 7.5 %collective-permute-start.7 = (bf16[528,128]{1,0:T(8,128)(2,1)S(1)}, bf16[528,128]{1,0:T(8,128)(2,1)S(1)}, u32[]{:S(2)}, u32[]{:S(2)}) collective-permute-start(bf16[528,128]{1,0:T(8,128)(2,1)S(1)} %get-tuple-element.32), channel_id=1, source_target_pairs={{0,192},{32,224},{64,0},{96,32},{128,64},{160,96},{192,128},{224,1... | collective-permute-start | bytes 405512 | tf_op jit(solution)/shard_map/ppermute | solution.py:416
  70.5 6.1 %copy-start.3 = (f32[2,512]{1,0:T(2,128)S(1)}, f32[2,512]{1,0:T(2,128)}, u32[]{:S(2)}) copy-start(f32[2,512]{1,0:T(2,128)} %refs_9_.1) | copy-start | bytes 12292
  71.0 4.3 %collective-permute-start.10 = (bf16[528,128]{1,0:T(8,128)(2,1)S(1)}, bf16[528,128]{1,0:T(8,128)(2,1)S(1)}, u32[]{:S(2)}, u32[]{:S(2)}) collective-permute-start(bf16[528,128]{1,0:T(8,128)(2,1)S(1)} %collective-permute-done.6.own.refs_2_), channel_id=1, source_target_pairs={{0,32},{32,0},{64,96},{96,64},{128,160},{160,128},{192,224},{224,1... | collective-permute-start | bytes 405512 | tf_op jit(solution)/shard_map/ppermute | solution.py:486
  74.3 2.0 %collective-permute-start.8 = (bf16[528,128]{1,0:T(8,128)(2,1)S(1)}, bf16[528,128]{1,0:T(8,128)(2,1)S(1)}, u32[]{:S(2)}, u32[]{:S(2)}) collective-permute-start(bf16[528,128]{1,0:T(8,128)(2,1)S(1)} %collective-permute-done.5.refs_1_), channel_id=1, source_target_pairs={{0,32},{32,0},{64,96},{96,64},{128,160},{160,128},{192,224},{224,1... | collective-permute-start | bytes 405512 | tf_op jit(solution)/shard_map/ppermute | solution.py:486
  75.3 1.4 %collective-permute-start.9 = (bf16[528,128]{1,0:T(8,128)(2,1)S(1)}, bf16[528,128]{1,0:T(8,128)(2,1)S(1)}, u32[]{:S(2)}, u32[]{:S(2)}) collective-permute-start(bf16[528,128]{1,0:T(8,128)(2,1)S(1)} %collective-permute-done.7.refs_3_), channel_id=1, source_target_pairs={{0,32},{32,0},{64,96},{96,64},{128,160},{160,128},{192,224},{224,1... | collective-permute-start | bytes 405512 | tf_op jit(solution)/shard_map/ppermute | solution.py:486

commit v17 on v15

--- a/solution.py
+++ b/solution.py
@@ -490,7 +490,7 @@
     return call(
         functools.partial(image_kernel, scale_out, chips), (square, shape(2, n_vis, dtype=f32)), "image",
         "v" * (chips + 6), outs="aa",
-        scratch=[both, pltpu.VMEM((side, side), f32), pltpu.VMEM((2, n_vis), f32), pltpu.SemaphoreType.DMA((5,))],
+        scratch=[both, pltpu.VMEM((side, side), f32), pltpu.VMEM((2, n_vis), f32), pltpu.SemaphoreType.DMA((3,))],
         cost=10**9,
     )(*back, rest[1], rest[3], first, back_row, back_col, observed)
 

time: 78.9 us -> 78.9 us (level)
  no operation moved by 1% of the time
where the time goes in v17:
time: 78.9 us; the launch traced here: 78.8 us
  blocking collectives  37.5 us (48%)
  starting transfers between devices  19.1 us (24%)
  Pallas kernels  14.2 us (18%)
  waiting for transfers between devices  6.93 us (9%)
  between operations  0.96 us (1%)
    all_to_all x2, blocking collectives, exchange(): lax.all_to_all(blocks, axes, 0, 0, tiled=True, axis_index_groups=groups)  37.5 us
    ppermute x6, starting transfers between devices, turned(): moved = {k: lax.ppermute(blocks[k], 'frow', turns[k]) for k in (2, 1, 3)}  8.16 us
    ppermute x6, waiting for transfers between devices, turned(): moved = {k: lax.ppermute(blocks[k], 'frow', turns[k]) for k in (2, 1, 3)}  5.51 us
    ppermute x1, starting transfers between devices, shards(): pieces_other = lax.ppermute(pieces, 'frow', swap)  4.69 us
    ppermute x1, starting transfers between devices, shards(): other = lax.ppermute(send, 'frow', swap)  3.32 us
    ppermute x3, starting transfers between devices, shards(): rest = {k: lax.ppermute(back[k], 'frow', swap) for k in (2, 1, 3)}  2.97 us
    pallas_call x1, Pallas kernels, shards(): call(functools.partial(send_columns_kernel, cols_count), (shape(side + 16...  2.34 us
    pallas_call x1, Pallas kernels, shards(): call(functools.partial(image_kernel, scale_out, chips), (square, shape(2,...  1.95 us
  transfers between devices with their start and end apart: 11, of which 8 were waited for; matrix products, arithmetic and copies ran while one was open for 0% of the time, Pallas kernels for 9%

profile of v17, /device:TPU:1, one launch (start us, length us, event | category | flops | bytes accessed | tf_op | source)
XLA Modules:
  0.0 78.8 jit_solution(17810680361757849246)
XLA Ops:
  0.6 0.0 copy-start.6
  0.6 0.0 copy-start.4
  0.7 0.0 copy-start.5
  0.7 2.3 %send_columns.1 = (bf16[528,512]{1,0:T(8,128)(2,1)}, bf16[16,256]{1,0:T(8,128)(2,1)}) custom-call(s32[2]{0:T(128)} %offsets_col.1, bf16[512,512]{1,0:T(8,128)(2,1)} %facet.3, s32[1,512]{1,0:T(1,128)} %bitcast.3, s32[1,512]{1,0:T(1,128)} %bitcast.4, s32[1,512]{1,0:T(1,128)} %bitcast.5, f32[2,512]{1,0:T(2,128)} %refs_9_.1), custom_call_target="tpu_custom_call" | custom-call | flops 1000000000 | bytes 1048576 | tf_op jit(solution)/shard_map/send_columns/pallas_call | solution.py:423
  3.0 0.0 copy-start.2
  3.0 3.3 %collective-permute-start = (bf16[528,512]{1,0:T(8,128)(2,1)}, bf16[528,512]{1,0:T(8,128)(2,1)S(1)}, u32[]{:S(2)}, u32[]{:S(2)}) collective-permute-start(bf16[528,512]{1,0:T(8,128)(2,1)} %get-tuple-element.20), channel_id=1, source_target_pairs={{0,32},{32,0},{64,96},{96,64},{128,160},{160,128},{192,224},{224,1... | collective-permute-start | bytes 1622024 | tf_op jit(solution)/shard_map/ppermute | solution.py:433
  6.3 0.0 copy-done.6
  6.3 0.0 copy-done.4
  6.3 0.0 copy-done.5
  6.3 1.9 %own_tables.1 = (bf16[512,512]{1,0:T(8,128)(2,1)S(1)}, bf16[4,256,1024]{2,1,0:T(8,128)(2,1)S(1)}) custom-call(s32[2]{0:T(128)S(1)} %copy-done.5, s32[2]{0:T(128)S(1)} %copy-done.6, bf16[512,512]{1,0:T(8,128)(2,1)S(1)} %copy-done.4), custom_call_target="tpu_custom_call" | custom-call | flops 1000000000 | bytes 1048576 | tf_op jit(solution)/shard_map/own_tables/pallas_call | solution.py:434
  8.3 0.0 collective-permute-done.other
  8.3 0.5 contribution.7
  8.7 1.1 %collective-permute-start.3 = (bf16[576,128]{1,0:T(8,128)(2,1)S(1)}, bf16[576,128]{1,0:T(8,128)(2,1)S(1)}, u32[]{:S(2)}, u32[]{:S(2)}) collective-permute-start(bf16[576,128]{1,0:T(8,128)(2,1)S(1)} %contribution.7), channel_id=1, source_target_pairs={{0,128},{32,160},{64,192},{96,224},{128,0},{160,32},{192,64},{224,... | collective-permute-start | bytes 442376 | tf_op jit(solution)/shard_map/ppermute | solution.py:416
  9.8 0.4 contribution.5
  10.3 0.9 %collective-permute-start.2 = (bf16[576,128]{1,0:T(8,128)(2,1)S(1)}, bf16[576,128]{1,0:T(8,128)(2,1)S(1)}, u32[]{:S(2)}, u32[]{:S(2)}) collective-permute-start(bf16[576,128]{1,0:T(8,128)(2,1)S(1)} %contribution.5), channel_id=1, source_target_pairs={{0,192},{32,224},{64,0},{96,32},{128,64},{160,96},{192,128},{224,1... | collective-permute-start | bytes 442376 | tf_op jit(solution)/shard_map/ppermute | solution.py:416
  11.2 0.4 contribution.4
  11.7 0.7 collective-permute-start.1
  12.3 1.4 %back_tables.1 = (bf16[512,1024]{1,0:T(8,128)(2,1)S(1)}, bf16[1024,512]{1,0:T(8,128)(2,1)S(1)}) custom-call(s32[2]{0:T(128)S(1)} %copy-done.5, s32[2]{0:T(128)S(1)} %copy-done.6), custom_call_target="tpu_custom_call" | custom-call | flops 1000000000 | bytes 1048576 | tf_op jit(solution)/shard_map/back_tables/pallas_call | solution.py:449
  13.7 0.5 contribution.6.refs_0_
  14.2 1.4 %collective-permute-done.3.refs_1_.refs_2_ = bf16[576,128]{1,0:T(8,128)(2,1)S(1)} collective-permute-done((bf16[576,128]{1,0:T(8,128)(2,1)S(1)}, bf16[576,128]{1,0:T(8,128)(2,1)S(1)}, u32[]{:S(2)}, u32[]{:S(2)}) %collective-permute-start.3) | collective-permute-done | bytes 147488 | tf_op jit(solution)/shard_map/ppermute | solution.py:416
  15.6 0.8 first_sums.1.refs_2_
  16.4 0.7 collective-permute-done.2.refs_1_.refs_3_
  17.1 1.6 %collective-permute-done.1.refs_0_.refs_1_ = bf16[576,128]{1,0:T(8,128)(2,1)S(1)} collective-permute-done((bf16[576,128]{1,0:T(8,128)(2,1)S(1)}, bf16[576,128]{1,0:T(8,128)(2,1)S(1)}, u32[]{:S(2)}, u32[]{:S(2)}) %collective-permute-start.1) | collective-permute-done | bytes 147488 | tf_op jit(solution)/shard_map/ppermute | solution.py:416
  18.7 0.8 gridding.1
  19.5 20.6 %all_to_all.10.pieces = bf16[32,40,128]{2,1,0:T(8,128)(2,1)S(1)} all-to-all(bf16[32,40,128]{2,1,0:T(8,128)(2,1)S(1)} %gridding.1), channel_id=1, replica_groups=mesh['frow'=8,'fcol'=32] {'fcol'}, dimensions={0} | all-to-all | bytes 655360 | tf_op jit(solution)/shard_map/all_to_all | solution.py:398
  40.1 0.1 pieces_sum.1
  40.2 0.0 copy-start.1
  40.2 16.9 %all_to_all.11.pieces = bf16[32,40,128]{2,1,0:T(8,128)(2,1)S(1)} all-to-all(bf16[32,40,128]{2,1,0:T(8,128)(2,1)S(1)} %pieces_sum.1), channel_id=1, replica_groups=mesh['frow'=8,'fcol'=32] {'fcol'}, dimensions={0} | all-to-all | bytes 655360 | tf_op jit(solution)/shard_map/all_to_all | solution.py:398
  57.1 4.7 %collective-permute-start.4 = (bf16[32,40,128]{2,1,0:T(8,128)(2,1)S(1)}, bf16[32,40,128]{2,1,0:T(8,128)(2,1)S(1)}, u32[]{:S(2)}, u32[]{:S(2)}) collective-permute-start(bf16[32,40,128]{2,1,0:T(8,128)(2,1)S(1)} %all_to_all.11.pieces), channel_id=1, source_target_pairs={{0,32},{32,0},{64,96},{96,64},{128,160},{160,128},{192,224},{224,1... | collective-permute-start | bytes 983048 | tf_op jit(solution)/shard_map/ppermute | solution.py:460
  61.8 0.4 own_half.1
  62.2 0.8 %collective-permute-done.4.other = bf16[32,40,128]{2,1,0:T(8,128)(2,1)S(1)} collective-permute-done((bf16[32,40,128]{2,1,0:T(8,128)(2,1)S(1)}, bf16[32,40,128]{2,1,0:T(8,128)(2,1)S(1)}, u32[]{:S(2)}, u32[]{:S(2)}) %collective-permute-start.4) | collective-permute-done | bytes 327712 | tf_op jit(solution)/shard_map/ppermute | solution.py:460
  63.0 1.6 %grids.1 = (bf16[528,128]{1,0:T(8,128)(2,1)S(1)}, bf16[528,128]{1,0:T(8,128)(2,1)S(1)}, bf16[528,128]{1,0:T(8,128)(2,1)S(1)}, bf16[528,128]{1,0:T(8,128)(2,1)S(1)}, bf16[512,128]{1,0:T(8,128)(2,1)S(1)}) custom-call(f32[3,256,128]{2,1,0:T(8,128)S(1)} %get-tuple-element.23.own, f32[256,512]{1,0:T(8,128)S(1)} %get-tuple-element.24.own_wide, ...), custom_call_target="tpu_custom_call" | custom-call | flops 1000000000 | bytes 1048576 | tf_op jit(solution)/shard_map/grids/pallas_call | solution.py:471
  64.6 2.8 %collective-permute-start.6 = (bf16[528,128]{1,0:T(8,128)(2,1)S(1)}, bf16[528,128]{1,0:T(8,128)(2,1)S(1)}, u32[]{:S(2)}, u32[]{:S(2)}) collective-permute-start(bf16[528,128]{1,0:T(8,128)(2,1)S(1)} %get-tuple-element.28), channel_id=1, source_target_pairs={{0,128},{32,160},{64,192},{96,224},{128,0},{160,32},{192,64},{224,... | collective-permute-start | bytes 405512 | tf_op jit(solution)/shard_map/ppermute | solution.py:416
  67.4 0.4 collective-permute-start.5
  67.8 2.3 %collective-permute-start.7 = (bf16[528,128]{1,0:T(8,128)(2,1)S(1)}, bf16[528,128]{1,0:T(8,128)(2,1)S(1)}, u32[]{:S(2)}, u32[]{:S(2)}) collective-permute-start(bf16[528,128]{1,0:T(8,128)(2,1)S(1)} %get-tuple-element.32), channel_id=1, source_target_pairs={{0,192},{32,224},{64,0},{96,32},{128,64},{160,96},{192,128},{224,1... | collective-permute-start | bytes 405512 | tf_op jit(solution)/shard_map/ppermute | solution.py:416
  70.1 0.4 first_part.1.first
  70.5 0.0 copy-start.3
  70.5 0.5 collective-permute-done.6.own.refs_2_
  71.0 2.0 %collective-permute-start.10 = (bf16[528,128]{1,0:T(8,128)(2,1)S(1)}, bf16[528,128]{1,0:T(8,128)(2,1)S(1)}, u32[]{:S(2)}, u32[]{:S(2)}) collective-permute-start(bf16[528,128]{1,0:T(8,128)(2,1)S(1)} %collective-permute-done.6.own.refs_2_), channel_id=1, source_target_pairs={{0,32},{32,0},{64,96},{96,64},{128,160},{160,128},{192,224},{224,1... | collective-permute-start | bytes 405512 | tf_op jit(solution)/shard_map/ppermute | solution.py:486
  73.0 1.3 %collective-permute-done.5.refs_1_ = bf16[528,128]{1,0:T(8,128)(2,1)S(1)} collective-permute-done((bf16[528,128]{1,0:T(8,128)(2,1)S(1)}, bf16[528,128]{1,0:T(8,128)(2,1)S(1)}, u32[]{:S(2)}, u32[]{:S(2)}) %collective-permute-start.5) | collective-permute-done | bytes 135200 | tf_op jit(solution)/shard_map/ppermute | solution.py:416
  74.3 1.0 %collective-permute-start.8 = (bf16[528,128]{1,0:T(8,128)(2,1)S(1)}, bf16[528,128]{1,0:T(8,128)(2,1)S(1)}, u32[]{:S(2)}, u32[]{:S(2)}) collective-permute-start(bf16[528,128]{1,0:T(8,128)(2,1)S(1)} %collective-permute-done.5.refs_1_), channel_id=1, source_target_pairs={{0,32},{32,0},{64,96},{96,64},{128,160},{160,128},{192,224},{224,1... | collective-permute-start | bytes 405512 | tf_op jit(solution)/shard_map/ppermute | solution.py:486
  75.3 0.0 collective-permute-done.7.refs_3_
  75.3 0.0 collective-permute-start.9
  75.3 0.0 collective-permute-done.10.rest
  75.3 0.7 own_column.1.refs_6_
  76.0 0.2 collective-permute-done.8.refs_4_
  76.3 0.4 collective-permute-done.9.refs_5_
  76.6 2.0 %image.1 = (f32[512,512]{1,0:T(8,128)}, f32[2,512]{1,0:T(2,128)}) custom-call(bf16[528,128]{1,0:T(8,128)(2,1)S(1)} %get-tuple-element.26.own.refs_0_, bf16[528,128]{1,0:T(8,128)(2,1)S(1)} %collective-permute-done.5.refs_1_, bf16[528,128]{1,0:T(8,128)(2,1)S(1)} %collective-permute-done.6.own.refs_2_, bf16[528,128]{1,0:T(8,128)(2,1)S(1)} %collective-permute-done.7.refs_3_, ...), custom_call_target="tpu_custom_call" | custom-call | flops 1000000000 | bytes 1048576 | tf_op jit(solution)/shard_map/image/pallas_call | solution.py:490
  (5 shorter events, 0.0 us)
Async XLA Ops:
  0.6 5.7 %copy-start.6 = (s32[2]{0:T(128)S(1)}, s32[2]{0:T(128)}, u32[]{:S(2)}) copy-start(s32[2]{0:T(128)} %offsets_col.1) | copy-start | bytes 28
  0.6 5.7 %copy-start.4 = (bf16[512,512]{1,0:T(8,128)(2,1)S(1)}, bf16[512,512]{1,0:T(8,128)(2,1)}, u32[]{:S(2)}) copy-start(bf16[512,512]{1,0:T(8,128)(2,1)} %facet.3) | copy-start | bytes 1572868
  0.7 5.7 %copy-start.5 = (s32[2]{0:T(128)S(1)}, s32[2]{0:T(128)}, u32[]{:S(2)}) copy-start(s32[2]{0:T(128)} %offsets_row.1) | copy-start | bytes 28
  3.0 5.3 %copy-start.2 = (bf16[16,256]{1,0:T(8,128)(2,1)S(1)}, bf16[16,256]{1,0:T(8,128)(2,1)}, u32[]{:S(2)}) copy-start(bf16[16,256]{1,0:T(8,128)(2,1)} %get-tuple-element.19.own_vis) | copy-start | bytes 24580
  3.0 5.2 %collective-permute-start = (bf16[528,512]{1,0:T(8,128)(2,1)}, bf16[528,512]{1,0:T(8,128)(2,1)S(1)}, u32[]{:S(2)}, u32[]{:S(2)}) collective-permute-start(bf16[528,512]{1,0:T(8,128)(2,1)} %get-tuple-element.20), channel_id=1, source_target_pairs={{0,32},{32,0},{64,96},{96,64},{128,160},{160,128},{192,224},{224,1... | collective-permute-start | bytes 1622024 | tf_op jit(solution)/shard_map/ppermute | solution.py:433
  8.7 6.9 %collective-permute-start.3 = (bf16[576,128]{1,0:T(8,128)(2,1)S(1)}, bf16[576,128]{1,0:T(8,128)(2,1)S(1)}, u32[]{:S(2)}, u32[]{:S(2)}) collective-permute-start(bf16[576,128]{1,0:T(8,128)(2,1)S(1)} %contribution.7), channel_id=1, source_target_pairs={{0,128},{32,160},{64,192},{96,224},{128,0},{160,32},{192,64},{224,... | collective-permute-start | bytes 442376 | tf_op jit(solution)/shard_map/ppermute | solution.py:416
  10.3 6.8 %collective-permute-start.2 = (bf16[576,128]{1,0:T(8,128)(2,1)S(1)}, bf16[576,128]{1,0:T(8,128)(2,1)S(1)}, u32[]{:S(2)}, u32[]{:S(2)}) collective-permute-start(bf16[576,128]{1,0:T(8,128)(2,1)S(1)} %contribution.5), channel_id=1, source_target_pairs={{0,192},{32,224},{64,0},{96,32},{128,64},{160,96},{192,128},{224,1... | collective-permute-start | bytes 442376 | tf_op jit(solution)/shard_map/ppermute | solution.py:416
  11.7 7.1 %collective-permute-start.1 = (bf16[576,128]{1,0:T(8,128)(2,1)S(1)}, bf16[576,128]{1,0:T(8,128)(2,1)S(1)}, u32[]{:S(2)}, u32[]{:S(2)}) collective-permute-start(bf16[576,128]{1,0:T(8,128)(2,1)S(1)} %contribution.4), channel_id=1, source_target_pairs={{0,64},{32,96},{64,128},{96,160},{128,192},{160,224},{192,0},{224,... | collective-permute-start | bytes 442376 | tf_op jit(solution)/shard_map/ppermute | solution.py:416
  18.7 43.0 %copy-start = (bf16[512,512]{1,0:T(8,128)(2,1)S(1)}, bf16[512,512]{1,0:T(8,128)(2,1)}, u32[]{:S(2)}) copy-start(bf16[512,512]{1,0:T(8,128)(2,1)} %constant.4.clone.forward.refs_5_.refs_6_) | copy-start | bytes 1572868
  40.2 22.8 %copy-start.1 = (bf16[512,512]{1,0:T(8,128)(2,1)S(1)}, bf16[512,512]{1,0:T(8,128)(2,1)}, u32[]{:S(2)}) copy-start(bf16[512,512]{1,0:T(8,128)(2,1)} %constant.5.clone.refs_4_.refs_7_) | copy-start | bytes 1572868
  57.1 5.9 %collective-permute-start.4 = (bf16[32,40,128]{2,1,0:T(8,128)(2,1)S(1)}, bf16[32,40,128]{2,1,0:T(8,128)(2,1)S(1)}, u32[]{:S(2)}, u32[]{:S(2)}) collective-permute-start(bf16[32,40,128]{2,1,0:T(8,128)(2,1)S(1)} %all_to_all.11.pieces), channel_id=1, source_target_pairs={{0,32},{32,0},{64,96},{96,64},{128,160},{160,128},{192,224},{224,1... | collective-permute-start | bytes 983048 | tf_op jit(solution)/shard_map/ppermute | solution.py:460
  64.6 6.4 %collective-permute-start.6 = (bf16[528,128]{1,0:T(8,128)(2,1)S(1)}, bf16[528,128]{1,0:T(8,128)(2,1)S(1)}, u32[]{:S(2)}, u32[]{:S(2)}) collective-permute-start(bf16[528,128]{1,0:T(8,128)(2,1)S(1)} %get-tuple-element.28), channel_id=1, source_target_pairs={{0,128},{32,160},{64,192},{96,224},{128,0},{160,32},{192,64},{224,... | collective-permute-start | bytes 405512 | tf_op jit(solution)/shard_map/ppermute | solution.py:416
  67.4 6.9 %collective-permute-start.5 = (bf16[528,128]{1,0:T(8,128)(2,1)S(1)}, bf16[528,128]{1,0:T(8,128)(2,1)S(1)}, u32[]{:S(2)}, u32[]{:S(2)}) collective-permute-start(bf16[528,128]{1,0:T(8,128)(2,1)S(1)} %get-tuple-element.27), channel_id=1, source_target_pairs={{0,64},{32,96},{64,128},{96,160},{128,192},{160,224},{192,0},{224,... | collective-permute-start | bytes 405512 | tf_op jit(solution)/shard_map/ppermute | solution.py:416
  67.8 7.5 %collective-permute-start.7 = (bf16[528,128]{1,0:T(8,128)(2,1)S(1)}, bf16[528,128]{1,0:T(8,128)(2,1)S(1)}, u32[]{:S(2)}, u32[]{:S(2)}) collective-permute-start(bf16[528,128]{1,0:T(8,128)(2,1)S(1)} %get-tuple-element.32), channel_id=1, source_target_pairs={{0,192},{32,224},{64,0},{96,32},{128,64},{160,96},{192,128},{224,1... | collective-permute-start | bytes 405512 | tf_op jit(solution)/shard_map/ppermute | solution.py:416
  70.5 6.1 %copy-start.3 = (f32[2,512]{1,0:T(2,128)S(1)}, f32[2,512]{1,0:T(2,128)}, u32[]{:S(2)}) copy-start(f32[2,512]{1,0:T(2,128)} %refs_9_.1) | copy-start | bytes 12292
  71.0 4.3 %collective-permute-start.10 = (bf16[528,128]{1,0:T(8,128)(2,1)S(1)}, bf16[528,128]{1,0:T(8,128)(2,1)S(1)}, u32[]{:S(2)}, u32[]{:S(2)}) collective-permute-start(bf16[528,128]{1,0:T(8,128)(2,1)S(1)} %collective-permute-done.6.own.refs_2_), channel_id=1, source_target_pairs={{0,32},{32,0},{64,96},{96,64},{128,160},{160,128},{192,224},{224,1... | collective-permute-start | bytes 405512 | tf_op jit(solution)/shard_map/ppermute | solution.py:486
  74.3 2.0 %collective-permute-start.8 = (bf16[528,128]{1,0:T(8,128)(2,1)S(1)}, bf16[528,128]{1,0:T(8,128)(2,1)S(1)}, u32[]{:S(2)}, u32[]{:S(2)}) collective-permute-start(bf16[528,128]{1,0:T(8,128)(2,1)S(1)} %collective-permute-done.5.refs_1_), channel_id=1, source_target_pairs={{0,32},{32,0},{64,96},{96,64},{128,160},{160,128},{192,224},{224,1... | collective-permute-start | bytes 405512 | tf_op jit(solution)/shard_map/ppermute | solution.py:486
  75.3 1.4 %collective-permute-start.9 = (bf16[528,128]{1,0:T(8,128)(2,1)S(1)}, bf16[528,128]{1,0:T(8,128)(2,1)S(1)}, u32[]{:S(2)}, u32[]{:S(2)}) collective-permute-start(bf16[528,128]{1,0:T(8,128)(2,1)S(1)} %collective-permute-done.7.refs_3_), channel_id=1, source_target_pairs={{0,32},{32,0},{64,96},{96,64},{128,160},{160,128},{192,224},{224,1... | collective-permute-start | bytes 405512 | tf_op jit(solution)/shard_map/ppermute | solution.py:486
